TPU v7x, 32 devices: a whole 2x2x4 slice. The times are simulated.
32 devices in a mesh: phi: 2 (over x), row: 4 (over y, core), mass: 4 (over z).
Axes of the slice: x: 2, y: 2, z: 4, core: 2. Of those that a mesh axis runs over, the one named last changes fastest.
Arguments:
- density: float32 [256, 64, 512], P('mass', 'phi', 'row'), may hold values from 0.05 to 1
- cotangent: float32 [256, 64, 512], P('mass', 'phi', 'row'), may hold values from -6 to 6
- drift_in: float32 [256, 512], P('mass'), may hold values from 0.02 to 0.3
- drift_out: float32 [256, 512], P('mass'), may hold values from 0.02 to 0.3
- spread: float32 [256], P('mass'), may hold values from 0.01 to 0.15
- dest_bins: int32 [256], replicated, may hold values from 1 to 254, as said below
- bott_split: float32 [256], replicated, may hold values from 0.05 to 0.95
- coag_rate: float32 [256], replicated, may hold values from 0.05 to 0.3
- frag_pairs: int32 [4, 4], replicated, may hold values from 0 to 1, as said below
- frag_gain: float32 [256, 256], replicated, may hold values from 0.001 to 0.02
- frag_rate: float32 [256], replicated, may hold values from 0.02 to 0.2
- collide_speed: float32 [64, 512], P('phi', 'row'), may hold values from 0.2 to 5
- frag_speed: float32 [512], P('row'), may hold values from 0.5 to 2
- regime: int32 [64, 512], P('phi', 'row'), may hold values 0 or 1
Outputs:
- density_adjoint: float32 [256, 64, 512], P('mass', 'phi', 'row')
- speed_gradient: float32 [512], P('row')
Inputs may be any that keep to these rules, and one draw needn't show every extreme that they name: dest_bins[j] lies between j + 1 and j + 6, but never above 254; dest_bins[0] is 1 and the top bins map to 254. frag_pairs is 1 on the diagonal and in the first row, 0 below the diagonal.
All inputs are finite; a program needn't handle non-finite values. No bound on the sum of `regime` on one device may be relied on, other than what follows from the above.
Results may differ from a plain program's by a relative error of at most 0.000078.
Values sent between devices are 32-bit elements; how exact they have to be, the bound alone decides.
No kernel may reach another device: no remote copies, remote signals or barrier semaphores. Data moves between devices by JAX's collectives and lax.ppermute only.
A program may use at most 128 MiB of HBM per device.

v0:
```python
import jax
import jax.numpy as jnp
from jax import lax
from jax.sharding import PartitionSpec as P

RANGE = 64


gate_width = 0.5
highest = lax.Precision.HIGHEST
contract_rows = (((0,), (0,)), ((), ()))


def padded_2(value, sides, width):
    for axis, dim in sides:
        count, length = (lax.axis_size(axis), value.shape[dim])
        up = [(i, (i + 1) % count) for i in range(count)]
        down = [(j, i) for i, j in up]
        last = lax.slice_in_dim(value, length - width, length, axis=dim)
        initial = lax.slice_in_dim(value, 0, width, axis=dim)
        before = lax.ppermute(last, axis, up)
        after = lax.ppermute(initial, axis, down)
        value = jnp.concatenate([before, value, after], axis=dim)
    return value


def coag_matrix(dest_bins, bott_split, coag_rate):
    number = dest_bins.shape[0]
    row_ids = jnp.arange(number, dtype=jnp.int32)[:, None]
    col_ids = jnp.arange(number, dtype=jnp.int32)[None, :]
    target = dest_bins[None, :]
    lower_part = (row_ids == target).astype(jnp.float32) * (1.0 - bott_split)[None, :]
    upper_part = (row_ids == target + 1).astype(jnp.float32) * bott_split[None, :]
    keeper = (row_ids == col_ids).astype(jnp.float32)
    return (lower_part + upper_part - keeper) * coag_rate[None, :]


def frag_matrix(frag_pairs, frag_gain, frag_rate):
    number = frag_gain.shape[0]
    blocks = jnp.repeat(jnp.repeat(frag_pairs, RANGE, axis=0), RANGE, axis=1).astype(jnp.float32)
    row_ids = jnp.arange(number, dtype=jnp.int32)[:, None]
    col_ids = jnp.arange(number, dtype=jnp.int32)[None, :]
    below_diag = (row_ids <= col_ids).astype(jnp.float32)
    keeper = (row_ids == col_ids).astype(jnp.float32)
    return frag_gain * blocks * below_diag - keeper * frag_rate[None, :]


def rimmed(field):
    return padded_2(field, (("phi", 1), ("row", 2)), 1)


def matmul(left, right):
    return jnp.dot(left, right, precision=highest, preferred_element_type=jnp.float32)


def tmatmul(left, right):
    return lax.dot_general(
        left, right, contract_rows, precision=highest, preferred_element_type=jnp.float32
    )


def per_device(
    density,
    cotangent,
    drift_in,
    drift_out,
    spread,
    dest_bins,
    bott_split,
    coag_rate,
    frag_pairs,
    frag_gain,
    frag_rate,
    collide_speed,
    frag_speed,
    regime,
):
    own_bins, azimuth, radial = density.shape
    cell_count = azimuth * radial
    first_bin = lax.axis_index("mass") * own_bins
    row_index = lax.axis_index("row")
    radial_total = radial * lax.axis_size("row")
    coag_full = coag_matrix(dest_bins, bott_split, coag_rate)
    frag_full = frag_matrix(frag_pairs, frag_gain, frag_rate)
    coag_cols = lax.dynamic_slice_in_dim(coag_full, first_bin, own_bins, 1)
    frag_cols = lax.dynamic_slice_in_dim(frag_full, first_bin, own_bins, 1)
    coag_rows = lax.dynamic_slice_in_dim(coag_full, first_bin, own_bins, 0)
    frag_rows = lax.dynamic_slice_in_dim(frag_full, first_bin, own_bins, 0)
    in_pad = jnp.pad(drift_in, ((0, 0), (1, 1)))
    out_pad = jnp.pad(drift_out, ((0, 0), (1, 1)))
    in_ext = lax.dynamic_slice_in_dim(in_pad, row_index * radial, radial + 2, 1)
    out_ext = lax.dynamic_slice_in_dim(out_pad, row_index * radial, radial + 2, 1)
    in_local = in_ext[:, 1:-1]
    out_local = out_ext[:, 1:-1]
    global_rad = row_index * radial + jnp.arange(radial, dtype=jnp.int32)
    in_back = in_local * (global_rad >= 1).astype(jnp.float32)[None, :]
    out_back = out_local * (global_rad <= radial_total - 2).astype(jnp.float32)[None, :]
    center = 1.0 - in_local - out_local - 2.0 * spread[:, None]
    sigma = jax.nn.sigmoid((collide_speed - frag_speed[None, :]) / gate_width)
    flagged = regime.astype(jnp.float32)
    frag_gate = flagged * sigma
    gate_slope = -flagged * sigma * (1.0 - sigma) / gate_width

    def forward_move(field):
        padded = rimmed(field)
        beside_all = padded[:, :-2, 1:-1] + padded[:, 2:, 1:-1]
        return (
            center[:, None, :] * field
            + in_ext[:, None, 2:] * padded[:, 1:-1, 2:]
            + out_ext[:, None, :-2] * padded[:, 1:-1, :-2]
            + spread[:, None, None] * beside_all
        )

    def backward_move(field):
        padded = rimmed(field)
        beside_all = padded[:, :-2, 1:-1] + padded[:, 2:, 1:-1]
        return (
            center[:, None, :] * field
            + in_back[:, None, :] * padded[:, 1:-1, :-2]
            + out_back[:, None, :] * padded[:, 1:-1, 2:]
            + spread[:, None, None] * beside_all
        )

    moved_first = forward_move(density)
    flat_moved = moved_first.reshape(own_bins, cell_count)
    flat_gated = (frag_gate[None] * moved_first).reshape(own_bins, cell_count)
    mixed_first = lax.psum_scatter(
        matmul(coag_cols, flat_moved) + matmul(frag_cols, flat_gated),
        "mass",
        scatter_dimension=0,
        tiled=True,
    )
    state_first = moved_first + mixed_first.reshape(own_bins, azimuth, radial)
    moved_second = forward_move(state_first)

    def adjoint_mass(weight):
        flat_weight = weight.reshape(own_bins, cell_count)
        summed = lax.psum_scatter(
            jnp.stack((tmatmul(coag_rows, flat_weight), tmatmul(frag_rows, flat_weight)), axis=1),
            "mass",
            scatter_dimension=0,
            tiled=True,
        )
        coag_back = summed[:, 0]
        frag_back = summed[:, 1]
        return (
            coag_back.reshape(own_bins, azimuth, radial),
            frag_back.reshape(own_bins, azimuth, radial),
        )

    coag_second, frag_second = adjoint_mass(cotangent)
    weight_second = cotangent + (coag_second + frag_gate[None] * frag_second)
    adjoint_first = backward_move(weight_second)
    coag_first, frag_first = adjoint_mass(adjoint_first)
    weight_first = adjoint_first + (coag_first + frag_gate[None] * frag_first)
    density_adjoint = backward_move(weight_first)
    products = jnp.sum(moved_first * frag_first + moved_second * frag_second, axis=0)
    local_sum = jnp.sum(gate_slope * products, axis=0)
    speed_gradient = lax.psum(local_sum, ("phi", "mass"))
    return (density_adjoint, speed_gradient)


def solution(mesh):
    in_specs = (
        P("mass", "phi", "row"),
        P("mass", "phi", "row"),
        P("mass", None),
        P("mass", None),
        P("mass"),
        P(),
        P(),
        P(),
        P(),
        P(),
        P(),
        P("phi", "row"),
        P("row"),
        P("phi", "row"),
    )
    out_specs = (P("mass", "phi", "row"), P("row"))
    return jax.shard_map(
        per_device, mesh=mesh, in_specs=in_specs, out_specs=out_specs, check_vma=False
    )
```

profile of v0, /device:TPU:0, one launch (start us, length us, event | category | flops | bytes accessed | tf_op | source)
XLA Modules:
  0.0 459.8 jit_solution(6868748674762265569)
XLA Ops:
  11.4 5.1 %convolution_bitcast_fusion.2 = f32[256,1,4096]{2,0,1:T(8,128)S(1)} fusion(f32[8,8,32,128]{3,2,1,0:T(8,128)} %bitcast.58, f32[256,256]{0,1:T(8,128)S(1)} %fusion.45, s32[]{:T(128)S(6)} %select_n.5), kind=kOutput, calls=%fused_computation.4 | convolution fusion | flops 805306368 | bytes 5373956 | tf_op jit(solution)/shard_map/dot_general | solution.py:57
  16.8 3.8 convolution_bitcast_fusion.3
  20.6 3.8 pad_maximum_fusion
  24.5 3.0 copy.246
  28.4 2.9 collective-permute-start.9
  46.0 8.9 %broadcast_multiply_fusion = (f32[64,32,128]{0,1,2:T(8,128)}, f32[64,32,128]{0,1,2:T(8,128)S(1)}) fusion(f32[32,128]{0,1:T(8,128)S(1)} %copy.237, f32[64,1,128]{0,1,2:T(1,128)} %copy-done.23, f32[64,32,128]{0,1,2:T(8,128)} %copy-done.6, f32[64,1,128]{0,1,2:T(1,128)} %copy-done.24, f32[64]{0:T(128)} %param.18, f32[64,34,1]{0,1,2:T(8,128)S(1)} %copy.255, ...), kind=kLoop, calls=%fused_computation.85 | loop fusion | flops 4456448 | bytes 3343616 | tf_op jit(solution)/shard_map/mul | solution.py:126
  57.5 3.9 copy.260
  61.4 5.1 %fusion.33 = f32[256,4096]{1,0:T(8,128)S(1)} fusion(f32[8,8,32,128]{3,2,1,0:T(8,128)} %bitcast.68, f32[256,256]{0,1:T(8,128)} %copy-done.11, s32[]{:T(128)S(6)} %select_n.5), kind=kOutput, calls=%fused_computation.74 | convolution fusion | flops 805306368 | bytes 5308420 | tf_op jit(solution)/shard_map/dot_general | solution.py:53
  66.5 5.8 %convolution_add_fusion = f32[256,4096]{1,0:T(8,128)} fusion(f32[256,4096]{1,0:T(8,128)S(1)} %fusion.33, f32[8,8,32,128]{3,2,1,0:T(8,128)S(1)} %bitcast.62, f32[256,256]{0,1:T(8,128)S(1)} %fusion.45, s32[]{:T(128)S(6)} %select_n.5), kind=kOutput, calls=%fused_computation.6 | convolution fusion | flops 806354944 | bytes 9502724 | tf_op jit(solution)/shard_map/dot_general | solution.py:53
  72.6 2.9 copy.240
  75.5 96.2 %reduce-scatter.4.cloned.1.call-done = f32[64,2,4096]{2,0,1:T(8,128)} async-done(((f32[256,2,4096]{2,0,1:T(8,128)}), f32[64,2,4096]{2,0,1:T(8,128)}) %reduce-scatter.4.cloned.1.call-update) | async-done | bytes 2097168 | tf_op jit(solution)/shard_map/reduce_scatter | solution.py:138
  173.7 2.9 copy.239
  176.8 2.9 copy.238
  179.7 4.0 add_add_fusion.1
  186.0 2.8 collective-permute-done.1
  193.9 4.6 fusion.26
  198.4 3.0 copy.243
  201.5 3.8 convolution_bitcast_fusion
  205.3 3.8 convolution_bitcast_fusion.1
  209.0 3.8 pad_maximum_fusion.1
  212.9 38.7 %reduce-scatter.8.cloned.1.call-done = f32[64,4096]{1,0:T(8,128)} async-done(((f32[256,4096]{1,0:T(8,128)}), f32[64,4096]{1,0:T(8,128)}) %reduce-scatter.8.cloned.1.call-update) | async-done | bytes 1048592 | tf_op jit(solution)/shard_map/reduce_scatter | solution.py:127
  253.0 2.9 copy.261
  255.9 2.7 add.142
  260.8 2.8 collective-permute-done.13
  269.3 129.8 %reduce-scatter.6.cloned.1.call-done = f32[64,2,4096]{2,0,1:T(8,128)} async-done(((f32[256,2,4096]{2,0,1:T(8,128)}), f32[64,2,4096]{2,0,1:T(8,128)}) %reduce-scatter.6.cloned.1.call-update) | async-done | bytes 2097168 | tf_op jit(solution)/shard_map/reduce_scatter | solution.py:138
  402.0 2.9 copy.245
  406.4 3.0 copy.244
  409.5 5.9 %add_add_fusion = f32[64,32,128]{0,1,2:T(8,128)S(1)} fusion(f32[64,32,128]{0,1,2:T(8,128)} %copy.245, f32[64,32,128]{0,1,2:T(8,128)} %copy.244, f32[32,128]{0,1:T(8,128)S(1)} %copy.237, f32[64,1,128]{0,1,2:T(1,128)S(1)} %copy-done.18, f32[64,32,128]{0,1,2:T(8,128)S(1)} %add_add_fusion.1, f32[64,1,128]{0,1,2:T(1,128)S(1)} %copy-done.20, f32[64]{0:T(128)} %param.18, ...), kind=kLoop, calls=%fused_computation.70 | loop fusion | flops 4980736 | bytes 4392192 | tf_op jit(solution)/shard_map/add | solution.py:155
  419.1 2.9 fusion.5
  423.3 21.2 %psum.7 = f32[128]{0:T(128)} all-reduce(f32[128]{0:T(128)S(1)} %multiply_reduce_fusion), channel_id=1, replica_groups=mesh['phi'=2,'row'=4,'mass'=4] {'phi','mass'}, use_global_device_ids=true, to_apply=%region_5.6 | all-reduce | flops 128 | bytes 1024 | tf_op jit(solution)/shard_map/psum | solution.py:159
  444.5 4.4 fusion.19
  448.9 3.9 copy.268
  (170 shorter events, 50.1 us)
Async XLA Ops:
  7.2 164.6 %reduce-scatter.4.cloned.1.call-start = ((), (), s32[]{:S(2)}) async-start(), calls=%async_computation.3 | async-start | bytes 10485760 | tf_op jit(solution)/shard_map/reduce_scatter | solution.py:138
  24.5 227.1 %reduce-scatter.8.cloned.1.call-start = ((), (), s32[]{:S(2)}) async-start(), calls=%async_computation.5 | async-start | bytes 5242880 | tf_op jit(solution)/shard_map/reduce_scatter | solution.py:127
  27.5 17.7 %copy-start.6 = (f32[64,32,128]{0,1,2:T(8,128)}, f32[64,32,128]{0,1,2:T(8,128)S(1)}, u32[]{:S(2)}) copy-start(f32[64,32,128]{0,1,2:T(8,128)S(1)} %copy.246) | copy-start | bytes 3145732
  27.6 11.7 %copy-start.35 = (s32[32,128]{1,0:T(8,128)S(1)}, s32[32,128]{1,0:T(8,128)}, u32[]{:S(2)}) copy-start(s32[32,128]{1,0:T(8,128)} %param.27) | copy-start | bytes 49156
  28.4 5.6 %collective-permute-start.9 = (f32[64,1,128]{0,1,2:T(1,128)}, f32[64,1,128]{0,1,2:T(1,128)S(1)}, u32[]{:S(2)}, u32[]{:S(2)}) collective-permute-start(f32[64,1,128]{0,1,2:T(1,128)} %get-tuple-element.27), channel_id=1, source_target_pairs={{16,0},{0,16},{17,1},{1,17},{18,2},{2,18},{19,3},{3,19},{20,4},{4,... | collective-permute-start | bytes 98312 | tf_op jit(solution)/shard_map/ppermute | solution.py:22
  31.4 4.5 collective-permute-start.8
  36.5 8.1 %collective-permute-start.11 = (f32[64,34,1]{0,2,1:T(1,128)}, f32[64,34,1]{0,2,1:T(1,128)}, u32[]{:S(2)}, u32[]{:S(2)}) collective-permute-start(f32[64,34,1]{0,2,1:T(1,128)} %copy.254), channel_id=1, source_target_pairs={{0,4},{4,8},{8,12},{12,0},{1,5},{5,9},{9,13},{13,1},{2,6},{6,10},{... | collective-permute-start | bytes 26120 | tf_op jit(solution)/shard_map/ppermute | solution.py:21
  37.1 8.2 %collective-permute-start.10 = (f32[64,34,1]{0,2,1:T(1,128)}, f32[64,34,1]{0,2,1:T(1,128)}, u32[]{:S(2)}, u32[]{:S(2)}) collective-permute-start(f32[64,34,1]{0,2,1:T(1,128)} %copy.251), channel_id=1, source_target_pairs={{4,0},{8,4},{12,8},{0,12},{5,1},{9,5},{13,9},{1,13},{6,2},{10,6},{... | collective-permute-start | bytes 26120 | tf_op jit(solution)/shard_map/ppermute | solution.py:22
  72.4 326.7 %reduce-scatter.6.cloned.1.call-start = ((), (), s32[]{:S(2)}) async-start(), calls=%async_computation.4 | async-start | bytes 10485760 | tf_op jit(solution)/shard_map/reduce_scatter | solution.py:138
  183.8 10.1 %copy-start.38 = (f32[64]{0:T(128)S(1)}, f32[64]{0:T(128)}, u32[]{:S(2)}) copy-start(f32[64]{0:T(128)} %param.18) | copy-start | bytes 772
  183.9 4.9 %collective-permute-start.1 = (f32[64,1,128]{0,1,2:T(1,128)S(1)}, f32[64,1,128]{0,1,2:T(1,128)S(1)}, u32[]{:S(2)}, u32[]{:S(2)}) collective-permute-start(f32[64,1,128]{0,1,2:T(1,128)S(1)} %get-tuple-element.33), channel_id=1, source_target_pairs={{16,0},{0,16},{17,1},{1,17},{18,2},{2,18},{19,3},{3,19},{20,4},{4,... | collective-permute-start | bytes 98312 | tf_op jit(solution)/shard_map/ppermute | solution.py:22
  185.4 4.3 collective-permute-start
  189.7 1.8 collective-permute-start.3
  190.0 3.2 collective-permute-start.2
  258.7 4.9 %collective-permute-start.13 = (f32[64,1,128]{0,1,2:T(1,128)S(1)}, f32[64,1,128]{0,1,2:T(1,128)S(1)}, u32[]{:S(2)}, u32[]{:S(2)}) collective-permute-start(f32[64,1,128]{0,1,2:T(1,128)S(1)} %get-tuple-element.25), channel_id=1, source_target_pairs={{16,0},{0,16},{17,1},{1,17},{18,2},{2,18},{19,3},{3,19},{20,4},{4,... | collective-permute-start | bytes 98312 | tf_op jit(solution)/shard_map/ppermute | solution.py:22
  260.3 4.3 collective-permute-start.12
  263.7 138.1 %copy-start.25 = (f32[64,1,128]{0,1,2:T(1,128)}, f32[64,1,128]{0,1,2:T(1,128)S(1)}, u32[]{:S(2)}) copy-start(f32[64,1,128]{0,1,2:T(1,128)S(1)} %collective-permute-done.13) | copy-start | bytes 98308
  264.6 137.2 %copy-start.27 = (f32[64,1,128]{0,1,2:T(1,128)}, f32[64,1,128]{0,1,2:T(1,128)S(1)}, u32[]{:S(2)}) copy-start(f32[64,1,128]{0,1,2:T(1,128)S(1)} %collective-permute-done.12) | copy-start | bytes 98308
  264.8 3.2 collective-permute-start.15
  264.9 3.7 collective-permute-start.14
  409.4 9.6 %copy-start.1 = (f32[64,32,128]{0,1,2:T(8,128)S(1)}, f32[64,32,128]{0,1,2:T(8,128)}, u32[]{:S(2)}) copy-start(f32[64,32,128]{0,1,2:T(8,128)} %copy-done) | copy-start | bytes 3145732
  409.4 9.6 %copy-start.3 = (f32[64,32,128]{0,1,2:T(8,128)S(1)}, f32[64,32,128]{0,1,2:T(8,128)}, u32[]{:S(2)}) copy-start(f32[64,32,128]{0,1,2:T(8,128)} %copy-done.2) | copy-start | bytes 3145732
  409.4 9.6 %copy-start.7 = (f32[64,32,128]{0,1,2:T(8,128)S(1)}, f32[64,32,128]{0,1,2:T(8,128)}, u32[]{:S(2)}) copy-start(f32[64,32,128]{0,1,2:T(8,128)} %copy.238) | copy-start | bytes 3145732
  409.4 9.6 %copy-start.8 = (f32[64,32,128]{0,1,2:T(8,128)S(1)}, f32[64,32,128]{0,1,2:T(8,128)}, u32[]{:S(2)}) copy-start(f32[64,32,128]{0,1,2:T(8,128)} %copy.244) | copy-start | bytes 3145732
  409.4 9.6 %copy-start.21 = (f32[64,128]{0,1:T(8,128)S(1)}, f32[64,128]{0,1:T(8,128)}, u32[]{:S(2)}) copy-start(f32[64,128]{0,1:T(8,128)} %copy.253) | copy-start | bytes 98308
  409.4 9.6 %copy-start.22 = (f32[64,128]{0,1:T(8,128)S(1)}, f32[64,128]{0,1:T(8,128)}, u32[]{:S(2)}) copy-start(f32[64,128]{0,1:T(8,128)} %copy.247) | copy-start | bytes 98308
  409.4 9.6 %copy-start.26 = (f32[64,1,128]{0,1,2:T(1,128)S(1)}, f32[64,1,128]{0,1,2:T(1,128)}, u32[]{:S(2)}) copy-start(f32[64,1,128]{0,1,2:T(1,128)} %copy-done.25) | copy-start | bytes 98308
  409.4 9.6 %copy-start.28 = (f32[64,1,128]{0,1,2:T(1,128)S(1)}, f32[64,1,128]{0,1,2:T(1,128)}, u32[]{:S(2)}) copy-start(f32[64,1,128]{0,1,2:T(1,128)} %copy-done.27) | copy-start | bytes 98308
  416.9 5.2 %collective-permute-start.5 = (f32[64,1,128]{0,1,2:T(1,128)S(1)}, f32[64,1,128]{0,1,2:T(1,128)S(1)}, u32[]{:S(2)}, u32[]{:S(2)}) collective-permute-start(f32[64,1,128]{0,1,2:T(1,128)S(1)} %get-tuple-element.29), channel_id=1, source_target_pairs={{16,0},{0,16},{17,1},{1,17},{18,2},{2,18},{19,3},{3,19},{20,4},{4,... | collective-permute-start | bytes 98312 | tf_op jit(solution)/shard_map/ppermute | solution.py:22
  418.4 4.3 collective-permute-start.4
  422.7 21.8 %collective-permute-start.7 = (f32[64,34,1]{0,1,2:T(8,128)S(1)}, f32[64,34,1]{0,1,2:T(8,128)S(1)}, u32[]{:S(2)}, u32[]{:S(2)}) collective-permute-start(f32[64,34,1]{0,1,2:T(8,128)S(1)} %get-tuple-element.21), channel_id=1, source_target_pairs={{4,0},{8,4},{12,8},{0,12},{5,1},{9,5},{13,9},{1,13},{6,2},{10,6},{... | collective-permute-start | bytes 26120 | tf_op jit(solution)/shard_map/ppermute | solution.py:22
  423.0 21.5 %collective-permute-start.6 = (f32[64,34,1]{0,1,2:T(8,128)S(1)}, f32[64,34,1]{0,1,2:T(8,128)S(1)}, u32[]{:S(2)}, u32[]{:S(2)}) collective-permute-start(f32[64,34,1]{0,1,2:T(8,128)S(1)} %get-tuple-element.20), channel_id=1, source_target_pairs={{0,4},{4,8},{8,12},{12,0},{1,5},{5,9},{9,13},{13,1},{2,6},{6,10},{... | collective-permute-start | bytes 26120 | tf_op jit(solution)/shard_map/ppermute | solution.py:21
  (32 other events, 150.0 us)
Sparse Core Ops, SparseCore 0:
  24.6 147.1 reduce-scatter.3
  174.1 77.4 reduce-scatter.7
  254.1 144.9 reduce-scatter.5
where the time goes:
time: 468 us; the launch traced here: 460 us
  waiting for transfers between devices  279 us (60%)
  local copies, waits for them, and re-layouts  55.1 us (12%)
  other arithmetic  47.6 us (10%)
  matrix products  27.3 us (6%)
  blocking collectives  21.2 us (5%)
  between operations  15.1 us (3%)
  starting transfers between devices  14.7 us (3%)
    reduce_scatter x2, waiting for transfers between devices, adjoint_mass(): lax.psum_scatter(jnp.stack((tmatmul(coag_rows, flat_weight), tmatmul(frag...  226 us
    reduce_scatter x1, waiting for transfers between devices, per_device(): lax.psum_scatter(matmul(coag_cols, flat_moved) + matmul(frag_cols, flat_g...  38.7 us
    psum x1, blocking collectives, per_device(): speed_gradient = lax.psum(local_sum, ('phi', 'mass'))  21.2 us
    unnamed x101, local copies, waits for them, and re-layouts  20.8 us
    dot_general x4, matrix products, tmatmul(): lax.dot_general(left, right, contract_rows, precision=highest, preferred_...  16.4 us
    ppermute x8, starting transfers between devices, padded_2(): after = lax.ppermute(initial, axis, down)  12.1 us
    dot_general x2, matrix products, matmul(): jnp.dot(left, right, precision=highest, preferred_element_type=jnp.float32)  11 us
  transfers between devices with their start and end apart: 19, of which 12 were waited for; matrix products, arithmetic and copies ran while one was open for 19% of the time, Pallas kernels for 0%

commit v1 on v0

v1 whole, which is shorter than its diff:
```python
import functools
import math

import jax
import jax.numpy as jnp
from jax import lax
from jax.experimental import pallas as pl
from jax.experimental.pallas import tpu as pltpu
from jax.sharding import PartitionSpec as P

RANGE = 64
LANES = 128
GROUPS = 4
EDGE = 16
gate_width = 0.5
first_dims = (((0,), (0,)), ((), ()))
VMEM_LIMIT = 56 * 2**20


def coag_matrix(dest_bins, bott_split, coag_rate):
    number = dest_bins.shape[0]
    row_ids = jnp.arange(number, dtype=jnp.int32)[:, None]
    col_ids = jnp.arange(number, dtype=jnp.int32)[None, :]
    target = dest_bins[None, :]
    lower_part = (row_ids == target).astype(jnp.float32) * (1.0 - bott_split)[None, :]
    upper_part = (row_ids == target + 1).astype(jnp.float32) * bott_split[None, :]
    keeper = (row_ids == col_ids).astype(jnp.float32)
    return (lower_part + upper_part - keeper) * coag_rate[None, :] + keeper


def frag_matrix(frag_pairs, frag_gain, frag_rate):
    number = frag_gain.shape[0]
    blocks = jnp.repeat(jnp.repeat(frag_pairs, RANGE, axis=0), RANGE, axis=1).astype(jnp.float32)
    row_ids = jnp.arange(number, dtype=jnp.int32)[:, None]
    col_ids = jnp.arange(number, dtype=jnp.int32)[None, :]
    below_diag = (row_ids <= col_ids).astype(jnp.float32)
    keeper = (row_ids == col_ids).astype(jnp.float32)
    return frag_gain * blocks * below_diag - keeper * frag_rate[None, :]


def halves(matrix):
    high = lax.reduce_precision(matrix, 8, 7)
    return high.astype(jnp.bfloat16), (matrix - high).astype(jnp.bfloat16)


def split(value):
    high = value.astype(jnp.bfloat16)
    return high, (value - high.astype(jnp.float32)).astype(jnp.bfloat16)


def product(value, high_ref, low_ref, dims=(((1,), (0,)), ((), ()))):
    high, low = split(value)
    dot = functools.partial(lax.dot_general, dimension_numbers=dims, preferred_element_type=jnp.float32)
    return dot(high, high_ref[...]) + (dot(high, low_ref[...]) + dot(low, high_ref[...]))


def stencil(slab, index, center, lower, upper, side, start, size):
    rows = pl.ds(start, size)
    return (
        center * slab[(*index(0), rows)]
        + lower * slab[(*index(0), pl.ds(start - 1, size))]
        + upper * slab[(*index(0), pl.ds(start + 1, size))]
        + side * (slab[(*index(-1), rows)] + slab[(*index(1), rows)])
    )


def forward_kernel(
    azimuth,
    radial,
    own_ref,
    next_ref,
    own_az_ref,
    next_az_ref,
    strip_ref,
    gate_ref,
    slope_ref,
    center_ref,
    lower_ref,
    upper_ref,
    side_ref,
    high_ref,
    low_ref,
    moved_ref,
    second_ref,
    slab,
    mixed,
):
    inner = pl.ds(EDGE, radial)
    wide = radial + 16

    def place(row, source, other, start, stride):
        bins = jnp.concatenate(
            [source[pl.ds(start, RANGE, stride=stride), :], other[pl.ds(start, RANGE, stride=stride), :]], axis=0
        )
        slab[row, inner, :] = bins.T
        tile = strip_ref[row]
        slab[row, pl.ds(EDGE - 8, 8), :] = tile
        slab[row, pl.ds(EDGE + radial, 8), :] = tile

    for row, k in ((0, 0), (1, 1), (azimuth + 2, 2), (azimuth + 3, 3)):
        place(row, own_az_ref, next_az_ref, k, 4)

    @pl.loop(0, azimuth)
    def _(a):
        place(a + 2, own_ref, next_ref, a, azimuth)

    def move(a):
        moved = stencil(
            slab,
            lambda d: (a + d,),
            center_ref[1, pl.ds(8, wide), :],
            lower_ref[1, pl.ds(8, wide), :],
            upper_ref[1, pl.ds(8, wide), :],
            side_ref[1:2, :],
            8,
            wide,
        )
        gated = gate_ref[a, pl.ds(8, wide), :] * moved
        result = product(jnp.concatenate([moved, gated], axis=1), high_ref, low_ref)
        mixed[a, 0, pl.ds(8, wide), :] = result[:, :LANES]
        mixed[a, 1, pl.ds(8, wide), :] = result[:, LANES:]
        return moved[8 : 8 + radial]

    move(1)
    move(azimuth + 2)

    @pl.loop(0, azimuth)
    def _(a):
        moved_ref[a] = slope_ref[a] * move(a + 2)

    @pl.loop(0, azimuth)
    def _(a):
        for t in range(2):
            second = stencil(
                mixed,
                lambda d: (a + 2 + d, t),
                center_ref[t, inner, :],
                lower_ref[t, inner, :],
                upper_ref[t, inner, :],
                side_ref[t : t + 1, :],
                EDGE,
                radial,
            )
            second_ref[a, t] = slope_ref[a] * second


def adjoint_kernel(azimuth, radial, low_row, high_row, *refs):
    first, last = low_row == 0, high_row == azimuth + 4
    refs = list(refs)

    def take(number):
        taken = refs[:number]
        del refs[:number]
        return taken

    slots = take(4)
    sides = take(4) if first or last else None
    strip_ref, gate_ref, second_ref, moved_ref = take(4)
    center_ref, lower_ref, upper_ref, side_ref = take(4)
    high1_ref, low1_ref, high2_ref, low2_ref = take(4)
    carry_second, carry_first, carry_sum = (None, None, None) if first else take(3)
    own_out, next_out, sum_out = take(3)
    keep_second, keep_first = (None, None) if last else take(2)
    second, initial = take(2)

    inner = pl.ds(EDGE, radial)
    wide = radial + 16
    outer = pl.ds(8, wide)
    base = low_row if first else low_row - 2
    first_low, first_high = (1 if first else low_row - 1), high_row - 1
    first_base = first_low if first else first_low - 2
    out_low, out_high = first_base + 1, first_high - 1

    if first:
        sum_out[...] = jnp.zeros_like(sum_out)
    else:
        second[pl.ds(0, 2)] = carry_second[...]
        initial[pl.ds(0, 2)] = carry_first[...]
        sum_out[...] = carry_sum[...]

    rows = high_row - low_row
    strips = product(strip_ref[pl.ds(low_row, rows)].reshape(rows * 8, 4 * RANGE), high1_ref, low1_ref)
    for i in range(rows):
        piece = strips[i * 8 : i * 8 + 8]
        for start in (EDGE - 8, EDGE + radial):
            gate = gate_ref[low_row + i, pl.ds(start, 8), :]
            for t in range(2):
                second[low_row + i - base, t, pl.ds(start, 8), :] = (
                    piece[:, t * LANES : (t + 1) * LANES] + gate * piece[:, (t + 2) * LANES : (t + 3) * LANES]
                )

    def weigh(row, sources, start, stride):
        bins = jnp.concatenate([source[pl.ds(start, RANGE, stride=stride), :] for source in sources], axis=0)
        result = product(bins, high1_ref, low1_ref, first_dims)
        gate = gate_ref[row, inner, :]
        frag = (result[:, 2 * LANES : 3 * LANES], result[:, 3 * LANES :])
        for t in range(2):
            second[row - base, t, inner, :] = result[:, t * LANES : (t + 1) * LANES] + gate * frag[t]
        return frag

    own_low, own_high = max(low_row, 2), min(high_row, azimuth + 2)

    if first:
        weigh(0, sides, 0, 4)
        weigh(1, sides, 1, 4)

    @pl.loop(own_low, own_high)
    def _(row):
        frag = weigh(row, slots, row - own_low, own_high - own_low)
        sum_out[...] += second_ref[row - 2, 0] * frag[0] + second_ref[row - 2, 1] * frag[1]

    if last:
        weigh(azimuth + 2, sides, 2, 4)
        weigh(azimuth + 3, sides, 3, 4)

    def adjoin(row):
        parts = [
            stencil(
                second,
                lambda d: (row - base + d, t),
                center_ref[t, outer, :],
                lower_ref[t, outer, :],
                upper_ref[t, outer, :],
                side_ref[t : t + 1, :],
                8,
                wide,
            )
            for t in range(2)
        ]
        result = product(jnp.concatenate(parts, axis=1), high2_ref, low2_ref)
        frag = result[:, LANES:]
        initial[row - first_base, outer, :] = result[:, :LANES] + gate_ref[row, outer, :] * frag
        return frag[8 : 8 + radial]

    if first:
        adjoin(1)

    @pl.loop(max(first_low, 2), min(first_high, azimuth + 2))
    def _(row):
        sum_out[...] += moved_ref[row - 2] * adjoin(row)

    if last:
        adjoin(azimuth + 2)

    @pl.loop(out_low, out_high)
    def _(row):
        result = stencil(
            initial,
            lambda d: (row - first_base + d,),
            center_ref[1, inner, :],
            lower_ref[1, inner, :],
            upper_ref[1, inner, :],
            side_ref[1:2, :],
            EDGE,
            radial,
        ).T
        own_out[row - out_low] = result[:RANGE]
        next_out[row - out_low] = result[RANGE:]

    if not last:
        keep_second[...] = second[pl.ds(high_row - 2 - base, 2)]
        keep_first[...] = initial[pl.ds(first_high - 2 - first_base, 2)]


def call(kernel, outs, scratch, flops, operands):
    size = sum(x.size * x.dtype.itemsize for x in operands) + sum(4 * math.prod(o) for o in outs)
    vmem = pl.BlockSpec(memory_space=pltpu.VMEM)
    return pl.pallas_call(
        kernel,
        out_shape=[jax.ShapeDtypeStruct(o, jnp.float32) for o in outs],
        in_specs=[vmem] * len(operands),
        out_specs=[vmem] * len(outs),
        scratch_shapes=[pltpu.VMEM(s, jnp.float32) for s in scratch],
        compiler_params=pltpu.CompilerParams(vmem_limit_bytes=VMEM_LIMIT),
        cost_estimate=pl.CostEstimate(flops=flops, bytes_accessed=size, transcendentals=0),
    )(*operands)


def per_device(
    density,
    cotangent,
    drift_in,
    drift_out,
    spread,
    dest_bins,
    bott_split,
    coag_rate,
    frag_pairs,
    frag_gain,
    frag_rate,
    collide_speed,
    frag_speed,
    regime,
):
    own_bins, azimuth, radial = density.shape
    ranges = lax.axis_size("mass")
    place = lax.axis_index("mass")
    row_index = lax.axis_index("row")
    phis, rows = lax.axis_size("phi"), lax.axis_size("row")
    up = [(i, i + 1) for i in range(ranges - 2)]
    up_two = [(i, i + 2) for i in range(ranges - 3)]
    down = [(i + 1, i) for i in range(ranges - 1)]
    ending = [(ranges - 1, ranges - 2)]
    returning = [(ranges - 2, ranges - 1)]

    cuts = [azimuth * k // GROUPS for k in range(GROUPS + 1)]
    pieces = [cotangent[:, i:j] for i, j in zip(cuts, cuts[1:])]
    gathered = [
        [
            lax.ppermute(piece, "mass", up_two),
            lax.ppermute(piece, "mass", up),
            piece,
            lax.ppermute(piece, "mass", down),
        ]
        for piece in pieces
    ]
    density_next = lax.ppermute(density, "mass", ending)

    sigma = jax.nn.sigmoid((collide_speed - frag_speed[None, :]) / gate_width)
    flagged = regime.astype(jnp.float32)
    frag_gate = flagged * sigma
    gate_slope = -flagged * sigma * (1.0 - sigma) / gate_width
    gate_slope = gate_slope * (place < ranges - 1).astype(jnp.float32)

    def band(low, high):
        return jnp.concatenate([cotangent[:, low:high], density[:, low:high], frag_gate[None, low:high]], axis=0)

    ring = [(i, (i + 1) % phis) for i in range(phis)]
    back = [(j, i) for i, j in ring]
    before = lax.ppermute(band(azimuth - 2, azimuth), "phi", ring)
    after = lax.ppermute(band(0, 2), "phi", back)

    def columns(low, high):
        body = band(0, azimuth)[:, :, low:high]
        whole = jnp.concatenate([before[:, :, low:high], body, after[:, :, low:high]], axis=1)
        return whole.transpose(1, 2, 0).reshape(2 * (azimuth + 4), 2 * own_bins + 1)

    line = [(i, i + 1) for i in range(rows - 1)]
    left = lax.ppermute(columns(radial - 2, radial), "row", line).reshape(azimuth + 4, 2, -1)
    right = lax.ppermute(columns(0, 2), "row", [(j, i) for i, j in line]).reshape(azimuth + 4, 2, -1)

    gates = jnp.concatenate([before[-1], frag_gate, after[-1]], axis=0)
    gap = jnp.zeros((azimuth + 4, EDGE - 2), jnp.float32)
    gates = jnp.concatenate([gap, left[:, :, -1], gates, right[:, :, -1], gap], axis=1)
    gate_wide = jnp.broadcast_to(gates[:, :, None], gates.shape + (LANES,))
    slope_wide = jnp.broadcast_to(gate_slope[:, :, None], gate_slope.shape + (LANES,))

    def window(drift):
        padded = jnp.pad(drift, ((0, 0), (EDGE, EDGE)))
        wide = lax.dynamic_slice_in_dim(padded, row_index * radial, radial + 2 * EDGE, 1)
        return wide.T

    drifts = jnp.concatenate([window(drift_in), window(drift_out)], axis=0)
    spreads = jnp.broadcast_to(spread[None, :], (8, own_bins))
    edges = jnp.concatenate([left[:, :, :-1], right[:, :, :-1]], axis=1).reshape(4 * (azimuth + 4), 2 * own_bins)
    sides = jnp.concatenate([before[:-1], after[:-1]], axis=1)
    edges_cot, edges_den = edges[:, :own_bins], edges[:, own_bins:]
    sides_cot, sides_den = sides[:own_bins], sides[own_bins:]

    def packed(parts):
        return jnp.concatenate([p.reshape(-1, LANES) for p in parts], axis=0)

    def unpacked(message, parts):
        out, at = [], 0
        for p in parts:
            size = p.size // LANES
            out.append(message[at : at + size].reshape(p.shape))
            at += size
        return out

    own_parts = [edges_cot, sides_cot, drifts, spreads]
    message = packed(own_parts)
    far = unpacked(lax.ppermute(message, "mass", up_two), own_parts)
    near = unpacked(lax.ppermute(message, "mass", up), own_parts)
    over = unpacked(lax.ppermute(message, "mass", down), own_parts)
    den_parts = [edges_den, sides_den]
    den_over = unpacked(lax.ppermute(packed(den_parts), "mass", ending), den_parts)

    def strip_of(edge_list):
        wide = jnp.concatenate(edge_list, axis=1).reshape(azimuth + 4, 4, -1)
        blank = jnp.zeros((azimuth + 4, 4, wide.shape[2]), jnp.float32)
        return jnp.concatenate([wide[:, 2:], blank, wide[:, :2]], axis=1)

    by_slot = [far, near, own_parts, over]
    strip_cot = strip_of([s[0] for s in by_slot])
    strip_den = strip_of([edges_den, den_over[0]])
    sides_by_slot = [s[1].reshape(own_bins * 4, radial) for s in by_slot]

    def tiled(wide):
        return wide.reshape(wide.shape[0], 2, LANES).transpose(1, 0, 2)

    length = radial + 2 * EDGE
    drift_wide = tiled(jnp.concatenate([s[2] for s in by_slot], axis=1))
    inward, outward = drift_wide[:, :length], drift_wide[:, length:]
    side = tiled(jnp.concatenate([s[3] for s in by_slot], axis=1)[:1])[:, 0]
    center = 1.0 - inward - outward - 2.0 * side[:, None, :]
    inward_next = jnp.concatenate([inward[:, 1:], inward[:, :1]], axis=1)
    outward_last = jnp.concatenate([outward[:, -1:], outward[:, :-1]], axis=1)

    def related(matrix):
        padded = jnp.pad(matrix, ((2 * RANGE, RANGE), (2 * RANGE, RANGE)))
        return lax.dynamic_slice(padded, (place * RANGE, place * RANGE), (4 * RANGE, 4 * RANGE))

    coag = related(coag_matrix(dest_bins, bott_split, coag_rate))
    frag = related(frag_matrix(frag_pairs, frag_gain, frag_rate))
    both = halves(jnp.concatenate([coag, frag], axis=1))
    upper_half = jnp.concatenate([coag[:, 2 * RANGE :], frag[:, 2 * RANGE :]], axis=1)
    own_cols = halves(upper_half)
    own_rows = halves(upper_half.T)

    moved, second = call(
        functools.partial(forward_kernel, azimuth, radial),
        [(azimuth, radial, LANES), (azimuth, 2, radial, LANES)],
        [(azimuth + 4, length, LANES), (azimuth + 4, 2, length, LANES)],
        6 * (azimuth + 2) * (radial + 16) * 256 * 256,
        [
            density.reshape(own_bins * azimuth, radial),
            density_next.reshape(own_bins * azimuth, radial),
            sides_den.reshape(own_bins * 4, radial),
            den_over[1].reshape(own_bins * 4, radial),
            strip_den,
            gate_wide,
            slope_wide,
            center,
            outward_last,
            inward_next,
            side,
            *own_rows,
        ],
    )

    own_outs, next_outs, carry = [], [], []
    for g in range(GROUPS):
        first, last = g == 0, g == GROUPS - 1
        low_row = 0 if first else cuts[g] + 2
        high_row = azimuth + 4 if last else cuts[g + 1] + 2
        new = high_row - low_row
        n_out = (azimuth + 2 if last else high_row - 2) - (2 if first else low_row - 2)
        operands = [x.reshape(-1, radial) for x in gathered[g]]
        if first or last:
            operands += sides_by_slot
        operands += [strip_cot, gate_wide, second, moved, center, inward, outward, side, *both, *own_cols, *carry]
        outs = [(n_out, RANGE, radial), (n_out, RANGE, radial), (radial, LANES)]
        if not last:
            outs += [(2, 2, length, LANES), (2, length, LANES)]
        own_out, next_out, total, *kept = call(
            functools.partial(adjoint_kernel, azimuth, radial, low_row, high_row),
            outs,
            [(new + 2, 2, length, LANES), (new + 2, length, LANES)],
            6 * new * (radial + 16) * 256 * 768,
            operands,
        )
        carry = [*kept, total]
        own_outs.append(own_out)
        next_outs.append(lax.ppermute(next_out, "mass", returning))
    is_last = place == ranges - 1
    result = jnp.concatenate(
        [jnp.where(is_last, there, here) for here, there in zip(own_outs, next_outs)], axis=0
    ).transpose(1, 0, 2)
    speed_gradient = lax.psum(jnp.sum(total, axis=1), ("phi", "mass"))
    return (result, speed_gradient)


def solution(mesh):
    in_specs = (
        P("mass", "phi", "row"),
        P("mass", "phi", "row"),
        P("mass", None),
        P("mass", None),
        P("mass"),
        P(),
        P(),
        P(),
        P(),
        P(),
        P(),
        P("phi", "row"),
        P("row"),
        P("phi", "row"),
    )
    out_specs = (P("mass", "phi", "row"), P("row"))
    return jax.shard_map(
        per_device, mesh=mesh, in_specs=in_specs, out_specs=out_specs, check_vma=False
    )
```

time: 468 us -> 188 us (0.40); the launches traced: 460 us -> 188 us
  waiting for transfers between devices: 279 us -> 3.51 us
  Pallas kernels: 0 us -> 65.5 us
  starting transfers between devices: 14.7 us -> 51.1 us
  other arithmetic: 47.6 us -> 11.7 us
  matrix products: 27.3 us -> 0 us
  local copies, waits for them, and re-layouts: 55.1 us -> 28.8 us
  between operations: 15.1 us -> 1.87 us
    reduce_scatter x3 -> x0, waiting for transfers between devices: 265 us -> none  [the longest x2 226 us: adjoint_mass(): lax.psum_scatter(jnp.stack((tmatmul(coag_rows, flat_weight), tmatmul(frag...]
    pallas_call x0 -> x5, Pallas kernels: none -> 65.5 us  [call(): pl.pallas_call(kernel, out_shape=[jax.ShapeDtypeStruct(o, jnp.float32) fo...]
    ppermute x16 -> x25, starting transfers between devices: 14.4 us -> 51.1 us  [the longest x4 22.5 us: per_device(): lax.ppermute(piece, 'mass', up_two)]
    dot_general x6 -> x0, matrix products: 27.3 us -> none  [the longest x4 16.4 us: tmatmul(): lax.dot_general(left, right, contract_rows, precision=highest, preferred_...]
    add x5 -> x1, other arithmetic: 21.6 us -> 0.08 us  [coag_matrix(): return (lower_part + upper_part - keeper) * coag_rate[None, :] + keeper]
    another operation x4 -> x0, local copies, waits for them, and re-layouts: 11.8 us -> none  [the longest x2 5.91 us: adjoint_mass(): frag_back.reshape(own_bins, azimuth, radial)]
    unnamed x101 -> x87, local copies, waits for them, and re-layouts: 20.8 us -> 9.37 us
    ppermute x16 -> x25, waiting for transfers between devices: 13.9 us -> 3.51 us  [the longest x1 3.33 us: per_device(): lax.ppermute(columns(0, 2), 'row', [(j, i) for i, j in line])]
  transfers between devices with their start and end apart: 19 -> 25, of which waited for: 12 -> 2; matrix products, arithmetic and copies ran while one was open for 19% -> 20% of each run, Pallas kernels for 0% -> 35%
where the time goes in v1:
time: 188 us
  Pallas kernels  65.5 us (35%)
  starting transfers between devices  51.1 us (27%)
  local copies, waits for them, and re-layouts  28.8 us (15%)
  blocking collectives  25.1 us (13%)
  other arithmetic  11.7 us (6%)
  waiting for transfers between devices  3.51 us (2%)
    pallas_call x5, Pallas kernels, call(): pl.pallas_call(kernel, out_shape=[jax.ShapeDtypeStruct(o, jnp.float32) fo...  65.5 us
    psum x1, blocking collectives, per_device(): speed_gradient = lax.psum(jnp.sum(total, axis=1), ('phi', 'mass'))  25.1 us
    ppermute x4, starting transfers between devices, per_device(): lax.ppermute(piece, 'mass', up_two)  22.5 us
    unnamed x87, local copies, waits for them, and re-layouts  9.37 us
    ppermute x4, starting transfers between devices, per_device(): lax.ppermute(piece, 'mass', up)  8.46 us
    ppermute x4, starting transfers between devices, per_device(): lax.ppermute(piece, 'mass', down)  5.34 us
  transfers between devices with their start and end apart: 25, of which 2 were waited for; matrix products, arithmetic and copies ran while one was open for 20% of the time, Pallas kernels for 35%

profile of v1, /device:TPU:0, one launch (start us, length us, event | category | flops | bytes accessed | tf_op | source)
XLA Modules:
  0.0 187.5 jit_solution(14691593845230334030)
XLA Ops:
  0.6 1.8 collective-permute-start.10
  6.1 2.9 %collective-permute-start.3 = (f32[129,2,128]{2,0,1:T(8,128)}, f32[129,2,128]{2,0,1:T(8,128)S(1)}, u32[]{:S(2)}, u32[]{:S(2)}) collective-permute-start(f32[129,2,128]{2,0,1:T(8,128)} %pad_maximum_fusion.10), channel_id=1, source_target_pairs={{0,16},{16,0},{1,17},{17,1},{2,18},{18,2},{3,19},{19,3},{4,20},{20... | collective-permute-start | bytes 396296 | tf_op jit(solution)/shard_map/ppermute | solution.py:330
  9.8 1.3 slice_bitcast_fusion.3
  11.2 5.3 %collective-permute-start = (f32[64,8,128]{2,1,0:T(8,128)}, f32[64,8,128]{2,1,0:T(8,128)}, u32[]{:S(2)}, u32[]{:S(2)}) collective-permute-start(f32[64,8,128]{2,1,0:T(8,128)} %get-tuple-element.63), channel_id=1, source_target_pairs={{0,2},{4,6},{8,10},{12,14},{16,18},{20,22},{24,26},{28,30}} | collective-permute-start | bytes 786440 | tf_op jit(solution)/shard_map/ppermute | solution.py:310
  21.4 1.9 copy.158
  23.3 4.1 %copy.159 = f32[64,32,128]{0,1,2:T(8,128)} copy(f32[64,32,128]{2,1,0:T(8,128)} %param.14) | data formatting | bytes 2097152 | tf_op args[0]
  27.5 2.8 %copy.160 = f32[1,32,128]{0,1,2:T(8,128)} copy(f32[1,32,128]{2,1,0:T(8,128)S(1)} %bitcast.84) | data formatting | bytes 32768 | tf_op jit(solution)/shard_map/broadcast_in_dim | solution.py:326
  34.7 1.3 collective-permute-start.5
  36.1 1.3 collective-permute-start.6
  37.7 3.3 %collective-permute-done.6 = f32[72,129]{1,0:T(8,128)S(1)} collective-permute-done((f32[72,129]{1,0:T(8,128)S(1)}, f32[72,129]{1,0:T(8,128)S(1)}, u32[]{:S(2)}, u32[]{:S(2)}) %collective-permute-start.6) | collective-permute-done | bytes 37184 | tf_op jit(solution)/shard_map/ppermute | solution.py:340
  42.3 1.3 collective-permute-start.7
  43.6 1.3 collective-permute-start.8
  45.4 1.3 collective-permute-start.9
  48.4 4.6 %collective-permute-start.1 = (f32[64,8,128]{2,1,0:T(8,128)}, f32[64,8,128]{2,1,0:T(8,128)S(1)}, u32[]{:S(2)}, u32[]{:S(2)}) collective-permute-start(f32[64,8,128]{2,1,0:T(8,128)} %get-tuple-element.63), channel_id=1, source_target_pairs={{0,1},{1,2},{4,5},{5,6},{8,9},{9,10},{12,13},{13,14},{16,17},{17,1... | collective-permute-start | bytes 786440 | tf_op jit(solution)/shard_map/ppermute | solution.py:311
  54.6 8.1 %collective-permute-start.13 = (f32[64,8,128]{2,1,0:T(8,128)S(1)}, f32[64,8,128]{2,1,0:T(8,128)S(1)}, u32[]{:S(2)}, u32[]{:S(2)}) collective-permute-start(f32[64,8,128]{2,1,0:T(8,128)S(1)} %copy-done.13), channel_id=1, source_target_pairs={{0,2},{4,6},{8,10},{12,14},{16,18},{20,22},{24,26},{28,30}} | collective-permute-start | bytes 786440 | tf_op jit(solution)/shard_map/ppermute | solution.py:310
  68.3 1.3 collective-permute-start.14
  69.7 1.3 collective-permute-start.15
  71.0 4.5 %collective-permute-start.17 = (f32[64,8,128]{2,1,0:T(8,128)S(1)}, f32[64,8,128]{2,1,0:T(8,128)S(1)}, u32[]{:S(2)}, u32[]{:S(2)}) collective-permute-start(f32[64,8,128]{2,1,0:T(8,128)S(1)} %copy-done.12), channel_id=1, source_target_pairs={{0,2},{4,6},{8,10},{12,14},{16,18},{20,22},{24,26},{28,30}} | collective-permute-start | bytes 786440 | tf_op jit(solution)/shard_map/ppermute | solution.py:310
  76.2 2.1 %broadcast_in_dim.67.gate_ref.refs_9_.refs_5_ = f32[36,160,128]{2,1,0:T(8,128)} broadcast(f32[36,160]{1,0:T(8,128)S(1)} %concatenate.100), dimensions={0,1} | broadcast | bytes 2972160 | tf_op jit(solution)/shard_map/broadcast_in_dim | solution.py:345
  78.3 1.9 %broadcast_in_dim.69.slope_ref = f32[32,128,128]{2,1,0:T(8,128)} broadcast(f32[32,128]{1,0:T(8,128)S(1)} %get-tuple-element.93), dimensions={0,1} | broadcast | bytes 2113536 | tf_op jit(solution)/shard_map/broadcast_in_dim | solution.py:346
  80.2 20.0 %shard_map.149 = (f32[32,128,128]{2,1,0:T(8,128)}, f32[32,2,128,128]{3,2,1,0:T(8,128)}) custom-call(f32[2048,128]{1,0:T(8,128)} %bitcast.62, f32[2048,128]{1,0:T(8,128)} %bitcast.21.next_ref, f32[256,128]{1,0:T(8,128)} %bitcast.67, f32[256,128]{1,0:T(8,128)} %slice.250.next_az_ref, f32[36,8,128]{2,1,0:T(8,128)} %fusion.4.strip_ref, ...), custom_call_target="tpu_custom_call" | custom-call | flops 1925185536 | bytes 14599168 | tf_op jit(solution)/shard_map/pallas_call | solution.py:268
  100.2 1.3 collective-permute-start.18
  101.6 1.3 collective-permute-start.19
  102.9 4.5 %collective-permute-start.21 = (f32[64,8,128]{2,1,0:T(8,128)S(1)}, f32[64,8,128]{2,1,0:T(8,128)S(1)}, u32[]{:S(2)}, u32[]{:S(2)}) collective-permute-start(f32[64,8,128]{2,1,0:T(8,128)S(1)} %copy-done.11), channel_id=1, source_target_pairs={{0,2},{4,6},{8,10},{12,14},{16,18},{20,22},{24,26},{28,30}} | collective-permute-start | bytes 786440 | tf_op jit(solution)/shard_map/ppermute | solution.py:310
  107.5 1.3 collective-permute-start.22
  108.8 1.5 collective-permute-start.23
  110.3 11.0 %shard_map.150 = (f32[6,64,128]{2,1,0:T(8,128)}, f32[6,64,128]{2,1,0:T(8,128)}, f32[128,128]{1,0:T(8,128)}, f32[2,2,160,128]{3,2,1,0:T(8,128)}, f32[2,160,128]{2,1,0:T(8,128)}) custom-call(f32[512,128]{1,0:T(8,128)} %bitcast.refs_0_, f32[512,128]{1,0:T(8,128)} %bitcast.73, f32[512,128]{1,0:T(8,128)} %get-tuple-element.58.refs_2_, f32[512,128]{1,0:T(8,128)} %bitcast.74, ...), custom_call_target="tpu_custom_call" | custom-call | flops 1698693120 | bytes 13337600 | tf_op jit(solution)/shard_map/pallas_call | solution.py:268
  121.4 11.1 %shard_map.151 = (f32[8,64,128]{2,1,0:T(8,128)}, f32[8,64,128]{2,1,0:T(8,128)}, f32[128,128]{1,0:T(8,128)}, f32[2,2,160,128]{3,2,1,0:T(8,128)}, f32[2,160,128]{2,1,0:T(8,128)}) custom-call(f32[512,128]{1,0:T(8,128)} %bitcast.75, f32[512,128]{1,0:T(8,128)} %bitcast.79, f32[512,128]{1,0:T(8,128)} %get-tuple-element.59.refs_2_, f32[512,128]{1,0:T(8,128)} %bitcast.81, ...), custom_call_target="tpu_custom_call" | custom-call | flops 1358954496 | bytes 13501440 | tf_op jit(solution)/shard_map/pallas_call | solution.py:268
  133.9 11.1 %shard_map.152 = (f32[8,64,128]{2,1,0:T(8,128)}, f32[8,64,128]{2,1,0:T(8,128)}, f32[128,128]{1,0:T(8,128)}, f32[2,2,160,128]{3,2,1,0:T(8,128)}, f32[2,160,128]{2,1,0:T(8,128)}) custom-call(f32[512,128]{1,0:T(8,128)} %bitcast.76, f32[512,128]{1,0:T(8,128)} %bitcast.82, f32[512,128]{1,0:T(8,128)} %get-tuple-element.60.refs_2_, f32[512,128]{1,0:T(8,128)} %bitcast.83, ...), custom_call_target="tpu_custom_call" | custom-call | flops 1358954496 | bytes 13501440 | tf_op jit(solution)/shard_map/pallas_call | solution.py:268
  146.5 12.3 %shard_map.153 = (f32[10,64,128]{2,1,0:T(8,128)}, f32[10,64,128]{2,1,0:T(8,128)}, f32[128,128]{1,0:T(8,128)}) custom-call(f32[512,128]{1,0:T(8,128)} %bitcast.77, f32[512,128]{1,0:T(8,128)} %bitcast.78, f32[512,128]{1,0:T(8,128)} %get-tuple-element.61.refs_2_, f32[512,128]{1,0:T(8,128)} %bitcast.80, f32[256,128]{1,0:T(8,128)} %slice.237.refs_4_, ...), custom_call_target="tpu_custom_call" | custom-call | flops 1698693120 | bytes 13665280 | tf_op jit(solution)/shard_map/pallas_call | solution.py:268
  160.5 25.1 %psum.7 = f32[128]{0:T(128)} all-reduce(f32[128]{0:T(128)S(1)} %reduce_sum.9), channel_id=1, replica_groups=mesh['phi'=2,'row'=4,'mass'=4] {'phi','mass'}, use_global_device_ids=true, to_apply=%region_1.2 | all-reduce | flops 128 | bytes 1024 | tf_op jit(solution)/shard_map/psum | solution.py:460
  186.0 1.6 copy.183
  (227 shorter events, 29.7 us)
Async XLA Ops:
  0.6 70.3 %collective-permute-start.10 = (f32[64,32,128]{2,1,0:T(8,128)}, f32[64,32,128]{2,1,0:T(8,128)}, u32[]{:S(2)}, u32[]{:S(2)}) collective-permute-start(f32[64,32,128]{2,1,0:T(8,128)} %param.14), channel_id=1, source_target_pairs={{3,2},{7,6},{11,10},{15,14},{19,18},{23,22},{27,26},{31,30}} | collective-permute-start | bytes 3145736 | tf_op jit(solution)/shard_map/ppermute | solution.py:317
  6.1 26.8 %collective-permute-start.3 = (f32[129,2,128]{2,0,1:T(8,128)}, f32[129,2,128]{2,0,1:T(8,128)S(1)}, u32[]{:S(2)}, u32[]{:S(2)}) collective-permute-start(f32[129,2,128]{2,0,1:T(8,128)} %pad_maximum_fusion.10), channel_id=1, source_target_pairs={{0,16},{16,0},{1,17},{17,1},{2,18},{18,2},{3,19},{19,3},{4,20},{20... | collective-permute-start | bytes 396296 | tf_op jit(solution)/shard_map/ppermute | solution.py:330
  9.8 23.4 %collective-permute-start.4 = (f32[129,2,128]{2,0,1:T(8,128)}, f32[129,2,128]{2,0,1:T(8,128)S(1)}, u32[]{:S(2)}, u32[]{:S(2)}) collective-permute-start(f32[129,2,128]{2,0,1:T(8,128)} %pad_maximum_fusion.11), channel_id=1, source_target_pairs={{16,0},{0,16},{17,1},{1,17},{18,2},{2,18},{19,3},{3,19},{20,4},{4,... | collective-permute-start | bytes 396296 | tf_op jit(solution)/shard_map/ppermute | solution.py:331
  11.2 57.2 %collective-permute-start = (f32[64,8,128]{2,1,0:T(8,128)}, f32[64,8,128]{2,1,0:T(8,128)}, u32[]{:S(2)}, u32[]{:S(2)}) collective-permute-start(f32[64,8,128]{2,1,0:T(8,128)} %get-tuple-element.63), channel_id=1, source_target_pairs={{0,2},{4,6},{8,10},{12,14},{16,18},{20,22},{24,26},{28,30}} | collective-permute-start | bytes 786440 | tf_op jit(solution)/shard_map/ppermute | solution.py:310
  34.7 2.9 %collective-permute-start.5 = (f32[72,129]{1,0:T(8,128)S(1)}, f32[72,129]{1,0:T(8,128)S(1)}, u32[]{:S(2)}, u32[]{:S(2)}) collective-permute-start(f32[72,129]{1,0:T(8,128)S(1)} %reshape.155), channel_id=1, source_target_pairs={{0,4},{4,8},{8,12},{1,5},{5,9},{9,13},{2,6},{6,10},{10,14},{3,7},{... | collective-permute-start | bytes 111464 | tf_op jit(solution)/shard_map/ppermute | solution.py:339
  36.1 4.9 %collective-permute-start.6 = (f32[72,129]{1,0:T(8,128)S(1)}, f32[72,129]{1,0:T(8,128)S(1)}, u32[]{:S(2)}, u32[]{:S(2)}) collective-permute-start(f32[72,129]{1,0:T(8,128)S(1)} %reshape.157), channel_id=1, source_target_pairs={{4,0},{8,4},{12,8},{5,1},{9,5},{13,9},{6,2},{10,6},{14,10},{7,3},{... | collective-permute-start | bytes 111464 | tf_op jit(solution)/shard_map/ppermute | solution.py:340
  41.2 21.7 %copy-start.6 = (f32[160,64]{1,0:T(8,128)S(1)}, f32[160,64]{1,0:T(8,128)}, u32[]{:S(2)}) copy-start(f32[160,64]{1,0:T(8,128)} %copy-done.5) | copy-start | bytes 122884
  41.4 4.1 %collective-permute-start.11 = (f32[328,128]{1,0:T(8,128)S(1)}, f32[328,128]{1,0:T(8,128)S(1)}, u32[]{:S(2)}, u32[]{:S(2)}) collective-permute-start(f32[328,128]{1,0:T(8,128)S(1)} %pad_maximum_fusion.4), channel_id=1, source_target_pairs={{3,2},{7,6},{11,10},{15,14},{19,18},{23,22},{27,26},{31,30}} | collective-permute-start | bytes 503816 | tf_op jit(solution)/shard_map/ppermute | solution.py:377
  42.1 20.9 %copy-start.1 = (f32[64,4,128]{2,1,0:T(4,128)}, f32[64,4,128]{2,1,0:T(4,128)S(1)}, u32[]{:S(2)}) copy-start(f32[64,4,128]{2,1,0:T(4,128)S(1)} %copy.170) | copy-start | bytes 393220
  42.3 6.2 %collective-permute-start.7 = (f32[492,128]{1,0:T(8,128)S(1)}, f32[492,128]{1,0:T(8,128)S(1)}, u32[]{:S(2)}, u32[]{:S(2)}) collective-permute-start(f32[492,128]{1,0:T(8,128)S(1)} %pad_maximum_fusion.3), channel_id=1, source_target_pairs={{0,2},{4,6},{8,10},{12,14},{16,18},{20,22},{24,26},{28,30}} | collective-permute-start | bytes 755720 | tf_op jit(solution)/shard_map/ppermute | solution.py:373
  43.6 9.6 %collective-permute-start.8 = (f32[492,128]{1,0:T(8,128)S(1)}, f32[492,128]{1,0:T(8,128)S(1)}, u32[]{:S(2)}, u32[]{:S(2)}) collective-permute-start(f32[492,128]{1,0:T(8,128)S(1)} %pad_maximum_fusion.3), channel_id=1, source_target_pairs={{0,1},{1,2},{4,5},{5,6},{8,9},{9,10},{12,13},{13,14},{16,17},{17,1... | collective-permute-start | bytes 755720 | tf_op jit(solution)/shard_map/ppermute | solution.py:374
  45.4 9.2 %collective-permute-start.9 = (f32[492,128]{1,0:T(8,128)S(1)}, f32[492,128]{1,0:T(8,128)S(1)}, u32[]{:S(2)}, u32[]{:S(2)}) collective-permute-start(f32[492,128]{1,0:T(8,128)S(1)} %pad_maximum_fusion.3), channel_id=1, source_target_pairs={{1,0},{2,1},{3,2},{5,4},{6,5},{7,6},{9,8},{10,9},{11,10},{13,12},{... | collective-permute-start | bytes 755720 | tf_op jit(solution)/shard_map/ppermute | solution.py:375
  48.4 21.2 %collective-permute-start.1 = (f32[64,8,128]{2,1,0:T(8,128)}, f32[64,8,128]{2,1,0:T(8,128)S(1)}, u32[]{:S(2)}, u32[]{:S(2)}) collective-permute-start(f32[64,8,128]{2,1,0:T(8,128)} %get-tuple-element.63), channel_id=1, source_target_pairs={{0,1},{1,2},{4,5},{5,6},{8,9},{9,10},{12,13},{13,14},{16,17},{17,1... | collective-permute-start | bytes 786440 | tf_op jit(solution)/shard_map/ppermute | solution.py:311
  53.2 47.0 %collective-permute-start.2 = (f32[64,8,128]{2,1,0:T(8,128)}, f32[64,8,128]{2,1,0:T(8,128)S(1)}, u32[]{:S(2)}, u32[]{:S(2)}) collective-permute-start(f32[64,8,128]{2,1,0:T(8,128)} %get-tuple-element.63), channel_id=1, source_target_pairs={{1,0},{2,1},{3,2},{5,4},{6,5},{7,6},{9,8},{10,9},{11,10},{13,12},{... | collective-permute-start | bytes 786440 | tf_op jit(solution)/shard_map/ppermute | solution.py:313
  54.6 46.9 %collective-permute-start.13 = (f32[64,8,128]{2,1,0:T(8,128)S(1)}, f32[64,8,128]{2,1,0:T(8,128)S(1)}, u32[]{:S(2)}, u32[]{:S(2)}) collective-permute-start(f32[64,8,128]{2,1,0:T(8,128)S(1)} %copy-done.13), channel_id=1, source_target_pairs={{0,2},{4,6},{8,10},{12,14},{16,18},{20,22},{24,26},{28,30}} | collective-permute-start | bytes 786440 | tf_op jit(solution)/shard_map/ppermute | solution.py:310
  68.3 34.5 %collective-permute-start.14 = (f32[64,8,128]{2,1,0:T(8,128)S(1)}, f32[64,8,128]{2,1,0:T(8,128)S(1)}, u32[]{:S(2)}, u32[]{:S(2)}) collective-permute-start(f32[64,8,128]{2,1,0:T(8,128)S(1)} %copy-done.13), channel_id=1, source_target_pairs={{0,1},{1,2},{4,5},{5,6},{8,9},{9,10},{12,13},{13,14},{16,17},{17,1... | collective-permute-start | bytes 786440 | tf_op jit(solution)/shard_map/ppermute | solution.py:311
  69.7 37.8 %collective-permute-start.15 = (f32[64,8,128]{2,1,0:T(8,128)S(1)}, f32[64,8,128]{2,1,0:T(8,128)S(1)}, u32[]{:S(2)}, u32[]{:S(2)}) collective-permute-start(f32[64,8,128]{2,1,0:T(8,128)S(1)} %copy-done.13), channel_id=1, source_target_pairs={{1,0},{2,1},{3,2},{5,4},{6,5},{7,6},{9,8},{10,9},{11,10},{13,12},{... | collective-permute-start | bytes 786440 | tf_op jit(solution)/shard_map/ppermute | solution.py:313
  71.0 37.8 %collective-permute-start.17 = (f32[64,8,128]{2,1,0:T(8,128)S(1)}, f32[64,8,128]{2,1,0:T(8,128)S(1)}, u32[]{:S(2)}, u32[]{:S(2)}) collective-permute-start(f32[64,8,128]{2,1,0:T(8,128)S(1)} %copy-done.12), channel_id=1, source_target_pairs={{0,2},{4,6},{8,10},{12,14},{16,18},{20,22},{24,26},{28,30}} | collective-permute-start | bytes 786440 | tf_op jit(solution)/shard_map/ppermute | solution.py:310
  80.2 22.7 %copy-start.11 = (f32[64,8,128]{2,1,0:T(8,128)S(1)}, f32[64,8,128]{2,1,0:T(8,128)}, u32[]{:S(2)}) copy-start(f32[64,8,128]{2,1,0:T(8,128)} %get-tuple-element.64) | copy-start | bytes 786436
  100.2 32.3 %collective-permute-start.18 = (f32[64,8,128]{2,1,0:T(8,128)S(1)}, f32[64,8,128]{2,1,0:T(8,128)S(1)}, u32[]{:S(2)}, u32[]{:S(2)}) collective-permute-start(f32[64,8,128]{2,1,0:T(8,128)S(1)} %copy-done.12), channel_id=1, source_target_pairs={{0,1},{1,2},{4,5},{5,6},{8,9},{9,10},{12,13},{13,14},{16,17},{17,1... | collective-permute-start | bytes 786440 | tf_op jit(solution)/shard_map/ppermute | solution.py:311
  101.6 31.6 %collective-permute-start.19 = (f32[64,8,128]{2,1,0:T(8,128)S(1)}, f32[64,8,128]{2,1,0:T(8,128)S(1)}, u32[]{:S(2)}, u32[]{:S(2)}) collective-permute-start(f32[64,8,128]{2,1,0:T(8,128)S(1)} %copy-done.12), channel_id=1, source_target_pairs={{1,0},{2,1},{3,2},{5,4},{6,5},{7,6},{9,8},{10,9},{11,10},{13,12},{... | collective-permute-start | bytes 786440 | tf_op jit(solution)/shard_map/ppermute | solution.py:313
  102.9 42.1 %collective-permute-start.21 = (f32[64,8,128]{2,1,0:T(8,128)S(1)}, f32[64,8,128]{2,1,0:T(8,128)S(1)}, u32[]{:S(2)}, u32[]{:S(2)}) collective-permute-start(f32[64,8,128]{2,1,0:T(8,128)S(1)} %copy-done.11), channel_id=1, source_target_pairs={{0,2},{4,6},{8,10},{12,14},{16,18},{20,22},{24,26},{28,30}} | collective-permute-start | bytes 786440 | tf_op jit(solution)/shard_map/ppermute | solution.py:310
  107.5 38.2 %collective-permute-start.22 = (f32[64,8,128]{2,1,0:T(8,128)S(1)}, f32[64,8,128]{2,1,0:T(8,128)S(1)}, u32[]{:S(2)}, u32[]{:S(2)}) collective-permute-start(f32[64,8,128]{2,1,0:T(8,128)S(1)} %copy-done.11), channel_id=1, source_target_pairs={{0,1},{1,2},{4,5},{5,6},{8,9},{9,10},{12,13},{13,14},{16,17},{17,1... | collective-permute-start | bytes 786440 | tf_op jit(solution)/shard_map/ppermute | solution.py:311
  108.8 36.9 %collective-permute-start.23 = (f32[64,8,128]{2,1,0:T(8,128)S(1)}, f32[64,8,128]{2,1,0:T(8,128)S(1)}, u32[]{:S(2)}, u32[]{:S(2)}) collective-permute-start(f32[64,8,128]{2,1,0:T(8,128)S(1)} %copy-done.11), channel_id=1, source_target_pairs={{1,0},{2,1},{3,2},{5,4},{6,5},{7,6},{9,8},{10,9},{11,10},{13,12},{... | collective-permute-start | bytes 786440 | tf_op jit(solution)/shard_map/ppermute | solution.py:313
  132.5 53.1 %collective-permute-start.12 = (f32[6,64,128]{2,1,0:T(8,128)S(1)}, f32[6,64,128]{2,1,0:T(8,128)S(1)}, u32[]{:S(2)}, u32[]{:S(2)}) collective-permute-start(f32[6,64,128]{2,1,0:T(8,128)S(1)} %copy-done.38), channel_id=1, source_target_pairs={{2,3},{6,7},{10,11},{14,15},{18,19},{22,23},{26,27},{30,31}} | collective-permute-start | bytes 589832 | tf_op jit(solution)/shard_map/ppermute | solution.py:455
  133.2 52.4 %collective-permute-start.16 = (f32[8,64,128]{2,1,0:T(8,128)}, f32[8,64,128]{2,1,0:T(8,128)S(1)}, u32[]{:S(2)}, u32[]{:S(2)}) collective-permute-start(f32[8,64,128]{2,1,0:T(8,128)} %get-tuple-element.29), channel_id=1, source_target_pairs={{2,3},{6,7},{10,11},{14,15},{18,19},{22,23},{26,27},{30,31}} | collective-permute-start | bytes 786440 | tf_op jit(solution)/shard_map/ppermute | solution.py:455
  145.0 40.7 %collective-permute-start.20 = (f32[8,64,128]{2,1,0:T(8,128)}, f32[8,64,128]{2,1,0:T(8,128)S(1)}, u32[]{:S(2)}, u32[]{:S(2)}) collective-permute-start(f32[8,64,128]{2,1,0:T(8,128)} %get-tuple-element.34), channel_id=1, source_target_pairs={{2,3},{6,7},{10,11},{14,15},{18,19},{22,23},{26,27},{30,31}} | collective-permute-start | bytes 786440 | tf_op jit(solution)/shard_map/ppermute | solution.py:455
  146.5 39.1 %copy-start.28 = (f32[6,64,128]{2,1,0:T(8,128)S(1)}, f32[6,64,128]{2,1,0:T(8,128)}, u32[]{:S(2)}) copy-start(f32[6,64,128]{2,1,0:T(8,128)} %get-tuple-element.25) | copy-start | bytes 589828
  146.5 39.1 %copy-start.26 = (f32[8,64,128]{2,1,0:T(8,128)S(1)}, f32[8,64,128]{2,1,0:T(8,128)}, u32[]{:S(2)}) copy-start(f32[8,64,128]{2,1,0:T(8,128)} %get-tuple-element.30) | copy-start | bytes 786436
  146.5 39.2 %copy-start.27 = (f32[8,64,128]{2,1,0:T(8,128)S(1)}, f32[8,64,128]{2,1,0:T(8,128)}, u32[]{:S(2)}) copy-start(f32[8,64,128]{2,1,0:T(8,128)} %get-tuple-element.35) | copy-start | bytes 786436
  158.8 27.0 %copy-start.10 = (f32[10,64,128]{2,1,0:T(8,128)S(1)}, f32[10,64,128]{2,1,0:T(8,128)}, u32[]{:S(2)}) copy-start(f32[10,64,128]{2,1,0:T(8,128)} %get-tuple-element.40) | copy-start | bytes 983044
  158.8 27.0 %collective-permute-start.24 = (f32[10,64,128]{2,1,0:T(8,128)}, f32[10,64,128]{2,1,0:T(8,128)S(1)}, u32[]{:S(2)}, u32[]{:S(2)}) collective-permute-start(f32[10,64,128]{2,1,0:T(8,128)} %get-tuple-element.39), channel_id=1, source_target_pairs={{2,3},{6,7},{10,11},{14,15},{18,19},{22,23},{26,27},{30,31}} | collective-permute-start | bytes 983048 | tf_op jit(solution)/shard_map/ppermute | solution.py:455
  (32 other events, 256.3 us)

commit v2 on v1

v2 whole, which is shorter than its diff:
```python
import functools
import math

import jax
import jax.numpy as jnp
from jax import lax
from jax.experimental import pallas as pl
from jax.experimental.pallas import tpu as pltpu
from jax.sharding import PartitionSpec as P

RANGE = 64
LANES = 128
EDGE = 16
gate_width = 0.5
BATCH = 4
VMEM_LIMIT = 56 * 2**20


def coag_matrix(dest_bins, bott_split, coag_rate):
    number = dest_bins.shape[0]
    row_ids = jnp.arange(number, dtype=jnp.int32)[:, None]
    col_ids = jnp.arange(number, dtype=jnp.int32)[None, :]
    target = dest_bins[None, :]
    lower_part = (row_ids == target).astype(jnp.float32) * (1.0 - bott_split)[None, :]
    upper_part = (row_ids == target + 1).astype(jnp.float32) * bott_split[None, :]
    keeper = (row_ids == col_ids).astype(jnp.float32)
    return (lower_part + upper_part - keeper) * coag_rate[None, :] + keeper


def frag_matrix(frag_pairs, frag_gain, frag_rate):
    number = frag_gain.shape[0]
    blocks = jnp.repeat(jnp.repeat(frag_pairs, RANGE, axis=0), RANGE, axis=1).astype(jnp.float32)
    row_ids = jnp.arange(number, dtype=jnp.int32)[:, None]
    col_ids = jnp.arange(number, dtype=jnp.int32)[None, :]
    below_diag = (row_ids <= col_ids).astype(jnp.float32)
    keeper = (row_ids == col_ids).astype(jnp.float32)
    return frag_gain * blocks * below_diag - keeper * frag_rate[None, :]


def stacked(matrix):
    high = lax.reduce_precision(matrix, 8, 7)
    return jnp.concatenate([high, high, matrix - high], axis=0).astype(jnp.bfloat16)


def split(value):
    high = value.astype(jnp.bfloat16)
    return high, (value - high.astype(jnp.float32)).astype(jnp.bfloat16)


def product(value, table_ref, axis=1):
    high, low = split(value)
    return lax.dot_general(
        jnp.concatenate([high, low, high], axis=axis),
        table_ref[...],
        (((axis,), (0,)), ((), ())),
        preferred_element_type=jnp.float32,
    )


def stencil(slab, index, center, lower, upper, side, start, size):
    rows = pl.ds(start, size)
    return (
        center * slab[(*index(0), rows)]
        + lower * slab[(*index(0), pl.ds(start - 1, size))]
        + upper * slab[(*index(0), pl.ds(start + 1, size))]
        + side * (slab[(*index(-1), rows)] + slab[(*index(1), rows)])
    )


def batches(low, high):
    return [range(i, min(i + BATCH, high)) for i in range(low, high, BATCH)]


def edge_kernel(azimuth, radial, cot_ref, den_ref, sides_ref, first_ref, last_ref):
    def put(row, cot, den):
        wide = jnp.concatenate([cot, den], axis=0).T
        first_ref[row] = wide[:2]
        last_ref[row] = wide[radial - 2 :]

    for row, k in ((0, 0), (1, 1), (azimuth + 2, 2), (azimuth + 3, 3)):
        both = sides_ref[pl.ds(k, 2 * RANGE, stride=4), :]
        put(row, both[:RANGE], both[RANGE:])

    @pl.loop(0, azimuth // BATCH)
    def _(b):
        for k in range(BATCH):
            a = b * BATCH + k
            put(
                a + 2,
                cot_ref[pl.ds(a, RANGE, stride=azimuth), :],
                den_ref[pl.ds(a, RANGE, stride=azimuth), :],
            )


def forward_kernel(azimuth, radial, cuts, *refs):
    own_ref, next_ref, own_az_ref, next_az_ref, strip_ref, gate_ref, slope_ref = refs[:7]
    center_ref, lower_ref, upper_ref, side_ref, table_ref = refs[7:12]
    moved_refs, second_refs = refs[12 : 12 + len(cuts) - 1], refs[12 + len(cuts) - 1 : -2]
    slab, mixed = refs[-2:]
    inner = pl.ds(EDGE, radial)
    wide = radial + 16
    outer = pl.ds(8, wide)

    def place(row, source, other, start, stride):
        bins = jnp.concatenate(
            [source[pl.ds(start, RANGE, stride=stride), :], other[pl.ds(start, RANGE, stride=stride), :]], axis=0
        )
        slab[row, inner, :] = bins.T
        tile = strip_ref[row]
        slab[row, pl.ds(EDGE - 8, 8), :] = tile
        slab[row, pl.ds(EDGE + radial, 8), :] = tile

    for row, k in ((0, 0), (1, 1), (azimuth + 2, 2), (azimuth + 3, 3)):
        place(row, own_az_ref, next_az_ref, k, 4)

    @pl.loop(0, azimuth // BATCH)
    def _(b):
        for k in range(BATCH):
            place(b * BATCH + k + 2, own_ref, next_ref, b * BATCH + k, azimuth)

    def move(rows):
        parts = []
        for a in rows:
            moved = stencil(
                slab,
                lambda d: (a + d,),
                center_ref[1, outer, :],
                lower_ref[1, outer, :],
                upper_ref[1, outer, :],
                side_ref[1:2, :],
                8,
                wide,
            )
            parts.append(jnp.concatenate([moved, gate_ref[a, outer, :] * moved], axis=1))
        result = product(jnp.concatenate(parts, axis=0), table_ref)
        for k, a in enumerate(rows):
            mixed[a, 0, outer, :] = result[k * wide : (k + 1) * wide, :LANES]
            mixed[a, 1, outer, :] = result[k * wide : (k + 1) * wide, LANES:]
        return [part[8 : 8 + radial, :LANES] for part in parts]

    move([1, azimuth + 2])

    for g, (low, high) in enumerate(zip(cuts, cuts[1:])):

        @pl.loop(0, (high - low) // BATCH)
        def _(b):
            rows = [low + b * BATCH + k for k in range(BATCH)]
            for a, moved in zip(rows, move([a + 2 for a in rows])):
                moved_refs[g][a - low] = slope_ref[a] * moved

    for g, (low, high) in enumerate(zip(cuts, cuts[1:])):

        @pl.loop(low, high)
        def _(a):
            for t in range(2):
                second = stencil(
                    mixed,
                    lambda d: (a + 2 + d, t),
                    center_ref[t, inner, :],
                    lower_ref[t, inner, :],
                    upper_ref[t, inner, :],
                    side_ref[t : t + 1, :],
                    EDGE,
                    radial,
                )
                second_refs[g][a - low, t] = slope_ref[a] * second


def adjoint_kernel(azimuth, radial, low_row, high_row, *refs):
    first, last = low_row == 0, high_row == azimuth + 4
    refs = list(refs)

    def take(number):
        taken = refs[:number]
        del refs[:number]
        return taken

    slots = take(4)
    sides = take(4) if first or last else None
    strip_ref, gate_ref, second_ref, moved_ref = take(4)
    center_ref, lower_ref, upper_ref, side_ref = take(4)
    table1_ref, table2_ref = take(2)
    carry_second, carry_first, carry_sum, moved_before = (None, None, None, None) if first else take(4)
    own_out, next_out, sum_out = take(3)
    keep_second, keep_first = (None, None) if last else take(2)
    second, initial = take(2)

    inner = pl.ds(EDGE, radial)
    wide = radial + 16
    outer = pl.ds(8, wide)
    base = low_row if first else low_row - 2
    first_low, first_high = (1 if first else low_row - 1), high_row - 1
    first_base = first_low if first else first_low - 2
    out_low, out_high = first_base + 1, first_high - 1
    own_low, own_high = max(low_row, 2), min(high_row, azimuth + 2)
    gate_low = max(low_row - 1, 0)

    if not first:
        second[pl.ds(0, 2)] = carry_second[...]
        initial[pl.ds(0, 2)] = carry_first[...]

    rows = high_row - low_row
    strips = product(strip_ref[...].reshape(rows * 8, 4 * RANGE), table1_ref)
    for i in range(rows):
        piece = strips[i * 8 : i * 8 + 8]
        for start in (EDGE - 8, EDGE + radial):
            gate = gate_ref[low_row + i - gate_low, pl.ds(start, 8), :]
            for t in range(2):
                second[low_row + i - base, t, pl.ds(start, 8), :] = (
                    piece[:, t * LANES : (t + 1) * LANES] + gate * piece[:, (t + 2) * LANES : (t + 3) * LANES]
                )

    def bins_of(row):
        if row < 2 or row >= azimuth + 2:
            sources, start, stride = sides, (row if row < 2 else row - azimuth), 4
        else:
            sources, start, stride = slots, row - own_low, own_high - own_low
        return jnp.concatenate([source[pl.ds(start, RANGE, stride=stride), :] for source in sources], axis=0)

    total = jnp.zeros((radial, LANES), jnp.float32) if first else carry_sum[...]
    for group in batches(low_row, high_row):
        result = product(jnp.concatenate([bins_of(row) for row in group], axis=1), table1_ref, 0)
        for k, row in enumerate(group):
            part = result[k * radial : (k + 1) * radial]
            gate = gate_ref[row - gate_low, inner, :]
            for t in range(2):
                frag = part[:, (t + 2) * LANES : (t + 3) * LANES]
                second[row - base, t, inner, :] = part[:, t * LANES : (t + 1) * LANES] + gate * frag
                if own_low <= row < own_high:
                    total += second_ref[row - own_low, t] * frag

    for group in batches(first_low, first_high):
        parts = []
        for row in group:
            halves = [
                stencil(
                    second,
                    lambda d: (row - base + d, t),
                    center_ref[t, outer, :],
                    lower_ref[t, outer, :],
                    upper_ref[t, outer, :],
                    side_ref[t : t + 1, :],
                    8,
                    wide,
                )
                for t in range(2)
            ]
            parts.append(jnp.concatenate(halves, axis=1))
        result = product(jnp.concatenate(parts, axis=0), table2_ref)
        for k, row in enumerate(group):
            part = result[k * wide : (k + 1) * wide]
            frag = part[:, LANES:]
            initial[row - first_base, outer, :] = part[:, :LANES] + gate_ref[row - gate_low, outer, :] * frag
            if own_low <= row < own_high:
                total += moved_ref[row - own_low] * frag[8 : 8 + radial]
            elif 2 <= row < own_low:
                total += moved_before[0] * frag[8 : 8 + radial]
    sum_out[...] = total

    for row in range(out_low, out_high):
        result = stencil(
            initial,
            lambda d: (row - first_base + d,),
            center_ref[1, inner, :],
            lower_ref[1, inner, :],
            upper_ref[1, inner, :],
            side_ref[1:2, :],
            EDGE,
            radial,
        ).T
        own_out[row - out_low] = result[:RANGE]
        next_out[row - out_low] = result[RANGE:]

    if not last:
        keep_second[...] = second[pl.ds(high_row - 2 - base, 2)]
        keep_first[...] = initial[pl.ds(first_high - 2 - first_base, 2)]


def call(kernel, outs, scratch, flops, operands):
    size = sum(x.size * x.dtype.itemsize for x in operands) + sum(4 * math.prod(o) for o in outs)
    vmem = pl.BlockSpec(memory_space=pltpu.VMEM)
    return pl.pallas_call(
        kernel,
        out_shape=[jax.ShapeDtypeStruct(o, jnp.float32) for o in outs],
        in_specs=[vmem] * len(operands),
        out_specs=[vmem] * len(outs),
        scratch_shapes=[pltpu.VMEM(s, jnp.float32) for s in scratch],
        compiler_params=pltpu.CompilerParams(vmem_limit_bytes=VMEM_LIMIT),
        cost_estimate=pl.CostEstimate(flops=flops, bytes_accessed=size, transcendentals=0),
    )(*operands)


def per_device(
    density,
    cotangent,
    drift_in,
    drift_out,
    spread,
    dest_bins,
    bott_split,
    coag_rate,
    frag_pairs,
    frag_gain,
    frag_rate,
    collide_speed,
    frag_speed,
    regime,
):
    own_bins, azimuth, radial = density.shape
    place = lax.axis_index("mass")
    row_index = lax.axis_index("row")
    phis, rows = lax.axis_size("phi"), lax.axis_size("row")
    cuts = [0, azimuth // 2, 3 * azimuth // 4, azimuth]
    spans = list(zip(cuts, cuts[1:]))

    def far(x):
        return lax.ppermute(x, "mass", [(0, 2), (2, 1), (1, 0)])

    def near(x):
        return lax.ppermute(x, "mass", [(0, 1), (1, 2)])

    def ending(x):
        return lax.ppermute(x, "mass", [(3, 2)])

    def returning(x):
        return lax.ppermute(x, "mass", [(2, 3)])

    slot_ranges = [
        jnp.where(place == 2, 0, jnp.where(place == 3, 4, place + 1)),
        jnp.where((place == 1) | (place == 2), place - 1, 4),
        place,
        jnp.where(place == 2, 3, 4),
    ]

    density_next = ending(density)
    pieces = [cotangent[:, i:j] for i, j in spans]
    gathered = [[far(piece), near(piece), piece, ending(piece)] for piece in pieces]

    sigma = jax.nn.sigmoid((collide_speed - frag_speed[None, :]) / gate_width)
    flagged = regime.astype(jnp.float32)
    frag_gate = flagged * sigma
    gate_slope = -flagged * sigma * (1.0 - sigma) / gate_width
    gate_slope = gate_slope * (place < 3).astype(jnp.float32)

    def band(low, high):
        gate_rows = jnp.broadcast_to(frag_gate[None, low:high], (8, high - low, radial))
        return jnp.concatenate([cotangent[:, low:high], density[:, low:high], gate_rows], axis=0)

    upper_band, lower_band = band(azimuth - 2, azimuth), band(0, 2)
    if phis == 2:
        other = lax.ppermute(jnp.concatenate([upper_band, lower_band], axis=1), "phi", [(0, 1), (1, 0)])
    else:
        ring = [(i, (i + 1) % phis) for i in range(phis)]
        other = jnp.concatenate(
            [lax.ppermute(upper_band, "phi", ring), lax.ppermute(lower_band, "phi", [(j, i) for i, j in ring])], axis=1
        )
    sides = other[: 2 * own_bins]
    sides_cot, sides_den = sides[:own_bins], sides[own_bins:]
    gates = jnp.concatenate([other[-1, :2], frag_gate, other[-1, 2:]], axis=0)

    first_cols, last_cols = call(
        functools.partial(edge_kernel, azimuth, radial),
        [(azimuth + 4, 2, LANES)] * 2,
        [],
        10**7,
        [
            cotangent.reshape(own_bins * azimuth, radial),
            density.reshape(own_bins * azimuth, radial),
            sides.reshape(2 * own_bins * 4, radial),
        ],
    )
    count = azimuth + 4

    def with_gate(cols, gate_cols):
        flat = jnp.pad(gate_cols.reshape(-1), (0, LANES - 2 * count)).reshape(1, LANES)
        return jnp.concatenate([cols.reshape(2 * count, LANES), jnp.broadcast_to(flat, (8, LANES))], axis=0)

    line = [(i, i + 1) for i in range(rows - 1)]
    left = lax.ppermute(with_gate(last_cols, gates[:, radial - 2 :]), "row", line)
    right = lax.ppermute(with_gate(first_cols, gates[:, :2]), "row", [(j, i) for i, j in line])
    left_cols, right_cols = (x[: 2 * count].reshape(count, 2, LANES) for x in (left, right))
    left_gate, right_gate = (x[2 * count, : 2 * count].reshape(count, 2) for x in (left, right))

    gap = jnp.zeros((count, EDGE - 2), jnp.float32)
    gates = jnp.concatenate([gap, left_gate, gates, right_gate, gap], axis=1)
    gate_wide = jnp.broadcast_to(gates[:, :, None], gates.shape + (LANES,))
    slope_wide = jnp.broadcast_to(gate_slope[:, :, None], gate_slope.shape + (LANES,))

    drift_in, drift_out, spread, frag_gain, other = lax.optimization_barrier(
        (drift_in, drift_out, spread, frag_gain, other)
    )

    def window(drift):
        padded = jnp.pad(drift, ((0, 0), (EDGE, EDGE)))
        wide = lax.dynamic_slice_in_dim(padded, row_index * radial, radial + 2 * EDGE, 1)
        return wide.T

    length = radial + 2 * EDGE
    drifts = jnp.concatenate([window(drift_in), window(drift_out)], axis=0)
    spreads = jnp.broadcast_to(spread[None, :], (8, own_bins))
    edges = jnp.concatenate([left_cols, right_cols], axis=1)
    edges_cot, edges_den = edges[:, :, :own_bins], edges[:, :, own_bins:]

    def packed(parts):
        return jnp.concatenate([p.reshape(-1, LANES) for p in parts], axis=0)

    def unpacked(message, parts):
        out, at = [], 0
        for p in parts:
            size = p.size // LANES
            out.append(message[at : at + size].reshape(p.shape))
            at += size
        return out

    own_parts = [edges_cot, sides_cot, drifts, spreads]
    den_parts = [edges_den, sides_den]
    message = packed(own_parts)
    *over, den_edges, den_sides = unpacked(ending(packed(own_parts + den_parts)), own_parts + den_parts)
    by_slot = [unpacked(far(message), own_parts), unpacked(near(message), own_parts), own_parts, over]

    def strip_of(edge_list):
        wide = jnp.concatenate(edge_list, axis=2)
        blank = jnp.zeros((count, 4, wide.shape[2]), jnp.float32)
        return jnp.concatenate([wide[:, 2:], blank, wide[:, :2]], axis=1)

    strip_cot = strip_of([s[0] for s in by_slot])
    strip_den = strip_of([edges_den, den_edges])
    sides_by_slot = [s[1].reshape(own_bins * 4, radial) for s in by_slot]

    def tiled(wide):
        return wide.reshape(wide.shape[0], 2, LANES).transpose(1, 0, 2)

    drift_wide = tiled(jnp.concatenate([s[2] for s in by_slot], axis=1))
    inward, outward = drift_wide[:, :length], drift_wide[:, length:]
    side = tiled(jnp.concatenate([s[3] for s in by_slot], axis=1)[:1])[:, 0]
    center = 1.0 - inward - outward - 2.0 * side[:, None, :]
    inward_next = jnp.concatenate([inward[:, 1:], inward[:, :1]], axis=1)
    outward_last = jnp.concatenate([outward[:, -1:], outward[:, :-1]], axis=1)

    def chosen(matrix, axis):
        return jnp.concatenate(
            [lax.dynamic_slice_in_dim(matrix, r * RANGE, RANGE, axis) for r in slot_ranges], axis=axis
        )

    def related(matrix):
        return chosen(chosen(jnp.pad(matrix, ((0, RANGE), (0, RANGE))), 0), 1)

    coag = related(coag_matrix(dest_bins, bott_split, coag_rate))
    frag = related(frag_matrix(frag_pairs, frag_gain, frag_rate))
    both = stacked(jnp.concatenate([coag, frag], axis=1))
    upper_half = jnp.concatenate([coag[:, 2 * RANGE :], frag[:, 2 * RANGE :]], axis=1)
    own_cols = stacked(upper_half)
    own_rows = stacked(upper_half.T)

    products = call(
        functools.partial(forward_kernel, azimuth, radial, cuts),
        [(j - i, radial, LANES) for i, j in spans] + [(j - i, 2, radial, LANES) for i, j in spans],
        [(count, length, LANES), (count, 2, length, LANES)],
        6 * (azimuth + 2) * (radial + 16) * 256 * 256,
        [
            density.reshape(own_bins * azimuth, radial),
            density_next.reshape(own_bins * azimuth, radial),
            sides_den.reshape(own_bins * 4, radial),
            den_sides.reshape(own_bins * 4, radial),
            strip_den,
            gate_wide,
            slope_wide,
            center,
            outward_last,
            inward_next,
            side,
            own_rows,
        ],
    )
    groups = len(spans)
    moved, second = products[:groups], products[groups:]

    own_outs, next_outs, carry = [], [], []
    for g in range(groups):
        first, last = g == 0, g == groups - 1
        low_row = 0 if first else cuts[g] + 2
        high_row = azimuth + 4 if last else cuts[g + 1] + 2
        new = high_row - low_row
        n_out = (azimuth + 2 if last else high_row - 2) - (2 if first else low_row - 2)
        operands = [x.reshape(-1, radial) for x in gathered[g]]
        if first or last:
            operands += sides_by_slot
        operands += [strip_cot[low_row:high_row], gate_wide[max(low_row - 1, 0) : high_row], second[g], moved[g]]
        operands += [center, inward, outward, side, both, own_cols, *carry]
        if not first:
            operands.append(moved[g - 1][-1:])
        outs = [(n_out, RANGE, radial), (n_out, RANGE, radial), (radial, LANES)]
        if not last:
            outs += [(2, 2, length, LANES), (2, length, LANES)]
        own_out, next_out, total, *kept = call(
            functools.partial(adjoint_kernel, azimuth, radial, low_row, high_row),
            outs,
            [(new + 2, 2, length, LANES), (new + 2, length, LANES)],
            6 * new * (radial + 16) * 256 * 768,
            operands,
        )
        carry = [*kept, total]
        own_outs.append(own_out)
        next_outs.append(returning(next_out))
    result = jnp.concatenate(
        [jnp.where(place == 3, there, here) for here, there in zip(own_outs, next_outs)], axis=0
    ).transpose(1, 0, 2)
    speed_gradient = jnp.sum(total, axis=1)
    size = lax.axis_size("mass")
    shares = [
        lax.ppermute(speed_gradient, "mass", [(i, (i + k) % size) for i in range(size)]) for k in range(1, size)
    ]
    shares = jnp.stack([*reversed(shares), speed_gradient] * 2)
    speed_gradient = jnp.sum(lax.dynamic_slice_in_dim(shares, size - 1 - place, size, 0), axis=0)
    step = 1
    while step < phis:
        speed_gradient += lax.ppermute(speed_gradient, "phi", [(i, i ^ step) for i in range(phis)])
        step *= 2
    return (result, speed_gradient)


def solution(mesh):
    in_specs = (
        P("mass", "phi", "row"),
        P("mass", "phi", "row"),
        P("mass", None),
        P("mass", None),
        P("mass"),
        P(),
        P(),
        P(),
        P(),
        P(),
        P(),
        P("phi", "row"),
        P("row"),
        P("phi", "row"),
    )
    out_specs = (P("mass", "phi", "row"), P("row"))
    return jax.shard_map(
        per_device, mesh=mesh, in_specs=in_specs, out_specs=out_specs, check_vma=False
    )
```

time: 188 us -> 152 us (0.81)
  the two profiles are of different devices: /device:TPU:0 before, /device:TPU:24 now
where the time goes in v2:
time: 152 us; the launch traced here: 151 us
  starting transfers between devices  48.2 us (32%)
  Pallas kernels  38.5 us (25%)
  local copies, waits for them, and re-layouts  32.2 us (21%)
  waiting for transfers between devices  19.5 us (13%)
  other arithmetic  11 us (7%)
  between operations  1.57 us (1%)
    pallas_call x5, Pallas kernels, call(): pl.pallas_call(kernel, out_shape=[jax.ShapeDtypeStruct(o, jnp.float32) fo...  38.5 us
    ppermute x5, starting transfers between devices, ending(): return lax.ppermute(x, 'mass', [(3, 2)])  25.6 us
    ppermute x3, waiting for transfers between devices, returning(): return lax.ppermute(x, 'mass', [(2, 3)])  11.8 us
    broadcast_in_dim x4, local copies, waits for them, and re-layouts, per_device(): gate_wide = jnp.broadcast_to(gates[:, :, None], gates.shape + (LANES,))  6.03 us
    slice x12, local copies, waits for them, and re-layouts, unpacked(): out.append(message[at:at + size].reshape(p.shape))  5.31 us
    ppermute x3, starting transfers between devices, per_device(): lax.ppermute(speed_gradient, 'mass', [(i, (i + k) % size) for i in range(...  5.16 us
    ppermute x3, waiting for transfers between devices, per_device(): lax.ppermute(speed_gradient, 'mass', [(i, (i + k) % size) for i in range(...  4.75 us
    ppermute x4, starting transfers between devices, near(): return lax.ppermute(x, 'mass', [(0, 1), (1, 2)])  4.13 us
  transfers between devices with their start and end apart: 23, of which 7 were waited for; matrix products, arithmetic and copies ran while one was open for 27% of the time, Pallas kernels for 25%

profile of v2, /device:TPU:24, one launch (start us, length us, event | category | flops | bytes accessed | tf_op | source)
XLA Modules:
  0.0 151.0 jit_solution(13056628233690346834)
XLA Ops:
  0.7 2.6 %collective-permute-start.9 = (f32[64,32,128]{2,1,0:T(8,128)}, f32[64,32,128]{2,1,0:T(8,128)S(1)}, u32[]{:S(2)}, u32[]{:S(2)}) collective-permute-start(f32[64,32,128]{2,1,0:T(8,128)} %param.14), channel_id=1, source_target_pairs={{3,2},{7,6},{11,10},{15,14},{19,18},{23,22},{27,26},{31,30}} | collective-permute-start | bytes 3145736 | tf_op jit(solution)/shard_map/ppermute | solution.py:323
  6.5 1.6 %collective-permute-start.3 = (f32[136,4,128]{2,1,0:T(4,128)S(1)}, f32[136,4,128]{2,1,0:T(4,128)S(1)}, u32[]{:S(2)}, u32[]{:S(2)}) collective-permute-start(f32[136,4,128]{2,1,0:T(4,128)S(1)} %maximum_maximum_fusion), channel_id=1, source_target_pairs={{0,16},{16,0},{1,17},{17,1},{2,18},{18,2},{3,19},{19,3},{4,20},{20... | collective-permute-start | bytes 835592 | tf_op jit(solution)/shard_map/ppermute | solution.py:351
  8.0 1.9 %slice.179 = f32[64,16,128]{2,1,0:T(8,128)} slice(f32[64,32,128]{2,1,0:T(8,128)} %param.15), slice={[0:64], [0:16], [0:128]} | slice | bytes 1048576 | tf_op jit(solution)/shard_map/slice | solution.py:336
  9.9 1.6 %collective-permute-start = (f32[64,16,128]{2,1,0:T(8,128)}, f32[64,16,128]{2,1,0:T(8,128)}, u32[]{:S(2)}, u32[]{:S(2)}) collective-permute-start(f32[64,16,128]{2,1,0:T(8,128)} %slice.179), channel_id=1, source_target_pairs={{0,2},{2,1},{1,0},{4,6},{6,5},{5,4},{8,10},{10,9},{9,8},{12,14},{1... | collective-permute-start | bytes 1572872 | tf_op jit(solution)/shard_map/ppermute | solution.py:317
  16.9 4.0 %shard_map.149 = (f32[36,2,128]{2,1,0:T(2,128)}, f32[36,2,128]{2,1,0:T(2,128)}) custom-call(f32[2048,128]{1,0:T(8,128)} %bitcast.54, f32[2048,128]{1,0:T(8,128)} %bitcast.52, f32[512,128]{1,0:T(8,128)} %bitcast.62), custom_call_target="tpu_custom_call" | custom-call | flops 10000000 | bytes 2433024 | tf_op jit(solution)/shard_map/pallas_call | solution.py:282
  21.7 1.3 collective-permute-start.4
  29.9 1.5 %collective-permute-start.8 = (f32[820,128]{1,0:T(8,128)S(1)}, f32[820,128]{1,0:T(8,128)S(1)}, u32[]{:S(2)}, u32[]{:S(2)}) collective-permute-start(f32[820,128]{1,0:T(8,128)S(1)} %concatenate.99), channel_id=1, source_target_pairs={{3,2},{7,6},{11,10},{15,14},{19,18},{23,22},{27,26},{31,30}} | collective-permute-start | bytes 1259528 | tf_op jit(solution)/shard_map/ppermute | solution.py:323
  32.8 1.3 collective-permute-start.7
  36.3 1.4 collective-permute-start.1
  37.8 13.9 %collective-permute-start.2 = (f32[64,16,128]{2,1,0:T(8,128)}, f32[64,16,128]{2,1,0:T(8,128)}, u32[]{:S(2)}, u32[]{:S(2)}) collective-permute-start(f32[64,16,128]{2,1,0:T(8,128)} %slice.179), channel_id=1, source_target_pairs={{3,2},{7,6},{11,10},{15,14},{19,18},{23,22},{27,26},{31,30}} | collective-permute-start | bytes 1572872 | tf_op jit(solution)/shard_map/ppermute | solution.py:323
  55.2 1.6 %slice.247.refs_5_ = f32[256,128]{1,0:T(8,128)} slice(f32[492,128]{1,0:T(8,128)} %collective-permute-done.7), slice={[72:328], [0:128]} | slice | bytes 262144 | tf_op jit(solution)/shard_map/slice | solution.py:411
  64.3 2.1 %broadcast_in_dim.88.refs_5_ = f32[36,160,128]{2,1,0:T(8,128)} broadcast(f32[36,160]{1,0:T(8,128)S(1)} %concatenate.102), dimensions={0,1} | broadcast | bytes 2972160 | tf_op jit(solution)/shard_map/broadcast_in_dim | solution.py:386
  66.3 1.9 %broadcast_in_dim.89.refs_6_ = f32[32,128,128]{2,1,0:T(8,128)} broadcast(f32[32,128]{1,0:T(8,128)S(1)} %get-tuple-element.105), dimensions={0,1} | broadcast | bytes 2113536 | tf_op jit(solution)/shard_map/broadcast_in_dim | solution.py:387
  68.3 13.4 %shard_map.150 = (f32[16,128,128]{2,1,0:T(8,128)}, f32[8,128,128]{2,1,0:T(8,128)}, f32[8,128,128]{2,1,0:T(8,128)}, f32[16,2,128,128]{3,2,1,0:T(8,128)}, f32[8,2,...) custom-call(f32[2048,128]{1,0:T(8,128)} %bitcast.53, f32[2048,128]{1,0:T(8,128)} %bitcast.61, f32[256,128]{1,0:T(8,128)} %bitcast.60, ...), custom_call_target="tpu_custom_call" | custom-call | flops 1925185536 | bytes 14730240 | tf_op jit(solution)/shard_map/pallas_call | solution.py:282
  81.7 2.4 %collective-permute-start.13 = (f32[64,8,128]{2,1,0:T(8,128)}, f32[64,8,128]{2,1,0:T(8,128)S(1)}, u32[]{:S(2)}, u32[]{:S(2)}) collective-permute-start(f32[64,8,128]{2,1,0:T(8,128)} %get-tuple-element.61), channel_id=1, source_target_pairs={{3,2},{7,6},{11,10},{15,14},{19,18},{23,22},{27,26},{31,30}} | collective-permute-start | bytes 786440 | tf_op jit(solution)/shard_map/ppermute | solution.py:323
  85.5 5.4 %collective-permute-start.17 = (f32[64,8,128]{2,1,0:T(8,128)S(1)}, f32[64,8,128]{2,1,0:T(8,128)S(1)}, u32[]{:S(2)}, u32[]{:S(2)}) collective-permute-start(f32[64,8,128]{2,1,0:T(8,128)S(1)} %copy-done.11), channel_id=1, source_target_pairs={{3,2},{7,6},{11,10},{15,14},{19,18},{23,22},{27,26},{31,30}} | collective-permute-start | bytes 786440 | tf_op jit(solution)/shard_map/ppermute | solution.py:323
  90.9 1.6 %broadcast_in_dim.86.refs_9_ = f32[18,160,128]{2,1,0:T(8,128)} broadcast(f32[18,160]{1,0:T(8,128)S(1)} %slice-done), dimensions={0,1} | broadcast | bytes 1486080 | tf_op jit(solution)/shard_map/broadcast_in_dim | solution.py:386
  92.5 9.1 %shard_map.151 = (f32[14,64,128]{2,1,0:T(8,128)}, f32[14,64,128]{2,1,0:T(8,128)}, f32[128,128]{1,0:T(8,128)}, f32[2,2,160,128]{3,2,1,0:T(8,128)}, f32[2,160,128]{2,1,0:T(8,128)}) custom-call(f32[1024,128]{1,0:T(8,128)} %bitcast.refs_0_, f32[1024,128]{1,0:T(8,128)} %bitcast.1.refs_1_, f32[1024,128]{1,0:T(8,128)} %bitcast.2.refs_2_, ...), custom_call_target="tpu_custom_call" | custom-call | flops 3057647616 | bytes 10535936 | tf_op jit(solution)/shard_map/pallas_call | solution.py:282
  101.6 1.5 slice.229.refs_17_
  104.2 5.6 %shard_map.152 = (f32[8,64,128]{2,1,0:T(8,128)}, f32[8,64,128]{2,1,0:T(8,128)}, f32[128,128]{1,0:T(8,128)}, f32[2,2,160,128]{3,2,1,0:T(8,128)}, f32[2,160,128]{2,1,0:T(8,128)}) custom-call(f32[512,128]{1,0:T(8,128)} %bitcast.64, f32[512,128]{1,0:T(8,128)} %bitcast.65, f32[512,128]{1,0:T(8,128)} %get-tuple-element.58.refs_2_, f32[512,128]{1,0:T(8,128)} %bitcast.66, ...), custom_call_target="tpu_custom_call" | custom-call | flops 1358954496 | bytes 6800384 | tf_op jit(solution)/shard_map/pallas_call | solution.py:282
  109.8 1.3 collective-permute-start.14
  111.8 1.5 slice.233.refs_21_
  114.5 6.3 %shard_map.153 = (f32[10,64,128]{2,1,0:T(8,128)}, f32[10,64,128]{2,1,0:T(8,128)}, f32[128,128]{1,0:T(8,128)}) custom-call(f32[512,128]{1,0:T(8,128)} %bitcast.67, f32[512,128]{1,0:T(8,128)} %bitcast.68, f32[512,128]{1,0:T(8,128)} %get-tuple-element.59.refs_2_, f32[512,128]{1,0:T(8,128)} %bitcast.69, f32[256,128]{1,0:T(8,128)} %slice.246.refs_4_, ...), custom_call_target="tpu_custom_call" | custom-call | flops 1698693120 | bytes 7144448 | tf_op jit(solution)/shard_map/pallas_call | solution.py:282
  120.8 1.4 collective-permute-start.18
  123.2 2.7 %collective-permute-start.19 = (f32[128]{0:T(128)S(1)}, f32[128]{0:T(128)S(1)}, u32[]{:S(2)}, u32[]{:S(2)}) collective-permute-start(f32[128]{0:T(128)S(1)} %reduce_sum.18), channel_id=1, source_target_pairs={{0,3},{1,0},{2,1},{3,2},{4,7},{5,4},{6,5},{7,6},{8,11},{9,8},{10,9... | collective-permute-start | bytes 1544 | tf_op jit(solution)/shard_map/ppermute | solution.py:511
  125.9 2.4 %collective-permute-start.21 = (f32[128]{0:T(128)S(1)}, f32[128]{0:T(128)S(1)}, u32[]{:S(2)}, u32[]{:S(2)}) collective-permute-start(f32[128]{0:T(128)S(1)} %reduce_sum.18), channel_id=1, source_target_pairs={{0,1},{1,2},{2,3},{3,0},{4,5},{5,6},{6,7},{7,4},{8,9},{9,10},{10,1... | collective-permute-start | bytes 1544 | tf_op jit(solution)/shard_map/ppermute | solution.py:511
  128.6 1.8 %collective-permute-done.20 = f32[128]{0:T(128)S(1)} collective-permute-done((f32[128]{0:T(128)S(1)}, f32[128]{0:T(128)S(1)}, u32[]{:S(2)}, u32[]{:S(2)}) %collective-permute-start.20) | collective-permute-done | bytes 544 | tf_op jit(solution)/shard_map/ppermute | solution.py:511
  130.4 2.8 %collective-permute-done.21 = f32[128]{0:T(128)S(1)} collective-permute-done((f32[128]{0:T(128)S(1)}, f32[128]{0:T(128)S(1)}, u32[]{:S(2)}, u32[]{:S(2)}) %collective-permute-start.21) | collective-permute-done | bytes 544 | tf_op jit(solution)/shard_map/ppermute | solution.py:511
  133.2 1.5 %collective-permute-start.22 = (f32[128]{0:T(128)S(1)}, f32[128]{0:T(128)S(1)}, u32[]{:S(2)}, u32[]{:S(2)}) collective-permute-start(f32[128]{0:T(128)S(1)} %fusion.8), channel_id=1, source_target_pairs={{0,16},{16,0},{1,17},{17,1},{2,18},{18,2},{3,19},{19,3},{4,20},{20... | collective-permute-start | bytes 1544 | tf_op jit(solution)/shard_map/ppermute | solution.py:517
  134.7 1.3 collective-permute-start.10
  137.4 11.8 %collective-permute-done.10 = f32[14,64,128]{2,1,0:T(8,128)S(1)} collective-permute-done((f32[14,64,128]{2,1,0:T(8,128)S(1)}, f32[14,64,128]{2,1,0:T(8,128)S(1)}, u32[]{:S(2)}, u32[]{:S(2)}) %collective-permute-start.10) | collective-permute-done | bytes 458784 | tf_op jit(solution)/shard_map/ppermute | solution.py:326
  149.4 1.6 %copy.28 = f32[64,32,128]{2,1,0:T(8,128)} copy(f32[64,32,128]{2,0,1:T(8,128)S(1)} %maximum_bitcast_fusion) | data formatting | bytes 2097152
  (203 shorter events, 37.4 us)
Async XLA Ops:
  0.6 10.9 %copy-start.21 = (s32[256]{0:T(256)S(1)}, s32[256]{0:T(256)}, u32[]{:S(2)}) copy-start(s32[256]{0:T(256)} %param.19) | copy-start | bytes 3076
  0.7 11.0 %copy-start.22 = (s32[4,4]{1,0:T(4,128)S(1)}, s32[4,4]{1,0:T(4,128)}, u32[]{:S(2)}) copy-start(s32[4,4]{1,0:T(4,128)} %param.22) | copy-start | bytes 196
  0.7 62.9 %collective-permute-start.9 = (f32[64,32,128]{2,1,0:T(8,128)}, f32[64,32,128]{2,1,0:T(8,128)S(1)}, u32[]{:S(2)}, u32[]{:S(2)}) collective-permute-start(f32[64,32,128]{2,1,0:T(8,128)} %param.14), channel_id=1, source_target_pairs={{3,2},{7,6},{11,10},{15,14},{19,18},{23,22},{27,26},{31,30}} | collective-permute-start | bytes 3145736 | tf_op jit(solution)/shard_map/ppermute | solution.py:323
  6.5 8.2 %collective-permute-start.3 = (f32[136,4,128]{2,1,0:T(4,128)S(1)}, f32[136,4,128]{2,1,0:T(4,128)S(1)}, u32[]{:S(2)}, u32[]{:S(2)}) collective-permute-start(f32[136,4,128]{2,1,0:T(4,128)S(1)} %maximum_maximum_fusion), channel_id=1, source_target_pairs={{0,16},{16,0},{1,17},{17,1},{2,18},{18,2},{3,19},{19,3},{4,20},{20... | collective-permute-start | bytes 835592 | tf_op jit(solution)/shard_map/ppermute | solution.py:351
  9.9 74.2 %collective-permute-start = (f32[64,16,128]{2,1,0:T(8,128)}, f32[64,16,128]{2,1,0:T(8,128)}, u32[]{:S(2)}, u32[]{:S(2)}) collective-permute-start(f32[64,16,128]{2,1,0:T(8,128)} %slice.179), channel_id=1, source_target_pairs={{0,2},{2,1},{1,0},{4,6},{6,5},{5,4},{8,10},{10,9},{9,8},{12,14},{1... | collective-permute-start | bytes 1572872 | tf_op jit(solution)/shard_map/ppermute | solution.py:317
  21.7 5.8 %collective-permute-start.4 = (f32[80,128]{1,0:T(8,128)S(1)}, f32[80,128]{1,0:T(8,128)S(1)}, u32[]{:S(2)}, u32[]{:S(2)}) collective-permute-start(f32[80,128]{1,0:T(8,128)S(1)} %pad_maximum_fusion.14), channel_id=1, source_target_pairs={{0,4},{4,8},{8,12},{1,5},{5,9},{9,13},{2,6},{6,10},{10,14},{3,7},{... | collective-permute-start | bytes 122888 | tf_op jit(solution)/shard_map/ppermute | solution.py:379
  23.9 4.9 %collective-permute-start.5 = (f32[80,128]{1,0:T(8,128)S(1)}, f32[80,128]{1,0:T(8,128)S(1)}, u32[]{:S(2)}, u32[]{:S(2)}) collective-permute-start(f32[80,128]{1,0:T(8,128)S(1)} %pad_maximum_fusion.15), channel_id=1, source_target_pairs={{4,0},{8,4},{12,8},{5,1},{9,5},{13,9},{6,2},{10,6},{14,10},{7,3},{... | collective-permute-start | bytes 122888 | tf_op jit(solution)/shard_map/ppermute | solution.py:380
  29.9 26.8 %collective-permute-start.8 = (f32[820,128]{1,0:T(8,128)S(1)}, f32[820,128]{1,0:T(8,128)S(1)}, u32[]{:S(2)}, u32[]{:S(2)}) collective-permute-start(f32[820,128]{1,0:T(8,128)S(1)} %concatenate.99), channel_id=1, source_target_pairs={{3,2},{7,6},{11,10},{15,14},{19,18},{23,22},{27,26},{31,30}} | collective-permute-start | bytes 1259528 | tf_op jit(solution)/shard_map/ppermute | solution.py:323
  32.2 4.1 %collective-permute-start.6 = (f32[492,128]{1,0:T(8,128)}, f32[492,128]{1,0:T(8,128)S(1)}, u32[]{:S(2)}, u32[]{:S(2)}) collective-permute-start(f32[492,128]{1,0:T(8,128)} %pad_maximum_fusion.7), channel_id=1, source_target_pairs={{0,2},{2,1},{1,0},{4,6},{6,5},{5,4},{8,10},{10,9},{9,8},{12,14},{1... | collective-permute-start | bytes 755720 | tf_op jit(solution)/shard_map/ppermute | solution.py:317
  32.8 5.0 %collective-permute-start.7 = (f32[492,128]{1,0:T(8,128)}, f32[492,128]{1,0:T(8,128)}, u32[]{:S(2)}, u32[]{:S(2)}) collective-permute-start(f32[492,128]{1,0:T(8,128)} %pad_maximum_fusion.7), channel_id=1, source_target_pairs={{0,1},{1,2},{4,5},{5,6},{8,9},{9,10},{12,13},{13,14},{16,17},{17,1... | collective-permute-start | bytes 755720 | tf_op jit(solution)/shard_map/ppermute | solution.py:320
  36.3 28.0 %copy-start.4 = (f32[36,160]{1,0:T(8,128)}, f32[36,160]{1,0:T(8,128)S(1)}, u32[]{:S(2)}) copy-start(f32[36,160]{1,0:T(8,128)S(1)} %concatenate.102) | copy-start | bytes 69124
  36.3 48.5 %collective-permute-start.1 = (f32[64,16,128]{2,1,0:T(8,128)}, f32[64,16,128]{2,1,0:T(8,128)}, u32[]{:S(2)}, u32[]{:S(2)}) collective-permute-start(f32[64,16,128]{2,1,0:T(8,128)} %slice.179), channel_id=1, source_target_pairs={{0,1},{1,2},{4,5},{5,6},{8,9},{9,10},{12,13},{13,14},{16,17},{17,1... | collective-permute-start | bytes 1572872 | tf_op jit(solution)/shard_map/ppermute | solution.py:320
  37.8 47.7 %collective-permute-start.2 = (f32[64,16,128]{2,1,0:T(8,128)}, f32[64,16,128]{2,1,0:T(8,128)}, u32[]{:S(2)}, u32[]{:S(2)}) collective-permute-start(f32[64,16,128]{2,1,0:T(8,128)} %slice.179), channel_id=1, source_target_pairs={{3,2},{7,6},{11,10},{15,14},{19,18},{23,22},{27,26},{31,30}} | collective-permute-start | bytes 1572872 | tf_op jit(solution)/shard_map/ppermute | solution.py:323
  56.7 25.0 %collective-permute-start.11 = (f32[64,8,128]{2,1,0:T(8,128)}, f32[64,8,128]{2,1,0:T(8,128)S(1)}, u32[]{:S(2)}, u32[]{:S(2)}) collective-permute-start(f32[64,8,128]{2,1,0:T(8,128)} %get-tuple-element.61), channel_id=1, source_target_pairs={{0,2},{2,1},{1,0},{4,6},{6,5},{5,4},{8,10},{10,9},{9,8},{12,14},{1... | collective-permute-start | bytes 786440 | tf_op jit(solution)/shard_map/ppermute | solution.py:317
  63.6 39.5 %collective-permute-start.12 = (f32[64,8,128]{2,1,0:T(8,128)}, f32[64,8,128]{2,1,0:T(8,128)S(1)}, u32[]{:S(2)}, u32[]{:S(2)}) collective-permute-start(f32[64,8,128]{2,1,0:T(8,128)} %get-tuple-element.61), channel_id=1, source_target_pairs={{0,1},{1,2},{4,5},{5,6},{8,9},{9,10},{12,13},{13,14},{16,17},{17,1... | collective-permute-start | bytes 786440 | tf_op jit(solution)/shard_map/ppermute | solution.py:320
  68.3 15.8 %copy-start.11 = (f32[64,8,128]{2,1,0:T(8,128)S(1)}, f32[64,8,128]{2,1,0:T(8,128)}, u32[]{:S(2)}) copy-start(f32[64,8,128]{2,1,0:T(8,128)} %get-tuple-element.60) | copy-start | bytes 786436
  68.3 22.6 %slice-start = ((f32[36,160]{1,0:T(8,128)}), f32[18,160]{1,0:T(8,128)S(1)}, s32[]{:S(2)}) async-start(f32[36,160]{1,0:T(8,128)} %copy-done.4), calls=%async_computation | async-start | bytes 49152 | tf_op jit(solution)/shard_map/slice | solution.py:488
  81.7 19.9 %copy-start.7 = (f32[64,8,128]{2,1,0:T(8,128)}, f32[64,8,128]{2,1,0:T(8,128)S(1)}, u32[]{:S(2)}) copy-start(f32[64,8,128]{2,1,0:T(8,128)S(1)} %collective-permute-done.11) | copy-start | bytes 786436
  81.7 21.4 %collective-permute-start.13 = (f32[64,8,128]{2,1,0:T(8,128)}, f32[64,8,128]{2,1,0:T(8,128)S(1)}, u32[]{:S(2)}, u32[]{:S(2)}) collective-permute-start(f32[64,8,128]{2,1,0:T(8,128)} %get-tuple-element.61), channel_id=1, source_target_pairs={{3,2},{7,6},{11,10},{15,14},{19,18},{23,22},{27,26},{31,30}} | collective-permute-start | bytes 786440 | tf_op jit(solution)/shard_map/ppermute | solution.py:323
  84.1 29.1 %collective-permute-start.15 = (f32[64,8,128]{2,1,0:T(8,128)S(1)}, f32[64,8,128]{2,1,0:T(8,128)S(1)}, u32[]{:S(2)}, u32[]{:S(2)}) collective-permute-start(f32[64,8,128]{2,1,0:T(8,128)S(1)} %copy-done.11), channel_id=1, source_target_pairs={{0,2},{2,1},{1,0},{4,6},{6,5},{5,4},{8,10},{10,9},{9,8},{12,14},{1... | collective-permute-start | bytes 786440 | tf_op jit(solution)/shard_map/ppermute | solution.py:317
  84.8 28.4 %collective-permute-start.16 = (f32[64,8,128]{2,1,0:T(8,128)S(1)}, f32[64,8,128]{2,1,0:T(8,128)S(1)}, u32[]{:S(2)}, u32[]{:S(2)}) collective-permute-start(f32[64,8,128]{2,1,0:T(8,128)S(1)} %copy-done.11), channel_id=1, source_target_pairs={{0,1},{1,2},{4,5},{5,6},{8,9},{9,10},{12,13},{13,14},{16,17},{17,1... | collective-permute-start | bytes 786440 | tf_op jit(solution)/shard_map/ppermute | solution.py:320
  85.5 27.8 %collective-permute-start.17 = (f32[64,8,128]{2,1,0:T(8,128)S(1)}, f32[64,8,128]{2,1,0:T(8,128)S(1)}, u32[]{:S(2)}, u32[]{:S(2)}) collective-permute-start(f32[64,8,128]{2,1,0:T(8,128)S(1)} %copy-done.11), channel_id=1, source_target_pairs={{3,2},{7,6},{11,10},{15,14},{19,18},{23,22},{27,26},{31,30}} | collective-permute-start | bytes 786440 | tf_op jit(solution)/shard_map/ppermute | solution.py:323
  109.8 27.5 %collective-permute-start.14 = (f32[8,64,128]{2,1,0:T(8,128)}, f32[8,64,128]{2,1,0:T(8,128)S(1)}, u32[]{:S(2)}, u32[]{:S(2)}) collective-permute-start(f32[8,64,128]{2,1,0:T(8,128)} %get-tuple-element.42), channel_id=1, source_target_pairs={{2,3},{6,7},{10,11},{14,15},{18,19},{22,23},{26,27},{30,31}} | collective-permute-start | bytes 786440 | tf_op jit(solution)/shard_map/ppermute | solution.py:326
  114.5 20.2 %copy-start.27 = (f32[14,64,128]{2,1,0:T(8,128)S(1)}, f32[14,64,128]{2,1,0:T(8,128)}, u32[]{:S(2)}) copy-start(f32[14,64,128]{2,1,0:T(8,128)} %get-tuple-element.35) | copy-start | bytes 1376260
  114.5 22.8 %copy-start.12 = (f32[8,64,128]{2,1,0:T(8,128)S(1)}, f32[8,64,128]{2,1,0:T(8,128)}, u32[]{:S(2)}) copy-start(f32[8,64,128]{2,1,0:T(8,128)} %get-tuple-element.43) | copy-start | bytes 786436
  120.8 28.4 %copy-start.6 = (f32[14,64,128]{2,1,0:T(8,128)S(1)}, f32[14,64,128]{2,1,0:T(8,128)}, u32[]{:S(2)}) copy-start(f32[14,64,128]{2,1,0:T(8,128)} %get-tuple-element.36) | copy-start | bytes 1376260
  120.8 16.5 %collective-permute-start.18 = (f32[10,64,128]{2,1,0:T(8,128)}, f32[10,64,128]{2,1,0:T(8,128)S(1)}, u32[]{:S(2)}, u32[]{:S(2)}) collective-permute-start(f32[10,64,128]{2,1,0:T(8,128)} %get-tuple-element.49), channel_id=1, source_target_pairs={{2,3},{6,7},{10,11},{14,15},{18,19},{22,23},{26,27},{30,31}} | collective-permute-start | bytes 983048 | tf_op jit(solution)/shard_map/ppermute | solution.py:326
  123.2 5.4 %collective-permute-start.19 = (f32[128]{0:T(128)S(1)}, f32[128]{0:T(128)S(1)}, u32[]{:S(2)}, u32[]{:S(2)}) collective-permute-start(f32[128]{0:T(128)S(1)} %reduce_sum.18), channel_id=1, source_target_pairs={{0,3},{1,0},{2,1},{3,2},{4,7},{5,4},{6,5},{7,6},{8,11},{9,8},{10,9... | collective-permute-start | bytes 1544 | tf_op jit(solution)/shard_map/ppermute | solution.py:511
  125.9 4.4 %collective-permute-start.20 = (f32[128]{0:T(128)S(1)}, f32[128]{0:T(128)S(1)}, u32[]{:S(2)}, u32[]{:S(2)}) collective-permute-start(f32[128]{0:T(128)S(1)} %reduce_sum.18), channel_id=1, source_target_pairs={{0,2},{1,3},{2,0},{3,1},{4,6},{5,7},{6,4},{7,5},{8,10},{9,11},{10,... | collective-permute-start | bytes 1544 | tf_op jit(solution)/shard_map/ppermute | solution.py:511
  125.9 7.2 %collective-permute-start.21 = (f32[128]{0:T(128)S(1)}, f32[128]{0:T(128)S(1)}, u32[]{:S(2)}, u32[]{:S(2)}) collective-permute-start(f32[128]{0:T(128)S(1)} %reduce_sum.18), channel_id=1, source_target_pairs={{0,1},{1,2},{2,3},{3,0},{4,5},{5,6},{6,7},{7,4},{8,9},{9,10},{10,1... | collective-permute-start | bytes 1544 | tf_op jit(solution)/shard_map/ppermute | solution.py:511
  133.2 3.6 %collective-permute-start.22 = (f32[128]{0:T(128)S(1)}, f32[128]{0:T(128)S(1)}, u32[]{:S(2)}, u32[]{:S(2)}) collective-permute-start(f32[128]{0:T(128)S(1)} %fusion.8), channel_id=1, source_target_pairs={{0,16},{16,0},{1,17},{17,1},{2,18},{18,2},{3,19},{19,3},{4,20},{20... | collective-permute-start | bytes 1544 | tf_op jit(solution)/shard_map/ppermute | solution.py:517
  134.7 14.5 %collective-permute-start.10 = (f32[14,64,128]{2,1,0:T(8,128)S(1)}, f32[14,64,128]{2,1,0:T(8,128)S(1)}, u32[]{:S(2)}, u32[]{:S(2)}) collective-permute-start(f32[14,64,128]{2,1,0:T(8,128)S(1)} %copy-done.27), channel_id=1, source_target_pairs={{2,3},{6,7},{10,11},{14,15},{18,19},{22,23},{26,27},{30,31}} | collective-permute-start | bytes 1376264 | tf_op jit(solution)/shard_map/ppermute | solution.py:326
  (20 other events, 97.0 us)

commit v3 on v2

--- a/solution.py
+++ b/solution.py
@@ -1,5 +1,4 @@
 import functools
-import math
 
 import jax
 import jax.numpy as jnp
@@ -13,6 +12,7 @@
 EDGE = 16
 gate_width = 0.5
 BATCH = 4
+MICRO = 3 * 10**6
 VMEM_LIMIT = 56 * 2**20
 
 
@@ -71,52 +71,73 @@
     return [range(i, min(i + BATCH, high)) for i in range(low, high, BATCH)]
 
 
-def edge_kernel(azimuth, radial, cot_ref, den_ref, sides_ref, first_ref, last_ref):
-    def put(row, cot, den):
-        wide = jnp.concatenate([cot, den], axis=0).T
-        first_ref[row] = wide[:2]
-        last_ref[row] = wide[radial - 2 :]
-
-    for row, k in ((0, 0), (1, 1), (azimuth + 2, 2), (azimuth + 3, 3)):
-        both = sides_ref[pl.ds(k, 2 * RANGE, stride=4), :]
-        put(row, both[:RANGE], both[RANGE:])
-
-    @pl.loop(0, azimuth // BATCH)
+def edge_kernel(count, radial, cot_ref, den_ref, first_ref, last_ref):
+    @pl.loop(0, count // BATCH)
     def _(b):
         for k in range(BATCH):
             a = b * BATCH + k
-            put(
-                a + 2,
-                cot_ref[pl.ds(a, RANGE, stride=azimuth), :],
-                den_ref[pl.ds(a, RANGE, stride=azimuth), :],
-            )
+            rows = pl.ds(a, RANGE, stride=count)
+            wide = jnp.concatenate([cot_ref[rows, :], den_ref[rows, :]], axis=0).T
+            first_ref[a] = wide[:2]
+            last_ref[a] = wide[radial - 2 :]
+
+
+def halo_starts(azimuth):
+    cot_sides = 4 * (azimuth + 4)
+    return cot_sides, cot_sides + 4 * RANGE, cot_sides + 8 * RANGE
+
+
+def pair(left, right, half):
+    lanes = slice(half * RANGE, (half + 1) * RANGE)
+    return jnp.concatenate([left[:, lanes], right[:, lanes]], axis=1)
+
+
+def load_shares(shares, length, center_ref, lower_ref, upper_ref, side_ref):
+    for t in range(2):
+        left, right = [ref[pl.ds(start, length + 8), :] for ref, start in shares[2 * t : 2 * t + 2]]
+        inward = pair(left[:length], right[:length], 0)
+        outward = pair(left[:length], right[:length], 1)
+        side = pair(left[length:], right[length:], 0)[:1]
+        lower_ref[t] = inward
+        upper_ref[t] = outward
+        side_ref[t : t + 1] = side
+        center_ref[t] = 1.0 - inward - outward - 2.0 * side
 
 
 def forward_kernel(azimuth, radial, cuts, *refs):
-    own_ref, next_ref, own_az_ref, next_az_ref, strip_ref, gate_ref, slope_ref = refs[:7]
-    center_ref, lower_ref, upper_ref, side_ref, table_ref = refs[7:12]
-    moved_refs, second_refs = refs[12 : 12 + len(cuts) - 1], refs[12 + len(cuts) - 1 : -2]
-    slab, mixed = refs[-2:]
+    own_ref, next_ref, far_ref, near_ref, share_ref, own_halo, next_halo, gate_ref, slope_ref, table_ref = refs[:10]
+    refs = refs[10:]
+    groups = len(cuts) - 1
+    moved_refs, second_refs = refs[:groups], refs[groups : 2 * groups]
+    center_ref, inward_ref, outward_ref, side_ref, slab, mixed = refs[2 * groups :]
     inner = pl.ds(EDGE, radial)
     wide = radial + 16
     outer = pl.ds(8, wide)
+    length = radial + 2 * EDGE
+    cot_sides, den_sides, halo_end = halo_starts(azimuth)
+    first_rows = RANGE * cuts[1]
+    shares = [(far_ref, first_rows), (near_ref, first_rows), (share_ref, 0), (next_halo, halo_end)]
+    load_shares(shares, length, center_ref, inward_ref, outward_ref, side_ref)
 
     def place(row, source, other, start, stride):
         bins = jnp.concatenate(
             [source[pl.ds(start, RANGE, stride=stride), :], other[pl.ds(start, RANGE, stride=stride), :]], axis=0
         )
         slab[row, inner, :] = bins.T
-        tile = strip_ref[row]
-        slab[row, pl.ds(EDGE - 8, 8), :] = tile
-        slab[row, pl.ds(EDGE + radial, 8), :] = tile
 
     for row, k in ((0, 0), (1, 1), (azimuth + 2, 2), (azimuth + 3, 3)):
-        place(row, own_az_ref, next_az_ref, k, 4)
+        place(row, own_halo, next_halo, den_sides + k, 4)
 
     @pl.loop(0, azimuth // BATCH)
     def _(b):
         for k in range(BATCH):
             place(b * BATCH + k + 2, own_ref, next_ref, b * BATCH + k, azimuth)
+
+    for row in range(azimuth + 4):
+        cells = slice(4 * row, 4 * row + 4)
+        strip = pair(own_halo[cells], next_halo[cells], 1)
+        slab[row, pl.ds(EDGE - 2, 2), :] = strip[:2]
+        slab[row, pl.ds(EDGE + radial, 2), :] = strip[2:]
 
     def move(rows):
         parts = []
@@ -125,8 +146,8 @@
                 slab,
                 lambda d: (a + d,),
                 center_ref[1, outer, :],
-                lower_ref[1, outer, :],
-                upper_ref[1, outer, :],
+                outward_ref[1, pl.ds(7, wide), :],
+                inward_ref[1, pl.ds(9, wide), :],
                 side_ref[1:2, :],
                 8,
                 wide,
@@ -157,8 +178,8 @@
                     mixed,
                     lambda d: (a + 2 + d, t),
                     center_ref[t, inner, :],
-                    lower_ref[t, inner, :],
-                    upper_ref[t, inner, :],
+                    outward_ref[t, pl.ds(EDGE - 1, radial), :],
+                    inward_ref[t, pl.ds(EDGE + 1, radial), :],
                     side_ref[t : t + 1, :],
                     EDGE,
                     radial,
@@ -166,7 +187,7 @@
                 second_refs[g][a - low, t] = slope_ref[a] * second
 
 
-def adjoint_kernel(azimuth, radial, low_row, high_row, *refs):
+def adjoint_kernel(azimuth, radial, low_row, high_row, offsets, *refs):
     first, last = low_row == 0, high_row == azimuth + 4
     refs = list(refs)
 
@@ -176,14 +197,14 @@
         return taken
 
     slots = take(4)
-    sides = take(4) if first or last else None
-    strip_ref, gate_ref, second_ref, moved_ref = take(4)
+    halos = take(4)
     center_ref, lower_ref, upper_ref, side_ref = take(4)
+    gate_ref, second_ref, moved_ref = take(3)
     table1_ref, table2_ref = take(2)
     carry_second, carry_first, carry_sum, moved_before = (None, None, None, None) if first else take(4)
     own_out, next_out, sum_out = take(3)
     keep_second, keep_first = (None, None) if last else take(2)
-    second, initial = take(2)
+    second, initial = refs
 
     inner = pl.ds(EDGE, radial)
     wide = radial + 16
@@ -199,23 +220,27 @@
         second[pl.ds(0, 2)] = carry_second[...]
         initial[pl.ds(0, 2)] = carry_first[...]
 
-    rows = high_row - low_row
-    strips = product(strip_ref[...].reshape(rows * 8, 4 * RANGE), table1_ref)
-    for i in range(rows):
-        piece = strips[i * 8 : i * 8 + 8]
-        for start in (EDGE - 8, EDGE + radial):
-            gate = gate_ref[low_row + i - gate_low, pl.ds(start, 8), :]
+    cot_sides = halo_starts(azimuth)[0]
+
+    cells = slice(4 * low_row, 4 * high_row)
+    edges = [halo[cells] for halo in halos]
+    edges = product(jnp.concatenate([pair(*edges[:2], 0), pair(*edges[2:], 0)], axis=1), table1_ref)
+    for row in range(low_row, high_row):
+        piece = edges[4 * (row - low_row) : 4 * (row - low_row) + 4]
+        for start, k in ((EDGE - 2, 0), (EDGE + radial, 2)):
+            gate = gate_ref[row - gate_low, pl.ds(start, 2), :]
             for t in range(2):
-                second[low_row + i - base, t, pl.ds(start, 8), :] = (
-                    piece[:, t * LANES : (t + 1) * LANES] + gate * piece[:, (t + 2) * LANES : (t + 3) * LANES]
+                second[row - base, t, pl.ds(start, 2), :] = (
+                    piece[k : k + 2, t * LANES : (t + 1) * LANES]
+                    + gate * piece[k : k + 2, (t + 2) * LANES : (t + 3) * LANES]
                 )
 
     def bins_of(row):
         if row < 2 or row >= azimuth + 2:
-            sources, start, stride = sides, (row if row < 2 else row - azimuth), 4
+            starts = [(halo, cot_sides + (row if row < 2 else row - azimuth), 4) for halo in halos]
         else:
-            sources, start, stride = slots, row - own_low, own_high - own_low
-        return jnp.concatenate([source[pl.ds(start, RANGE, stride=stride), :] for source in sources], axis=0)
+            starts = [(slot, row - 2 - offset, stride) for slot, (offset, stride) in zip(slots, offsets)]
+        return jnp.concatenate([ref[pl.ds(start, RANGE, stride=stride), :] for ref, start, stride in starts], axis=0)
 
     total = jnp.zeros((radial, LANES), jnp.float32) if first else carry_sum[...]
     for group in batches(low_row, high_row):
@@ -276,8 +301,7 @@
         keep_first[...] = initial[pl.ds(first_high - 2 - first_base, 2)]
 
 
-def call(kernel, outs, scratch, flops, operands):
-    size = sum(x.size * x.dtype.itemsize for x in operands) + sum(4 * math.prod(o) for o in outs)
+def call(kernel, outs, scratch, operands, micros=1):
     vmem = pl.BlockSpec(memory_space=pltpu.VMEM)
     return pl.pallas_call(
         kernel,
@@ -286,7 +310,7 @@
         out_specs=[vmem] * len(outs),
         scratch_shapes=[pltpu.VMEM(s, jnp.float32) for s in scratch],
         compiler_params=pltpu.CompilerParams(vmem_limit_bytes=VMEM_LIMIT),
-        cost_estimate=pl.CostEstimate(flops=flops, bytes_accessed=size, transcendentals=0),
+        cost_estimate=pl.CostEstimate(flops=0, bytes_accessed=micros * MICRO, transcendentals=0),
     )(*operands)
 
 
@@ -332,9 +356,24 @@
         jnp.where(place == 2, 3, 4),
     ]
 
+    count = azimuth + 4
+    length = radial + 2 * EDGE
+
+    def flat(x):
+        return x.reshape(-1, LANES)
+
+    def window(drift):
+        padded = jnp.pad(drift, ((0, 0), (EDGE, EDGE)))
+        wide = lax.dynamic_slice_in_dim(padded, row_index * radial, length, 1)
+        return wide.T
+
+    spreads = jnp.broadcast_to(jnp.concatenate([spread, spread])[None, :], (8, LANES))
+    shares = jnp.concatenate([jnp.concatenate([window(drift_in), window(drift_out)], axis=1), spreads], axis=0)
+
     density_next = ending(density)
     pieces = [cotangent[:, i:j] for i, j in spans]
-    gathered = [[far(piece), near(piece), piece, ending(piece)] for piece in pieces]
+    opening = jnp.concatenate([flat(pieces[0]), shares], axis=0)
+    far_first, near_first = far(opening), near(opening)
 
     sigma = jax.nn.sigmoid((collide_speed - frag_speed[None, :]) / gate_width)
     flagged = regime.astype(jnp.float32)
@@ -355,29 +394,30 @@
             [lax.ppermute(upper_band, "phi", ring), lax.ppermute(lower_band, "phi", [(j, i) for i, j in ring])], axis=1
         )
     sides = other[: 2 * own_bins]
-    sides_cot, sides_den = sides[:own_bins], sides[own_bins:]
     gates = jnp.concatenate([other[-1, :2], frag_gate, other[-1, 2:]], axis=0)
 
-    first_cols, last_cols = call(
-        functools.partial(edge_kernel, azimuth, radial),
-        [(azimuth + 4, 2, LANES)] * 2,
-        [],
-        10**7,
-        [
-            cotangent.reshape(own_bins * azimuth, radial),
-            density.reshape(own_bins * azimuth, radial),
-            sides.reshape(2 * own_bins * 4, radial),
-        ],
-    )
-    count = azimuth + 4
-
-    def with_gate(cols, gate_cols):
-        flat = jnp.pad(gate_cols.reshape(-1), (0, LANES - 2 * count)).reshape(1, LANES)
-        return jnp.concatenate([cols.reshape(2 * count, LANES), jnp.broadcast_to(flat, (8, LANES))], axis=0)
+    def edge_cells(cot, den):
+        number = cot.shape[1]
+        return call(
+            functools.partial(edge_kernel, number, radial),
+            [(number, 2, LANES)] * 2,
+            [],
+            [flat(cot), flat(den)],
+        )
+
+    own_edges = edge_cells(cotangent, density)
+    side_edges = edge_cells(sides[:own_bins], sides[own_bins:])
+
+    def with_gate(own, side, gate_cols):
+        gate_row = jnp.pad(gate_cols.reshape(-1), (0, LANES - 2 * count)).reshape(1, LANES)
+        parts = [flat(side[:2]), flat(own), flat(side[2:]), jnp.broadcast_to(gate_row, (8, LANES))]
+        return jnp.concatenate(parts, axis=0)
 
     line = [(i, i + 1) for i in range(rows - 1)]
-    left = lax.ppermute(with_gate(last_cols, gates[:, radial - 2 :]), "row", line)
-    right = lax.ppermute(with_gate(first_cols, gates[:, :2]), "row", [(j, i) for i, j in line])
+    left = lax.ppermute(with_gate(own_edges[1], side_edges[1], gates[:, radial - 2 :]), "row", line)
+    right = lax.ppermute(
+        with_gate(own_edges[0], side_edges[0], gates[:, :2]), "row", [(j, i) for i, j in line]
+    )
     left_cols, right_cols = (x[: 2 * count].reshape(count, 2, LANES) for x in (left, right))
     left_gate, right_gate = (x[2 * count, : 2 * count].reshape(count, 2) for x in (left, right))
 
@@ -386,56 +426,9 @@
     gate_wide = jnp.broadcast_to(gates[:, :, None], gates.shape + (LANES,))
     slope_wide = jnp.broadcast_to(gate_slope[:, :, None], gate_slope.shape + (LANES,))
 
-    drift_in, drift_out, spread, frag_gain, other = lax.optimization_barrier(
-        (drift_in, drift_out, spread, frag_gain, other)
-    )
-
-    def window(drift):
-        padded = jnp.pad(drift, ((0, 0), (EDGE, EDGE)))
-        wide = lax.dynamic_slice_in_dim(padded, row_index * radial, radial + 2 * EDGE, 1)
-        return wide.T
-
-    length = radial + 2 * EDGE
-    drifts = jnp.concatenate([window(drift_in), window(drift_out)], axis=0)
-    spreads = jnp.broadcast_to(spread[None, :], (8, own_bins))
-    edges = jnp.concatenate([left_cols, right_cols], axis=1)
-    edges_cot, edges_den = edges[:, :, :own_bins], edges[:, :, own_bins:]
-
-    def packed(parts):
-        return jnp.concatenate([p.reshape(-1, LANES) for p in parts], axis=0)
-
-    def unpacked(message, parts):
-        out, at = [], 0
-        for p in parts:
-            size = p.size // LANES
-            out.append(message[at : at + size].reshape(p.shape))
-            at += size
-        return out
-
-    own_parts = [edges_cot, sides_cot, drifts, spreads]
-    den_parts = [edges_den, sides_den]
-    message = packed(own_parts)
-    *over, den_edges, den_sides = unpacked(ending(packed(own_parts + den_parts)), own_parts + den_parts)
-    by_slot = [unpacked(far(message), own_parts), unpacked(near(message), own_parts), own_parts, over]
-
-    def strip_of(edge_list):
-        wide = jnp.concatenate(edge_list, axis=2)
-        blank = jnp.zeros((count, 4, wide.shape[2]), jnp.float32)
-        return jnp.concatenate([wide[:, 2:], blank, wide[:, :2]], axis=1)
-
-    strip_cot = strip_of([s[0] for s in by_slot])
-    strip_den = strip_of([edges_den, den_edges])
-    sides_by_slot = [s[1].reshape(own_bins * 4, radial) for s in by_slot]
-
-    def tiled(wide):
-        return wide.reshape(wide.shape[0], 2, LANES).transpose(1, 0, 2)
-
-    drift_wide = tiled(jnp.concatenate([s[2] for s in by_slot], axis=1))
-    inward, outward = drift_wide[:, :length], drift_wide[:, length:]
-    side = tiled(jnp.concatenate([s[3] for s in by_slot], axis=1)[:1])[:, 0]
-    center = 1.0 - inward - outward - 2.0 * side[:, None, :]
-    inward_next = jnp.concatenate([inward[:, 1:], inward[:, :1]], axis=1)
-    outward_last = jnp.concatenate([outward[:, -1:], outward[:, :-1]], axis=1)
+    frag_gain, other = lax.optimization_barrier((frag_gain, other))
+    edges = flat(jnp.concatenate([left_cols, right_cols], axis=1))
+    halos = jnp.concatenate([edges, flat(sides)], axis=0)
 
     def chosen(matrix, axis):
         return jnp.concatenate(
@@ -452,28 +445,39 @@
     own_cols = stacked(upper_half)
     own_rows = stacked(upper_half.T)
 
+    halos_next = ending(jnp.concatenate([halos, shares], axis=0))
+    short, pieces[0], far_first, near_first, gate_wide, slope_wide, both, own_cols, own_rows = lax.optimization_barrier(
+        (halos[: halo_starts(azimuth)[1]], pieces[0], far_first, near_first, gate_wide, slope_wide, both, own_cols, own_rows)
+    )
+    gathered = [[far_first, near_first, pieces[0], ending(pieces[0])]]
+    halo_refs = [far(short), near(short), halos, halos_next]
+    late = cotangent[:, cuts[1] :]
+    halos_next, late, *rest = lax.optimization_barrier((halos_next, late, *pieces[1:]))
+    halo_refs[3] = halos_next
+    late_next = ending(late)
+    gathered += [[far(piece), near(piece), piece, late_next] for piece in rest]
+
+    coefs = [(2, length, LANES)] * 3 + [(2, LANES)]
     products = call(
         functools.partial(forward_kernel, azimuth, radial, cuts),
-        [(j - i, radial, LANES) for i, j in spans] + [(j - i, 2, radial, LANES) for i, j in spans],
+        [(j - i, radial, LANES) for i, j in spans] + [(j - i, 2, radial, LANES) for i, j in spans] + coefs,
         [(count, length, LANES), (count, 2, length, LANES)],
-        6 * (azimuth + 2) * (radial + 16) * 256 * 256,
         [
-            density.reshape(own_bins * azimuth, radial),
-            density_next.reshape(own_bins * azimuth, radial),
-            sides_den.reshape(own_bins * 4, radial),
-            den_sides.reshape(own_bins * 4, radial),
-            strip_den,
+            flat(density),
+            flat(density_next),
+            far_first,
+            near_first,
+            shares,
+            halos,
+            halos_next,
             gate_wide,
             slope_wide,
-            center,
-            outward_last,
-            inward_next,
-            side,
             own_rows,
         ],
+        13,
     )
     groups = len(spans)
-    moved, second = products[:groups], products[groups:]
+    moved, second, coefs = products[:groups], products[groups : 2 * groups], products[2 * groups :]
 
     own_outs, next_outs, carry = [], [], []
     for g in range(groups):
@@ -482,22 +486,22 @@
         high_row = azimuth + 4 if last else cuts[g + 1] + 2
         new = high_row - low_row
         n_out = (azimuth + 2 if last else high_row - 2) - (2 if first else low_row - 2)
-        operands = [x.reshape(-1, radial) for x in gathered[g]]
-        if first or last:
-            operands += sides_by_slot
-        operands += [strip_cot[low_row:high_row], gate_wide[max(low_row - 1, 0) : high_row], second[g], moved[g]]
-        operands += [center, inward, outward, side, both, own_cols, *carry]
+        operands = [flat(x) for x in gathered[g]]
+        own = (cuts[g], cuts[g + 1] - cuts[g])
+        offsets = [own, own, own, own if first else (cuts[1], azimuth - cuts[1])]
+        operands += [*halo_refs, *coefs, gate_wide[max(low_row - 1, 0) : high_row], second[g], moved[g]]
+        operands += [both, own_cols, *carry]
         if not first:
             operands.append(moved[g - 1][-1:])
         outs = [(n_out, RANGE, radial), (n_out, RANGE, radial), (radial, LANES)]
         if not last:
             outs += [(2, 2, length, LANES), (2, length, LANES)]
         own_out, next_out, total, *kept = call(
-            functools.partial(adjoint_kernel, azimuth, radial, low_row, high_row),
+            functools.partial(adjoint_kernel, azimuth, radial, low_row, high_row, offsets),
             outs,
             [(new + 2, 2, length, LANES), (new + 2, length, LANES)],
-            6 * new * (radial + 16) * 256 * 768,
             operands,
+            2 + new // 2,
         )
         carry = [*kept, total]
         own_outs.append(own_out)

time: 152 us -> 152 us (level)
  local copies, waits for them, and re-layouts: 32.2 us -> 26.1 us
  Pallas kernels: 38.5 us -> 40.9 us
  waiting for transfers between devices: 19.5 us -> 21.8 us
    ppermute x5 -> x4, starting transfers between devices: 25.6 us -> 11.9 us  [ending(): return lax.ppermute(x, 'mass', [(3, 2)])]
    ppermute x3, starting transfers between devices: 5.16 us -> 15.6 us  [per_device(): lax.ppermute(speed_gradient, 'mass', [(i, (i + k) % size) for i in range(...]
    slice x19 -> x2, local copies, waits for them, and re-layouts: 7.35 us -> 1.42 us  [the longest x1 0.73 us: per_device(): side_edges = edge_cells(sides[:own_bins], sides[own_bins:])]
    broadcast_in_dim x4 -> x1, local copies, waits for them, and re-layouts: 6.03 us -> 0.82 us  [per_device(): gate_wide = jnp.broadcast_to(gates[:, :, None], gates.shape + (LANES,))]
    slice x4 -> x3, local copies, waits for them, and re-layouts: 0.01 us -> 4.39 us  [per_device(): gate_wide[max(low_row - 1, 0):high_row]]
    unnamed x57 -> x67, local copies, waits for them, and re-layouts: 1.97 us -> 5.96 us
    ppermute x5 -> x4, waiting for transfers between devices: 0.01 us -> 3.06 us  [ending(): return lax.ppermute(x, 'mass', [(3, 2)])]
    pallas_call x5 -> x6, Pallas kernels: 38.5 us -> 40.9 us  [call(): pl.pallas_call(kernel, out_shape=[jax.ShapeDtypeStruct(o, jnp.float32) fo...]
  transfers between devices with their start and end apart: 23 -> 22, of which waited for: 7 -> 7; matrix products, arithmetic and copies ran while one was open for 27% -> 19% of each run, Pallas kernels for 25% -> 27%
where the time goes in v3:
time: 152 us; the launch traced here: 150 us
  starting transfers between devices  47.5 us (31%)
  Pallas kernels  40.9 us (27%)
  local copies, waits for them, and re-layouts  26.1 us (17%)
  waiting for transfers between devices  21.8 us (14%)
  other arithmetic  12 us (8%)
    pallas_call x6, Pallas kernels, call(): pl.pallas_call(kernel, out_shape=[jax.ShapeDtypeStruct(o, jnp.float32) fo...  40.9 us
    ppermute x3, starting transfers between devices, per_device(): lax.ppermute(speed_gradient, 'mass', [(i, (i + k) % size) for i in range(...  15.6 us
    ppermute x4, starting transfers between devices, ending(): return lax.ppermute(x, 'mass', [(3, 2)])  11.9 us
    ppermute x3, waiting for transfers between devices, returning(): return lax.ppermute(x, 'mass', [(2, 3)])  11.4 us
    unnamed x67, local copies, waits for them, and re-layouts  5.96 us
    ppermute x4, starting transfers between devices, near(): return lax.ppermute(x, 'mass', [(0, 1), (1, 2)])  5.54 us
    ppermute x4, starting transfers between devices, far(): return lax.ppermute(x, 'mass', [(0, 2), (2, 1), (1, 0)])  4.73 us
    slice x3, local copies, waits for them, and re-layouts, per_device(): gate_wide[max(low_row - 1, 0):high_row]  4.39 us
  transfers between devices with their start and end apart: 22, of which 7 were waited for; matrix products, arithmetic and copies ran while one was open for 19% of the time, Pallas kernels for 27%

profile of v3, /device:TPU:24, one launch (start us, length us, event | category | flops | bytes accessed | tf_op | source)
XLA Modules:
  0.0 149.7 jit_solution(11931093617134140892)
XLA Ops:
  2.7 2.1 %fusion.8 = (f32[64,16,128]{2,1,0:T(8,128)S(1)}, f32[64,16,128]{2,1,0:T(8,128)}) fusion(f32[64,32,128]{2,1,0:T(8,128)} %param.15), kind=kLoop, calls=%fused_computation.71 | loop fusion | bytes 2097152 | tf_op jit(solution)/shard_map/slice | solution.py:374
  6.5 1.5 collective-permute-start.4
  8.0 3.9 %collective-permute-start.9 = (f32[64,32,128]{2,1,0:T(8,128)}, f32[64,32,128]{2,1,0:T(8,128)S(1)}, u32[]{:S(2)}, u32[]{:S(2)}) collective-permute-start(f32[64,32,128]{2,1,0:T(8,128)} %param.14), channel_id=1, source_target_pairs={{3,2},{7,6},{11,10},{15,14},{19,18},{23,22},{27,26},{31,30}} | collective-permute-start | bytes 3145736 | tf_op jit(solution)/shard_map/ppermute | solution.py:347
  15.5 1.6 %collective-permute-start = (f32[136,4,128]{2,1,0:T(4,128)S(1)}, f32[136,4,128]{2,1,0:T(4,128)S(1)}, u32[]{:S(2)}, u32[]{:S(2)}) collective-permute-start(f32[136,4,128]{2,1,0:T(4,128)S(1)} %maximum_maximum_fusion), channel_id=1, source_target_pairs={{0,16},{16,0},{1,17},{17,1},{2,18},{18,2},{3,19},{19,3},{4,20},{20... | collective-permute-start | bytes 835592 | tf_op jit(solution)/shard_map/ppermute | solution.py:390
  17.6 3.8 %shard_map.150 = (f32[32,2,128]{2,1,0:T(2,128)}, f32[32,2,128]{2,1,0:T(2,128)}) custom-call(f32[2048,128]{1,0:T(8,128)} %bitcast.45, f32[2048,128]{1,0:T(8,128)} %bitcast.4.den_ref.refs_0_), custom_call_target="tpu_custom_call" | custom-call | bytes 3000000 | tf_op jit(solution)/shard_map/pallas_call | solution.py:306
  21.5 2.0 %collective-permute-done = f32[136,4,128]{2,1,0:T(4,128)S(1)} collective-permute-done((f32[136,4,128]{2,1,0:T(4,128)S(1)}, f32[136,4,128]{2,1,0:T(4,128)S(1)}, u32[]{:S(2)}, u32[]{:S(2)}) %collective-permute-start) | collective-permute-done | bytes 278560 | tf_op jit(solution)/shard_map/ppermute | solution.py:390
  30.0 1.7 %shard_map.149 = (f32[4,2,128]{2,1,0:T(2,128)}, f32[4,2,128]{2,1,0:T(2,128)}) custom-call(f32[256,128]{1,0:T(8,128)} %bitcast.59, f32[256,128]{1,0:T(8,128)} %bitcast.58), custom_call_target="tpu_custom_call" | custom-call | bytes 3000000 | tf_op jit(solution)/shard_map/pallas_call | solution.py:306
  39.7 1.5 %collective-permute-start.8 = (f32[824,128]{1,0:T(8,128)}, f32[824,128]{1,0:T(8,128)S(1)}, u32[]{:S(2)}, u32[]{:S(2)}) collective-permute-start(f32[824,128]{1,0:T(8,128)} %pad_maximum_fusion.3), channel_id=1, source_target_pairs={{3,2},{7,6},{11,10},{15,14},{19,18},{23,22},{27,26},{31,30}} | collective-permute-start | bytes 1265672 | tf_op jit(solution)/shard_map/ppermute | solution.py:347
  43.3 2.0 %broadcast_in_dim.27.refs_8_ = f32[32,128,128]{2,1,0:T(8,128)} broadcast(f32[32,128]{1,0:T(8,128)S(1)} %copy-done.19), dimensions={0,1} | broadcast | bytes 2113536 | tf_op jit(solution)/shard_map/broadcast_in_dim | solution.py:427
  45.2 1.4 collective-permute-start.5
  46.8 3.0 %collective-permute-done.8.refs_6_.refs_7_ = f32[824,128]{1,0:T(8,128)S(1)} collective-permute-done((f32[824,128]{1,0:T(8,128)}, f32[824,128]{1,0:T(8,128)S(1)}, u32[]{:S(2)}, u32[]{:S(2)}) %collective-permute-start.8) | collective-permute-done | bytes 421920 | tf_op jit(solution)/shard_map/ppermute | solution.py:347
  49.8 5.1 %collective-permute-start.13 = (f32[64,16,128]{2,1,0:T(8,128)S(1)}, f32[64,16,128]{2,1,0:T(8,128)}, u32[]{:S(2)}, u32[]{:S(2)}) collective-permute-start(f32[64,16,128]{2,1,0:T(8,128)S(1)} %copy-done.13), channel_id=1, source_target_pairs={{3,2},{7,6},{11,10},{15,14},{19,18},{23,22},{27,26},{31,30}} | collective-permute-start | bytes 1572872 | tf_op jit(solution)/shard_map/ppermute | solution.py:347
  54.9 1.3 collective-permute-start.6
  57.6 1.3 collective-permute-start.11
  58.9 1.4 collective-permute-start.12
  61.0 1.4 collective-permute-start.15
  63.2 1.3 collective-permute-start.16
  68.4 13.9 %shard_map.151 = (f32[16,128,128]{2,1,0:T(8,128)}, f32[8,128,128]{2,1,0:T(8,128)}, f32[8,128,128]{2,1,0:T(8,128)}, f32[16,2,128,128]{3,2,1,0:T(8,128)}, f32[8,2,...) custom-call(f32[2048,128]{1,0:T(8,128)} %bitcast.4.den_ref.refs_0_, ...), custom_call_target="tpu_custom_call" | custom-call | bytes 39000000 | tf_op jit(solution)/shard_map/pallas_call | solution.py:306
  82.3 1.5 slice.127.refs_20_
  83.8 9.0 %shard_map.152 = (f32[14,64,128]{2,1,0:T(8,128)}, f32[14,64,128]{2,1,0:T(8,128)}, f32[128,128]{1,0:T(8,128)}, f32[2,2,160,128]{3,2,1,0:T(8,128)}, f32[2,160,128]{2,1,0:T(8,128)}) custom-call(f32[1192,128]{1,0:T(8,128)} %copy-done.7, f32[1192,128]{1,0:T(8,128)} %collective-permute-done.4.refs_3_.refs_1_, f32[1024,128]{1,0:T(8,128)} %bitcast.47, ...), custom_call_target="tpu_custom_call" | custom-call | bytes 33000000 | tf_op jit(solution)/shard_map/pallas_call | solution.py:306
  92.8 6.0 %shard_map.153 = (f32[8,64,128]{2,1,0:T(8,128)}, f32[8,64,128]{2,1,0:T(8,128)}, f32[128,128]{1,0:T(8,128)}, f32[2,2,160,128]{3,2,1,0:T(8,128)}, f32[2,160,128]{2,1,0:T(8,128)}) custom-call(f32[512,128]{1,0:T(8,128)} %bitcast.24.refs_0_, f32[512,128]{1,0:T(8,128)} %bitcast.25.refs_1_, f32[512,128]{1,0:T(8,128)} %bitcast.56, f32[1024,128]{1,0:T(8,128)} %bitcast.27.refs_3_, ...), custom_call_target="tpu_custom_call" | custom-call | bytes 18000000 | tf_op jit(solution)/shard_map/pallas_call | solution.py:306
  100.1 2.2 %slice.128.refs_12_ = f32[11,160,128]{2,1,0:T(8,128)} slice(f32[36,160,128]{2,1,0:T(8,128)} %copy-done), slice={[25:36], [0:160], [0:128]} | slice | bytes 1802240 | tf_op jit(solution)/shard_map/slice | solution.py:492
  102.3 1.5 slice.129.refs_20_
  103.7 6.5 %shard_map.154 = (f32[10,64,128]{2,1,0:T(8,128)}, f32[10,64,128]{2,1,0:T(8,128)}, f32[128,128]{1,0:T(8,128)}) custom-call(f32[512,128]{1,0:T(8,128)} %bitcast.28.refs_0_, f32[512,128]{1,0:T(8,128)} %bitcast.29.refs_1_, f32[512,128]{1,0:T(8,128)} %bitcast.55, f32[1024,128]{1,0:T(8,128)} %bitcast.27.refs_3_, f32[400,128]{1,0:T(8,128)} %collective-permute-done.6.refs_4_, ...), custom_call_target="tpu_custom_call" | custom-call | bytes 21000000 | tf_op jit(solution)/shard_map/pallas_call | solution.py:306
  110.3 1.4 collective-permute-start.17
  112.7 11.9 %collective-permute-start.18 = (f32[128]{0:T(128)S(1)}, f32[128]{0:T(128)S(1)}, u32[]{:S(2)}, u32[]{:S(2)}) collective-permute-start(f32[128]{0:T(128)S(1)} %reduce_sum.18), channel_id=1, source_target_pairs={{0,3},{1,0},{2,1},{3,2},{4,7},{5,4},{6,5},{7,6},{8,11},{9,8},{10,9... | collective-permute-start | bytes 1544 | tf_op jit(solution)/shard_map/ppermute | solution.py:515
  124.5 1.5 collective-permute-start.19
  126.0 2.3 %collective-permute-start.20 = (f32[128]{0:T(128)S(1)}, f32[128]{0:T(128)S(1)}, u32[]{:S(2)}, u32[]{:S(2)}) collective-permute-start(f32[128]{0:T(128)S(1)} %reduce_sum.18), channel_id=1, source_target_pairs={{0,1},{1,2},{2,3},{3,0},{4,5},{5,6},{6,7},{7,4},{8,9},{9,10},{10,1... | collective-permute-start | bytes 1544 | tf_op jit(solution)/shard_map/ppermute | solution.py:515
  129.0 3.2 %collective-permute-done.20 = f32[128]{0:T(128)S(1)} collective-permute-done((f32[128]{0:T(128)S(1)}, f32[128]{0:T(128)S(1)}, u32[]{:S(2)}, u32[]{:S(2)}) %collective-permute-start.20) | collective-permute-done | bytes 544 | tf_op jit(solution)/shard_map/ppermute | solution.py:515
  132.3 1.5 %collective-permute-start.21 = (f32[128]{0:T(128)S(1)}, f32[128]{0:T(128)S(1)}, u32[]{:S(2)}, u32[]{:S(2)}) collective-permute-start(f32[128]{0:T(128)S(1)} %fusion.7), channel_id=1, source_target_pairs={{0,16},{16,0},{1,17},{17,1},{2,18},{18,2},{3,19},{19,3},{4,20},{20... | collective-permute-start | bytes 1544 | tf_op jit(solution)/shard_map/ppermute | solution.py:521
  136.5 11.4 %collective-permute-done.10 = f32[14,64,128]{2,1,0:T(8,128)S(1)} collective-permute-done((f32[14,64,128]{2,1,0:T(8,128)S(1)}, f32[14,64,128]{2,1,0:T(8,128)S(1)}, u32[]{:S(2)}, u32[]{:S(2)}) %collective-permute-start.10) | collective-permute-done | bytes 458784 | tf_op jit(solution)/shard_map/ppermute | solution.py:350
  148.1 1.6 %copy.25 = f32[64,32,128]{2,1,0:T(8,128)} copy(f32[64,32,128]{2,0,1:T(8,128)S(1)} %maximum_bitcast_fusion) | data formatting | bytes 2097152
  (164 shorter events, 36.8 us)
Async XLA Ops:
  4.9 12.2 %copy-start.24 = (f32[256]{0:T(256)S(1)}, f32[256]{0:T(256)}, u32[]{:S(2)}) copy-start(f32[256]{0:T(256)} %param.20) | copy-start | bytes 3076
  4.9 12.2 %copy-start.26 = (s32[4,4]{1,0:T(4,128)S(1)}, s32[4,4]{1,0:T(4,128)}, u32[]{:S(2)}) copy-start(s32[4,4]{1,0:T(4,128)} %param.22) | copy-start | bytes 196
  5.8 35.7 %collective-permute-start.3 = (f32[1192,128]{1,0:T(8,128)}, f32[1192,128]{1,0:T(8,128)S(1)}, u32[]{:S(2)}, u32[]{:S(2)}) collective-permute-start(f32[1192,128]{1,0:T(8,128)} %pad_maximum_fusion.1), channel_id=1, source_target_pairs={{0,2},{2,1},{1,0},{4,6},{6,5},{5,4},{8,10},{10,9},{9,8},{12,14},{1... | collective-permute-start | bytes 1830920 | tf_op jit(solution)/shard_map/ppermute | solution.py:341
  6.5 35.9 %collective-permute-start.4 = (f32[1192,128]{1,0:T(8,128)}, f32[1192,128]{1,0:T(8,128)}, u32[]{:S(2)}, u32[]{:S(2)}) collective-permute-start(f32[1192,128]{1,0:T(8,128)} %pad_maximum_fusion.1), channel_id=1, source_target_pairs={{0,1},{1,2},{4,5},{5,6},{8,9},{9,10},{12,13},{13,14},{16,17},{17,1... | collective-permute-start | bytes 1830920 | tf_op jit(solution)/shard_map/ppermute | solution.py:344
  8.0 53.0 %collective-permute-start.9 = (f32[64,32,128]{2,1,0:T(8,128)}, f32[64,32,128]{2,1,0:T(8,128)S(1)}, u32[]{:S(2)}, u32[]{:S(2)}) collective-permute-start(f32[64,32,128]{2,1,0:T(8,128)} %param.14), channel_id=1, source_target_pairs={{3,2},{7,6},{11,10},{15,14},{19,18},{23,22},{27,26},{31,30}} | collective-permute-start | bytes 3145736 | tf_op jit(solution)/shard_map/ppermute | solution.py:347
  15.5 7.9 %collective-permute-start = (f32[136,4,128]{2,1,0:T(4,128)S(1)}, f32[136,4,128]{2,1,0:T(4,128)S(1)}, u32[]{:S(2)}, u32[]{:S(2)}) collective-permute-start(f32[136,4,128]{2,1,0:T(4,128)S(1)} %maximum_maximum_fusion), channel_id=1, source_target_pairs={{0,16},{16,0},{1,17},{17,1},{2,18},{18,2},{3,19},{19,3},{4,20},{20... | collective-permute-start | bytes 835592 | tf_op jit(solution)/shard_map/ppermute | solution.py:390
  32.4 5.7 %collective-permute-start.1 = (f32[80,128]{1,0:T(8,128)S(1)}, f32[80,128]{1,0:T(8,128)S(1)}, u32[]{:S(2)}, u32[]{:S(2)}) collective-permute-start(f32[80,128]{1,0:T(8,128)S(1)} %pad_maximum_fusion.11), channel_id=1, source_target_pairs={{0,4},{4,8},{8,12},{1,5},{5,9},{9,13},{2,6},{6,10},{10,14},{3,7},{... | collective-permute-start | bytes 122888 | tf_op jit(solution)/shard_map/ppermute | solution.py:417
  33.8 4.9 %collective-permute-start.2 = (f32[80,128]{1,0:T(8,128)S(1)}, f32[80,128]{1,0:T(8,128)S(1)}, u32[]{:S(2)}, u32[]{:S(2)}) collective-permute-start(f32[80,128]{1,0:T(8,128)S(1)} %pad_maximum_fusion.12), channel_id=1, source_target_pairs={{4,0},{8,4},{12,8},{5,1},{9,5},{13,9},{6,2},{10,6},{14,10},{7,3},{... | collective-permute-start | bytes 122888 | tf_op jit(solution)/shard_map/ppermute | solution.py:418
  39.7 10.1 %collective-permute-start.8 = (f32[824,128]{1,0:T(8,128)}, f32[824,128]{1,0:T(8,128)S(1)}, u32[]{:S(2)}, u32[]{:S(2)}) collective-permute-start(f32[824,128]{1,0:T(8,128)} %pad_maximum_fusion.3), channel_id=1, source_target_pairs={{3,2},{7,6},{11,10},{15,14},{19,18},{23,22},{27,26},{31,30}} | collective-permute-start | bytes 1265672 | tf_op jit(solution)/shard_map/ppermute | solution.py:347
  43.2 23.4 %copy-start = (f32[36,160,128]{2,1,0:T(8,128)}, f32[36,160,128]{2,1,0:T(8,128)S(1)}, u32[]{:S(2)}) copy-start(f32[36,160,128]{2,1,0:T(8,128)S(1)} %broadcast_in_dim.26.refs_7_) | copy-start | bytes 8847364
  43.3 21.2 %copy-start.6 = (f32[128,4,128]{2,1,0:T(4,128)S(1)}, f32[128,4,128]{2,1,0:T(4,128)}, u32[]{:S(2)}) copy-start(f32[128,4,128]{2,1,0:T(4,128)} %copy-done.5) | copy-start | bytes 786436
  45.2 17.1 %collective-permute-start.5 = (f32[64,16,128]{2,1,0:T(8,128)S(1)}, f32[64,16,128]{2,1,0:T(8,128)S(1)}, u32[]{:S(2)}, u32[]{:S(2)}) collective-permute-start(f32[64,16,128]{2,1,0:T(8,128)S(1)} %copy-done.4), channel_id=1, source_target_pairs={{3,2},{7,6},{11,10},{15,14},{19,18},{23,22},{27,26},{31,30}} | collective-permute-start | bytes 1572872 | tf_op jit(solution)/shard_map/ppermute | solution.py:347
  46.7 19.9 %copy-start.9 = (f32[64,8,128]{2,1,0:T(8,128)}, f32[64,8,128]{2,1,0:T(8,128)S(1)}, u32[]{:S(2)}) copy-start(f32[64,8,128]{2,1,0:T(8,128)S(1)} %get-tuple-element.75) | copy-start | bytes 786436
  46.8 19.8 %copy-start.10 = (f32[64,8,128]{2,1,0:T(8,128)}, f32[64,8,128]{2,1,0:T(8,128)S(1)}, u32[]{:S(2)}) copy-start(f32[64,8,128]{2,1,0:T(8,128)S(1)} %get-tuple-element.66) | copy-start | bytes 786436
  49.8 16.8 %copy-start.2 = (f32[824,128]{1,0:T(8,128)}, f32[824,128]{1,0:T(8,128)S(1)}, u32[]{:S(2)}) copy-start(f32[824,128]{1,0:T(8,128)S(1)} %collective-permute-done.8.refs_6_.refs_7_) | copy-start | bytes 1265668
  49.8 43.0 %collective-permute-start.13 = (f32[64,16,128]{2,1,0:T(8,128)S(1)}, f32[64,16,128]{2,1,0:T(8,128)}, u32[]{:S(2)}, u32[]{:S(2)}) collective-permute-start(f32[64,16,128]{2,1,0:T(8,128)S(1)} %copy-done.13), channel_id=1, source_target_pairs={{3,2},{7,6},{11,10},{15,14},{19,18},{23,22},{27,26},{31,30}} | collective-permute-start | bytes 1572872 | tf_op jit(solution)/shard_map/ppermute | solution.py:347
  54.9 2.7 %collective-permute-start.6 = (f32[400,128]{1,0:T(8,128)S(1)}, f32[400,128]{1,0:T(8,128)}, u32[]{:S(2)}, u32[]{:S(2)}) collective-permute-start(f32[400,128]{1,0:T(8,128)S(1)} %fusion.4), channel_id=1, source_target_pairs={{0,2},{2,1},{1,0},{4,6},{6,5},{5,4},{8,10},{10,9},{9,8},{12,14},{1... | collective-permute-start | bytes 614408 | tf_op jit(solution)/shard_map/ppermute | solution.py:341
  56.2 2.7 %collective-permute-start.7 = (f32[400,128]{1,0:T(8,128)S(1)}, f32[400,128]{1,0:T(8,128)}, u32[]{:S(2)}, u32[]{:S(2)}) collective-permute-start(f32[400,128]{1,0:T(8,128)S(1)} %fusion.4), channel_id=1, source_target_pairs={{0,1},{1,2},{4,5},{5,6},{8,9},{9,10},{12,13},{13,14},{16,17},{17,1... | collective-permute-start | bytes 614408 | tf_op jit(solution)/shard_map/ppermute | solution.py:344
  57.6 35.2 %collective-permute-start.11 = (f32[64,8,128]{2,1,0:T(8,128)S(1)}, f32[64,8,128]{2,1,0:T(8,128)}, u32[]{:S(2)}, u32[]{:S(2)}) collective-permute-start(f32[64,8,128]{2,1,0:T(8,128)S(1)} %get-tuple-element.66), channel_id=1, source_target_pairs={{0,2},{2,1},{1,0},{4,6},{6,5},{5,4},{8,10},{10,9},{9,8},{12,14},{1... | collective-permute-start | bytes 786440 | tf_op jit(solution)/shard_map/ppermute | solution.py:341
  58.9 33.9 %collective-permute-start.12 = (f32[64,8,128]{2,1,0:T(8,128)S(1)}, f32[64,8,128]{2,1,0:T(8,128)}, u32[]{:S(2)}, u32[]{:S(2)}) collective-permute-start(f32[64,8,128]{2,1,0:T(8,128)S(1)} %get-tuple-element.66), channel_id=1, source_target_pairs={{0,1},{1,2},{4,5},{5,6},{8,9},{9,10},{12,13},{13,14},{16,17},{17,1... | collective-permute-start | bytes 786440 | tf_op jit(solution)/shard_map/ppermute | solution.py:344
  61.0 42.7 %collective-permute-start.15 = (f32[64,8,128]{2,1,0:T(8,128)S(1)}, f32[64,8,128]{2,1,0:T(8,128)}, u32[]{:S(2)}, u32[]{:S(2)}) collective-permute-start(f32[64,8,128]{2,1,0:T(8,128)S(1)} %get-tuple-element.75), channel_id=1, source_target_pairs={{0,2},{2,1},{1,0},{4,6},{6,5},{5,4},{8,10},{10,9},{9,8},{12,14},{1... | collective-permute-start | bytes 786440 | tf_op jit(solution)/shard_map/ppermute | solution.py:341
  63.2 40.6 %collective-permute-start.16 = (f32[64,8,128]{2,1,0:T(8,128)S(1)}, f32[64,8,128]{2,1,0:T(8,128)}, u32[]{:S(2)}, u32[]{:S(2)}) collective-permute-start(f32[64,8,128]{2,1,0:T(8,128)S(1)} %get-tuple-element.75), channel_id=1, source_target_pairs={{0,1},{1,2},{4,5},{5,6},{8,9},{9,10},{12,13},{13,14},{16,17},{17,1... | collective-permute-start | bytes 786440 | tf_op jit(solution)/shard_map/ppermute | solution.py:344
  98.8 37.6 %collective-permute-start.14 = (f32[8,64,128]{2,1,0:T(8,128)}, f32[8,64,128]{2,1,0:T(8,128)S(1)}, u32[]{:S(2)}, u32[]{:S(2)}) collective-permute-start(f32[8,64,128]{2,1,0:T(8,128)} %get-tuple-element.73), channel_id=1, source_target_pairs={{2,3},{6,7},{10,11},{14,15},{18,19},{22,23},{26,27},{30,31}} | collective-permute-start | bytes 786440 | tf_op jit(solution)/shard_map/ppermute | solution.py:350
  103.7 30.1 %copy-start.30 = (f32[14,64,128]{2,1,0:T(8,128)S(1)}, f32[14,64,128]{2,1,0:T(8,128)}, u32[]{:S(2)}) copy-start(f32[14,64,128]{2,1,0:T(8,128)} %get-tuple-element.64) | copy-start | bytes 1376260
  103.7 32.7 %copy-start.17 = (f32[8,64,128]{2,1,0:T(8,128)S(1)}, f32[8,64,128]{2,1,0:T(8,128)}, u32[]{:S(2)}) copy-start(f32[8,64,128]{2,1,0:T(8,128)} %get-tuple-element.74) | copy-start | bytes 786436
  110.3 37.6 %copy-start.15 = (f32[14,64,128]{2,1,0:T(8,128)S(1)}, f32[14,64,128]{2,1,0:T(8,128)}, u32[]{:S(2)}) copy-start(f32[14,64,128]{2,1,0:T(8,128)} %get-tuple-element.65) | copy-start | bytes 1376260
  110.3 26.1 %collective-permute-start.17 = (f32[10,64,128]{2,1,0:T(8,128)}, f32[10,64,128]{2,1,0:T(8,128)S(1)}, u32[]{:S(2)}, u32[]{:S(2)}) collective-permute-start(f32[10,64,128]{2,1,0:T(8,128)} %get-tuple-element.81), channel_id=1, source_target_pairs={{2,3},{6,7},{10,11},{14,15},{18,19},{22,23},{26,27},{30,31}} | collective-permute-start | bytes 983048 | tf_op jit(solution)/shard_map/ppermute | solution.py:350
  112.7 15.6 %collective-permute-start.18 = (f32[128]{0:T(128)S(1)}, f32[128]{0:T(128)S(1)}, u32[]{:S(2)}, u32[]{:S(2)}) collective-permute-start(f32[128]{0:T(128)S(1)} %reduce_sum.18), channel_id=1, source_target_pairs={{0,3},{1,0},{2,1},{3,2},{4,7},{5,4},{6,5},{7,6},{8,11},{9,8},{10,9... | collective-permute-start | bytes 1544 | tf_op jit(solution)/shard_map/ppermute | solution.py:515
  124.5 4.4 %collective-permute-start.19 = (f32[128]{0:T(128)S(1)}, f32[128]{0:T(128)S(1)}, u32[]{:S(2)}, u32[]{:S(2)}) collective-permute-start(f32[128]{0:T(128)S(1)} %reduce_sum.18), channel_id=1, source_target_pairs={{0,2},{1,3},{2,0},{3,1},{4,6},{5,7},{6,4},{7,5},{8,10},{9,11},{10,... | collective-permute-start | bytes 1544 | tf_op jit(solution)/shard_map/ppermute | solution.py:515
  126.0 6.2 %collective-permute-start.20 = (f32[128]{0:T(128)S(1)}, f32[128]{0:T(128)S(1)}, u32[]{:S(2)}, u32[]{:S(2)}) collective-permute-start(f32[128]{0:T(128)S(1)} %reduce_sum.18), channel_id=1, source_target_pairs={{0,1},{1,2},{2,3},{3,0},{4,5},{5,6},{6,7},{7,4},{8,9},{9,10},{10,1... | collective-permute-start | bytes 1544 | tf_op jit(solution)/shard_map/ppermute | solution.py:515
  132.3 3.6 %collective-permute-start.21 = (f32[128]{0:T(128)S(1)}, f32[128]{0:T(128)S(1)}, u32[]{:S(2)}, u32[]{:S(2)}) collective-permute-start(f32[128]{0:T(128)S(1)} %fusion.7), channel_id=1, source_target_pairs={{0,16},{16,0},{1,17},{17,1},{2,18},{18,2},{3,19},{19,3},{4,20},{20... | collective-permute-start | bytes 1544 | tf_op jit(solution)/shard_map/ppermute | solution.py:521
  133.8 14.1 %collective-permute-start.10 = (f32[14,64,128]{2,1,0:T(8,128)S(1)}, f32[14,64,128]{2,1,0:T(8,128)S(1)}, u32[]{:S(2)}, u32[]{:S(2)}) collective-permute-start(f32[14,64,128]{2,1,0:T(8,128)S(1)} %copy-done.30), channel_id=1, source_target_pairs={{2,3},{6,7},{10,11},{14,15},{18,19},{22,23},{26,27},{30,31}} | collective-permute-start | bytes 1376264 | tf_op jit(solution)/shard_map/ppermute | solution.py:350
  (22 other events, 125.9 us)

commit v4 on v3

--- a/solution.py
+++ b/solution.py
@@ -71,20 +71,98 @@
     return [range(i, min(i + BATCH, high)) for i in range(low, high, BATCH)]
 
 
-def edge_kernel(count, radial, cot_ref, den_ref, first_ref, last_ref):
-    @pl.loop(0, count // BATCH)
+def side_kernel(azimuth, cot_ref, den_ref, collide_ref, speed_ref, regime_ref, sides_ref, gate_ref, slope_ref):
+    sigma = jax.nn.sigmoid((collide_ref[...] - speed_ref[...]) / gate_width)
+    flagged = regime_ref[...].astype(jnp.float32)
+    gate = flagged * sigma
+    gate_ref[...] = gate
+    ahead = (lax.axis_index("mass") < 3).astype(jnp.float32)
+    slope = -flagged * sigma * (1.0 - sigma) / gate_width * ahead
+    slope_ref[:, :azimuth] = slope.T
+    for k, row in enumerate((azimuth - 2, azimuth - 1, 0, 1)):
+        source, target = pl.ds(row, RANGE, stride=azimuth), pl.ds(k, RANGE, stride=4)
+        sides_ref[target, :] = cot_ref[source, :]
+        sides_ref[pl.ds(4 * RANGE + k, RANGE, stride=4), :] = den_ref[source, :]
+        sides_ref[8 * RANGE + k : 8 * RANGE + k + 1, :] = gate[row : row + 1]
+    sides_ref[8 * RANGE + 4 :, :] = jnp.zeros((4, sides_ref.shape[1]), jnp.float32)
+
+
+def opening_kernel(azimuth, radial, first_rows, *refs):
+    cot_ref, den_ref, in_ref, out_ref, spread_ref, opening_ref, shares_ref, first_ref, last_ref = refs
+
+    block, blocks = lax.axis_index("row"), lax.axis_size("row")
+
+    def window(number):
+        lanes = pl.ds(pl.multiple_of(number * radial, radial), radial)
+        return jnp.concatenate([in_ref[:, lanes], out_ref[:, lanes]], axis=0).T
+
+    before = window(jnp.maximum(block - 1, 0))[radial - EDGE :] * (block > 0).astype(jnp.float32)
+    after = window(jnp.minimum(block + 1, blocks - 1))[:EDGE] * (block < blocks - 1).astype(jnp.float32)
+    spread = jnp.concatenate([spread_ref[...], spread_ref[...]], axis=1)
+    spread = jnp.broadcast_to(spread, (8, LANES))
+    shares = jnp.concatenate([before, window(block), after, spread], axis=0)
+    shares_ref[...] = shares
+    opening_ref[RANGE * first_rows :, :] = shares
+    for b in range(RANGE):
+        opening_ref[b * first_rows : (b + 1) * first_rows, :] = cot_ref[b * azimuth : b * azimuth + first_rows, :]
+
+    @pl.loop(0, azimuth // BATCH)
     def _(b):
         for k in range(BATCH):
             a = b * BATCH + k
-            rows = pl.ds(a, RANGE, stride=count)
+            rows = pl.ds(a, RANGE, stride=azimuth)
             wide = jnp.concatenate([cot_ref[rows, :], den_ref[rows, :]], axis=0).T
             first_ref[a] = wide[:2]
             last_ref[a] = wide[radial - 2 :]
 
 
+def radial_kernel(azimuth, radial, sides_ref, first_ref, last_ref, gate_ref, left_ref, right_ref, table_ref):
+    count = azimuth + 4
+    gates = jnp.concatenate(
+        [
+            sides_ref[8 * RANGE : 8 * RANGE + 2, :],
+            gate_ref[...],
+            sides_ref[8 * RANGE + 2 : 8 * RANGE + 4, :],
+            jnp.zeros((LANES - count, radial), jnp.float32),
+        ],
+        axis=0,
+    ).T
+    table_ref[...] = gates
+    for out_ref, own_ref, start in ((left_ref, last_ref, radial - 2), (right_ref, first_ref, 0)):
+        for k, row in ((0, 0), (1, 1), (2, azimuth + 2), (3, azimuth + 3)):
+            wide = sides_ref[pl.ds(k, 2 * RANGE, stride=4), :].T
+            out_ref[2 * row : 2 * row + 2, :] = wide[start : start + 2]
+        out_ref[4 : 4 + 2 * azimuth, :] = own_ref[...]
+        out_ref[2 * count : 2 * count + 2, :] = gates[start : start + 2]
+        out_ref[2 * count + 2 :, :] = jnp.zeros((6, LANES), jnp.float32)
+
+
+def halo_kernel(azimuth, radial, left_ref, right_ref, sides_ref, shares_ref, gates_ref, *refs):
+    long_ref, short_ref, table_ref = refs
+    count = azimuth + 4
+    for k in range(2):
+        for source, start in ((left_ref, k), (right_ref, 2 + k)):
+            cells = source[pl.ds(k, count, stride=2), :]
+            long_ref[pl.ds(start, count, stride=4), :] = cells
+            short_ref[pl.ds(start, count, stride=4), :] = cells
+    cot_sides, den_sides, end = halo_starts(azimuth)
+    long_ref[cot_sides:end, :] = sides_ref[: end - cot_sides, :]
+    short_ref[cot_sides:den_sides, :] = sides_ref[: den_sides - cot_sides, :]
+    long_ref[end:, :] = shares_ref[...]
+    table_ref[...] = jnp.zeros(table_ref.shape, jnp.float32)
+    table_ref[EDGE - 2 : EDGE, :] = left_ref[2 * count : 2 * count + 2, :]
+    table_ref[EDGE : EDGE + radial, :] = gates_ref[...]
+    table_ref[EDGE + radial : EDGE + radial + 2, :] = right_ref[2 * count : 2 * count + 2, :]
+
+
 def halo_starts(azimuth):
     cot_sides = 4 * (azimuth + 4)
     return cot_sides, cot_sides + 4 * RANGE, cot_sides + 8 * RANGE
+
+
+def widened(ref, rows, lane):
+    value = ref[rows, lane : lane + 1]
+    return jnp.broadcast_to(value, (value.shape[0], LANES))
 
 
 def pair(left, right, half):
@@ -152,7 +230,7 @@
                 8,
                 wide,
             )
-            parts.append(jnp.concatenate([moved, gate_ref[a, outer, :] * moved], axis=1))
+            parts.append(jnp.concatenate([moved, widened(gate_ref, outer, a) * moved], axis=1))
         result = product(jnp.concatenate(parts, axis=0), table_ref)
         for k, a in enumerate(rows):
             mixed[a, 0, outer, :] = result[k * wide : (k + 1) * wide, :LANES]
@@ -162,17 +240,13 @@
     move([1, azimuth + 2])
 
     for g, (low, high) in enumerate(zip(cuts, cuts[1:])):
-
-        @pl.loop(0, (high - low) // BATCH)
-        def _(b):
-            rows = [low + b * BATCH + k for k in range(BATCH)]
+        for rows in batches(low, high):
             for a, moved in zip(rows, move([a + 2 for a in rows])):
-                moved_refs[g][a - low] = slope_ref[a] * moved
+                moved_refs[g][a - low] = widened(slope_ref, slice(None), a) * moved
 
     for g, (low, high) in enumerate(zip(cuts, cuts[1:])):
-
-        @pl.loop(low, high)
-        def _(a):
+        for a in range(low, high):
+            slope = widened(slope_ref, slice(None), a)
             for t in range(2):
                 second = stencil(
                     mixed,
@@ -184,7 +258,7 @@
                     EDGE,
                     radial,
                 )
-                second_refs[g][a - low, t] = slope_ref[a] * second
+                second_refs[g][a - low, t] = slope * second
 
 
 def adjoint_kernel(azimuth, radial, low_row, high_row, offsets, *refs):
@@ -214,7 +288,6 @@
     first_base = first_low if first else first_low - 2
     out_low, out_high = first_base + 1, first_high - 1
     own_low, own_high = max(low_row, 2), min(high_row, azimuth + 2)
-    gate_low = max(low_row - 1, 0)
 
     if not first:
         second[pl.ds(0, 2)] = carry_second[...]
@@ -228,7 +301,7 @@
     for row in range(low_row, high_row):
         piece = edges[4 * (row - low_row) : 4 * (row - low_row) + 4]
         for start, k in ((EDGE - 2, 0), (EDGE + radial, 2)):
-            gate = gate_ref[row - gate_low, pl.ds(start, 2), :]
+            gate = widened(gate_ref, pl.ds(start, 2), row)
             for t in range(2):
                 second[row - base, t, pl.ds(start, 2), :] = (
                     piece[k : k + 2, t * LANES : (t + 1) * LANES]
@@ -247,7 +320,7 @@
         result = product(jnp.concatenate([bins_of(row) for row in group], axis=1), table1_ref, 0)
         for k, row in enumerate(group):
             part = result[k * radial : (k + 1) * radial]
-            gate = gate_ref[row - gate_low, inner, :]
+            gate = widened(gate_ref, inner, row)
             for t in range(2):
                 frag = part[:, (t + 2) * LANES : (t + 3) * LANES]
                 second[row - base, t, inner, :] = part[:, t * LANES : (t + 1) * LANES] + gate * frag
@@ -275,7 +348,7 @@
         for k, row in enumerate(group):
             part = result[k * wide : (k + 1) * wide]
             frag = part[:, LANES:]
-            initial[row - first_base, outer, :] = part[:, :LANES] + gate_ref[row - gate_low, outer, :] * frag
+            initial[row - first_base, outer, :] = part[:, :LANES] + widened(gate_ref, outer, row) * frag
             if own_low <= row < own_high:
                 total += moved_ref[row - own_low] * frag[8 : 8 + radial]
             elif 2 <= row < own_low:
@@ -332,7 +405,6 @@
 ):
     own_bins, azimuth, radial = density.shape
     place = lax.axis_index("mass")
-    row_index = lax.axis_index("row")
     phis, rows = lax.axis_size("phi"), lax.axis_size("row")
     cuts = [0, azimuth // 2, 3 * azimuth // 4, azimuth]
     spans = list(zip(cuts, cuts[1:]))
@@ -358,77 +430,59 @@
 
     count = azimuth + 4
     length = radial + 2 * EDGE
+    share_rows, (cot_sides, den_sides, halo_rows) = length + 8, halo_starts(azimuth)
 
     def flat(x):
         return x.reshape(-1, LANES)
 
-    def window(drift):
-        padded = jnp.pad(drift, ((0, 0), (EDGE, EDGE)))
-        wide = lax.dynamic_slice_in_dim(padded, row_index * radial, length, 1)
-        return wide.T
-
-    spreads = jnp.broadcast_to(jnp.concatenate([spread, spread])[None, :], (8, LANES))
-    shares = jnp.concatenate([jnp.concatenate([window(drift_in), window(drift_out)], axis=1), spreads], axis=0)
+    sides, gate, slope = call(
+        functools.partial(side_kernel, azimuth),
+        [(8 * own_bins + 8, LANES), (azimuth, radial), (radial, LANES)],
+        [],
+        [flat(cotangent), flat(density), collide_speed, frag_speed[None, :], regime],
+        2,
+    )
+    ring = [(i, (i + 1) % phis) for i in range(phis)]
+    other = lax.ppermute(sides, "phi", ring)
+    if phis > 2:
+        after = lax.ppermute(sides, "phi", [(j, i) for i, j in ring])
+        from_last = lax.broadcasted_iota(jnp.int32, other.shape, 0) % 4 < 2
+        other = jnp.where(from_last, other, after)
+
+    spread_row, gate = lax.optimization_barrier((spread[None, :], gate))
+    opening, shares, first_cells, last_cells = call(
+        functools.partial(opening_kernel, azimuth, radial, cuts[1]),
+        [
+            (cuts[1] * own_bins + share_rows, LANES),
+            (share_rows, LANES),
+            (azimuth, 2, LANES),
+            (azimuth, 2, LANES),
+        ],
+        [],
+        [flat(cotangent), flat(density), drift_in, drift_out, spread_row],
+        5,
+    )
+    pieces = [cotangent[:, i:j] for i, j in spans]
 
     density_next = ending(density)
-    pieces = [cotangent[:, i:j] for i, j in spans]
-    opening = jnp.concatenate([flat(pieces[0]), shares], axis=0)
     far_first, near_first = far(opening), near(opening)
-
-    sigma = jax.nn.sigmoid((collide_speed - frag_speed[None, :]) / gate_width)
-    flagged = regime.astype(jnp.float32)
-    frag_gate = flagged * sigma
-    gate_slope = -flagged * sigma * (1.0 - sigma) / gate_width
-    gate_slope = gate_slope * (place < 3).astype(jnp.float32)
-
-    def band(low, high):
-        gate_rows = jnp.broadcast_to(frag_gate[None, low:high], (8, high - low, radial))
-        return jnp.concatenate([cotangent[:, low:high], density[:, low:high], gate_rows], axis=0)
-
-    upper_band, lower_band = band(azimuth - 2, azimuth), band(0, 2)
-    if phis == 2:
-        other = lax.ppermute(jnp.concatenate([upper_band, lower_band], axis=1), "phi", [(0, 1), (1, 0)])
-    else:
-        ring = [(i, (i + 1) % phis) for i in range(phis)]
-        other = jnp.concatenate(
-            [lax.ppermute(upper_band, "phi", ring), lax.ppermute(lower_band, "phi", [(j, i) for i, j in ring])], axis=1
-        )
-    sides = other[: 2 * own_bins]
-    gates = jnp.concatenate([other[-1, :2], frag_gate, other[-1, 2:]], axis=0)
-
-    def edge_cells(cot, den):
-        number = cot.shape[1]
-        return call(
-            functools.partial(edge_kernel, number, radial),
-            [(number, 2, LANES)] * 2,
-            [],
-            [flat(cot), flat(den)],
-        )
-
-    own_edges = edge_cells(cotangent, density)
-    side_edges = edge_cells(sides[:own_bins], sides[own_bins:])
-
-    def with_gate(own, side, gate_cols):
-        gate_row = jnp.pad(gate_cols.reshape(-1), (0, LANES - 2 * count)).reshape(1, LANES)
-        parts = [flat(side[:2]), flat(own), flat(side[2:]), jnp.broadcast_to(gate_row, (8, LANES))]
-        return jnp.concatenate(parts, axis=0)
-
+    left_cells, right_cells, gates = call(
+        functools.partial(radial_kernel, azimuth, radial),
+        [(2 * count + 8, LANES), (2 * count + 8, LANES), (radial, LANES)],
+        [],
+        [other, flat(first_cells), flat(last_cells), gate],
+    )
     line = [(i, i + 1) for i in range(rows - 1)]
-    left = lax.ppermute(with_gate(own_edges[1], side_edges[1], gates[:, radial - 2 :]), "row", line)
-    right = lax.ppermute(
-        with_gate(own_edges[0], side_edges[0], gates[:, :2]), "row", [(j, i) for i, j in line]
-    )
-    left_cols, right_cols = (x[: 2 * count].reshape(count, 2, LANES) for x in (left, right))
-    left_gate, right_gate = (x[2 * count, : 2 * count].reshape(count, 2) for x in (left, right))
-
-    gap = jnp.zeros((count, EDGE - 2), jnp.float32)
-    gates = jnp.concatenate([gap, left_gate, gates, right_gate, gap], axis=1)
-    gate_wide = jnp.broadcast_to(gates[:, :, None], gates.shape + (LANES,))
-    slope_wide = jnp.broadcast_to(gate_slope[:, :, None], gate_slope.shape + (LANES,))
-
-    frag_gain, other = lax.optimization_barrier((frag_gain, other))
-    edges = flat(jnp.concatenate([left_cols, right_cols], axis=1))
-    halos = jnp.concatenate([edges, flat(sides)], axis=0)
+    left = lax.ppermute(left_cells, "row", line)
+    right = lax.ppermute(right_cells, "row", [(j, i) for i, j in line])
+    halos, short, gates = call(
+        functools.partial(halo_kernel, azimuth, radial),
+        [(halo_rows + share_rows, LANES), (den_sides, LANES), (length, LANES)],
+        [],
+        [left, right, other, shares, gates],
+    )
+
+    frag_gain, halos = lax.optimization_barrier((frag_gain, halos))
 
     def chosen(matrix, axis):
         return jnp.concatenate(
@@ -445,20 +499,20 @@
     own_cols = stacked(upper_half)
     own_rows = stacked(upper_half.T)
 
-    halos_next = ending(jnp.concatenate([halos, shares], axis=0))
-    short, pieces[0], far_first, near_first, gate_wide, slope_wide, both, own_cols, own_rows = lax.optimization_barrier(
-        (halos[: halo_starts(azimuth)[1]], pieces[0], far_first, near_first, gate_wide, slope_wide, both, own_cols, own_rows)
-    )
-    gathered = [[far_first, near_first, pieces[0], ending(pieces[0])]]
+    halos_next = ending(halos)
     halo_refs = [far(short), near(short), halos, halos_next]
-    late = cotangent[:, cuts[1] :]
-    halos_next, late, *rest = lax.optimization_barrier((halos_next, late, *pieces[1:]))
+    halos_next, late, pieces[0], pieces[1] = lax.optimization_barrier(
+        (halos_next, cotangent[:, cuts[1] :], pieces[0], pieces[1])
+    )
     halo_refs[3] = halos_next
     late_next = ending(late)
-    gathered += [[far(piece), near(piece), piece, late_next] for piece in rest]
+    gathered = [
+        [far_first, near_first, pieces[0], ending(pieces[0])],
+        [far(pieces[1]), near(pieces[1]), pieces[1], late_next],
+    ]
 
     coefs = [(2, length, LANES)] * 3 + [(2, LANES)]
-    products = call(
+    products = list(call(
         functools.partial(forward_kernel, azimuth, radial, cuts),
         [(j - i, radial, LANES) for i, j in spans] + [(j - i, 2, radial, LANES) for i, j in spans] + coefs,
         [(count, length, LANES), (count, 2, length, LANES)],
@@ -470,13 +524,15 @@
             shares,
             halos,
             halos_next,
-            gate_wide,
-            slope_wide,
+            gates,
+            slope,
             own_rows,
         ],
         13,
-    )
+    ))
     groups = len(spans)
+    products[0], pieces[2] = lax.optimization_barrier((products[0], pieces[2]))
+    gathered.append([far(pieces[2]), near(pieces[2]), pieces[2], late_next])
     moved, second, coefs = products[:groups], products[groups : 2 * groups], products[2 * groups :]
 
     own_outs, next_outs, carry = [], [], []
@@ -489,7 +545,7 @@
         operands = [flat(x) for x in gathered[g]]
         own = (cuts[g], cuts[g + 1] - cuts[g])
         offsets = [own, own, own, own if first else (cuts[1], azimuth - cuts[1])]
-        operands += [*halo_refs, *coefs, gate_wide[max(low_row - 1, 0) : high_row], second[g], moved[g]]
+        operands += [*halo_refs, *coefs, gates, second[g], moved[g]]
         operands += [both, own_cols, *carry]
         if not first:
             operands.append(moved[g - 1][-1:])
@@ -506,9 +562,6 @@
         carry = [*kept, total]
         own_outs.append(own_out)
         next_outs.append(returning(next_out))
-    result = jnp.concatenate(
-        [jnp.where(place == 3, there, here) for here, there in zip(own_outs, next_outs)], axis=0
-    ).transpose(1, 0, 2)
     speed_gradient = jnp.sum(total, axis=1)
     size = lax.axis_size("mass")
     shares = [
@@ -520,6 +573,10 @@
     while step < phis:
         speed_gradient += lax.ppermute(speed_gradient, "phi", [(i, i ^ step) for i in range(phis)])
         step *= 2
+    next_outs = lax.optimization_barrier(next_outs)
+    result = jnp.concatenate(
+        [jnp.where(place == 3, there, here) for here, there in zip(own_outs, next_outs)], axis=0
+    ).transpose(1, 0, 2)
     return (result, speed_gradient)
 
 

time: 152 us -> 129 us (0.85)
  local copies, waits for them, and re-layouts: 26.1 us -> 15 us
  starting transfers between devices: 47.5 us -> 41.9 us
  other arithmetic: 12 us -> 8.93 us
  waiting for transfers between devices: 21.8 us -> 18.8 us
    ppermute x3, waiting for transfers between devices: 11.4 us -> 0.01 us  [returning(): return lax.ppermute(x, 'mass', [(2, 3)])]
    slice x14 -> x0, local copies, waits for them, and re-layouts: 8.13 us -> none  [the longest x3 4.39 us: per_device(): gate_wide[max(low_row - 1, 0):high_row]]
    ppermute x3, waiting for transfers between devices: 2.62 us -> 7.31 us  [the longest x1 4.13 us: per_device(): other = lax.ppermute(sides, 'phi', ring)]
    ppermute x3, waiting for transfers between devices: 3.94 us -> 8.29 us  [per_device(): lax.ppermute(speed_gradient, 'mass', [(i, (i + k) % size) for i in range(...]
    concatenate x11 -> x0, other arithmetic: 4.3 us -> none  [the longest x1 0.92 us: per_device(): opening = jnp.concatenate([flat(pieces[0]), shares], axis=0)]
    ppermute x3, starting transfers between devices: 15.6 us -> 12.6 us  [per_device(): lax.ppermute(speed_gradient, 'mass', [(i, (i + k) % size) for i in range(...]
    broadcast_in_dim x8 -> x0, local copies, waits for them, and re-layouts: 2.79 us -> none  [the longest x1 1.96 us: per_device(): jnp.broadcast_to(gate_slope[:, :, None], gate_slope.shape + (LANES,))]
    another operation x4, other arithmetic: 2.33 us -> 4.38 us
  transfers between devices with their start and end apart: 22 -> 22, of which waited for: 7 -> 6; matrix products, arithmetic and copies ran while one was open for 19% -> 15% of each run, Pallas kernels for 27% -> 27%
where the time goes in v4:
time: 129 us; the launch traced here: 128 us
  starting transfers between devices  41.9 us (32%)
  Pallas kernels  41.8 us (32%)
  waiting for transfers between devices  18.8 us (15%)
  local copies, waits for them, and re-layouts  15 us (12%)
  other arithmetic  8.93 us (7%)
    pallas_call x8, Pallas kernels, call(): pl.pallas_call(kernel, out_shape=[jax.ShapeDtypeStruct(o, jnp.float32) fo...  41.8 us
    ppermute x4, starting transfers between devices, ending(): return lax.ppermute(x, 'mass', [(3, 2)])  13.4 us
    ppermute x3, starting transfers between devices, per_device(): lax.ppermute(speed_gradient, 'mass', [(i, (i + k) % size) for i in range(...  12.6 us
    ppermute x3, waiting for transfers between devices, per_device(): lax.ppermute(speed_gradient, 'mass', [(i, (i + k) % size) for i in range(...  8.29 us
    unnamed x61, local copies, waits for them, and re-layouts  4.71 us
    another operation x4, other arithmetic  4.38 us
    ppermute x1, waiting for transfers between devices, per_device(): other = lax.ppermute(sides, 'phi', ring)  4.13 us
    ppermute x3, starting transfers between devices, returning(): return lax.ppermute(x, 'mass', [(2, 3)])  4.01 us
  transfers between devices with their start and end apart: 22, of which 6 were waited for; matrix products, arithmetic and copies ran while one was open for 15% of the time, Pallas kernels for 27%

profile of v4, /device:TPU:24, one launch (start us, length us, event | category | flops | bytes accessed | tf_op | source)
XLA Modules:
  0.0 127.7 jit_solution(6140538060403624478)
XLA Ops:
  0.6 2.5 %shard_map.149 = (f32[520,128]{1,0:T(8,128)}, f32[32,128]{1,0:T(8,128)}, f32[128,128]{1,0:T(8,128)}) custom-call(f32[2048,128]{1,0:T(8,128)} %bitcast.28, f32[2048,128]{1,0:T(8,128)} %bitcast.30, f32[32,128]{1,0:T(8,128)} %collide_ref.1, f32[1,128]{1,0:T(1,128)} %bitcast.51, s32[32,128]{1,0:T(8,128)} %regime_ref.1), custom_call_target="tpu_custom_call" | custom-call | bytes 6000000 | tf_op jit(solution)/shard_map/pallas_call | solution.py:379
  3.2 4.3 %shard_map.150 = (f32[1192,128]{1,0:T(8,128)}, f32[168,128]{1,0:T(8,128)}, f32[32,2,128]{2,1,0:T(2,128)}, f32[32,2,128]{2,1,0:T(2,128)}) custom-call(f32[2048,128]{1,0:T(8,128)} %bitcast.29, f32[2048,128]{1,0:T(8,128)} %bitcast.31, f32[64,512]{1,0:T(8,128)} %refs_2_.1, f32[64,512]{1,0:T(8,128)} %refs_3_.1, f32[1,64]{1,0:T(1,128)} %bitcast.52), custom_call_target="tpu_custom_call" | custom-call | bytes 15000000 | tf_op jit(solution)/shard_map/pallas_call | solution.py:379
  8.9 5.6 %collective-permute-start.9 = (f32[64,32,128]{2,1,0:T(8,128)S(1)}, f32[64,32,128]{2,1,0:T(8,128)}, u32[]{:S(2)}, u32[]{:S(2)}) collective-permute-start(f32[64,32,128]{2,1,0:T(8,128)S(1)} %copy-done.1), channel_id=1, source_target_pairs={{3,2},{7,6},{11,10},{15,14},{19,18},{23,22},{27,26},{31,30}} | collective-permute-start | bytes 3145736 | tf_op jit(solution)/shard_map/ppermute | solution.py:419
  14.6 1.5 %collective-permute-start.2 = (f32[520,128]{1,0:T(8,128)S(1)}, f32[520,128]{1,0:T(8,128)S(1)}, u32[]{:S(2)}, u32[]{:S(2)}) collective-permute-start(f32[520,128]{1,0:T(8,128)S(1)} %copy-done.28), channel_id=1, source_target_pairs={{0,16},{16,0},{1,17},{17,1},{2,18},{18,2},{3,19},{19,3},{4,20},{20... | collective-permute-start | bytes 798728 | tf_op jit(solution)/shard_map/ppermute | solution.py:446
  18.0 4.1 %collective-permute-done.2.sides_ref = f32[520,128]{1,0:T(8,128)S(1)} collective-permute-done((f32[520,128]{1,0:T(8,128)S(1)}, f32[520,128]{1,0:T(8,128)S(1)}, u32[]{:S(2)}, u32[]{:S(2)}) %collective-permute-start.2) | collective-permute-done | bytes 266272 | tf_op jit(solution)/shard_map/ppermute | solution.py:446
  22.9 1.8 %shard_map.151 = (f32[80,128]{1,0:T(8,128)}, f32[80,128]{1,0:T(8,128)}, f32[128,128]{1,0:T(8,128)}) custom-call(f32[520,128]{1,0:T(8,128)} %copy-done.8, f32[64,128]{1,0:T(8,128)} %bitcast.41, f32[64,128]{1,0:T(8,128)} %bitcast.42, f32[32,128]{1,0:T(8,128)} %get-tuple-element.57.gate_ref), custom_call_target="tpu_custom_call" | custom-call | bytes 3000000 | tf_op jit(solution)/shard_map/pallas_call | solution.py:379
  26.0 1.3 %collective-permute-start.4 = (f32[80,128]{1,0:T(8,128)}, f32[80,128]{1,0:T(8,128)S(1)}, u32[]{:S(2)}, u32[]{:S(2)}) collective-permute-start(f32[80,128]{1,0:T(8,128)} %get-tuple-element.59), channel_id=1, source_target_pairs={{4,0},{8,4},{12,8},{5,1},{9,5},{13,9},{6,2},{10,6},{14,10},{7,3},{... | collective-permute-start | bytes 122888 | tf_op jit(solution)/shard_map/ppermute | solution.py:477
  27.9 3.2 %collective-permute-done.4.right_ref = f32[80,128]{1,0:T(8,128)S(1)} collective-permute-done((f32[80,128]{1,0:T(8,128)}, f32[80,128]{1,0:T(8,128)S(1)}, u32[]{:S(2)}, u32[]{:S(2)}) %collective-permute-start.4) | collective-permute-done | bytes 40992 | tf_op jit(solution)/shard_map/ppermute | solution.py:477
  31.7 1.9 %shard_map.152 = (f32[824,128]{1,0:T(8,128)}, f32[400,128]{1,0:T(8,128)}, f32[160,128]{1,0:T(8,128)}) custom-call(f32[80,128]{1,0:T(8,128)} %copy-done.21, f32[80,128]{1,0:T(8,128)} %copy-done.22, f32[520,128]{1,0:T(8,128)} %copy-done.8, f32[168,128]{1,0:T(8,128)} %get-tuple-element.60.shares_ref.refs_4_, f32[128,128]{1,0:T(8,128)} %get-tuple-element.61.gates_ref), custom_call_target="tpu_custom_call" | custom-call | bytes 3000000 | tf_op jit(solution)/shard_map/pallas_call | solution.py:379
  34.7 1.3 %collective-permute-start.5 = (f32[824,128]{1,0:T(8,128)S(1)}, f32[824,128]{1,0:T(8,128)S(1)}, u32[]{:S(2)}, u32[]{:S(2)}) collective-permute-start(f32[824,128]{1,0:T(8,128)S(1)} %copy-done.2), channel_id=1, source_target_pairs={{3,2},{7,6},{11,10},{15,14},{19,18},{23,22},{27,26},{31,30}} | collective-permute-start | bytes 1265672 | tf_op jit(solution)/shard_map/ppermute | solution.py:419
  37.0 2.2 %concatenate.37 = f32[256,512]{1,0:T(8,128)} concatenate(f32[256,64]{1,0:T(8,128)} %get-tuple-element.117, f32[256,64]{1,0:T(8,128)} %get-tuple-element.116, f32[256,64]{1,0:T(8,128)S(1)} %get-tuple-element.119, f32[256,64]{1,0:T(8,128)S(1)} %get-tuple-element.118, f32[256,64]{1,0:T(8,128)} %get-tuple-element.113, f32[256,64]{1,0:T(8,128)} %get-tuple-element.112, ...), dimensions={1} | concatenate | bytes 1048576 | tf_op jit(solution)/shard_map/concatenate | solution.py:497
  39.2 1.9 %reduce-precision_convert_fusion = (bf16[256,512]{1,0:T(8,128)(2,1)}, bf16[256,512]{1,0:T(8,128)(2,1)}) fusion(f32[256,512]{1,0:T(8,128)} %concatenate.37), kind=kLoop, calls=%fused_computation.3 | loop fusion | flops 524288 | bytes 1048576 | tf_op jit(solution)/shard_map/convert.3
  41.1 1.7 %reduce-precision_convert_fusion.1 = (bf16[256,256]{1,0:T(8,128)(2,1)}, f32[256,256]{1,0:T(8,128)S(1)}) fusion(f32[256,64]{1,0:T(8,128)S(1)} %get-tuple-element.114, f32[256,64]{1,0:T(8,128)} %get-tuple-element.115, f32[256,64]{1,0:T(8,128)S(1)} %get-tuple-element.118, f32[256,64]{1,0:T(8,128)S(1)} %get-tuple-element.119), kind=kLoop, calls=%fused_computation.18 | loop fusion | flops 327680 | bytes 655360 | tf_op jit(solution)/shard_map/convert
  44.0 5.2 %collective-permute-start.6 = (f32[64,16,128]{2,1,0:T(8,128)}, f32[64,16,128]{2,1,0:T(8,128)}, u32[]{:S(2)}, u32[]{:S(2)}) collective-permute-start(f32[64,16,128]{2,1,0:T(8,128)} %get-tuple-element.64), channel_id=1, source_target_pairs={{3,2},{7,6},{11,10},{15,14},{19,18},{23,22},{27,26},{31,30}} | collective-permute-start | bytes 1572872 | tf_op jit(solution)/shard_map/ppermute | solution.py:419
  49.2 1.3 %collective-permute-start.13 = (f32[64,16,128]{2,1,0:T(8,128)}, f32[64,16,128]{2,1,0:T(8,128)S(1)}, u32[]{:S(2)}, u32[]{:S(2)}) collective-permute-start(f32[64,16,128]{2,1,0:T(8,128)} %get-tuple-element.79), channel_id=1, source_target_pairs={{3,2},{7,6},{11,10},{15,14},{19,18},{23,22},{27,26},{31,30}} | collective-permute-start | bytes 1572872 | tf_op jit(solution)/shard_map/ppermute | solution.py:419
  52.0 1.3 %collective-permute-start.8 = (f32[400,128]{1,0:T(8,128)}, f32[400,128]{1,0:T(8,128)}, u32[]{:S(2)}, u32[]{:S(2)}) collective-permute-start(f32[400,128]{1,0:T(8,128)} %get-tuple-element.65), channel_id=1, source_target_pairs={{0,1},{1,2},{4,5},{5,6},{8,9},{9,10},{12,13},{13,14},{16,17},{17,1... | collective-permute-start | bytes 614408 | tf_op jit(solution)/shard_map/ppermute | solution.py:416
  54.9 1.7 %pad_maximum_fusion.4.refs_16_ = bf16[768,256]{1,0:T(8,128)(2,1)} fusion(bf16[256,256]{1,0:T(8,128)(2,1)} %fusion.3, bf16[256,256]{1,0:T(8,128)(2,1)S(1)} %copy-done.12), kind=kLoop, calls=%fused_computation.16 | loop fusion | flops 1179648 | bytes 655360 | tf_op jit(solution)/shard_map/concatenate | solution.py:42
  56.7 9.8 %shard_map.153 = (f32[16,128,128]{2,1,0:T(8,128)}, f32[8,128,128]{2,1,0:T(8,128)}, f32[8,128,128]{2,1,0:T(8,128)}, f32[16,2,128,128]{3,2,1,0:T(8,128)}, f32[8,2,...) custom-call(f32[2048,128]{1,0:T(8,128)} %bitcast.32, ...), custom_call_target="tpu_custom_call" | custom-call | bytes 39000000 | tf_op jit(solution)/shard_map/pallas_call | solution.py:379
  69.7 9.1 %shard_map.154 = (f32[14,64,128]{2,1,0:T(8,128)}, f32[14,64,128]{2,1,0:T(8,128)}, f32[128,128]{1,0:T(8,128)}, f32[2,2,160,128]{3,2,1,0:T(8,128)}, f32[2,160,128]{2,1,0:T(8,128)}) custom-call(f32[1192,128]{1,0:T(8,128)} %copy-done.4, f32[1192,128]{1,0:T(8,128)} %copy-done.5, f32[1024,128]{1,0:T(8,128)} %bitcast.6.refs_2_, f32[1024,128]{1,0:T(8,128)} %bitcast.7.refs_3_, ...), custom_call_target="tpu_custom_call" | custom-call | bytes 33000000 | tf_op jit(solution)/shard_map/pallas_call | solution.py:379
  78.8 1.3 %collective-permute-start.10 = (f32[14,64,128]{2,1,0:T(8,128)}, f32[14,64,128]{2,1,0:T(8,128)S(1)}, u32[]{:S(2)}, u32[]{:S(2)}) collective-permute-start(f32[14,64,128]{2,1,0:T(8,128)} %get-tuple-element.77), channel_id=1, source_target_pairs={{2,3},{6,7},{10,11},{14,15},{18,19},{22,23},{26,27},{30,31}} | collective-permute-start | bytes 1376264 | tf_op jit(solution)/shard_map/ppermute | solution.py:422
  80.1 1.5 %slice.26.refs_20_ = f32[1,128,128]{2,1,0:T(8,128)} slice(f32[16,128,128]{2,1,0:T(8,128)} %get-tuple-element.76.refs_14_), slice={[15:16], [0:128], [0:128]} | slice | bytes 131072 | tf_op jit(solution)/shard_map/slice | solution.py:551
  81.5 1.5 %slice.27.refs_20_ = f32[1,128,128]{2,1,0:T(8,128)} slice(f32[8,128,128]{2,1,0:T(8,128)} %get-tuple-element.81.refs_14_), slice={[7:8], [0:128], [0:128]} | slice | bytes 131072 | tf_op jit(solution)/shard_map/slice | solution.py:551
  83.9 5.9 %shard_map.155 = (f32[8,64,128]{2,1,0:T(8,128)}, f32[8,64,128]{2,1,0:T(8,128)}, f32[128,128]{1,0:T(8,128)}, f32[2,2,160,128]{3,2,1,0:T(8,128)}, f32[2,160,128]{2,1,0:T(8,128)}) custom-call(f32[512,128]{1,0:T(8,128)} %bitcast.37, f32[512,128]{1,0:T(8,128)} %bitcast.40, f32[512,128]{1,0:T(8,128)} %bitcast.13.refs_2_, f32[1024,128]{1,0:T(8,128)} %bitcast.33, ...), custom_call_target="tpu_custom_call" | custom-call | bytes 18000000 | tf_op jit(solution)/shard_map/pallas_call | solution.py:379
  90.6 6.4 %shard_map.156 = (f32[10,64,128]{2,1,0:T(8,128)}, f32[10,64,128]{2,1,0:T(8,128)}, f32[128,128]{1,0:T(8,128)}) custom-call(f32[512,128]{1,0:T(8,128)} %bitcast.38, f32[512,128]{1,0:T(8,128)} %bitcast.39, f32[512,128]{1,0:T(8,128)} %bitcast.35, f32[1024,128]{1,0:T(8,128)} %bitcast.34, f32[400,128]{1,0:T(8,128)} %copy-done.7, ...), custom_call_target="tpu_custom_call" | custom-call | bytes 21000000 | tf_op jit(solution)/shard_map/pallas_call | solution.py:379
  97.1 1.4 %collective-permute-start.17 = (f32[10,64,128]{2,1,0:T(8,128)}, f32[10,64,128]{2,1,0:T(8,128)S(1)}, u32[]{:S(2)}, u32[]{:S(2)}) collective-permute-start(f32[10,64,128]{2,1,0:T(8,128)} %get-tuple-element.92), channel_id=1, source_target_pairs={{2,3},{6,7},{10,11},{14,15},{18,19},{22,23},{26,27},{30,31}} | collective-permute-start | bytes 983048 | tf_op jit(solution)/shard_map/ppermute | solution.py:422
  100.8 8.9 %collective-permute-start.18 = (f32[128]{0:T(128)S(1)}, f32[128]{0:T(128)S(1)}, u32[]{:S(2)}, u32[]{:S(2)}) collective-permute-start(f32[128]{0:T(128)S(1)} %reduce_sum.18), channel_id=1, source_target_pairs={{0,3},{1,0},{2,1},{3,2},{4,7},{5,4},{6,5},{7,6},{8,11},{9,8},{10,9... | collective-permute-start | bytes 1544 | tf_op jit(solution)/shard_map/ppermute | solution.py:568
  109.6 1.7 %collective-permute-start.19 = (f32[128]{0:T(128)S(1)}, f32[128]{0:T(128)S(1)}, u32[]{:S(2)}, u32[]{:S(2)}) collective-permute-start(f32[128]{0:T(128)S(1)} %reduce_sum.18), channel_id=1, source_target_pairs={{0,2},{1,3},{2,0},{3,1},{4,6},{5,7},{6,4},{7,5},{8,10},{9,11},{10,... | collective-permute-start | bytes 1544 | tf_op jit(solution)/shard_map/ppermute | solution.py:568
  112.3 2.0 %collective-permute-start.20 = (f32[128]{0:T(128)S(1)}, f32[128]{0:T(128)S(1)}, u32[]{:S(2)}, u32[]{:S(2)}) collective-permute-start(f32[128]{0:T(128)S(1)} %reduce_sum.18), channel_id=1, source_target_pairs={{0,1},{1,2},{2,3},{3,0},{4,5},{5,6},{6,7},{7,4},{8,9},{9,10},{10,1... | collective-permute-start | bytes 1544 | tf_op jit(solution)/shard_map/ppermute | solution.py:568
  114.3 7.3 %collective-permute-done.20 = f32[128]{0:T(128)S(1)} collective-permute-done((f32[128]{0:T(128)S(1)}, f32[128]{0:T(128)S(1)}, u32[]{:S(2)}, u32[]{:S(2)}) %collective-permute-start.20) | collective-permute-done | bytes 544 | tf_op jit(solution)/shard_map/ppermute | solution.py:568
  121.7 1.6 %collective-permute-start.21 = (f32[128]{0:T(128)S(1)}, f32[128]{0:T(128)S(1)}, u32[]{:S(2)}, u32[]{:S(2)}) collective-permute-start(f32[128]{0:T(128)S(1)} %fusion.4), channel_id=1, source_target_pairs={{0,16},{16,0},{1,17},{17,1},{2,18},{18,2},{3,19},{19,3},{4,20},{20... | collective-permute-start | bytes 1544 | tf_op jit(solution)/shard_map/ppermute | solution.py:574
  123.3 2.0 %collective-permute-done.21 = f32[128]{0:T(128)S(1)} collective-permute-done((f32[128]{0:T(128)S(1)}, f32[128]{0:T(128)S(1)}, u32[]{:S(2)}, u32[]{:S(2)}) %collective-permute-start.21) | collective-permute-done | bytes 544 | tf_op jit(solution)/shard_map/ppermute | solution.py:574
  126.1 1.6 %copy.21 = f32[64,32,128]{2,1,0:T(8,128)} copy(f32[64,32,128]{2,0,1:T(8,128)S(1)} %maximum_bitcast_fusion) | data formatting | bytes 2097152
  (117 shorter events, 21.6 us)
Async XLA Ops:
  3.2 12.9 %copy-start = (f32[64,32,128]{2,1,0:T(8,128)S(1)}, f32[64,32,128]{2,1,0:T(8,128)}, u32[]{:S(2)}) copy-start(f32[64,32,128]{2,1,0:T(8,128)} %param.15) | copy-start | bytes 3145732
  3.2 13.7 %copy-start.24 = (s32[256]{0:T(256)S(1)}, s32[256]{0:T(256)}, u32[]{:S(2)}) copy-start(s32[256]{0:T(256)} %param.19) | copy-start | bytes 3076
  3.2 13.7 %copy-start.23 = (f32[256]{0:T(256)S(1)}, f32[256]{0:T(256)}, u32[]{:S(2)}) copy-start(f32[256]{0:T(256)} %param.20) | copy-start | bytes 3076
  7.5 43.7 %collective-permute-start = (f32[1192,128]{1,0:T(8,128)}, f32[1192,128]{1,0:T(8,128)S(1)}, u32[]{:S(2)}, u32[]{:S(2)}) collective-permute-start(f32[1192,128]{1,0:T(8,128)} %get-tuple-element.53), channel_id=1, source_target_pairs={{0,2},{2,1},{1,0},{4,6},{6,5},{5,4},{8,10},{10,9},{9,8},{12,14},{1... | collective-permute-start | bytes 1830920 | tf_op jit(solution)/shard_map/ppermute | solution.py:413
  8.2 43.7 %collective-permute-start.1 = (f32[1192,128]{1,0:T(8,128)}, f32[1192,128]{1,0:T(8,128)S(1)}, u32[]{:S(2)}, u32[]{:S(2)}) collective-permute-start(f32[1192,128]{1,0:T(8,128)} %get-tuple-element.53), channel_id=1, source_target_pairs={{0,1},{1,2},{4,5},{5,6},{8,9},{9,10},{12,13},{13,14},{16,17},{17,1... | collective-permute-start | bytes 1830920 | tf_op jit(solution)/shard_map/ppermute | solution.py:416
  8.9 44.4 %collective-permute-start.9 = (f32[64,32,128]{2,1,0:T(8,128)S(1)}, f32[64,32,128]{2,1,0:T(8,128)}, u32[]{:S(2)}, u32[]{:S(2)}) collective-permute-start(f32[64,32,128]{2,1,0:T(8,128)S(1)} %copy-done.1), channel_id=1, source_target_pairs={{3,2},{7,6},{11,10},{15,14},{19,18},{23,22},{27,26},{31,30}} | collective-permute-start | bytes 3145736 | tf_op jit(solution)/shard_map/ppermute | solution.py:419
  14.6 12.7 %copy-start.26 = (f32[256]{0:T(256)S(1)}, f32[256]{0:T(256)}, u32[]{:S(2)}) copy-start(f32[256]{0:T(256)} %param.21) | copy-start | bytes 3076
  14.6 7.6 %collective-permute-start.2 = (f32[520,128]{1,0:T(8,128)S(1)}, f32[520,128]{1,0:T(8,128)S(1)}, u32[]{:S(2)}, u32[]{:S(2)}) collective-permute-start(f32[520,128]{1,0:T(8,128)S(1)} %copy-done.28), channel_id=1, source_target_pairs={{0,16},{16,0},{1,17},{17,1},{2,18},{18,2},{3,19},{19,3},{4,20},{20... | collective-permute-start | bytes 798728 | tf_op jit(solution)/shard_map/ppermute | solution.py:446
  16.9 16.7 %copy-start.19 = (f32[256,256]{1,0:T(8,128)S(1)}, f32[256,256]{1,0:T(8,128)}, u32[]{:S(2)}) copy-start(f32[256,256]{1,0:T(8,128)} %param.23) | copy-start | bytes 786436
  16.9 16.7 %copy-start.27 = (f32[256]{0:T(256)S(1)}, f32[256]{0:T(256)}, u32[]{:S(2)}) copy-start(f32[256]{0:T(256)} %param.24) | copy-start | bytes 3076
  24.7 3.2 %collective-permute-start.3 = (f32[80,128]{1,0:T(8,128)}, f32[80,128]{1,0:T(8,128)S(1)}, u32[]{:S(2)}, u32[]{:S(2)}) collective-permute-start(f32[80,128]{1,0:T(8,128)} %get-tuple-element.58), channel_id=1, source_target_pairs={{0,4},{4,8},{8,12},{1,5},{5,9},{9,13},{2,6},{6,10},{10,14},{3,7},{... | collective-permute-start | bytes 122888 | tf_op jit(solution)/shard_map/ppermute | solution.py:476
  26.0 5.1 %collective-permute-start.4 = (f32[80,128]{1,0:T(8,128)}, f32[80,128]{1,0:T(8,128)S(1)}, u32[]{:S(2)}, u32[]{:S(2)}) collective-permute-start(f32[80,128]{1,0:T(8,128)} %get-tuple-element.59), channel_id=1, source_target_pairs={{4,0},{8,4},{12,8},{5,1},{9,5},{13,9},{6,2},{10,6},{14,10},{7,3},{... | collective-permute-start | bytes 122888 | tf_op jit(solution)/shard_map/ppermute | solution.py:477
  34.7 9.3 %collective-permute-start.5 = (f32[824,128]{1,0:T(8,128)S(1)}, f32[824,128]{1,0:T(8,128)S(1)}, u32[]{:S(2)}, u32[]{:S(2)}) collective-permute-start(f32[824,128]{1,0:T(8,128)S(1)} %copy-done.2), channel_id=1, source_target_pairs={{3,2},{7,6},{11,10},{15,14},{19,18},{23,22},{27,26},{31,30}} | collective-permute-start | bytes 1265672 | tf_op jit(solution)/shard_map/ppermute | solution.py:419
  44.0 12.6 %copy-start.3 = (f32[824,128]{1,0:T(8,128)}, f32[824,128]{1,0:T(8,128)S(1)}, u32[]{:S(2)}) copy-start(f32[824,128]{1,0:T(8,128)S(1)} %collective-permute-done.5.refs_6_.refs_7_) | copy-start | bytes 1265668
  44.0 23.8 %collective-permute-start.6 = (f32[64,16,128]{2,1,0:T(8,128)}, f32[64,16,128]{2,1,0:T(8,128)}, u32[]{:S(2)}, u32[]{:S(2)}) collective-permute-start(f32[64,16,128]{2,1,0:T(8,128)} %get-tuple-element.64), channel_id=1, source_target_pairs={{3,2},{7,6},{11,10},{15,14},{19,18},{23,22},{27,26},{31,30}} | collective-permute-start | bytes 1572872 | tf_op jit(solution)/shard_map/ppermute | solution.py:419
  49.2 33.7 %collective-permute-start.13 = (f32[64,16,128]{2,1,0:T(8,128)}, f32[64,16,128]{2,1,0:T(8,128)S(1)}, u32[]{:S(2)}, u32[]{:S(2)}) collective-permute-start(f32[64,16,128]{2,1,0:T(8,128)} %get-tuple-element.79), channel_id=1, source_target_pairs={{3,2},{7,6},{11,10},{15,14},{19,18},{23,22},{27,26},{31,30}} | collective-permute-start | bytes 1572872 | tf_op jit(solution)/shard_map/ppermute | solution.py:419
  51.3 15.2 %collective-permute-start.7 = (f32[400,128]{1,0:T(8,128)}, f32[400,128]{1,0:T(8,128)S(1)}, u32[]{:S(2)}, u32[]{:S(2)}) collective-permute-start(f32[400,128]{1,0:T(8,128)} %get-tuple-element.65), channel_id=1, source_target_pairs={{0,2},{2,1},{1,0},{4,6},{6,5},{5,4},{8,10},{10,9},{9,8},{12,14},{1... | collective-permute-start | bytes 614408 | tf_op jit(solution)/shard_map/ppermute | solution.py:413
  52.0 15.2 %collective-permute-start.8 = (f32[400,128]{1,0:T(8,128)}, f32[400,128]{1,0:T(8,128)}, u32[]{:S(2)}, u32[]{:S(2)}) collective-permute-start(f32[400,128]{1,0:T(8,128)} %get-tuple-element.65), channel_id=1, source_target_pairs={{0,1},{1,2},{4,5},{5,6},{8,9},{9,10},{12,13},{13,14},{16,17},{17,1... | collective-permute-start | bytes 614408 | tf_op jit(solution)/shard_map/ppermute | solution.py:416
  53.3 25.4 %collective-permute-start.11 = (f32[64,8,128]{2,1,0:T(8,128)}, f32[64,8,128]{2,1,0:T(8,128)S(1)}, u32[]{:S(2)}, u32[]{:S(2)}) collective-permute-start(f32[64,8,128]{2,1,0:T(8,128)} %get-tuple-element.78), channel_id=1, source_target_pairs={{0,2},{2,1},{1,0},{4,6},{6,5},{5,4},{8,10},{10,9},{9,8},{12,14},{1... | collective-permute-start | bytes 786440 | tf_op jit(solution)/shard_map/ppermute | solution.py:413
  66.4 16.5 %collective-permute-start.12 = (f32[64,8,128]{2,1,0:T(8,128)}, f32[64,8,128]{2,1,0:T(8,128)S(1)}, u32[]{:S(2)}, u32[]{:S(2)}) collective-permute-start(f32[64,8,128]{2,1,0:T(8,128)} %get-tuple-element.78), channel_id=1, source_target_pairs={{0,1},{1,2},{4,5},{5,6},{8,9},{9,10},{12,13},{13,14},{16,17},{17,1... | collective-permute-start | bytes 786440 | tf_op jit(solution)/shard_map/ppermute | solution.py:416
  67.2 22.6 %collective-permute-start.15 = (f32[64,8,128]{2,1,0:T(8,128)S(1)}, f32[64,8,128]{2,1,0:T(8,128)S(1)}, u32[]{:S(2)}, u32[]{:S(2)}) collective-permute-start(f32[64,8,128]{2,1,0:T(8,128)S(1)} %copy-done.9), channel_id=1, source_target_pairs={{0,2},{2,1},{1,0},{4,6},{6,5},{5,4},{8,10},{10,9},{9,8},{12,14},{1... | collective-permute-start | bytes 786440 | tf_op jit(solution)/shard_map/ppermute | solution.py:413
  67.8 21.9 %collective-permute-start.16 = (f32[64,8,128]{2,1,0:T(8,128)S(1)}, f32[64,8,128]{2,1,0:T(8,128)S(1)}, u32[]{:S(2)}, u32[]{:S(2)}) collective-permute-start(f32[64,8,128]{2,1,0:T(8,128)S(1)} %copy-done.9), channel_id=1, source_target_pairs={{0,1},{1,2},{4,5},{5,6},{8,9},{9,10},{12,13},{13,14},{16,17},{17,1... | collective-permute-start | bytes 786440 | tf_op jit(solution)/shard_map/ppermute | solution.py:416
  78.8 47.1 %collective-permute-start.10 = (f32[14,64,128]{2,1,0:T(8,128)}, f32[14,64,128]{2,1,0:T(8,128)S(1)}, u32[]{:S(2)}, u32[]{:S(2)}) collective-permute-start(f32[14,64,128]{2,1,0:T(8,128)} %get-tuple-element.77), channel_id=1, source_target_pairs={{2,3},{6,7},{10,11},{14,15},{18,19},{22,23},{26,27},{30,31}} | collective-permute-start | bytes 1376264 | tf_op jit(solution)/shard_map/ppermute | solution.py:422
  90.6 35.2 %copy-start.13 = (f32[14,64,128]{2,1,0:T(8,128)S(1)}, f32[14,64,128]{2,1,0:T(8,128)}, u32[]{:S(2)}) copy-start(f32[14,64,128]{2,1,0:T(8,128)} %get-tuple-element.94) | copy-start | bytes 1376260
  97.1 28.8 %copy-start.20 = (f32[8,64,128]{2,1,0:T(8,128)S(1)}, f32[8,64,128]{2,1,0:T(8,128)}, u32[]{:S(2)}) copy-start(f32[8,64,128]{2,1,0:T(8,128)} %get-tuple-element.96) | copy-start | bytes 786436
  97.1 28.9 %copy-start.14 = (f32[10,64,128]{2,1,0:T(8,128)S(1)}, f32[10,64,128]{2,1,0:T(8,128)}, u32[]{:S(2)}) copy-start(f32[10,64,128]{2,1,0:T(8,128)} %get-tuple-element.98) | copy-start | bytes 983044
  97.1 28.8 %collective-permute-start.17 = (f32[10,64,128]{2,1,0:T(8,128)}, f32[10,64,128]{2,1,0:T(8,128)S(1)}, u32[]{:S(2)}, u32[]{:S(2)}) collective-permute-start(f32[10,64,128]{2,1,0:T(8,128)} %get-tuple-element.92), channel_id=1, source_target_pairs={{2,3},{6,7},{10,11},{14,15},{18,19},{22,23},{26,27},{30,31}} | collective-permute-start | bytes 983048 | tf_op jit(solution)/shard_map/ppermute | solution.py:422
  98.5 27.3 %collective-permute-start.14 = (f32[8,64,128]{2,1,0:T(8,128)S(1)}, f32[8,64,128]{2,1,0:T(8,128)S(1)}, u32[]{:S(2)}, u32[]{:S(2)}) collective-permute-start(f32[8,64,128]{2,1,0:T(8,128)S(1)} %copy-done.29), channel_id=1, source_target_pairs={{2,3},{6,7},{10,11},{14,15},{18,19},{22,23},{26,27},{30,31}} | collective-permute-start | bytes 786440 | tf_op jit(solution)/shard_map/ppermute | solution.py:422
  100.8 11.5 %collective-permute-start.18 = (f32[128]{0:T(128)S(1)}, f32[128]{0:T(128)S(1)}, u32[]{:S(2)}, u32[]{:S(2)}) collective-permute-start(f32[128]{0:T(128)S(1)} %reduce_sum.18), channel_id=1, source_target_pairs={{0,3},{1,0},{2,1},{3,2},{4,7},{5,4},{6,5},{7,6},{8,11},{9,8},{10,9... | collective-permute-start | bytes 1544 | tf_op jit(solution)/shard_map/ppermute | solution.py:568
  109.6 4.7 %collective-permute-start.19 = (f32[128]{0:T(128)S(1)}, f32[128]{0:T(128)S(1)}, u32[]{:S(2)}, u32[]{:S(2)}) collective-permute-start(f32[128]{0:T(128)S(1)} %reduce_sum.18), channel_id=1, source_target_pairs={{0,2},{1,3},{2,0},{3,1},{4,6},{5,7},{6,4},{7,5},{8,10},{9,11},{10,... | collective-permute-start | bytes 1544 | tf_op jit(solution)/shard_map/ppermute | solution.py:568
  112.3 9.3 %collective-permute-start.20 = (f32[128]{0:T(128)S(1)}, f32[128]{0:T(128)S(1)}, u32[]{:S(2)}, u32[]{:S(2)}) collective-permute-start(f32[128]{0:T(128)S(1)} %reduce_sum.18), channel_id=1, source_target_pairs={{0,1},{1,2},{2,3},{3,0},{4,5},{5,6},{6,7},{7,4},{8,9},{9,10},{10,1... | collective-permute-start | bytes 1544 | tf_op jit(solution)/shard_map/ppermute | solution.py:568
  121.7 3.6 %collective-permute-start.21 = (f32[128]{0:T(128)S(1)}, f32[128]{0:T(128)S(1)}, u32[]{:S(2)}, u32[]{:S(2)}) collective-permute-start(f32[128]{0:T(128)S(1)} %fusion.4), channel_id=1, source_target_pairs={{0,16},{16,0},{1,17},{17,1},{2,18},{18,2},{3,19},{19,3},{4,20},{20... | collective-permute-start | bytes 1544 | tf_op jit(solution)/shard_map/ppermute | solution.py:574
  (20 other events, 108.6 us)

commit v5 on v4

--- a/solution.py
+++ b/solution.py
@@ -14,32 +14,6 @@
 BATCH = 4
 MICRO = 3 * 10**6
 VMEM_LIMIT = 56 * 2**20
-
-
-def coag_matrix(dest_bins, bott_split, coag_rate):
-    number = dest_bins.shape[0]
-    row_ids = jnp.arange(number, dtype=jnp.int32)[:, None]
-    col_ids = jnp.arange(number, dtype=jnp.int32)[None, :]
-    target = dest_bins[None, :]
-    lower_part = (row_ids == target).astype(jnp.float32) * (1.0 - bott_split)[None, :]
-    upper_part = (row_ids == target + 1).astype(jnp.float32) * bott_split[None, :]
-    keeper = (row_ids == col_ids).astype(jnp.float32)
-    return (lower_part + upper_part - keeper) * coag_rate[None, :] + keeper
-
-
-def frag_matrix(frag_pairs, frag_gain, frag_rate):
-    number = frag_gain.shape[0]
-    blocks = jnp.repeat(jnp.repeat(frag_pairs, RANGE, axis=0), RANGE, axis=1).astype(jnp.float32)
-    row_ids = jnp.arange(number, dtype=jnp.int32)[:, None]
-    col_ids = jnp.arange(number, dtype=jnp.int32)[None, :]
-    below_diag = (row_ids <= col_ids).astype(jnp.float32)
-    keeper = (row_ids == col_ids).astype(jnp.float32)
-    return frag_gain * blocks * below_diag - keeper * frag_rate[None, :]
-
-
-def stacked(matrix):
-    high = lax.reduce_precision(matrix, 8, 7)
-    return jnp.concatenate([high, high, matrix - high], axis=0).astype(jnp.bfloat16)
 
 
 def split(value):
@@ -88,7 +62,7 @@
 
 
 def opening_kernel(azimuth, radial, first_rows, *refs):
-    cot_ref, den_ref, in_ref, out_ref, spread_ref, opening_ref, shares_ref, first_ref, last_ref = refs
+    cot_ref, den_ref, in_ref, out_ref, spread_ref, opening_ref, shares_ref, first_ref, last_ref, late_ref = refs
 
     block, blocks = lax.axis_index("row"), lax.axis_size("row")
 
@@ -105,6 +79,8 @@
     opening_ref[RANGE * first_rows :, :] = shares
     for b in range(RANGE):
         opening_ref[b * first_rows : (b + 1) * first_rows, :] = cot_ref[b * azimuth : b * azimuth + first_rows, :]
+        low, high = b * (azimuth - first_rows), (b + 1) * (azimuth - first_rows)
+        late_ref[low:high, :] = cot_ref[b * azimuth + first_rows : (b + 1) * azimuth, :]
 
     @pl.loop(0, azimuth // BATCH)
     def _(b):
@@ -145,19 +121,67 @@
             cells = source[pl.ds(k, count, stride=2), :]
             long_ref[pl.ds(start, count, stride=4), :] = cells
             short_ref[pl.ds(start, count, stride=4), :] = cells
-    cot_sides, den_sides, end = halo_starts(azimuth)
-    long_ref[cot_sides:end, :] = sides_ref[: end - cot_sides, :]
-    short_ref[cot_sides:den_sides, :] = sides_ref[: den_sides - cot_sides, :]
-    long_ref[end:, :] = shares_ref[...]
+    strips = 4 * count
+    short_ref[strips:, :] = sides_ref[: 4 * RANGE, :]
+    long_ref[strips : strips + 4 * RANGE, :] = sides_ref[4 * RANGE : 8 * RANGE, :]
+    long_ref[strips + 4 * RANGE :, :] = shares_ref[...]
     table_ref[...] = jnp.zeros(table_ref.shape, jnp.float32)
     table_ref[EDGE - 2 : EDGE, :] = left_ref[2 * count : 2 * count + 2, :]
     table_ref[EDGE : EDGE + radial, :] = gates_ref[...]
     table_ref[EDGE + radial : EDGE + radial + 2, :] = right_ref[2 * count : 2 * count + 2, :]
 
 
-def halo_starts(azimuth):
-    cot_sides = 4 * (azimuth + 4)
-    return cot_sides, cot_sides + 4 * RANGE, cot_sides + 8 * RANGE
+def slot_ranges():
+    place = lax.axis_index("mass")
+    return [
+        jnp.where(place == 2, 0, jnp.where(place == 3, 4, place + 1)),
+        jnp.where((place == 1) | (place == 2), place - 1, 4),
+        place,
+        jnp.where(place == 2, 3, 4),
+    ]
+
+
+def table_kernel(gain_ref, dest_ref, split_ref, coag_ref, frag_ref, pairs_ref, both_ref, cols_ref, rows_ref):
+    ranges = slot_ranges()
+    size = 4 * RANGE
+
+    def ordered(value, scales=(1, 1, 1, 1)):
+        parts = []
+        for r, scale in zip(ranges, scales):
+            part = jnp.zeros((value.shape[0], RANGE), value.dtype)
+            for q in range(4):
+                part = jnp.where(r == q, value[:, q * RANGE : (q + 1) * RANGE], part)
+            parts.append(part * scale)
+        return jnp.concatenate(parts, axis=1)
+
+    def bin_ids(axis):
+        ids = lax.broadcasted_iota(jnp.int32, (size, size), axis)
+        shift = jnp.zeros((size, size), jnp.int32)
+        for k, r in enumerate(ranges):
+            shift = jnp.where((ids >= k * RANGE) & (ids < (k + 1) * RANGE), (r - k) * RANGE, shift)
+        return ids + shift
+
+    gains = []
+    for r in ranges:
+        held = jnp.minimum(r, 3)
+        block = gain_ref[pl.ds(pl.multiple_of(held * RANGE, RANGE), RANGE), :]
+        scales = [
+            jnp.where((r < 4) & (c < 4), pairs_ref[held, jnp.minimum(c, 3)], 0).astype(jnp.float32) for c in ranges
+        ]
+        gains.append(ordered(block, scales))
+    row_ids, col_ids = bin_ids(0), bin_ids(1)
+    target = ordered(dest_ref[...])
+    upper = ordered(split_ref[...])
+    keeper = (row_ids == col_ids).astype(jnp.float32)
+    moved = jnp.where(row_ids == target, 1.0 - upper, 0.0) + jnp.where(row_ids == target + 1, upper, 0.0)
+    coag = (moved - keeper) * ordered(coag_ref[...]) + keeper
+    frag = jnp.where(row_ids <= col_ids, jnp.concatenate(gains, axis=0), 0.0) - keeper * ordered(frag_ref[...])
+    own = jnp.concatenate([coag[:, 2 * RANGE :], frag[:, 2 * RANGE :]], axis=1)
+    for ref, table in ((both_ref, jnp.concatenate([coag, frag], axis=1)), (cols_ref, own), (rows_ref, own.T)):
+        high, low = split(table)
+        ref[:size] = high
+        ref[size : 2 * size] = high
+        ref[2 * size :] = low
 
 
 def widened(ref, rows, lane):
@@ -192,9 +216,9 @@
     wide = radial + 16
     outer = pl.ds(8, wide)
     length = radial + 2 * EDGE
-    cot_sides, den_sides, halo_end = halo_starts(azimuth)
+    strips = 4 * (azimuth + 4)
     first_rows = RANGE * cuts[1]
-    shares = [(far_ref, first_rows), (near_ref, first_rows), (share_ref, 0), (next_halo, halo_end)]
+    shares = [(far_ref, first_rows), (near_ref, first_rows), (share_ref, 0), (next_halo, strips + 4 * RANGE)]
     load_shares(shares, length, center_ref, inward_ref, outward_ref, side_ref)
 
     def place(row, source, other, start, stride):
@@ -204,7 +228,7 @@
         slab[row, inner, :] = bins.T
 
     for row, k in ((0, 0), (1, 1), (azimuth + 2, 2), (azimuth + 3, 3)):
-        place(row, own_halo, next_halo, den_sides + k, 4)
+        place(row, own_halo, next_halo, strips + k, 4)
 
     @pl.loop(0, azimuth // BATCH)
     def _(b):
@@ -272,6 +296,7 @@
 
     slots = take(4)
     halos = take(4)
+    next_sides = take(1) if first or last else None
     center_ref, lower_ref, upper_ref, side_ref = take(4)
     gate_ref, second_ref, moved_ref = take(3)
     table1_ref, table2_ref = take(2)
@@ -292,8 +317,6 @@
     if not first:
         second[pl.ds(0, 2)] = carry_second[...]
         initial[pl.ds(0, 2)] = carry_first[...]
-
-    cot_sides = halo_starts(azimuth)[0]
 
     cells = slice(4 * low_row, 4 * high_row)
     edges = [halo[cells] for halo in halos]
@@ -310,7 +333,9 @@
 
     def bins_of(row):
         if row < 2 or row >= azimuth + 2:
-            starts = [(halo, cot_sides + (row if row < 2 else row - azimuth), 4) for halo in halos]
+            k = row if row < 2 else row - azimuth
+            starts = [(halo, 4 * (azimuth + 4) + k, 4) for halo in halos[:3]]
+            starts.append((next_sides[0], next_sides[0].shape[0] - 4 * RANGE + k, 4))
         else:
             starts = [(slot, row - 2 - offset, stride) for slot, (offset, stride) in zip(slots, offsets)]
         return jnp.concatenate([ref[pl.ds(start, RANGE, stride=stride), :] for ref, start, stride in starts], axis=0)
@@ -421,16 +446,9 @@
     def returning(x):
         return lax.ppermute(x, "mass", [(2, 3)])
 
-    slot_ranges = [
-        jnp.where(place == 2, 0, jnp.where(place == 3, 4, place + 1)),
-        jnp.where((place == 1) | (place == 2), place - 1, 4),
-        place,
-        jnp.where(place == 2, 3, 4),
-    ]
-
     count = azimuth + 4
     length = radial + 2 * EDGE
-    share_rows, (cot_sides, den_sides, halo_rows) = length + 8, halo_starts(azimuth)
+    share_rows, strip_rows = length + 8, 4 * count
 
     def flat(x):
         return x.reshape(-1, LANES)
@@ -450,19 +468,19 @@
         other = jnp.where(from_last, other, after)
 
     spread_row, gate = lax.optimization_barrier((spread[None, :], gate))
-    opening, shares, first_cells, last_cells = call(
+    opening, shares, first_cells, last_cells, late = call(
         functools.partial(opening_kernel, azimuth, radial, cuts[1]),
         [
             (cuts[1] * own_bins + share_rows, LANES),
             (share_rows, LANES),
             (azimuth, 2, LANES),
             (azimuth, 2, LANES),
+            (own_bins * (azimuth - cuts[1]), radial),
         ],
         [],
         [flat(cotangent), flat(density), drift_in, drift_out, spread_row],
         5,
     )
-    pieces = [cotangent[:, i:j] for i, j in spans]
 
     density_next = ending(density)
     far_first, near_first = far(opening), near(opening)
@@ -475,41 +493,41 @@
     line = [(i, i + 1) for i in range(rows - 1)]
     left = lax.ppermute(left_cells, "row", line)
     right = lax.ppermute(right_cells, "row", [(j, i) for i, j in line])
-    halos, short, gates = call(
+    gates, density_next = lax.optimization_barrier((gates, density_next))
+    long, short, gates = call(
         functools.partial(halo_kernel, azimuth, radial),
-        [(halo_rows + share_rows, LANES), (den_sides, LANES), (length, LANES)],
+        [(strip_rows + 4 * own_bins + share_rows, LANES), (strip_rows + 4 * own_bins, LANES), (length, LANES)],
         [],
         [left, right, other, shares, gates],
     )
 
-    frag_gain, halos = lax.optimization_barrier((frag_gain, halos))
-
-    def chosen(matrix, axis):
-        return jnp.concatenate(
-            [lax.dynamic_slice_in_dim(matrix, r * RANGE, RANGE, axis) for r in slot_ranges], axis=axis
-        )
-
-    def related(matrix):
-        return chosen(chosen(jnp.pad(matrix, ((0, RANGE), (0, RANGE))), 0), 1)
-
-    coag = related(coag_matrix(dest_bins, bott_split, coag_rate))
-    frag = related(frag_matrix(frag_pairs, frag_gain, frag_rate))
-    both = stacked(jnp.concatenate([coag, frag], axis=1))
-    upper_half = jnp.concatenate([coag[:, 2 * RANGE :], frag[:, 2 * RANGE :]], axis=1)
-    own_cols = stacked(upper_half)
-    own_rows = stacked(upper_half.T)
-
-    halos_next = ending(halos)
-    halo_refs = [far(short), near(short), halos, halos_next]
-    halos_next, late, pieces[0], pieces[1] = lax.optimization_barrier(
-        (halos_next, cotangent[:, cuts[1] :], pieces[0], pieces[1])
-    )
-    halo_refs[3] = halos_next
-    late_next = ending(late)
-    gathered = [
-        [far_first, near_first, pieces[0], ending(pieces[0])],
-        [far(pieces[1]), near(pieces[1]), pieces[1], late_next],
-    ]
+    frag_gain, long = lax.optimization_barrier((frag_gain, long))
+    vmem = pl.BlockSpec(memory_space=pltpu.VMEM)
+    total_bins = frag_gain.shape[0]
+    both, own_cols, own_rows = pl.pallas_call(
+        table_kernel,
+        out_shape=[jax.ShapeDtypeStruct((3 * total_bins, n * total_bins), jnp.bfloat16) for n in (2, 1, 1)],
+        in_specs=[vmem] * 5 + [pl.BlockSpec(memory_space=pltpu.SMEM)],
+        out_specs=[vmem] * 3,
+        compiler_params=pltpu.CompilerParams(vmem_limit_bytes=VMEM_LIMIT),
+        cost_estimate=pl.CostEstimate(flops=0, bytes_accessed=3 * MICRO, transcendentals=0),
+    )(
+        frag_gain,
+        dest_bins[None, :],
+        bott_split[None, :],
+        coag_rate[None, :],
+        frag_rate[None, :],
+        frag_pairs,
+    )
+
+    long_next = ending(long)
+    first_next = jnp.concatenate([opening[: own_bins * cuts[1]], other[: 4 * own_bins]], axis=0)
+    short, first_next, late, far_first, near_first, both = lax.optimization_barrier(
+        (short, first_next, late, far_first, near_first, both)
+    )
+    halo_refs = [far(short), near(short), short, long_next]
+    first_next = ending(first_next)
+    far_late, near_late = far(late), near(late)
 
     coefs = [(2, length, LANES)] * 3 + [(2, LANES)]
     products = list(call(
@@ -522,8 +540,8 @@
             far_first,
             near_first,
             shares,
-            halos,
-            halos_next,
+            long,
+            long_next,
             gates,
             slope,
             own_rows,
@@ -531,8 +549,10 @@
         13,
     ))
     groups = len(spans)
-    products[0], pieces[2] = lax.optimization_barrier((products[0], pieces[2]))
-    gathered.append([far(pieces[2]), near(pieces[2]), pieces[2], late_next])
+    products[0], halo_refs[0], halo_refs[1], late = lax.optimization_barrier(
+        (products[0], halo_refs[0], halo_refs[1], late)
+    )
+    gathered = [[far_first, near_first, opening, first_next], [far_late, near_late, late, ending(late)]]
     moved, second, coefs = products[:groups], products[groups : 2 * groups], products[2 * groups :]
 
     own_outs, next_outs, carry = [], [], []
@@ -542,10 +562,10 @@
         high_row = azimuth + 4 if last else cuts[g + 1] + 2
         new = high_row - low_row
         n_out = (azimuth + 2 if last else high_row - 2) - (2 if first else low_row - 2)
-        operands = [flat(x) for x in gathered[g]]
-        own = (cuts[g], cuts[g + 1] - cuts[g])
-        offsets = [own, own, own, own if first else (cuts[1], azimuth - cuts[1])]
-        operands += [*halo_refs, *coefs, gates, second[g], moved[g]]
+        operands = [*gathered[min(g, 1)]]
+        offsets = [(cuts[0], cuts[1]) if first else (cuts[1], azimuth - cuts[1])] * 4
+        operands += halo_refs + ([first_next] if first or last else [])
+        operands += [*coefs, gates, second[g], moved[g]]
         operands += [both, own_cols, *carry]
         if not first:
             operands.append(moved[g - 1][-1:])

time: 129 us -> 116 us (0.90)
  starting transfers between devices: 41.9 us -> 34.7 us
  other arithmetic: 8.93 us -> 1.75 us
  Pallas kernels: 41.8 us -> 47 us
  local copies, waits for them, and re-layouts: 15 us -> 9.84 us
  waiting for transfers between devices: 18.8 us -> 21.2 us
    ppermute x3, starting transfers between devices: 12.6 us -> 2.76 us  [per_device(): lax.ppermute(speed_gradient, 'mass', [(i, (i + k) % size) for i in range(...]
    ppermute x4, starting transfers between devices: 13.4 us -> 18 us  [ending(): return lax.ppermute(x, 'mass', [(3, 2)])]
    another operation x4 -> x0, other arithmetic: 4.38 us -> none
    pallas_call x0 -> x1, Pallas kernels: none -> 4.23 us  [per_device(): pl.pallas_call(table_kernel, out_shape=[jax.ShapeDtypeStruct((3 * total_b...]
    concatenate x2 -> x0, local copies, waits for them, and re-layouts: 3.1 us -> none  [the longest x1 2.18 us: per_device(): both = stacked(jnp.concatenate([coag, frag], axis=1))]
    ppermute x3, waiting for transfers between devices: 8.29 us -> 11 us  [per_device(): lax.ppermute(speed_gradient, 'mass', [(i, (i + k) % size) for i in range(...]
    concatenate x5 -> x1, other arithmetic: 2.72 us -> 0.04 us  [per_device(): jnp.concatenate([opening[:own_bins * cuts[1]], other[:4 * own_bins]], axi...]
    ppermute x1, waiting for transfers between devices: 4.13 us -> 6.36 us  [per_device(): other = lax.ppermute(sides, 'phi', ring)]
  transfers between devices with their start and end apart: 22 -> 20, of which waited for: 6 -> 6; matrix products, arithmetic and copies ran while one was open for 15% -> 6% of each run, Pallas kernels for 27% -> 41%
where the time goes in v5:
time: 116 us
  Pallas kernels  47 us (41%)
  starting transfers between devices  34.7 us (30%)
  waiting for transfers between devices  21.2 us (18%)
  local copies, waits for them, and re-layouts  9.84 us (8%)
  other arithmetic  1.75 us (2%)
    pallas_call x8, Pallas kernels, call(): pl.pallas_call(kernel, out_shape=[jax.ShapeDtypeStruct(o, jnp.float32) fo...  42.7 us
    ppermute x4, starting transfers between devices, ending(): return lax.ppermute(x, 'mass', [(3, 2)])  18 us
    ppermute x3, waiting for transfers between devices, per_device(): lax.ppermute(speed_gradient, 'mass', [(i, (i + k) % size) for i in range(...  11 us
    ppermute x1, waiting for transfers between devices, per_device(): other = lax.ppermute(sides, 'phi', ring)  6.36 us
    unnamed x39, local copies, waits for them, and re-layouts  4.88 us
    pallas_call x1, Pallas kernels, per_device(): pl.pallas_call(table_kernel, out_shape=[jax.ShapeDtypeStruct((3 * total_b...  4.23 us
    ppermute x3, starting transfers between devices, returning(): return lax.ppermute(x, 'mass', [(2, 3)])  4 us
    slice x2, local copies, waits for them, and re-layouts, per_device(): operands.append(moved[g - 1][-1:])  2.94 us
  transfers between devices with their start and end apart: 20, of which 6 were waited for; matrix products, arithmetic and copies ran while one was open for 6% of the time, Pallas kernels for 41%

profile of v5, /device:TPU:24, one launch (start us, length us, event | category | flops | bytes accessed | tf_op | source)
XLA Modules:
  0.0 115.5 jit_solution(15731866556664599878)
XLA Ops:
  0.6 2.4 %collective-permute-start.3 = (f32[64,32,128]{2,1,0:T(8,128)}, f32[64,32,128]{2,1,0:T(8,128)S(1)}, u32[]{:S(2)}, u32[]{:S(2)}) collective-permute-start(f32[64,32,128]{2,1,0:T(8,128)} %param.14), channel_id=1, source_target_pairs={{3,2},{7,6},{11,10},{15,14},{19,18},{23,22},{27,26},{31,30}} | collective-permute-start | bytes 3145736 | tf_op jit(solution)/shard_map/ppermute | solution.py:444
  3.1 2.5 %shard_map.149 = (f32[520,128]{1,0:T(8,128)}, f32[32,128]{1,0:T(8,128)}, f32[128,128]{1,0:T(8,128)}) custom-call(f32[2048,128]{1,0:T(8,128)} %bitcast.20, f32[2048,128]{1,0:T(8,128)} %bitcast.17, f32[32,128]{1,0:T(8,128)} %collide_ref.1, f32[1,128]{1,0:T(1,128)} %bitcast.37, s32[32,128]{1,0:T(8,128)} %regime_ref.1), custom_call_target="tpu_custom_call" | custom-call | bytes 6000000 | tf_op jit(solution)/shard_map/pallas_call | solution.py:404
  5.6 4.5 %shard_map.150 = (f32[1192,128]{1,0:T(8,128)}, f32[168,128]{1,0:T(8,128)}, f32[32,2,128]{2,1,0:T(2,128)}, f32[32,2,128]{2,1,0:T(2,128)}, f32[1024,128]{1,0:T(8,128)}) custom-call(f32[2048,128]{1,0:T(8,128)} %bitcast.21, f32[2048,128]{1,0:T(8,128)} %bitcast.18, f32[64,512]{1,0:T(8,128)} %refs_2_.1, f32[64,512]{1,0:T(8,128)} %refs_3_.1, f32[1,64]{1,0:T(1,128)} %bitcast.38), custom_call_target="tpu_custom_call" | custom-call | bytes 15000000 | tf_op jit(solution)/shard_map/pallas_call | solution.py:404
  11.6 1.6 %collective-permute-start = (f32[520,128]{1,0:T(8,128)S(1)}, f32[520,128]{1,0:T(8,128)S(1)}, u32[]{:S(2)}, u32[]{:S(2)}) collective-permute-start(f32[520,128]{1,0:T(8,128)S(1)} %copy-done.17), channel_id=1, source_target_pairs={{0,16},{16,0},{1,17},{17,1},{2,18},{18,2},{3,19},{19,3},{4,20},{20... | collective-permute-start | bytes 798728 | tf_op jit(solution)/shard_map/ppermute | solution.py:464
  13.2 6.4 %collective-permute-done.sides_ref = f32[520,128]{1,0:T(8,128)S(1)} collective-permute-done((f32[520,128]{1,0:T(8,128)S(1)}, f32[520,128]{1,0:T(8,128)S(1)}, u32[]{:S(2)}, u32[]{:S(2)}) %collective-permute-start) | collective-permute-done | bytes 266272 | tf_op jit(solution)/shard_map/ppermute | solution.py:464
  20.2 1.8 %shard_map.151 = (f32[80,128]{1,0:T(8,128)}, f32[80,128]{1,0:T(8,128)}, f32[128,128]{1,0:T(8,128)}) custom-call(f32[520,128]{1,0:T(8,128)} %copy-done.10, f32[64,128]{1,0:T(8,128)} %bitcast.23, f32[64,128]{1,0:T(8,128)} %bitcast.24, f32[32,128]{1,0:T(8,128)} %get-tuple-element.66.gate_ref), custom_call_target="tpu_custom_call" | custom-call | bytes 3000000 | tf_op jit(solution)/shard_map/pallas_call | solution.py:404
  22.1 1.3 %collective-permute-start.1 = (f32[80,128]{1,0:T(8,128)}, f32[80,128]{1,0:T(8,128)S(1)}, u32[]{:S(2)}, u32[]{:S(2)}) collective-permute-start(f32[80,128]{1,0:T(8,128)} %get-tuple-element.67), channel_id=1, source_target_pairs={{0,4},{4,8},{8,12},{1,5},{5,9},{9,13},{2,6},{6,10},{10,14},{3,7},{... | collective-permute-start | bytes 122888 | tf_op jit(solution)/shard_map/ppermute | solution.py:494
  23.4 1.3 %collective-permute-start.2 = (f32[80,128]{1,0:T(8,128)}, f32[80,128]{1,0:T(8,128)S(1)}, u32[]{:S(2)}, u32[]{:S(2)}) collective-permute-start(f32[80,128]{1,0:T(8,128)} %get-tuple-element.68), channel_id=1, source_target_pairs={{4,0},{8,4},{12,8},{5,1},{9,5},{13,9},{6,2},{10,6},{14,10},{7,3},{... | collective-permute-start | bytes 122888 | tf_op jit(solution)/shard_map/ppermute | solution.py:495
  24.7 1.1 slice.12
  26.7 1.7 %collective-permute-done.2.right_ref = f32[80,128]{1,0:T(8,128)S(1)} collective-permute-done((f32[80,128]{1,0:T(8,128)}, f32[80,128]{1,0:T(8,128)S(1)}, u32[]{:S(2)}, u32[]{:S(2)}) %collective-permute-start.2) | collective-permute-done | bytes 40992 | tf_op jit(solution)/shard_map/ppermute | solution.py:495
  29.0 1.9 %shard_map.152 = (f32[568,128]{1,0:T(8,128)}, f32[400,128]{1,0:T(8,128)}, f32[160,128]{1,0:T(8,128)}) custom-call(f32[80,128]{1,0:T(8,128)} %copy-done.15, f32[80,128]{1,0:T(8,128)} %copy-done.16, f32[520,128]{1,0:T(8,128)} %copy-done.10, f32[168,128]{1,0:T(8,128)} %get-tuple-element.69.shares_ref.refs_4_, f32[128,128]{1,0:T(8,128)} %get-tuple-element.71.gates_ref), custom_call_target="tpu_custom_call" | custom-call | bytes 3000000 | tf_op jit(solution)/shard_map/pallas_call | solution.py:404
  30.9 3.3 %collective-permute-start.7 = (f32[568,128]{1,0:T(8,128)}, f32[568,128]{1,0:T(8,128)S(1)}, u32[]{:S(2)}, u32[]{:S(2)}) collective-permute-start(f32[568,128]{1,0:T(8,128)} %get-tuple-element.82.refs_5_), channel_id=1, source_target_pairs={{3,2},{7,6},{11,10},{15,14},{19,18},{23,22},{27,26},{31,30}} | collective-permute-start | bytes 872456 | tf_op jit(solution)/shard_map/ppermute | solution.py:444
  34.3 4.2 %shard_map.153 = (bf16[768,512]{1,0:T(8,128)(2,1)}, bf16[768,256]{1,0:T(8,128)(2,1)}, bf16[768,256]{1,0:T(8,128)(2,1)}) custom-call(f32[256,256]{1,0:T(8,128)} %gain_ref, s32[1,256]{1,0:T(1,128)} %bitcast.33, f32[1,256]{1,0:T(1,128)} %bitcast.34, f32[1,256]{1,0:T(1,128)} %bitcast.35, f32[1,256]{1,0:T(1,128)} %bitcast.36, s32[4,4]{1,0:T(4,128)} %pairs_ref.1), custom_call_target="tpu_custom_call" | custom-call | bytes 9000000 | tf_op jit(solution)/shard_map/pallas_call | solution.py:507
  38.6 4.4 %collective-permute-start.6 = (f32[1280,128]{1,0:T(8,128)S(1)}, f32[1280,128]{1,0:T(8,128)S(1)}, u32[]{:S(2)}, u32[]{:S(2)}) collective-permute-start(f32[1280,128]{1,0:T(8,128)S(1)} %pad_maximum_fusion), channel_id=1, source_target_pairs={{3,2},{7,6},{11,10},{15,14},{19,18},{23,22},{27,26},{31,30}} | collective-permute-start | bytes 1966088 | tf_op jit(solution)/shard_map/ppermute | solution.py:444
  45.9 9.7 %shard_map.154 = (f32[16,128,128]{2,1,0:T(8,128)}, f32[8,128,128]{2,1,0:T(8,128)}, f32[8,128,128]{2,1,0:T(8,128)}, f32[16,2,128,128]{3,2,1,0:T(8,128)}, f32[8,2,...) custom-call(f32[2048,128]{1,0:T(8,128)} %bitcast.19, ...), custom_call_target="tpu_custom_call" | custom-call | bytes 39000000 | tf_op jit(solution)/shard_map/pallas_call | solution.py:404
  55.6 7.8 %collective-permute-start.13 = (f32[1024,128]{1,0:T(8,128)S(1)}, f32[1024,128]{1,0:T(8,128)S(1)}, u32[]{:S(2)}, u32[]{:S(2)}) collective-permute-start(f32[1024,128]{1,0:T(8,128)S(1)} %copy-done.4), channel_id=1, source_target_pairs={{3,2},{7,6},{11,10},{15,14},{19,18},{23,22},{27,26},{31,30}} | collective-permute-start | bytes 1572872 | tf_op jit(solution)/shard_map/ppermute | solution.py:444
  64.3 9.2 %shard_map.155 = (f32[14,64,128]{2,1,0:T(8,128)}, f32[14,64,128]{2,1,0:T(8,128)}, f32[128,128]{1,0:T(8,128)}, f32[2,2,160,128]{3,2,1,0:T(8,128)}, f32[2,160,128]{2,1,0:T(8,128)}) custom-call(f32[1192,128]{1,0:T(8,128)} %copy-done.2, f32[1192,128]{1,0:T(8,128)} %copy-done.3, f32[1192,128]{1,0:T(8,128)} %get-tuple-element.73.refs_2_, f32[1280,128]{1,0:T(8,128)} %copy-done, ...), custom_call_target="tpu_custom_call" | custom-call | bytes 33000000 | tf_op jit(solution)/shard_map/pallas_call | solution.py:404
  73.5 1.3 %collective-permute-start.10 = (f32[14,64,128]{2,1,0:T(8,128)}, f32[14,64,128]{2,1,0:T(8,128)S(1)}, u32[]{:S(2)}, u32[]{:S(2)}) collective-permute-start(f32[14,64,128]{2,1,0:T(8,128)} %get-tuple-element.99), channel_id=1, source_target_pairs={{2,3},{6,7},{10,11},{14,15},{18,19},{22,23},{26,27},{30,31}} | collective-permute-start | bytes 1376264 | tf_op jit(solution)/shard_map/ppermute | solution.py:447
  74.8 1.5 %slice.14.refs_20_ = f32[1,128,128]{2,1,0:T(8,128)} slice(f32[16,128,128]{2,1,0:T(8,128)} %get-tuple-element.96.refs_15_), slice={[15:16], [0:128], [0:128]} | slice | bytes 131072 | tf_op jit(solution)/shard_map/slice | solution.py:571
  76.2 1.5 %slice.15.refs_21_ = f32[1,128,128]{2,1,0:T(8,128)} slice(f32[8,128,128]{2,1,0:T(8,128)} %get-tuple-element.102.refs_14_), slice={[7:8], [0:128], [0:128]} | slice | bytes 131072 | tf_op jit(solution)/shard_map/slice | solution.py:571
  78.9 6.3 %shard_map.156 = (f32[8,64,128]{2,1,0:T(8,128)}, f32[8,64,128]{2,1,0:T(8,128)}, f32[128,128]{1,0:T(8,128)}, f32[2,2,160,128]{3,2,1,0:T(8,128)}, f32[2,160,128]{2,1,0:T(8,128)}) custom-call(f32[1024,128]{1,0:T(8,128)} %copy-done.5, f32[1024,128]{1,0:T(8,128)} %copy-done.6, f32[1024,128]{1,0:T(8,128)} %get-tuple-element.100.refs_2_, f32[1024,128]{1,0:T(8,128)} %copy-done.7, ...), custom_call_target="tpu_custom_call" | custom-call | bytes 18000000 | tf_op jit(solution)/shard_map/pallas_call | solution.py:404
  85.1 6.8 %shard_map.157 = (f32[10,64,128]{2,1,0:T(8,128)}, f32[10,64,128]{2,1,0:T(8,128)}, f32[128,128]{1,0:T(8,128)}) custom-call(f32[1024,128]{1,0:T(8,128)} %copy-done.5, f32[1024,128]{1,0:T(8,128)} %copy-done.6, f32[1024,128]{1,0:T(8,128)} %get-tuple-element.100.refs_2_, f32[1024,128]{1,0:T(8,128)} %copy-done.7, f32[400,128]{1,0:T(8,128)} %copy-done.8, ...), custom_call_target="tpu_custom_call" | custom-call | bytes 21000000 | tf_op jit(solution)/shard_map/pallas_call | solution.py:404
  92.0 1.4 %collective-permute-start.15 = (f32[10,64,128]{2,1,0:T(8,128)}, f32[10,64,128]{2,1,0:T(8,128)S(1)}, u32[]{:S(2)}, u32[]{:S(2)}) collective-permute-start(f32[10,64,128]{2,1,0:T(8,128)} %get-tuple-element.112), channel_id=1, source_target_pairs={{2,3},{6,7},{10,11},{14,15},{18,19},{22,23},{26,27},{30,31}} | collective-permute-start | bytes 983048 | tf_op jit(solution)/shard_map/ppermute | solution.py:447
  93.4 1.3 %collective-permute-start.14 = (f32[8,64,128]{2,1,0:T(8,128)S(1)}, f32[8,64,128]{2,1,0:T(8,128)S(1)}, u32[]{:S(2)}, u32[]{:S(2)}) collective-permute-start(f32[8,64,128]{2,1,0:T(8,128)S(1)} %copy-done.18), channel_id=1, source_target_pairs={{2,3},{6,7},{10,11},{14,15},{18,19},{22,23},{26,27},{30,31}} | collective-permute-start | bytes 786440 | tf_op jit(solution)/shard_map/ppermute | solution.py:447
  94.7 0.9 reduce_sum.18
  95.7 2.8 %collective-permute-start.16 = (f32[128]{0:T(128)S(1)}, f32[128]{0:T(128)S(1)}, u32[]{:S(2)}, u32[]{:S(2)}) collective-permute-start(f32[128]{0:T(128)S(1)} %reduce_sum.18), channel_id=1, source_target_pairs={{0,3},{1,0},{2,1},{3,2},{4,7},{5,4},{6,5},{7,6},{8,11},{9,8},{10,9... | collective-permute-start | bytes 1544 | tf_op jit(solution)/shard_map/ppermute | solution.py:588
  98.4 2.6 %collective-permute-done.16 = f32[128]{0:T(128)S(1)} collective-permute-done((f32[128]{0:T(128)S(1)}, f32[128]{0:T(128)S(1)}, u32[]{:S(2)}, u32[]{:S(2)}) %collective-permute-start.16) | collective-permute-done | bytes 544 | tf_op jit(solution)/shard_map/ppermute | solution.py:588
  101.1 1.8 %collective-permute-done.17 = f32[128]{0:T(128)S(1)} collective-permute-done((f32[128]{0:T(128)S(1)}, f32[128]{0:T(128)S(1)}, u32[]{:S(2)}, u32[]{:S(2)}) %collective-permute-start.17) | collective-permute-done | bytes 544 | tf_op jit(solution)/shard_map/ppermute | solution.py:588
  102.9 6.6 %collective-permute-done.18 = f32[128]{0:T(128)S(1)} collective-permute-done((f32[128]{0:T(128)S(1)}, f32[128]{0:T(128)S(1)}, u32[]{:S(2)}, u32[]{:S(2)}) %collective-permute-start.18) | collective-permute-done | bytes 544 | tf_op jit(solution)/shard_map/ppermute | solution.py:588
  109.5 1.5 %collective-permute-start.19 = (f32[128]{0:T(128)S(1)}, f32[128]{0:T(128)S(1)}, u32[]{:S(2)}, u32[]{:S(2)}) collective-permute-start(f32[128]{0:T(128)S(1)} %dynamic-slice_reduce_fusion), channel_id=1, source_target_pairs={{0,16},{16,0},{1,17},{17,1},{2,18},{18,2},{3,19},{19,3},{4,20},{20... | collective-permute-start | bytes 1544 | tf_op jit(solution)/shard_map/ppermute | solution.py:594
  111.1 2.1 %collective-permute-done.19 = f32[128]{0:T(128)S(1)} collective-permute-done((f32[128]{0:T(128)S(1)}, f32[128]{0:T(128)S(1)}, u32[]{:S(2)}, u32[]{:S(2)}) %collective-permute-start.19) | collective-permute-done | bytes 544 | tf_op jit(solution)/shard_map/ppermute | solution.py:594
  113.9 1.6 %copy.16 = f32[64,32,128]{2,1,0:T(8,128)} copy(f32[64,32,128]{2,0,1:T(8,128)S(1)} %maximum_bitcast_fusion) | data formatting | bytes 2097152
  (69 shorter events, 9.3 us)
Async XLA Ops:
  0.6 26.0 %collective-permute-start.3 = (f32[64,32,128]{2,1,0:T(8,128)}, f32[64,32,128]{2,1,0:T(8,128)S(1)}, u32[]{:S(2)}, u32[]{:S(2)}) collective-permute-start(f32[64,32,128]{2,1,0:T(8,128)} %param.14), channel_id=1, source_target_pairs={{3,2},{7,6},{11,10},{15,14},{19,18},{23,22},{27,26},{31,30}} | collective-permute-start | bytes 3145736 | tf_op jit(solution)/shard_map/ppermute | solution.py:444
  5.6 6.0 %copy-start.17 = (f32[520,128]{1,0:T(8,128)S(1)}, f32[520,128]{1,0:T(8,128)}, u32[]{:S(2)}) copy-start(f32[520,128]{1,0:T(8,128)} %get-tuple-element.61) | copy-start | bytes 798724
  10.1 34.3 %copy-start.4 = (f32[1024,128]{1,0:T(8,128)S(1)}, f32[1024,128]{1,0:T(8,128)}, u32[]{:S(2)}) copy-start(f32[1024,128]{1,0:T(8,128)} %get-tuple-element.100.refs_2_) | copy-start | bytes 1572868
  10.1 28.5 %collective-permute-start.4 = (f32[1192,128]{1,0:T(8,128)}, f32[1192,128]{1,0:T(8,128)S(1)}, u32[]{:S(2)}, u32[]{:S(2)}) collective-permute-start(f32[1192,128]{1,0:T(8,128)} %get-tuple-element.73.refs_2_), channel_id=1, source_target_pairs={{0,2},{2,1},{1,0},{4,6},{6,5},{5,4},{8,10},{10,9},{9,8},{12,14},{1... | collective-permute-start | bytes 1830920 | tf_op jit(solution)/shard_map/ppermute | solution.py:438
  10.9 27.7 %collective-permute-start.5 = (f32[1192,128]{1,0:T(8,128)}, f32[1192,128]{1,0:T(8,128)S(1)}, u32[]{:S(2)}, u32[]{:S(2)}) collective-permute-start(f32[1192,128]{1,0:T(8,128)} %get-tuple-element.73.refs_2_), channel_id=1, source_target_pairs={{0,1},{1,2},{4,5},{5,6},{8,9},{9,10},{12,13},{13,14},{16,17},{17,1... | collective-permute-start | bytes 1830920 | tf_op jit(solution)/shard_map/ppermute | solution.py:441
  11.6 7.9 %collective-permute-start = (f32[520,128]{1,0:T(8,128)S(1)}, f32[520,128]{1,0:T(8,128)S(1)}, u32[]{:S(2)}, u32[]{:S(2)}) collective-permute-start(f32[520,128]{1,0:T(8,128)S(1)} %copy-done.17), channel_id=1, source_target_pairs={{0,16},{16,0},{1,17},{17,1},{2,18},{18,2},{3,19},{19,3},{4,20},{20... | collective-permute-start | bytes 798728 | tf_op jit(solution)/shard_map/ppermute | solution.py:464
  22.1 4.6 %collective-permute-start.1 = (f32[80,128]{1,0:T(8,128)}, f32[80,128]{1,0:T(8,128)S(1)}, u32[]{:S(2)}, u32[]{:S(2)}) collective-permute-start(f32[80,128]{1,0:T(8,128)} %get-tuple-element.67), channel_id=1, source_target_pairs={{0,4},{4,8},{8,12},{1,5},{5,9},{9,13},{2,6},{6,10},{10,14},{3,7},{... | collective-permute-start | bytes 122888 | tf_op jit(solution)/shard_map/ppermute | solution.py:494
  23.4 5.1 %collective-permute-start.2 = (f32[80,128]{1,0:T(8,128)}, f32[80,128]{1,0:T(8,128)S(1)}, u32[]{:S(2)}, u32[]{:S(2)}) collective-permute-start(f32[80,128]{1,0:T(8,128)} %get-tuple-element.68), channel_id=1, source_target_pairs={{4,0},{8,4},{12,8},{5,1},{9,5},{13,9},{6,2},{10,6},{14,10},{7,3},{... | collective-permute-start | bytes 122888 | tf_op jit(solution)/shard_map/ppermute | solution.py:495
  26.7 19.2 %copy-start.11 = (f32[64,32,128]{2,1,0:T(8,128)}, f32[64,32,128]{2,1,0:T(8,128)S(1)}, u32[]{:S(2)}) copy-start(f32[64,32,128]{2,1,0:T(8,128)S(1)} %collective-permute-done.3) | copy-start | bytes 3145732
  26.7 1.8 %copy-start.15 = (f32[80,128]{1,0:T(8,128)}, f32[80,128]{1,0:T(8,128)S(1)}, u32[]{:S(2)}) copy-start(f32[80,128]{1,0:T(8,128)S(1)} %collective-permute-done.1.left_ref) | copy-start | bytes 122884
  30.9 14.2 %collective-permute-start.7 = (f32[568,128]{1,0:T(8,128)}, f32[568,128]{1,0:T(8,128)S(1)}, u32[]{:S(2)}, u32[]{:S(2)}) collective-permute-start(f32[568,128]{1,0:T(8,128)} %get-tuple-element.82.refs_5_), channel_id=1, source_target_pairs={{3,2},{7,6},{11,10},{15,14},{19,18},{23,22},{27,26},{31,30}} | collective-permute-start | bytes 872456 | tf_op jit(solution)/shard_map/ppermute | solution.py:444
  38.6 7.3 %copy-start.2 = (f32[1192,128]{1,0:T(8,128)}, f32[1192,128]{1,0:T(8,128)S(1)}, u32[]{:S(2)}) copy-start(f32[1192,128]{1,0:T(8,128)S(1)} %collective-permute-done.4.refs_2_.refs_0_) | copy-start | bytes 1830916
  38.6 7.3 %copy-start.3 = (f32[1192,128]{1,0:T(8,128)}, f32[1192,128]{1,0:T(8,128)S(1)}, u32[]{:S(2)}) copy-start(f32[1192,128]{1,0:T(8,128)S(1)} %collective-permute-done.5.refs_3_.refs_1_) | copy-start | bytes 1830916
  38.6 24.8 %collective-permute-start.6 = (f32[1280,128]{1,0:T(8,128)S(1)}, f32[1280,128]{1,0:T(8,128)S(1)}, u32[]{:S(2)}, u32[]{:S(2)}) collective-permute-start(f32[1280,128]{1,0:T(8,128)S(1)} %pad_maximum_fusion), channel_id=1, source_target_pairs={{3,2},{7,6},{11,10},{15,14},{19,18},{23,22},{27,26},{31,30}} | collective-permute-start | bytes 1966088 | tf_op jit(solution)/shard_map/ppermute | solution.py:444
  43.0 12.6 %collective-permute-start.8 = (f32[400,128]{1,0:T(8,128)}, f32[400,128]{1,0:T(8,128)S(1)}, u32[]{:S(2)}, u32[]{:S(2)}) collective-permute-start(f32[400,128]{1,0:T(8,128)} %get-tuple-element.87.refs_6_), channel_id=1, source_target_pairs={{0,2},{2,1},{1,0},{4,6},{6,5},{5,4},{8,10},{10,9},{9,8},{12,14},{1... | collective-permute-start | bytes 614408 | tf_op jit(solution)/shard_map/ppermute | solution.py:438
  43.7 11.9 %collective-permute-start.9 = (f32[400,128]{1,0:T(8,128)}, f32[400,128]{1,0:T(8,128)S(1)}, u32[]{:S(2)}, u32[]{:S(2)}) collective-permute-start(f32[400,128]{1,0:T(8,128)} %get-tuple-element.87.refs_6_), channel_id=1, source_target_pairs={{0,1},{1,2},{4,5},{5,6},{8,9},{9,10},{12,13},{13,14},{16,17},{17,1... | collective-permute-start | bytes 614408 | tf_op jit(solution)/shard_map/ppermute | solution.py:441
  44.4 33.3 %collective-permute-start.11 = (f32[1024,128]{1,0:T(8,128)S(1)}, f32[1024,128]{1,0:T(8,128)S(1)}, u32[]{:S(2)}, u32[]{:S(2)}) collective-permute-start(f32[1024,128]{1,0:T(8,128)S(1)} %copy-done.4), channel_id=1, source_target_pairs={{0,2},{2,1},{1,0},{4,6},{6,5},{5,4},{8,10},{10,9},{9,8},{12,14},{1... | collective-permute-start | bytes 1572872 | tf_op jit(solution)/shard_map/ppermute | solution.py:438
  45.1 32.6 %collective-permute-start.12 = (f32[1024,128]{1,0:T(8,128)S(1)}, f32[1024,128]{1,0:T(8,128)S(1)}, u32[]{:S(2)}, u32[]{:S(2)}) collective-permute-start(f32[1024,128]{1,0:T(8,128)S(1)} %copy-done.4), channel_id=1, source_target_pairs={{0,1},{1,2},{4,5},{5,6},{8,9},{9,10},{12,13},{13,14},{16,17},{17,1... | collective-permute-start | bytes 1572872 | tf_op jit(solution)/shard_map/ppermute | solution.py:441
  55.6 7.8 %copy-start.8 = (f32[400,128]{1,0:T(8,128)}, f32[400,128]{1,0:T(8,128)S(1)}, u32[]{:S(2)}) copy-start(f32[400,128]{1,0:T(8,128)S(1)} %collective-permute-done.8.refs_4_) | copy-start | bytes 614404
  55.6 7.8 %copy-start.9 = (f32[400,128]{1,0:T(8,128)}, f32[400,128]{1,0:T(8,128)S(1)}, u32[]{:S(2)}) copy-start(f32[400,128]{1,0:T(8,128)S(1)} %collective-permute-done.9.refs_5_) | copy-start | bytes 614404
  55.6 22.1 %collective-permute-start.13 = (f32[1024,128]{1,0:T(8,128)S(1)}, f32[1024,128]{1,0:T(8,128)S(1)}, u32[]{:S(2)}, u32[]{:S(2)}) collective-permute-start(f32[1024,128]{1,0:T(8,128)S(1)} %copy-done.4), channel_id=1, source_target_pairs={{3,2},{7,6},{11,10},{15,14},{19,18},{23,22},{27,26},{31,30}} | collective-permute-start | bytes 1572872 | tf_op jit(solution)/shard_map/ppermute | solution.py:444
  73.5 40.1 %collective-permute-start.10 = (f32[14,64,128]{2,1,0:T(8,128)}, f32[14,64,128]{2,1,0:T(8,128)S(1)}, u32[]{:S(2)}, u32[]{:S(2)}) collective-permute-start(f32[14,64,128]{2,1,0:T(8,128)} %get-tuple-element.99), channel_id=1, source_target_pairs={{2,3},{6,7},{10,11},{14,15},{18,19},{22,23},{26,27},{30,31}} | collective-permute-start | bytes 1376264 | tf_op jit(solution)/shard_map/ppermute | solution.py:447
  85.1 8.3 %copy-start.18 = (f32[8,64,128]{2,1,0:T(8,128)S(1)}, f32[8,64,128]{2,1,0:T(8,128)}, u32[]{:S(2)}) copy-start(f32[8,64,128]{2,1,0:T(8,128)} %get-tuple-element.106) | copy-start | bytes 786436
  85.1 28.5 %copy-start.12 = (f32[14,64,128]{2,1,0:T(8,128)S(1)}, f32[14,64,128]{2,1,0:T(8,128)}, u32[]{:S(2)}) copy-start(f32[14,64,128]{2,1,0:T(8,128)} %get-tuple-element.114) | copy-start | bytes 1376260
  85.1 28.6 %copy-start.14 = (f32[8,64,128]{2,1,0:T(8,128)S(1)}, f32[8,64,128]{2,1,0:T(8,128)}, u32[]{:S(2)}) copy-start(f32[8,64,128]{2,1,0:T(8,128)} %get-tuple-element.116) | copy-start | bytes 786436
  92.0 21.8 %copy-start.13 = (f32[10,64,128]{2,1,0:T(8,128)S(1)}, f32[10,64,128]{2,1,0:T(8,128)}, u32[]{:S(2)}) copy-start(f32[10,64,128]{2,1,0:T(8,128)} %get-tuple-element.118) | copy-start | bytes 983044
  92.0 21.6 %collective-permute-start.15 = (f32[10,64,128]{2,1,0:T(8,128)}, f32[10,64,128]{2,1,0:T(8,128)S(1)}, u32[]{:S(2)}, u32[]{:S(2)}) collective-permute-start(f32[10,64,128]{2,1,0:T(8,128)} %get-tuple-element.112), channel_id=1, source_target_pairs={{2,3},{6,7},{10,11},{14,15},{18,19},{22,23},{26,27},{30,31}} | collective-permute-start | bytes 983048 | tf_op jit(solution)/shard_map/ppermute | solution.py:447
  93.4 20.2 %collective-permute-start.14 = (f32[8,64,128]{2,1,0:T(8,128)S(1)}, f32[8,64,128]{2,1,0:T(8,128)S(1)}, u32[]{:S(2)}, u32[]{:S(2)}) collective-permute-start(f32[8,64,128]{2,1,0:T(8,128)S(1)} %copy-done.18), channel_id=1, source_target_pairs={{2,3},{6,7},{10,11},{14,15},{18,19},{22,23},{26,27},{30,31}} | collective-permute-start | bytes 786440 | tf_op jit(solution)/shard_map/ppermute | solution.py:447
  95.7 5.4 %collective-permute-start.16 = (f32[128]{0:T(128)S(1)}, f32[128]{0:T(128)S(1)}, u32[]{:S(2)}, u32[]{:S(2)}) collective-permute-start(f32[128]{0:T(128)S(1)} %reduce_sum.18), channel_id=1, source_target_pairs={{0,3},{1,0},{2,1},{3,2},{4,7},{5,4},{6,5},{7,6},{8,11},{9,8},{10,9... | collective-permute-start | bytes 1544 | tf_op jit(solution)/shard_map/ppermute | solution.py:588
  98.4 4.4 %collective-permute-start.17 = (f32[128]{0:T(128)S(1)}, f32[128]{0:T(128)S(1)}, u32[]{:S(2)}, u32[]{:S(2)}) collective-permute-start(f32[128]{0:T(128)S(1)} %reduce_sum.18), channel_id=1, source_target_pairs={{0,2},{1,3},{2,0},{3,1},{4,6},{5,7},{6,4},{7,5},{8,10},{9,11},{10,... | collective-permute-start | bytes 1544 | tf_op jit(solution)/shard_map/ppermute | solution.py:588
  101.1 8.4 %collective-permute-start.18 = (f32[128]{0:T(128)S(1)}, f32[128]{0:T(128)S(1)}, u32[]{:S(2)}, u32[]{:S(2)}) collective-permute-start(f32[128]{0:T(128)S(1)} %reduce_sum.18), channel_id=1, source_target_pairs={{0,1},{1,2},{2,3},{3,0},{4,5},{5,6},{6,7},{7,4},{8,9},{9,10},{10,1... | collective-permute-start | bytes 1544 | tf_op jit(solution)/shard_map/ppermute | solution.py:588
  109.5 3.6 %collective-permute-start.19 = (f32[128]{0:T(128)S(1)}, f32[128]{0:T(128)S(1)}, u32[]{:S(2)}, u32[]{:S(2)}) collective-permute-start(f32[128]{0:T(128)S(1)} %dynamic-slice_reduce_fusion), channel_id=1, source_target_pairs={{0,16},{16,0},{1,17},{17,1},{2,18},{18,2},{3,19},{19,3},{4,20},{20... | collective-permute-start | bytes 1544 | tf_op jit(solution)/shard_map/ppermute | solution.py:594
  (7 other events, 5.8 us)

commit v6 on v5

--- a/solution.py
+++ b/solution.py
@@ -45,7 +45,9 @@
     return [range(i, min(i + BATCH, high)) for i in range(low, high, BATCH)]
 
 
-def side_kernel(azimuth, cot_ref, den_ref, collide_ref, speed_ref, regime_ref, sides_ref, gate_ref, slope_ref):
+def opening_kernel(azimuth, radial, first_rows, *refs):
+    cot_ref, den_ref, in_ref, out_ref, spread_ref, collide_ref, speed_ref, regime_ref = refs[:8]
+    sides_ref, gate_ref, slope_ref, opening_ref, shares_ref, first_ref, last_ref, late_ref = refs[8:]
     sigma = jax.nn.sigmoid((collide_ref[...] - speed_ref[...]) / gate_width)
     flagged = regime_ref[...].astype(jnp.float32)
     gate = flagged * sigma
@@ -58,11 +60,7 @@
         sides_ref[target, :] = cot_ref[source, :]
         sides_ref[pl.ds(4 * RANGE + k, RANGE, stride=4), :] = den_ref[source, :]
         sides_ref[8 * RANGE + k : 8 * RANGE + k + 1, :] = gate[row : row + 1]
-    sides_ref[8 * RANGE + 4 :, :] = jnp.zeros((4, sides_ref.shape[1]), jnp.float32)
-
-
-def opening_kernel(azimuth, radial, first_rows, *refs):
-    cot_ref, den_ref, in_ref, out_ref, spread_ref, opening_ref, shares_ref, first_ref, last_ref, late_ref = refs
+    sides_ref[8 * RANGE + 4 :, :] = jnp.zeros((4, radial), jnp.float32)
 
     block, blocks = lax.axis_index("row"), lax.axis_size("row")
 
@@ -266,7 +264,8 @@
     for g, (low, high) in enumerate(zip(cuts, cuts[1:])):
         for rows in batches(low, high):
             for a, moved in zip(rows, move([a + 2 for a in rows])):
-                moved_refs[g][a - low] = widened(slope_ref, slice(None), a) * moved
+                h, start = (g, max(low - 1, 0)) if a < high - 1 or high == azimuth else (g + 1, high - 1)
+                moved_refs[h][a - start] = widened(slope_ref, slice(None), a) * moved
 
     for g, (low, high) in enumerate(zip(cuts, cuts[1:])):
         for a in range(low, high):
@@ -300,7 +299,7 @@
     center_ref, lower_ref, upper_ref, side_ref = take(4)
     gate_ref, second_ref, moved_ref = take(3)
     table1_ref, table2_ref = take(2)
-    carry_second, carry_first, carry_sum, moved_before = (None, None, None, None) if first else take(4)
+    carry_second, carry_first, carry_sum = (None, None, None) if first else take(3)
     own_out, next_out, sum_out = take(3)
     keep_second, keep_first = (None, None) if last else take(2)
     second, initial = refs
@@ -374,11 +373,12 @@
             part = result[k * wide : (k + 1) * wide]
             frag = part[:, LANES:]
             initial[row - first_base, outer, :] = part[:, :LANES] + widened(gate_ref, outer, row) * frag
-            if own_low <= row < own_high:
-                total += moved_ref[row - own_low] * frag[8 : 8 + radial]
-            elif 2 <= row < own_low:
-                total += moved_before[0] * frag[8 : 8 + radial]
-    sum_out[...] = total
+            if 2 <= row < azimuth + 2:
+                total += moved_ref[row - max(first_low, 2)] * frag[8 : 8 + radial]
+    if last:
+        sum_out[...] = jnp.broadcast_to(jnp.sum(total.T, axis=0, keepdims=True), sum_out.shape)
+    else:
+        sum_out[...] = total
 
     for row in range(out_low, out_high):
         result = stencil(
@@ -431,7 +431,7 @@
     own_bins, azimuth, radial = density.shape
     place = lax.axis_index("mass")
     phis, rows = lax.axis_size("phi"), lax.axis_size("row")
-    cuts = [0, azimuth // 2, 3 * azimuth // 4, azimuth]
+    cuts = [0, 5 * azimuth // 8, azimuth]
     spans = list(zip(cuts, cuts[1:]))
 
     def far(x):
@@ -453,24 +453,12 @@
     def flat(x):
         return x.reshape(-1, LANES)
 
-    sides, gate, slope = call(
-        functools.partial(side_kernel, azimuth),
-        [(8 * own_bins + 8, LANES), (azimuth, radial), (radial, LANES)],
-        [],
-        [flat(cotangent), flat(density), collide_speed, frag_speed[None, :], regime],
-        2,
-    )
-    ring = [(i, (i + 1) % phis) for i in range(phis)]
-    other = lax.ppermute(sides, "phi", ring)
-    if phis > 2:
-        after = lax.ppermute(sides, "phi", [(j, i) for i, j in ring])
-        from_last = lax.broadcasted_iota(jnp.int32, other.shape, 0) % 4 < 2
-        other = jnp.where(from_last, other, after)
-
-    spread_row, gate = lax.optimization_barrier((spread[None, :], gate))
-    opening, shares, first_cells, last_cells, late = call(
+    sides, gate, slope, opening, shares, first_cells, last_cells, late = call(
         functools.partial(opening_kernel, azimuth, radial, cuts[1]),
         [
+            (8 * own_bins + 8, LANES),
+            (azimuth, radial),
+            (radial, LANES),
             (cuts[1] * own_bins + share_rows, LANES),
             (share_rows, LANES),
             (azimuth, 2, LANES),
@@ -478,9 +466,23 @@
             (own_bins * (azimuth - cuts[1]), radial),
         ],
         [],
-        [flat(cotangent), flat(density), drift_in, drift_out, spread_row],
-        5,
-    )
+        [
+            flat(cotangent),
+            flat(density),
+            drift_in,
+            drift_out,
+            spread[None, :],
+            collide_speed,
+            frag_speed[None, :],
+            regime,
+        ],
+    )
+    ring = [(i, (i + 1) % phis) for i in range(phis)]
+    other = lax.ppermute(sides, "phi", ring)
+    if phis > 2:
+        after = lax.ppermute(sides, "phi", [(j, i) for i, j in ring])
+        from_last = lax.broadcasted_iota(jnp.int32, other.shape, 0) % 4 < 2
+        other = jnp.where(from_last, other, after)
 
     density_next = ending(density)
     far_first, near_first = far(opening), near(opening)
@@ -522,17 +524,19 @@
 
     long_next = ending(long)
     first_next = jnp.concatenate([opening[: own_bins * cuts[1]], other[: 4 * own_bins]], axis=0)
-    short, first_next, late, far_first, near_first, both = lax.optimization_barrier(
-        (short, first_next, late, far_first, near_first, both)
-    )
     halo_refs = [far(short), near(short), short, long_next]
+    first_next, late, far_first, near_first, both = lax.optimization_barrier(
+        (first_next, late, far_first, near_first, both)
+    )
     first_next = ending(first_next)
     far_late, near_late = far(late), near(late)
 
     coefs = [(2, length, LANES)] * 3 + [(2, LANES)]
     products = list(call(
         functools.partial(forward_kernel, azimuth, radial, cuts),
-        [(j - i, radial, LANES) for i, j in spans] + [(j - i, 2, radial, LANES) for i, j in spans] + coefs,
+        [(j - (j < azimuth) - max(i - 1, 0), radial, LANES) for i, j in spans]
+        + [(j - i, 2, radial, LANES) for i, j in spans]
+        + coefs,
         [(count, length, LANES), (count, 2, length, LANES)],
         [
             flat(density),
@@ -567,9 +571,7 @@
         operands += halo_refs + ([first_next] if first or last else [])
         operands += [*coefs, gates, second[g], moved[g]]
         operands += [both, own_cols, *carry]
-        if not first:
-            operands.append(moved[g - 1][-1:])
-        outs = [(n_out, RANGE, radial), (n_out, RANGE, radial), (radial, LANES)]
+        outs = [(n_out, RANGE, radial), (n_out, RANGE, radial), (8, radial) if last else (radial, LANES)]
         if not last:
             outs += [(2, 2, length, LANES), (2, length, LANES)]
         own_out, next_out, total, *kept = call(
@@ -582,7 +584,7 @@
         carry = [*kept, total]
         own_outs.append(own_out)
         next_outs.append(returning(next_out))
-    speed_gradient = jnp.sum(total, axis=1)
+    speed_gradient = total[0]
     size = lax.axis_size("mass")
     shares = [
         lax.ppermute(speed_gradient, "mass", [(i, (i + k) % size) for i in range(size)]) for k in range(1, size)

time: 116 us -> 130 us (1.12)
  waiting for transfers between devices: 21.2 us -> 39.2 us
  Pallas kernels: 47 us -> 40.7 us
  starting transfers between devices: 34.7 us -> 39.7 us
  local copies, waits for them, and re-layouts: 9.84 us -> 7.61 us
    ppermute x4, waiting for transfers between devices: 0.01 us -> 22.1 us  [ending(): return lax.ppermute(x, 'mass', [(3, 2)])]
    pallas_call x8 -> x6, Pallas kernels: 42.7 us -> 36.4 us  [call(): pl.pallas_call(kernel, out_shape=[jax.ShapeDtypeStruct(o, jnp.float32) fo...]
    ppermute x4, starting transfers between devices: 18 us -> 22.1 us  [ending(): return lax.ppermute(x, 'mass', [(3, 2)])]
    ppermute x3, starting transfers between devices: 2.76 us -> 5.07 us  [per_device(): lax.ppermute(speed_gradient, 'mass', [(i, (i + k) % size) for i in range(...]
    slice x2 -> x1, local copies, waits for them, and re-layouts: 2.94 us -> 0.68 us  [per_device(): speed_gradient = total[0]]
    ppermute x3, waiting for transfers between devices: 11 us -> 9.04 us  [per_device(): lax.ppermute(speed_gradient, 'mass', [(i, (i + k) % size) for i in range(...]
    ppermute x3 -> x2, starting transfers between devices: 4 us -> 2.7 us  [returning(): return lax.ppermute(x, 'mass', [(2, 3)])]
    unnamed x39 -> x33, local copies, waits for them, and re-layouts: 4.88 us -> 4.87 us
  transfers between devices with their start and end apart: 20 -> 19, of which waited for: 6 -> 8; matrix products, arithmetic and copies ran while one was open for 6% -> 3% of each run, Pallas kernels for 41% -> 32%
where the time goes in v6:
time: 130 us; the launch traced here: 129 us
  Pallas kernels  40.7 us (31%)
  starting transfers between devices  39.7 us (31%)
  waiting for transfers between devices  39.2 us (30%)
  local copies, waits for them, and re-layouts  7.61 us (6%)
    pallas_call x6, Pallas kernels, call(): pl.pallas_call(kernel, out_shape=[jax.ShapeDtypeStruct(o, jnp.float32) fo...  36.4 us
    ppermute x4, starting transfers between devices, ending(): return lax.ppermute(x, 'mass', [(3, 2)])  22.1 us
    ppermute x4, waiting for transfers between devices, ending(): return lax.ppermute(x, 'mass', [(3, 2)])  22.1 us
    ppermute x3, waiting for transfers between devices, per_device(): lax.ppermute(speed_gradient, 'mass', [(i, (i + k) % size) for i in range(...  9.04 us
    ppermute x1, waiting for transfers between devices, per_device(): other = lax.ppermute(sides, 'phi', ring)  5.43 us
    ppermute x3, starting transfers between devices, per_device(): lax.ppermute(speed_gradient, 'mass', [(i, (i + k) % size) for i in range(...  5.07 us
    unnamed x33, local copies, waits for them, and re-layouts  4.87 us
    pallas_call x1, Pallas kernels, per_device(): pl.pallas_call(table_kernel, out_shape=[jax.ShapeDtypeStruct((3 * total_b...  4.22 us
  transfers between devices with their start and end apart: 19, of which 8 were waited for; matrix products, arithmetic and copies ran while one was open for 3% of the time, Pallas kernels for 32%

profile of v6, /device:TPU:24, one launch (start us, length us, event | category | flops | bytes accessed | tf_op | source)
XLA Modules:
  0.0 129.0 jit_solution(12190467531627254214)
XLA Ops:
  0.6 2.4 %collective-permute-start.5 = (f32[64,32,128]{2,1,0:T(8,128)}, f32[64,32,128]{2,1,0:T(8,128)S(1)}, u32[]{:S(2)}, u32[]{:S(2)}) collective-permute-start(f32[64,32,128]{2,1,0:T(8,128)} %param.14), channel_id=1, source_target_pairs={{3,2},{7,6},{11,10},{15,14},{19,18},{23,22},{27,26},{31,30}} | collective-permute-start | bytes 3145736 | tf_op jit(solution)/shard_map/ppermute | solution.py:444
  3.1 4.8 %shard_map.149 = (f32[520,128]{1,0:T(8,128)}, f32[32,128]{1,0:T(8,128)}, f32[128,128]{1,0:T(8,128)}, f32[1448,128]{1,0:T(8,128)}, f32[168,128]{1,0:T(8,128)}, /*...) custom-call(f32[2048,128]{1,0:T(8,128)} %bitcast.20, f32[2048,128]{1,0:T(8,128)} %bitcast.18, ...), custom_call_target="tpu_custom_call" | custom-call | bytes 3000000 | tf_op jit(solution)/shard_map/pallas_call | solution.py:404
  7.9 0.7 collective-permute-start.1
  8.6 0.7 collective-permute-start.2
  9.3 1.6 %collective-permute-start = (f32[520,128]{1,0:T(8,128)}, f32[520,128]{1,0:T(8,128)S(1)}, u32[]{:S(2)}, u32[]{:S(2)}) collective-permute-start(f32[520,128]{1,0:T(8,128)} %get-tuple-element.51), channel_id=1, source_target_pairs={{0,16},{16,0},{1,17},{17,1},{2,18},{18,2},{3,19},{19,3},{4,20},{20... | collective-permute-start | bytes 798728 | tf_op jit(solution)/shard_map/ppermute | solution.py:481
  10.8 1.1 slice.9
  12.0 5.4 %collective-permute-done.sides_ref = f32[520,128]{1,0:T(8,128)S(1)} collective-permute-done((f32[520,128]{1,0:T(8,128)}, f32[520,128]{1,0:T(8,128)S(1)}, u32[]{:S(2)}, u32[]{:S(2)}) %collective-permute-start) | collective-permute-done | bytes 266272 | tf_op jit(solution)/shard_map/ppermute | solution.py:481
  18.1 1.8 %shard_map.150 = (f32[80,128]{1,0:T(8,128)}, f32[80,128]{1,0:T(8,128)}, f32[128,128]{1,0:T(8,128)}) custom-call(f32[520,128]{1,0:T(8,128)} %copy-done.4, f32[64,128]{1,0:T(8,128)} %bitcast.22, f32[64,128]{1,0:T(8,128)} %bitcast.23, f32[32,128]{1,0:T(8,128)} %get-tuple-element.55.gate_ref), custom_call_target="tpu_custom_call" | custom-call | bytes 3000000 | tf_op jit(solution)/shard_map/pallas_call | solution.py:404
  19.9 1.3 collective-permute-start.3
  21.2 1.3 %collective-permute-start.4 = (f32[80,128]{1,0:T(8,128)}, f32[80,128]{1,0:T(8,128)S(1)}, u32[]{:S(2)}, u32[]{:S(2)}) collective-permute-start(f32[80,128]{1,0:T(8,128)} %get-tuple-element.57), channel_id=1, source_target_pairs={{4,0},{8,4},{12,8},{5,1},{9,5},{13,9},{6,2},{10,6},{14,10},{7,3},{... | collective-permute-start | bytes 122888 | tf_op jit(solution)/shard_map/ppermute | solution.py:497
  22.5 0.9 slice.12
  23.5 2.2 %collective-permute-done.5 = f32[64,32,128]{2,1,0:T(8,128)S(1)} collective-permute-done((f32[64,32,128]{2,1,0:T(8,128)}, f32[64,32,128]{2,1,0:T(8,128)S(1)}, u32[]{:S(2)}, u32[]{:S(2)}) %collective-permute-start.5) | collective-permute-done | bytes 1048608 | tf_op jit(solution)/shard_map/ppermute | solution.py:444
  26.9 1.9 %shard_map.151 = (f32[568,128]{1,0:T(8,128)}, f32[400,128]{1,0:T(8,128)}, f32[160,128]{1,0:T(8,128)}) custom-call(f32[80,128]{1,0:T(8,128)} %copy-done.14, f32[80,128]{1,0:T(8,128)} %copy-done.15, f32[520,128]{1,0:T(8,128)} %copy-done.4, f32[168,128]{1,0:T(8,128)} %get-tuple-element.58.shares_ref.refs_4_, f32[128,128]{1,0:T(8,128)} %get-tuple-element.60.gates_ref), custom_call_target="tpu_custom_call" | custom-call | bytes 3000000 | tf_op jit(solution)/shard_map/pallas_call | solution.py:404
  28.8 4.2 %shard_map.152 = (bf16[768,512]{1,0:T(8,128)(2,1)}, bf16[768,256]{1,0:T(8,128)(2,1)}, bf16[768,256]{1,0:T(8,128)(2,1)}) custom-call(f32[256,256]{1,0:T(8,128)} %gain_ref, s32[1,256]{1,0:T(1,128)} %bitcast.30, f32[1,256]{1,0:T(1,128)} %bitcast.31, f32[1,256]{1,0:T(1,128)} %bitcast.32, f32[1,256]{1,0:T(1,128)} %bitcast.33, s32[4,4]{1,0:T(4,128)} %pairs_ref.1), custom_call_target="tpu_custom_call" | custom-call | bytes 9000000 | tf_op jit(solution)/shard_map/pallas_call | solution.py:509
  33.0 13.3 %collective-permute-start.6 = (f32[1536,128]{1,0:T(8,128)S(1)}, f32[1536,128]{1,0:T(8,128)S(1)}, u32[]{:S(2)}, u32[]{:S(2)}) collective-permute-start(f32[1536,128]{1,0:T(8,128)S(1)} %pad_maximum_fusion), channel_id=1, source_target_pairs={{3,2},{7,6},{11,10},{15,14},{19,18},{23,22},{27,26},{31,30}} | collective-permute-start | bytes 2359304 | tf_op jit(solution)/shard_map/ppermute | solution.py:444
  46.3 1.3 %collective-permute-start.7 = (f32[568,128]{1,0:T(8,128)}, f32[568,128]{1,0:T(8,128)S(1)}, u32[]{:S(2)}, u32[]{:S(2)}) collective-permute-start(f32[568,128]{1,0:T(8,128)} %get-tuple-element.68.refs_5_), channel_id=1, source_target_pairs={{3,2},{7,6},{11,10},{15,14},{19,18},{23,22},{27,26},{31,30}} | collective-permute-start | bytes 872456 | tf_op jit(solution)/shard_map/ppermute | solution.py:444
  49.7 19.9 %collective-permute-done.7.refs_6_.refs_7_ = f32[568,128]{1,0:T(8,128)S(1)} collective-permute-done((f32[568,128]{1,0:T(8,128)}, f32[568,128]{1,0:T(8,128)S(1)}, u32[]{:S(2)}, u32[]{:S(2)}) %collective-permute-start.7) | collective-permute-done | bytes 290848 | tf_op jit(solution)/shard_map/ppermute | solution.py:444
  70.3 10.4 %shard_map.153 = (f32[19,128,128]{2,1,0:T(8,128)}, f32[13,128,128]{2,1,0:T(8,128)}, f32[20,2,128,128]{3,2,1,0:T(8,128)}, f32[12,2,128,128]{3,2,1,0:T(8,128)}, f3...) custom-call(f32[2048,128]{1,0:T(8,128)} %bitcast.19, ...), custom_call_target="tpu_custom_call" | custom-call | bytes 39000000 | tf_op jit(solution)/shard_map/pallas_call | solution.py:404
  80.8 5.1 %collective-permute-start.13 = (f32[768,128]{1,0:T(8,128)S(1)}, f32[768,128]{1,0:T(8,128)S(1)}, u32[]{:S(2)}, u32[]{:S(2)}) collective-permute-start(f32[768,128]{1,0:T(8,128)S(1)} %copy-done.10), channel_id=1, source_target_pairs={{3,2},{7,6},{11,10},{15,14},{19,18},{23,22},{27,26},{31,30}} | collective-permute-start | bytes 1179656 | tf_op jit(solution)/shard_map/ppermute | solution.py:444
  85.9 0.8 copy-done
  86.8 10.0 %shard_map.154 = (f32[18,64,128]{2,1,0:T(8,128)}, f32[18,64,128]{2,1,0:T(8,128)}, f32[128,128]{1,0:T(8,128)}, f32[2,2,160,128]{3,2,1,0:T(8,128)}, f32[2,160,128]{2,1,0:T(8,128)}) custom-call(f32[1448,128]{1,0:T(8,128)} %copy-done.1, f32[1448,128]{1,0:T(8,128)} %copy-done.2, f32[1448,128]{1,0:T(8,128)} %get-tuple-element.50.refs_2_, f32[1536,128]{1,0:T(8,128)} %copy-done, ...), custom_call_target="tpu_custom_call" | custom-call | bytes 39000000 | tf_op jit(solution)/shard_map/pallas_call | solution.py:404
  96.8 1.3 collective-permute-start.10
  98.1 0.7 copy-done.11
  99.2 7.5 %shard_map.155 = (f32[14,64,128]{2,1,0:T(8,128)}, f32[14,64,128]{2,1,0:T(8,128)}, f32[8,128]{1,0:T(8,128)}) custom-call(f32[768,128]{1,0:T(8,128)} %copy-done.11, f32[768,128]{1,0:T(8,128)} %copy-done.12, f32[768,128]{1,0:T(8,128)} %get-tuple-element.86.refs_2_, f32[768,128]{1,0:T(8,128)} %copy-done.13, f32[400,128]{1,0:T(8,128)} %copy-done.6, ...), custom_call_target="tpu_custom_call" | custom-call | bytes 27000000 | tf_op jit(solution)/shard_map/pallas_call | solution.py:404
  106.7 1.4 %collective-permute-start.14 = (f32[14,64,128]{2,1,0:T(8,128)}, f32[14,64,128]{2,1,0:T(8,128)S(1)}, u32[]{:S(2)}, u32[]{:S(2)}) collective-permute-start(f32[14,64,128]{2,1,0:T(8,128)} %get-tuple-element.92), channel_id=1, source_target_pairs={{2,3},{6,7},{10,11},{14,15},{18,19},{22,23},{26,27},{30,31}} | collective-permute-start | bytes 1376264 | tf_op jit(solution)/shard_map/ppermute | solution.py:447
  108.8 2.7 %collective-permute-start.15 = (f32[128]{0:T(128)S(1)}, f32[128]{0:T(128)S(1)}, u32[]{:S(2)}, u32[]{:S(2)}) collective-permute-start(f32[128]{0:T(128)S(1)} %get-tuple-element.101), channel_id=1, source_target_pairs={{0,3},{1,0},{2,1},{3,2},{4,7},{5,4},{6,5},{7,6},{8,11},{9,8},{10,9... | collective-permute-start | bytes 1544 | tf_op jit(solution)/shard_map/ppermute | solution.py:590
  111.5 2.4 %collective-permute-start.17 = (f32[128]{0:T(128)S(1)}, f32[128]{0:T(128)S(1)}, u32[]{:S(2)}, u32[]{:S(2)}) collective-permute-start(f32[128]{0:T(128)S(1)} %get-tuple-element.101), channel_id=1, source_target_pairs={{0,1},{1,2},{2,3},{3,0},{4,5},{5,6},{6,7},{7,4},{8,9},{9,10},{10,1... | collective-permute-start | bytes 1544 | tf_op jit(solution)/shard_map/ppermute | solution.py:590
  114.1 1.8 %collective-permute-done.16 = f32[128]{0:T(128)S(1)} collective-permute-done((f32[128]{0:T(128)S(1)}, f32[128]{0:T(128)S(1)}, u32[]{:S(2)}, u32[]{:S(2)}) %collective-permute-start.16) | collective-permute-done | bytes 544 | tf_op jit(solution)/shard_map/ppermute | solution.py:590
  116.0 7.0 %collective-permute-done.17 = f32[128]{0:T(128)S(1)} collective-permute-done((f32[128]{0:T(128)S(1)}, f32[128]{0:T(128)S(1)}, u32[]{:S(2)}, u32[]{:S(2)}) %collective-permute-start.17) | collective-permute-done | bytes 544 | tf_op jit(solution)/shard_map/ppermute | solution.py:590
  123.0 1.6 %collective-permute-start.18 = (f32[128]{0:T(128)S(1)}, f32[128]{0:T(128)S(1)}, u32[]{:S(2)}, u32[]{:S(2)}) collective-permute-start(f32[128]{0:T(128)S(1)} %dynamic-slice_reduce_fusion), channel_id=1, source_target_pairs={{0,16},{16,0},{1,17},{17,1},{2,18},{18,2},{3,19},{19,3},{4,20},{20... | collective-permute-start | bytes 1544 | tf_op jit(solution)/shard_map/ppermute | solution.py:596
  124.5 2.0 %collective-permute-done.18 = f32[128]{0:T(128)S(1)} collective-permute-done((f32[128]{0:T(128)S(1)}, f32[128]{0:T(128)S(1)}, u32[]{:S(2)}, u32[]{:S(2)}) %collective-permute-start.18) | collective-permute-done | bytes 544 | tf_op jit(solution)/shard_map/ppermute | solution.py:596
  127.4 1.6 %copy.16 = f32[64,32,128]{2,1,0:T(8,128)} copy(f32[64,32,128]{2,0,1:T(8,128)S(1)} %maximum_bitcast_fusion) | data formatting | bytes 2097152
  (56 shorter events, 6.8 us)
Async XLA Ops:
  0.6 25.1 %collective-permute-start.5 = (f32[64,32,128]{2,1,0:T(8,128)}, f32[64,32,128]{2,1,0:T(8,128)S(1)}, u32[]{:S(2)}, u32[]{:S(2)}) collective-permute-start(f32[64,32,128]{2,1,0:T(8,128)} %param.14), channel_id=1, source_target_pairs={{3,2},{7,6},{11,10},{15,14},{19,18},{23,22},{27,26},{31,30}} | collective-permute-start | bytes 3145736 | tf_op jit(solution)/shard_map/ppermute | solution.py:444
  7.9 25.2 %collective-permute-start.1 = (f32[1448,128]{1,0:T(8,128)}, f32[1448,128]{1,0:T(8,128)S(1)}, u32[]{:S(2)}, u32[]{:S(2)}) collective-permute-start(f32[1448,128]{1,0:T(8,128)} %get-tuple-element.50.refs_2_), channel_id=1, source_target_pairs={{0,2},{2,1},{1,0},{4,6},{6,5},{5,4},{8,10},{10,9},{9,8},{12,14},{1... | collective-permute-start | bytes 2224136 | tf_op jit(solution)/shard_map/ppermute | solution.py:438
  8.6 24.5 %collective-permute-start.2 = (f32[1448,128]{1,0:T(8,128)}, f32[1448,128]{1,0:T(8,128)S(1)}, u32[]{:S(2)}, u32[]{:S(2)}) collective-permute-start(f32[1448,128]{1,0:T(8,128)} %get-tuple-element.50.refs_2_), channel_id=1, source_target_pairs={{0,1},{1,2},{4,5},{5,6},{8,9},{9,10},{12,13},{13,14},{16,17},{17,1... | collective-permute-start | bytes 2224136 | tf_op jit(solution)/shard_map/ppermute | solution.py:441
  9.3 8.1 %collective-permute-start = (f32[520,128]{1,0:T(8,128)}, f32[520,128]{1,0:T(8,128)S(1)}, u32[]{:S(2)}, u32[]{:S(2)}) collective-permute-start(f32[520,128]{1,0:T(8,128)} %get-tuple-element.51), channel_id=1, source_target_pairs={{0,16},{16,0},{1,17},{17,1},{2,18},{18,2},{3,19},{19,3},{4,20},{20... | collective-permute-start | bytes 798728 | tf_op jit(solution)/shard_map/ppermute | solution.py:481
  12.0 37.0 %copy-start.10 = (f32[768,128]{1,0:T(8,128)S(1)}, f32[768,128]{1,0:T(8,128)}, u32[]{:S(2)}) copy-start(f32[768,128]{1,0:T(8,128)} %get-tuple-element.86.refs_2_) | copy-start | bytes 1179652
  19.9 5.8 %collective-permute-start.3 = (f32[80,128]{1,0:T(8,128)}, f32[80,128]{1,0:T(8,128)S(1)}, u32[]{:S(2)}, u32[]{:S(2)}) collective-permute-start(f32[80,128]{1,0:T(8,128)} %get-tuple-element.56), channel_id=1, source_target_pairs={{0,4},{4,8},{8,12},{1,5},{5,9},{9,13},{2,6},{6,10},{10,14},{3,7},{... | collective-permute-start | bytes 122888 | tf_op jit(solution)/shard_map/ppermute | solution.py:496
  21.2 5.1 %collective-permute-start.4 = (f32[80,128]{1,0:T(8,128)}, f32[80,128]{1,0:T(8,128)S(1)}, u32[]{:S(2)}, u32[]{:S(2)}) collective-permute-start(f32[80,128]{1,0:T(8,128)} %get-tuple-element.57), channel_id=1, source_target_pairs={{4,0},{8,4},{12,8},{5,1},{9,5},{13,9},{6,2},{10,6},{14,10},{7,3},{... | collective-permute-start | bytes 122888 | tf_op jit(solution)/shard_map/ppermute | solution.py:497
  25.7 44.6 %copy-start.5 = (f32[64,32,128]{2,1,0:T(8,128)}, f32[64,32,128]{2,1,0:T(8,128)S(1)}, u32[]{:S(2)}) copy-start(f32[64,32,128]{2,1,0:T(8,128)S(1)} %collective-permute-done.5) | copy-start | bytes 3145732
  33.0 37.3 %copy-start.1 = (f32[1448,128]{1,0:T(8,128)}, f32[1448,128]{1,0:T(8,128)S(1)}, u32[]{:S(2)}) copy-start(f32[1448,128]{1,0:T(8,128)S(1)} %collective-permute-done.1.refs_2_.refs_0_) | copy-start | bytes 2224132
  33.0 37.3 %copy-start.2 = (f32[1448,128]{1,0:T(8,128)}, f32[1448,128]{1,0:T(8,128)S(1)}, u32[]{:S(2)}) copy-start(f32[1448,128]{1,0:T(8,128)S(1)} %collective-permute-done.2.refs_3_.refs_1_) | copy-start | bytes 2224132
  33.0 52.9 %collective-permute-start.6 = (f32[1536,128]{1,0:T(8,128)S(1)}, f32[1536,128]{1,0:T(8,128)S(1)}, u32[]{:S(2)}, u32[]{:S(2)}) collective-permute-start(f32[1536,128]{1,0:T(8,128)S(1)} %pad_maximum_fusion), channel_id=1, source_target_pairs={{3,2},{7,6},{11,10},{15,14},{19,18},{23,22},{27,26},{31,30}} | collective-permute-start | bytes 2359304 | tf_op jit(solution)/shard_map/ppermute | solution.py:444
  46.3 23.3 %collective-permute-start.7 = (f32[568,128]{1,0:T(8,128)}, f32[568,128]{1,0:T(8,128)S(1)}, u32[]{:S(2)}, u32[]{:S(2)}) collective-permute-start(f32[568,128]{1,0:T(8,128)} %get-tuple-element.68.refs_5_), channel_id=1, source_target_pairs={{3,2},{7,6},{11,10},{15,14},{19,18},{23,22},{27,26},{31,30}} | collective-permute-start | bytes 872456 | tf_op jit(solution)/shard_map/ppermute | solution.py:444
  47.6 33.1 %collective-permute-start.8 = (f32[400,128]{1,0:T(8,128)}, f32[400,128]{1,0:T(8,128)S(1)}, u32[]{:S(2)}, u32[]{:S(2)}) collective-permute-start(f32[400,128]{1,0:T(8,128)} %get-tuple-element.73.refs_6_), channel_id=1, source_target_pairs={{0,2},{2,1},{1,0},{4,6},{6,5},{5,4},{8,10},{10,9},{9,8},{12,14},{1... | collective-permute-start | bytes 614408 | tf_op jit(solution)/shard_map/ppermute | solution.py:438
  48.3 32.5 %collective-permute-start.9 = (f32[400,128]{1,0:T(8,128)}, f32[400,128]{1,0:T(8,128)S(1)}, u32[]{:S(2)}, u32[]{:S(2)}) collective-permute-start(f32[400,128]{1,0:T(8,128)} %get-tuple-element.73.refs_6_), channel_id=1, source_target_pairs={{0,1},{1,2},{4,5},{5,6},{8,9},{9,10},{12,13},{13,14},{16,17},{17,1... | collective-permute-start | bytes 614408 | tf_op jit(solution)/shard_map/ppermute | solution.py:441
  49.0 49.1 %collective-permute-start.11 = (f32[768,128]{1,0:T(8,128)S(1)}, f32[768,128]{1,0:T(8,128)S(1)}, u32[]{:S(2)}, u32[]{:S(2)}) collective-permute-start(f32[768,128]{1,0:T(8,128)S(1)} %copy-done.10), channel_id=1, source_target_pairs={{0,2},{2,1},{1,0},{4,6},{6,5},{5,4},{8,10},{10,9},{9,8},{12,14},{1... | collective-permute-start | bytes 1179656 | tf_op jit(solution)/shard_map/ppermute | solution.py:438
  69.6 0.7 copy-start.3
  69.6 28.5 %collective-permute-start.12 = (f32[768,128]{1,0:T(8,128)S(1)}, f32[768,128]{1,0:T(8,128)S(1)}, u32[]{:S(2)}, u32[]{:S(2)}) collective-permute-start(f32[768,128]{1,0:T(8,128)S(1)} %copy-done.10), channel_id=1, source_target_pairs={{0,1},{1,2},{4,5},{5,6},{8,9},{9,10},{12,13},{13,14},{16,17},{17,1... | collective-permute-start | bytes 1179656 | tf_op jit(solution)/shard_map/ppermute | solution.py:441
  80.8 5.2 %copy-start.6 = (f32[400,128]{1,0:T(8,128)}, f32[400,128]{1,0:T(8,128)S(1)}, u32[]{:S(2)}) copy-start(f32[400,128]{1,0:T(8,128)S(1)} %collective-permute-done.8.refs_4_) | copy-start | bytes 614404
  80.8 5.1 %copy-start.7 = (f32[400,128]{1,0:T(8,128)}, f32[400,128]{1,0:T(8,128)S(1)}, u32[]{:S(2)}) copy-start(f32[400,128]{1,0:T(8,128)S(1)} %collective-permute-done.9.refs_5_) | copy-start | bytes 614404
  80.8 17.3 %collective-permute-start.13 = (f32[768,128]{1,0:T(8,128)S(1)}, f32[768,128]{1,0:T(8,128)S(1)}, u32[]{:S(2)}, u32[]{:S(2)}) collective-permute-start(f32[768,128]{1,0:T(8,128)S(1)} %copy-done.10), channel_id=1, source_target_pairs={{3,2},{7,6},{11,10},{15,14},{19,18},{23,22},{27,26},{31,30}} | collective-permute-start | bytes 1179656 | tf_op jit(solution)/shard_map/ppermute | solution.py:444
  85.9 0.9 copy-start
  96.8 30.3 %collective-permute-start.10 = (f32[18,64,128]{2,1,0:T(8,128)}, f32[18,64,128]{2,1,0:T(8,128)S(1)}, u32[]{:S(2)}, u32[]{:S(2)}) collective-permute-start(f32[18,64,128]{2,1,0:T(8,128)} %get-tuple-element.85), channel_id=1, source_target_pairs={{2,3},{6,7},{10,11},{14,15},{18,19},{22,23},{26,27},{30,31}} | collective-permute-start | bytes 1769480 | tf_op jit(solution)/shard_map/ppermute | solution.py:447
  98.1 0.7 copy-start.11
  98.1 0.9 copy-start.12
  98.1 1.1 copy-start.13
  99.2 27.9 %copy-start.8 = (f32[18,64,128]{2,1,0:T(8,128)S(1)}, f32[18,64,128]{2,1,0:T(8,128)}, u32[]{:S(2)}) copy-start(f32[18,64,128]{2,1,0:T(8,128)} %get-tuple-element.94) | copy-start | bytes 1769476
  106.7 20.5 %copy-start.9 = (f32[14,64,128]{2,1,0:T(8,128)S(1)}, f32[14,64,128]{2,1,0:T(8,128)}, u32[]{:S(2)}) copy-start(f32[14,64,128]{2,1,0:T(8,128)} %get-tuple-element.96) | copy-start | bytes 1376260
  106.7 20.4 %collective-permute-start.14 = (f32[14,64,128]{2,1,0:T(8,128)}, f32[14,64,128]{2,1,0:T(8,128)S(1)}, u32[]{:S(2)}, u32[]{:S(2)}) collective-permute-start(f32[14,64,128]{2,1,0:T(8,128)} %get-tuple-element.92), channel_id=1, source_target_pairs={{2,3},{6,7},{10,11},{14,15},{18,19},{22,23},{26,27},{30,31}} | collective-permute-start | bytes 1376264 | tf_op jit(solution)/shard_map/ppermute | solution.py:447
  108.8 5.3 %collective-permute-start.15 = (f32[128]{0:T(128)S(1)}, f32[128]{0:T(128)S(1)}, u32[]{:S(2)}, u32[]{:S(2)}) collective-permute-start(f32[128]{0:T(128)S(1)} %get-tuple-element.101), channel_id=1, source_target_pairs={{0,3},{1,0},{2,1},{3,2},{4,7},{5,4},{6,5},{7,6},{8,11},{9,8},{10,9... | collective-permute-start | bytes 1544 | tf_op jit(solution)/shard_map/ppermute | solution.py:590
  111.5 4.4 %collective-permute-start.16 = (f32[128]{0:T(128)S(1)}, f32[128]{0:T(128)S(1)}, u32[]{:S(2)}, u32[]{:S(2)}) collective-permute-start(f32[128]{0:T(128)S(1)} %get-tuple-element.101), channel_id=1, source_target_pairs={{0,2},{1,3},{2,0},{3,1},{4,6},{5,7},{6,4},{7,5},{8,10},{9,11},{10,... | collective-permute-start | bytes 1544 | tf_op jit(solution)/shard_map/ppermute | solution.py:590
  111.5 11.4 %collective-permute-start.17 = (f32[128]{0:T(128)S(1)}, f32[128]{0:T(128)S(1)}, u32[]{:S(2)}, u32[]{:S(2)}) collective-permute-start(f32[128]{0:T(128)S(1)} %get-tuple-element.101), channel_id=1, source_target_pairs={{0,1},{1,2},{2,3},{3,0},{4,5},{5,6},{6,7},{7,4},{8,9},{9,10},{10,1... | collective-permute-start | bytes 1544 | tf_op jit(solution)/shard_map/ppermute | solution.py:590
  123.0 3.6 %collective-permute-start.18 = (f32[128]{0:T(128)S(1)}, f32[128]{0:T(128)S(1)}, u32[]{:S(2)}, u32[]{:S(2)}) collective-permute-start(f32[128]{0:T(128)S(1)} %dynamic-slice_reduce_fusion), channel_id=1, source_target_pairs={{0,16},{16,0},{1,17},{17,1},{2,18},{18,2},{3,19},{19,3},{4,20},{20... | collective-permute-start | bytes 1544 | tf_op jit(solution)/shard_map/ppermute | solution.py:596
  (3 other events, 2.0 us)

commit v7 on v6

--- a/solution.py
+++ b/solution.py
@@ -524,10 +524,10 @@
 
     long_next = ending(long)
     first_next = jnp.concatenate([opening[: own_bins * cuts[1]], other[: 4 * own_bins]], axis=0)
+    short, first_next, late, far_first, near_first, long_next, both = lax.optimization_barrier(
+        (short, first_next, late, far_first, near_first, long_next, both)
+    )
     halo_refs = [far(short), near(short), short, long_next]
-    first_next, late, far_first, near_first, both = lax.optimization_barrier(
-        (first_next, late, far_first, near_first, both)
-    )
     first_next = ending(first_next)
     far_late, near_late = far(late), near(late)
 

time: 130 us -> 111 us (0.85)
  waiting for transfers between devices: 39.2 us -> 22.1 us
    ppermute x4, waiting for transfers between devices: 22.1 us -> 3.38 us  [ending(): return lax.ppermute(x, 'mass', [(3, 2)])]
    unnamed x33 -> x35, local copies, waits for them, and re-layouts: 4.87 us -> 4.87 us
  transfers between devices with their start and end apart: 19 -> 19, of which waited for: 8 -> 8; matrix products, arithmetic and copies ran while one was open for 3% -> 2% of each run, Pallas kernels for 32% -> 37%
where the time goes in v7:
time: 111 us
  Pallas kernels  40.7 us (37%)
  starting transfers between devices  39.5 us (36%)
  waiting for transfers between devices  22.1 us (20%)
  local copies, waits for them, and re-layouts  6.72 us (6%)
    pallas_call x6, Pallas kernels, call(): pl.pallas_call(kernel, out_shape=[jax.ShapeDtypeStruct(o, jnp.float32) fo...  36.5 us
    ppermute x4, starting transfers between devices, ending(): return lax.ppermute(x, 'mass', [(3, 2)])  21.8 us
    ppermute x3, waiting for transfers between devices, per_device(): lax.ppermute(speed_gradient, 'mass', [(i, (i + k) % size) for i in range(...  9.3 us
    ppermute x1, waiting for transfers between devices, per_device(): other = lax.ppermute(sides, 'phi', ring)  6.57 us
    ppermute x3, starting transfers between devices, per_device(): lax.ppermute(speed_gradient, 'mass', [(i, (i + k) % size) for i in range(...  5.07 us
    unnamed x35, local copies, waits for them, and re-layouts  4.87 us
    pallas_call x1, Pallas kernels, per_device(): pl.pallas_call(table_kernel, out_shape=[jax.ShapeDtypeStruct((3 * total_b...  4.23 us
    ppermute x4, waiting for transfers between devices, ending(): return lax.ppermute(x, 'mass', [(3, 2)])  3.38 us
  transfers between devices with their start and end apart: 19, of which 8 were waited for; matrix products, arithmetic and copies ran while one was open for 2% of the time, Pallas kernels for 37%

profile of v7, /device:TPU:24, one launch (start us, length us, event | category | flops | bytes accessed | tf_op | source)
XLA Modules:
  0.0 110.8 jit_solution(126836151311234523)
XLA Ops:
  0.6 2.4 %collective-permute-start.3 = (f32[64,32,128]{2,1,0:T(8,128)}, f32[64,32,128]{2,1,0:T(8,128)S(1)}, u32[]{:S(2)}, u32[]{:S(2)}) collective-permute-start(f32[64,32,128]{2,1,0:T(8,128)} %param.14), channel_id=1, source_target_pairs={{3,2},{7,6},{11,10},{15,14},{19,18},{23,22},{27,26},{31,30}} | collective-permute-start | bytes 3145736 | tf_op jit(solution)/shard_map/ppermute | solution.py:444
  3.1 4.8 %shard_map.149 = (f32[520,128]{1,0:T(8,128)}, f32[32,128]{1,0:T(8,128)}, f32[128,128]{1,0:T(8,128)}, f32[1448,128]{1,0:T(8,128)}, f32[168,128]{1,0:T(8,128)}, /*...) custom-call(f32[2048,128]{1,0:T(8,128)} %bitcast.20, f32[2048,128]{1,0:T(8,128)} %bitcast.18, ...), custom_call_target="tpu_custom_call" | custom-call | bytes 3000000 | tf_op jit(solution)/shard_map/pallas_call | solution.py:404
  7.9 0.7 collective-permute-start.4
  8.6 0.7 collective-permute-start.5
  9.3 1.6 %collective-permute-start = (f32[520,128]{1,0:T(8,128)}, f32[520,128]{1,0:T(8,128)S(1)}, u32[]{:S(2)}, u32[]{:S(2)}) collective-permute-start(f32[520,128]{1,0:T(8,128)} %get-tuple-element.52), channel_id=1, source_target_pairs={{0,16},{16,0},{1,17},{17,1},{2,18},{18,2},{3,19},{19,3},{4,20},{20... | collective-permute-start | bytes 798728 | tf_op jit(solution)/shard_map/ppermute | solution.py:481
  10.8 6.6 %collective-permute-done.sides_ref = f32[520,128]{1,0:T(8,128)S(1)} collective-permute-done((f32[520,128]{1,0:T(8,128)}, f32[520,128]{1,0:T(8,128)S(1)}, u32[]{:S(2)}, u32[]{:S(2)}) %collective-permute-start) | collective-permute-done | bytes 266272 | tf_op jit(solution)/shard_map/ppermute | solution.py:481
  17.4 0.7 copy-done.4
  18.1 1.8 %shard_map.150 = (f32[80,128]{1,0:T(8,128)}, f32[80,128]{1,0:T(8,128)}, f32[128,128]{1,0:T(8,128)}) custom-call(f32[520,128]{1,0:T(8,128)} %copy-done.4, f32[64,128]{1,0:T(8,128)} %bitcast.22, f32[64,128]{1,0:T(8,128)} %bitcast.23, f32[32,128]{1,0:T(8,128)} %get-tuple-element.55.gate_ref), custom_call_target="tpu_custom_call" | custom-call | bytes 3000000 | tf_op jit(solution)/shard_map/pallas_call | solution.py:404
  20.0 1.4 %collective-permute-start.1 = (f32[80,128]{1,0:T(8,128)}, f32[80,128]{1,0:T(8,128)S(1)}, u32[]{:S(2)}, u32[]{:S(2)}) collective-permute-start(f32[80,128]{1,0:T(8,128)} %get-tuple-element.56), channel_id=1, source_target_pairs={{0,4},{4,8},{8,12},{1,5},{5,9},{9,13},{2,6},{6,10},{10,14},{3,7},{... | collective-permute-start | bytes 122888 | tf_op jit(solution)/shard_map/ppermute | solution.py:496
  21.4 1.3 %collective-permute-start.2 = (f32[80,128]{1,0:T(8,128)}, f32[80,128]{1,0:T(8,128)S(1)}, u32[]{:S(2)}, u32[]{:S(2)}) collective-permute-start(f32[80,128]{1,0:T(8,128)} %get-tuple-element.57), channel_id=1, source_target_pairs={{4,0},{8,4},{12,8},{5,1},{9,5},{13,9},{6,2},{10,6},{14,10},{7,3},{... | collective-permute-start | bytes 122888 | tf_op jit(solution)/shard_map/ppermute | solution.py:497
  22.7 3.0 %collective-permute-done.3 = f32[64,32,128]{2,1,0:T(8,128)S(1)} collective-permute-done((f32[64,32,128]{2,1,0:T(8,128)}, f32[64,32,128]{2,1,0:T(8,128)S(1)}, u32[]{:S(2)}, u32[]{:S(2)}) %collective-permute-start.3) | collective-permute-done | bytes 1048608 | tf_op jit(solution)/shard_map/ppermute | solution.py:444
  25.7 0.7 collective-permute-done.2.right_ref
  27.1 1.9 %shard_map.151 = (f32[568,128]{1,0:T(8,128)}, f32[400,128]{1,0:T(8,128)}, f32[160,128]{1,0:T(8,128)}) custom-call(f32[80,128]{1,0:T(8,128)} %copy-done.15, f32[80,128]{1,0:T(8,128)} %copy-done.16, f32[520,128]{1,0:T(8,128)} %copy-done.4, f32[168,128]{1,0:T(8,128)} %get-tuple-element.58.shares_ref.refs_4_, f32[128,128]{1,0:T(8,128)} %get-tuple-element.60.gates_ref), custom_call_target="tpu_custom_call" | custom-call | bytes 3000000 | tf_op jit(solution)/shard_map/pallas_call | solution.py:404
  29.0 3.8 %collective-permute-start.6 = (f32[568,128]{1,0:T(8,128)}, f32[568,128]{1,0:T(8,128)S(1)}, u32[]{:S(2)}, u32[]{:S(2)}) collective-permute-start(f32[568,128]{1,0:T(8,128)} %get-tuple-element.65.refs_5_), channel_id=1, source_target_pairs={{3,2},{7,6},{11,10},{15,14},{19,18},{23,22},{27,26},{31,30}} | collective-permute-start | bytes 872456 | tf_op jit(solution)/shard_map/ppermute | solution.py:444
  32.7 1.1 %slice.9 = f32[1280,128]{1,0:T(8,128)S(1)} slice(f32[1448,128]{1,0:T(8,128)} %get-tuple-element.62.refs_2_), slice={[0:1280], [0:128]} | slice | bytes 1310720 | tf_op jit(solution)/shard_map/slice | solution.py:526
  33.9 4.2 %shard_map.152 = (bf16[768,512]{1,0:T(8,128)(2,1)}, bf16[768,256]{1,0:T(8,128)(2,1)}, bf16[768,256]{1,0:T(8,128)(2,1)}) custom-call(f32[256,256]{1,0:T(8,128)} %gain_ref, s32[1,256]{1,0:T(1,128)} %bitcast.30, f32[1,256]{1,0:T(1,128)} %bitcast.31, f32[1,256]{1,0:T(1,128)} %bitcast.32, f32[1,256]{1,0:T(1,128)} %bitcast.33, s32[4,4]{1,0:T(4,128)} %pairs_ref.1), custom_call_target="tpu_custom_call" | custom-call | bytes 9000000 | tf_op jit(solution)/shard_map/pallas_call | solution.py:509
  38.5 7.8 %collective-permute-start.7 = (f32[1536,128]{1,0:T(8,128)S(1)}, f32[1536,128]{1,0:T(8,128)S(1)}, u32[]{:S(2)}, u32[]{:S(2)}) collective-permute-start(f32[1536,128]{1,0:T(8,128)S(1)} %pad_maximum_fusion), channel_id=1, source_target_pairs={{3,2},{7,6},{11,10},{15,14},{19,18},{23,22},{27,26},{31,30}} | collective-permute-start | bytes 2359304 | tf_op jit(solution)/shard_map/ppermute | solution.py:444
  49.1 10.5 %shard_map.153 = (f32[19,128,128]{2,1,0:T(8,128)}, f32[13,128,128]{2,1,0:T(8,128)}, f32[20,2,128,128]{3,2,1,0:T(8,128)}, f32[12,2,128,128]{3,2,1,0:T(8,128)}, f3...) custom-call(f32[2048,128]{1,0:T(8,128)} %bitcast.19, ...), custom_call_target="tpu_custom_call" | custom-call | bytes 39000000 | tf_op jit(solution)/shard_map/pallas_call | solution.py:404
  59.7 7.8 %collective-permute-start.13 = (f32[768,128]{1,0:T(8,128)S(1)}, f32[768,128]{1,0:T(8,128)S(1)}, u32[]{:S(2)}, u32[]{:S(2)}) collective-permute-start(f32[768,128]{1,0:T(8,128)S(1)} %copy-done.11), channel_id=1, source_target_pairs={{3,2},{7,6},{11,10},{15,14},{19,18},{23,22},{27,26},{31,30}} | collective-permute-start | bytes 1179656 | tf_op jit(solution)/shard_map/ppermute | solution.py:444
  67.5 0.8 copy-done
  68.4 10.0 %shard_map.154 = (f32[18,64,128]{2,1,0:T(8,128)}, f32[18,64,128]{2,1,0:T(8,128)}, f32[128,128]{1,0:T(8,128)}, f32[2,2,160,128]{3,2,1,0:T(8,128)}, f32[2,160,128]{2,1,0:T(8,128)}) custom-call(f32[1448,128]{1,0:T(8,128)} %copy-done.1, f32[1448,128]{1,0:T(8,128)} %copy-done.2, f32[1448,128]{1,0:T(8,128)} %get-tuple-element.62.refs_2_, f32[1536,128]{1,0:T(8,128)} %copy-done, ...), custom_call_target="tpu_custom_call" | custom-call | bytes 39000000 | tf_op jit(solution)/shard_map/pallas_call | solution.py:404
  78.4 1.3 %collective-permute-start.10 = (f32[18,64,128]{2,1,0:T(8,128)}, f32[18,64,128]{2,1,0:T(8,128)S(1)}, u32[]{:S(2)}, u32[]{:S(2)}) collective-permute-start(f32[18,64,128]{2,1,0:T(8,128)} %get-tuple-element.89), channel_id=1, source_target_pairs={{2,3},{6,7},{10,11},{14,15},{18,19},{22,23},{26,27},{30,31}} | collective-permute-start | bytes 1769480 | tf_op jit(solution)/shard_map/ppermute | solution.py:447
  79.7 0.7 copy-done.12
  80.8 7.5 %shard_map.155 = (f32[14,64,128]{2,1,0:T(8,128)}, f32[14,64,128]{2,1,0:T(8,128)}, f32[8,128]{1,0:T(8,128)}) custom-call(f32[768,128]{1,0:T(8,128)} %copy-done.12, f32[768,128]{1,0:T(8,128)} %copy-done.13, f32[768,128]{1,0:T(8,128)} %get-tuple-element.90.refs_2_, f32[768,128]{1,0:T(8,128)} %copy-done.14, f32[400,128]{1,0:T(8,128)} %copy-done.7, ...), custom_call_target="tpu_custom_call" | custom-call | bytes 27000000 | tf_op jit(solution)/shard_map/pallas_call | solution.py:404
  88.3 1.4 %collective-permute-start.14 = (f32[14,64,128]{2,1,0:T(8,128)}, f32[14,64,128]{2,1,0:T(8,128)S(1)}, u32[]{:S(2)}, u32[]{:S(2)}) collective-permute-start(f32[14,64,128]{2,1,0:T(8,128)} %get-tuple-element.96), channel_id=1, source_target_pairs={{2,3},{6,7},{10,11},{14,15},{18,19},{22,23},{26,27},{30,31}} | collective-permute-start | bytes 1376264 | tf_op jit(solution)/shard_map/ppermute | solution.py:447
  90.4 2.7 %collective-permute-start.15 = (f32[128]{0:T(128)S(1)}, f32[128]{0:T(128)S(1)}, u32[]{:S(2)}, u32[]{:S(2)}) collective-permute-start(f32[128]{0:T(128)S(1)} %get-tuple-element.105), channel_id=1, source_target_pairs={{0,3},{1,0},{2,1},{3,2},{4,7},{5,4},{6,5},{7,6},{8,11},{9,8},{10,9... | collective-permute-start | bytes 1544 | tf_op jit(solution)/shard_map/ppermute | solution.py:590
  93.1 2.4 %collective-permute-start.17 = (f32[128]{0:T(128)S(1)}, f32[128]{0:T(128)S(1)}, u32[]{:S(2)}, u32[]{:S(2)}) collective-permute-start(f32[128]{0:T(128)S(1)} %get-tuple-element.105), channel_id=1, source_target_pairs={{0,1},{1,2},{2,3},{3,0},{4,5},{5,6},{6,7},{7,4},{8,9},{9,10},{10,1... | collective-permute-start | bytes 1544 | tf_op jit(solution)/shard_map/ppermute | solution.py:590
  95.8 1.8 %collective-permute-done.16 = f32[128]{0:T(128)S(1)} collective-permute-done((f32[128]{0:T(128)S(1)}, f32[128]{0:T(128)S(1)}, u32[]{:S(2)}, u32[]{:S(2)}) %collective-permute-start.16) | collective-permute-done | bytes 544 | tf_op jit(solution)/shard_map/ppermute | solution.py:590
  97.6 7.2 %collective-permute-done.17 = f32[128]{0:T(128)S(1)} collective-permute-done((f32[128]{0:T(128)S(1)}, f32[128]{0:T(128)S(1)}, u32[]{:S(2)}, u32[]{:S(2)}) %collective-permute-start.17) | collective-permute-done | bytes 544 | tf_op jit(solution)/shard_map/ppermute | solution.py:590
  104.8 1.5 %collective-permute-start.18 = (f32[128]{0:T(128)S(1)}, f32[128]{0:T(128)S(1)}, u32[]{:S(2)}, u32[]{:S(2)}) collective-permute-start(f32[128]{0:T(128)S(1)} %dynamic-slice_reduce_fusion), channel_id=1, source_target_pairs={{0,16},{16,0},{1,17},{17,1},{2,18},{18,2},{3,19},{19,3},{4,20},{20... | collective-permute-start | bytes 1544 | tf_op jit(solution)/shard_map/ppermute | solution.py:596
  106.4 2.1 %collective-permute-done.18 = f32[128]{0:T(128)S(1)} collective-permute-done((f32[128]{0:T(128)S(1)}, f32[128]{0:T(128)S(1)}, u32[]{:S(2)}, u32[]{:S(2)}) %collective-permute-start.18) | collective-permute-done | bytes 544 | tf_op jit(solution)/shard_map/ppermute | solution.py:596
  109.2 1.6 %copy.16 = f32[64,32,128]{2,1,0:T(8,128)} copy(f32[64,32,128]{2,0,1:T(8,128)S(1)} %maximum_bitcast_fusion) | data formatting | bytes 2097152
  (59 shorter events, 5.9 us)
Async XLA Ops:
  0.6 25.1 %collective-permute-start.3 = (f32[64,32,128]{2,1,0:T(8,128)}, f32[64,32,128]{2,1,0:T(8,128)S(1)}, u32[]{:S(2)}, u32[]{:S(2)}) collective-permute-start(f32[64,32,128]{2,1,0:T(8,128)} %param.14), channel_id=1, source_target_pairs={{3,2},{7,6},{11,10},{15,14},{19,18},{23,22},{27,26},{31,30}} | collective-permute-start | bytes 3145736 | tf_op jit(solution)/shard_map/ppermute | solution.py:444
  7.9 30.3 %collective-permute-start.4 = (f32[1448,128]{1,0:T(8,128)}, f32[1448,128]{1,0:T(8,128)S(1)}, u32[]{:S(2)}, u32[]{:S(2)}) collective-permute-start(f32[1448,128]{1,0:T(8,128)} %get-tuple-element.62.refs_2_), channel_id=1, source_target_pairs={{0,2},{2,1},{1,0},{4,6},{6,5},{5,4},{8,10},{10,9},{9,8},{12,14},{1... | collective-permute-start | bytes 2224136 | tf_op jit(solution)/shard_map/ppermute | solution.py:438
  8.6 29.6 %collective-permute-start.5 = (f32[1448,128]{1,0:T(8,128)}, f32[1448,128]{1,0:T(8,128)S(1)}, u32[]{:S(2)}, u32[]{:S(2)}) collective-permute-start(f32[1448,128]{1,0:T(8,128)} %get-tuple-element.62.refs_2_), channel_id=1, source_target_pairs={{0,1},{1,2},{4,5},{5,6},{8,9},{9,10},{12,13},{13,14},{16,17},{17,1... | collective-permute-start | bytes 2224136 | tf_op jit(solution)/shard_map/ppermute | solution.py:441
  9.3 8.1 %collective-permute-start = (f32[520,128]{1,0:T(8,128)}, f32[520,128]{1,0:T(8,128)S(1)}, u32[]{:S(2)}, u32[]{:S(2)}) collective-permute-start(f32[520,128]{1,0:T(8,128)} %get-tuple-element.52), channel_id=1, source_target_pairs={{0,16},{16,0},{1,17},{17,1},{2,18},{18,2},{3,19},{19,3},{4,20},{20... | collective-permute-start | bytes 798728 | tf_op jit(solution)/shard_map/ppermute | solution.py:481
  20.0 13.9 %slice-start = ((f32[520,128]{1,0:T(8,128)}), f32[256,128]{1,0:T(8,128)S(1)}, s32[]{:S(2)}) async-start(f32[520,128]{1,0:T(8,128)} %copy-done.4), calls=%async_computation | async-start | bytes 262144 | tf_op jit(solution)/shard_map/slice | solution.py:526
  20.0 5.8 %collective-permute-start.1 = (f32[80,128]{1,0:T(8,128)}, f32[80,128]{1,0:T(8,128)S(1)}, u32[]{:S(2)}, u32[]{:S(2)}) collective-permute-start(f32[80,128]{1,0:T(8,128)} %get-tuple-element.56), channel_id=1, source_target_pairs={{0,4},{4,8},{8,12},{1,5},{5,9},{9,13},{2,6},{6,10},{10,14},{3,7},{... | collective-permute-start | bytes 122888 | tf_op jit(solution)/shard_map/ppermute | solution.py:496
  21.4 5.1 %collective-permute-start.2 = (f32[80,128]{1,0:T(8,128)}, f32[80,128]{1,0:T(8,128)S(1)}, u32[]{:S(2)}, u32[]{:S(2)}) collective-permute-start(f32[80,128]{1,0:T(8,128)} %get-tuple-element.57), channel_id=1, source_target_pairs={{4,0},{8,4},{12,8},{5,1},{9,5},{13,9},{6,2},{10,6},{14,10},{7,3},{... | collective-permute-start | bytes 122888 | tf_op jit(solution)/shard_map/ppermute | solution.py:497
  25.7 8.2 %copy-start.5 = (f32[64,32,128]{2,1,0:T(8,128)}, f32[64,32,128]{2,1,0:T(8,128)S(1)}, u32[]{:S(2)}) copy-start(f32[64,32,128]{2,1,0:T(8,128)S(1)} %collective-permute-done.3) | copy-start | bytes 3145732
  29.0 17.4 %copy-start.6 = (f32[400,128]{1,0:T(8,128)S(1)}, f32[400,128]{1,0:T(8,128)}, u32[]{:S(2)}) copy-start(f32[400,128]{1,0:T(8,128)} %get-tuple-element.77.refs_6_) | copy-start | bytes 614404
  29.0 18.7 %copy-start.11 = (f32[768,128]{1,0:T(8,128)S(1)}, f32[768,128]{1,0:T(8,128)}, u32[]{:S(2)}) copy-start(f32[768,128]{1,0:T(8,128)} %get-tuple-element.90.refs_2_) | copy-start | bytes 1179652
  29.0 9.6 %collective-permute-start.6 = (f32[568,128]{1,0:T(8,128)}, f32[568,128]{1,0:T(8,128)S(1)}, u32[]{:S(2)}, u32[]{:S(2)}) collective-permute-start(f32[568,128]{1,0:T(8,128)} %get-tuple-element.65.refs_5_), channel_id=1, source_target_pairs={{3,2},{7,6},{11,10},{15,14},{19,18},{23,22},{27,26},{31,30}} | collective-permute-start | bytes 872456 | tf_op jit(solution)/shard_map/ppermute | solution.py:444
  38.2 10.9 %copy-start.1 = (f32[1448,128]{1,0:T(8,128)}, f32[1448,128]{1,0:T(8,128)S(1)}, u32[]{:S(2)}) copy-start(f32[1448,128]{1,0:T(8,128)S(1)} %collective-permute-done.4.refs_2_.refs_0_) | copy-start | bytes 2224132
  38.2 10.9 %copy-start.2 = (f32[1448,128]{1,0:T(8,128)}, f32[1448,128]{1,0:T(8,128)S(1)}, u32[]{:S(2)}) copy-start(f32[1448,128]{1,0:T(8,128)S(1)} %collective-permute-done.5.refs_3_.refs_1_) | copy-start | bytes 2224132
  38.5 10.6 %copy-start.3 = (f32[568,128]{1,0:T(8,128)}, f32[568,128]{1,0:T(8,128)S(1)}, u32[]{:S(2)}) copy-start(f32[568,128]{1,0:T(8,128)S(1)} %collective-permute-done.6.refs_6_.refs_7_) | copy-start | bytes 872452
  38.5 28.9 %collective-permute-start.7 = (f32[1536,128]{1,0:T(8,128)S(1)}, f32[1536,128]{1,0:T(8,128)S(1)}, u32[]{:S(2)}, u32[]{:S(2)}) collective-permute-start(f32[1536,128]{1,0:T(8,128)S(1)} %pad_maximum_fusion), channel_id=1, source_target_pairs={{3,2},{7,6},{11,10},{15,14},{19,18},{23,22},{27,26},{31,30}} | collective-permute-start | bytes 2359304 | tf_op jit(solution)/shard_map/ppermute | solution.py:444
  46.3 13.3 %collective-permute-start.8 = (f32[400,128]{1,0:T(8,128)S(1)}, f32[400,128]{1,0:T(8,128)S(1)}, u32[]{:S(2)}, u32[]{:S(2)}) collective-permute-start(f32[400,128]{1,0:T(8,128)S(1)} %copy-done.6), channel_id=1, source_target_pairs={{0,2},{2,1},{1,0},{4,6},{6,5},{5,4},{8,10},{10,9},{9,8},{12,14},{1... | collective-permute-start | bytes 614408 | tf_op jit(solution)/shard_map/ppermute | solution.py:438
  47.0 12.6 %collective-permute-start.9 = (f32[400,128]{1,0:T(8,128)S(1)}, f32[400,128]{1,0:T(8,128)S(1)}, u32[]{:S(2)}, u32[]{:S(2)}) collective-permute-start(f32[400,128]{1,0:T(8,128)S(1)} %copy-done.6), channel_id=1, source_target_pairs={{0,1},{1,2},{4,5},{5,6},{8,9},{9,10},{12,13},{13,14},{16,17},{17,1... | collective-permute-start | bytes 614408 | tf_op jit(solution)/shard_map/ppermute | solution.py:441
  47.7 31.9 %collective-permute-start.11 = (f32[768,128]{1,0:T(8,128)S(1)}, f32[768,128]{1,0:T(8,128)S(1)}, u32[]{:S(2)}, u32[]{:S(2)}) collective-permute-start(f32[768,128]{1,0:T(8,128)S(1)} %copy-done.11), channel_id=1, source_target_pairs={{0,2},{2,1},{1,0},{4,6},{6,5},{5,4},{8,10},{10,9},{9,8},{12,14},{1... | collective-permute-start | bytes 1179656 | tf_op jit(solution)/shard_map/ppermute | solution.py:438
  48.4 31.3 %collective-permute-start.12 = (f32[768,128]{1,0:T(8,128)S(1)}, f32[768,128]{1,0:T(8,128)S(1)}, u32[]{:S(2)}, u32[]{:S(2)}) collective-permute-start(f32[768,128]{1,0:T(8,128)S(1)} %copy-done.11), channel_id=1, source_target_pairs={{0,1},{1,2},{4,5},{5,6},{8,9},{9,10},{12,13},{13,14},{16,17},{17,1... | collective-permute-start | bytes 1179656 | tf_op jit(solution)/shard_map/ppermute | solution.py:441
  59.6 7.9 %copy-start.7 = (f32[400,128]{1,0:T(8,128)}, f32[400,128]{1,0:T(8,128)S(1)}, u32[]{:S(2)}) copy-start(f32[400,128]{1,0:T(8,128)S(1)} %collective-permute-done.8.refs_4_) | copy-start | bytes 614404
  59.6 7.8 %copy-start.8 = (f32[400,128]{1,0:T(8,128)}, f32[400,128]{1,0:T(8,128)S(1)}, u32[]{:S(2)}) copy-start(f32[400,128]{1,0:T(8,128)S(1)} %collective-permute-done.9.refs_5_) | copy-start | bytes 614404
  59.7 20.0 %collective-permute-start.13 = (f32[768,128]{1,0:T(8,128)S(1)}, f32[768,128]{1,0:T(8,128)S(1)}, u32[]{:S(2)}, u32[]{:S(2)}) collective-permute-start(f32[768,128]{1,0:T(8,128)S(1)} %copy-done.11), channel_id=1, source_target_pairs={{3,2},{7,6},{11,10},{15,14},{19,18},{23,22},{27,26},{31,30}} | collective-permute-start | bytes 1179656 | tf_op jit(solution)/shard_map/ppermute | solution.py:444
  78.4 30.6 %collective-permute-start.10 = (f32[18,64,128]{2,1,0:T(8,128)}, f32[18,64,128]{2,1,0:T(8,128)S(1)}, u32[]{:S(2)}, u32[]{:S(2)}) collective-permute-start(f32[18,64,128]{2,1,0:T(8,128)} %get-tuple-element.89), channel_id=1, source_target_pairs={{2,3},{6,7},{10,11},{14,15},{18,19},{22,23},{26,27},{30,31}} | collective-permute-start | bytes 1769480 | tf_op jit(solution)/shard_map/ppermute | solution.py:447
  79.7 0.9 copy-start.13
  79.7 1.1 copy-start.14
  80.8 28.2 %copy-start.9 = (f32[18,64,128]{2,1,0:T(8,128)S(1)}, f32[18,64,128]{2,1,0:T(8,128)}, u32[]{:S(2)}) copy-start(f32[18,64,128]{2,1,0:T(8,128)} %get-tuple-element.98) | copy-start | bytes 1769476
  88.3 20.8 %copy-start.10 = (f32[14,64,128]{2,1,0:T(8,128)S(1)}, f32[14,64,128]{2,1,0:T(8,128)}, u32[]{:S(2)}) copy-start(f32[14,64,128]{2,1,0:T(8,128)} %get-tuple-element.100) | copy-start | bytes 1376260
  88.3 20.7 %collective-permute-start.14 = (f32[14,64,128]{2,1,0:T(8,128)}, f32[14,64,128]{2,1,0:T(8,128)S(1)}, u32[]{:S(2)}, u32[]{:S(2)}) collective-permute-start(f32[14,64,128]{2,1,0:T(8,128)} %get-tuple-element.96), channel_id=1, source_target_pairs={{2,3},{6,7},{10,11},{14,15},{18,19},{22,23},{26,27},{30,31}} | collective-permute-start | bytes 1376264 | tf_op jit(solution)/shard_map/ppermute | solution.py:447
  90.4 5.3 %collective-permute-start.15 = (f32[128]{0:T(128)S(1)}, f32[128]{0:T(128)S(1)}, u32[]{:S(2)}, u32[]{:S(2)}) collective-permute-start(f32[128]{0:T(128)S(1)} %get-tuple-element.105), channel_id=1, source_target_pairs={{0,3},{1,0},{2,1},{3,2},{4,7},{5,4},{6,5},{7,6},{8,11},{9,8},{10,9... | collective-permute-start | bytes 1544 | tf_op jit(solution)/shard_map/ppermute | solution.py:590
  93.1 4.4 %collective-permute-start.16 = (f32[128]{0:T(128)S(1)}, f32[128]{0:T(128)S(1)}, u32[]{:S(2)}, u32[]{:S(2)}) collective-permute-start(f32[128]{0:T(128)S(1)} %get-tuple-element.105), channel_id=1, source_target_pairs={{0,2},{1,3},{2,0},{3,1},{4,6},{5,7},{6,4},{7,5},{8,10},{9,11},{10,... | collective-permute-start | bytes 1544 | tf_op jit(solution)/shard_map/ppermute | solution.py:590
  93.1 11.7 %collective-permute-start.17 = (f32[128]{0:T(128)S(1)}, f32[128]{0:T(128)S(1)}, u32[]{:S(2)}, u32[]{:S(2)}) collective-permute-start(f32[128]{0:T(128)S(1)} %get-tuple-element.105), channel_id=1, source_target_pairs={{0,1},{1,2},{2,3},{3,0},{4,5},{5,6},{6,7},{7,4},{8,9},{9,10},{10,1... | collective-permute-start | bytes 1544 | tf_op jit(solution)/shard_map/ppermute | solution.py:590
  104.8 3.6 %collective-permute-start.18 = (f32[128]{0:T(128)S(1)}, f32[128]{0:T(128)S(1)}, u32[]{:S(2)}, u32[]{:S(2)}) collective-permute-start(f32[128]{0:T(128)S(1)} %dynamic-slice_reduce_fusion), channel_id=1, source_target_pairs={{0,16},{16,0},{1,17},{17,1},{2,18},{18,2},{3,19},{19,3},{4,20},{20... | collective-permute-start | bytes 1544 | tf_op jit(solution)/shard_map/ppermute | solution.py:596
  (5 other events, 3.7 us)

commit v8 on v7

--- a/solution.py
+++ b/solution.py
@@ -11,7 +11,7 @@
 LANES = 128
 EDGE = 16
 gate_width = 0.5
-BATCH = 4
+BATCH = 8
 MICRO = 3 * 10**6
 VMEM_LIMIT = 56 * 2**20
 
@@ -391,8 +391,9 @@
             EDGE,
             radial,
         ).T
-        own_out[row - out_low] = result[:RANGE]
-        next_out[row - out_low] = result[RANGE:]
+        rows = pl.ds(row - out_low, RANGE, stride=out_high - out_low)
+        own_out[rows, :] = result[:RANGE]
+        next_out[rows, :] = result[RANGE:]
 
     if not last:
         keep_second[...] = second[pl.ds(high_row - 2 - base, 2)]
@@ -431,7 +432,7 @@
     own_bins, azimuth, radial = density.shape
     place = lax.axis_index("mass")
     phis, rows = lax.axis_size("phi"), lax.axis_size("row")
-    cuts = [0, 5 * azimuth // 8, azimuth]
+    cuts = [0, azimuth // 2 + 2, azimuth]
     spans = list(zip(cuts, cuts[1:]))
 
     def far(x):
@@ -571,7 +572,7 @@
         operands += halo_refs + ([first_next] if first or last else [])
         operands += [*coefs, gates, second[g], moved[g]]
         operands += [both, own_cols, *carry]
-        outs = [(n_out, RANGE, radial), (n_out, RANGE, radial), (8, radial) if last else (radial, LANES)]
+        outs = [(RANGE * n_out, radial), (RANGE * n_out + 8 * first, radial), (8, radial) if last else (radial, LANES)]
         if not last:
             outs += [(2, 2, length, LANES), (2, length, LANES)]
         own_out, next_out, total, *kept = call(
@@ -585,20 +586,24 @@
         own_outs.append(own_out)
         next_outs.append(returning(next_out))
     speed_gradient = total[0]
+    step = 1
+    while step < phis:
+        speed_gradient += lax.ppermute(speed_gradient, "phi", [(i, i ^ step) for i in range(phis)])
+        step *= 2
     size = lax.axis_size("mass")
     shares = [
         lax.ppermute(speed_gradient, "mass", [(i, (i + k) % size) for i in range(size)]) for k in range(1, size)
     ]
     shares = jnp.stack([*reversed(shares), speed_gradient] * 2)
     speed_gradient = jnp.sum(lax.dynamic_slice_in_dim(shares, size - 1 - place, size, 0), axis=0)
-    step = 1
-    while step < phis:
-        speed_gradient += lax.ppermute(speed_gradient, "phi", [(i, i ^ step) for i in range(phis)])
-        step *= 2
     next_outs = lax.optimization_barrier(next_outs)
     result = jnp.concatenate(
-        [jnp.where(place == 3, there, here) for here, there in zip(own_outs, next_outs)], axis=0
-    ).transpose(1, 0, 2)
+        [
+            jnp.where(place == 3, there[: here.shape[0]], here).reshape(own_bins, -1, radial)
+            for here, there in zip(own_outs, next_outs)
+        ],
+        axis=1,
+    )
     return (result, speed_gradient)
 
 

time: 111 us -> 106 us (0.955); the launches traced: 111 us -> 104 us
  waiting for transfers between devices: 22.1 us -> 18.5 us
  starting transfers between devices: 39.5 us -> 36.5 us
  other arithmetic: 0.83 us -> 2.5 us
  local copies, waits for them, and re-layouts: 6.72 us -> 5.13 us
    ppermute x3, waiting for transfers between devices: 9.3 us -> 5.63 us  [per_device(): lax.ppermute(speed_gradient, 'mass', [(i, (i + k) % size) for i in range(...]
    ppermute x4, starting transfers between devices: 21.8 us -> 18.7 us  [ending(): return lax.ppermute(x, 'mass', [(3, 2)])]
    unnamed x35 -> x34, local copies, waits for them, and re-layouts: 4.87 us -> 3.32 us
    concatenate x0 -> x1, other arithmetic: none -> 1.13 us  [per_device(): jnp.concatenate([jnp.where(place == 3, there[:here.shape[0]], here).resha...]
  transfers between devices with their start and end apart: 19 -> 19, of which waited for: 8 -> 8; matrix products, arithmetic and copies ran while one was open for 2% -> 3% of each run, Pallas kernels for 37% -> 39%
where the time goes in v8:
time: 106 us; the launch traced here: 104 us
  Pallas kernels  40.5 us (38%)
  starting transfers between devices  36.5 us (34%)
  waiting for transfers between devices  18.5 us (17%)
  local copies, waits for them, and re-layouts  5.13 us (5%)
  other arithmetic  2.5 us (2%)
    pallas_call x6, Pallas kernels, call(): pl.pallas_call(kernel, out_shape=[jax.ShapeDtypeStruct(o, jnp.float32) fo...  36.2 us
    ppermute x4, starting transfers between devices, ending(): return lax.ppermute(x, 'mass', [(3, 2)])  18.7 us
    ppermute x1, waiting for transfers between devices, per_device(): other = lax.ppermute(sides, 'phi', ring)  6.57 us
    ppermute x3, waiting for transfers between devices, per_device(): lax.ppermute(speed_gradient, 'mass', [(i, (i + k) % size) for i in range(...  5.63 us
    ppermute x3, starting transfers between devices, per_device(): lax.ppermute(speed_gradient, 'mass', [(i, (i + k) % size) for i in range(...  5.06 us
    pallas_call x1, Pallas kernels, per_device(): pl.pallas_call(table_kernel, out_shape=[jax.ShapeDtypeStruct((3 * total_b...  4.25 us
    ppermute x4, waiting for transfers between devices, ending(): return lax.ppermute(x, 'mass', [(3, 2)])  3.68 us
    unnamed x34, local copies, waits for them, and re-layouts  3.32 us
  transfers between devices with their start and end apart: 19, of which 8 were waited for; matrix products, arithmetic and copies ran while one was open for 3% of the time, Pallas kernels for 39%

profile of v8, /device:TPU:24, one launch (start us, length us, event | category | flops | bytes accessed | tf_op | source)
XLA Modules:
  0.0 104.1 jit_solution(2435723918302629811)
XLA Ops:
  0.6 2.4 %collective-permute-start.3 = (f32[64,32,128]{2,1,0:T(8,128)}, f32[64,32,128]{2,1,0:T(8,128)S(1)}, u32[]{:S(2)}, u32[]{:S(2)}) collective-permute-start(f32[64,32,128]{2,1,0:T(8,128)} %param.14), channel_id=1, source_target_pairs={{3,2},{7,6},{11,10},{15,14},{19,18},{23,22},{27,26},{31,30}} | collective-permute-start | bytes 3145736 | tf_op jit(solution)/shard_map/ppermute | solution.py:445
  3.1 4.5 %shard_map.149 = (f32[520,128]{1,0:T(8,128)}, f32[32,128]{1,0:T(8,128)}, f32[128,128]{1,0:T(8,128)}, f32[1320,128]{1,0:T(8,128)}, f32[168,128]{1,0:T(8,128)}, /*...) custom-call(f32[2048,128]{1,0:T(8,128)} %bitcast.25, f32[2048,128]{1,0:T(8,128)} %bitcast.21, ...), custom_call_target="tpu_custom_call" | custom-call | bytes 3000000 | tf_op jit(solution)/shard_map/pallas_call | solution.py:405
  7.6 0.7 collective-permute-start.4
  8.3 0.7 collective-permute-start.5
  9.0 1.6 %collective-permute-start = (f32[520,128]{1,0:T(8,128)}, f32[520,128]{1,0:T(8,128)S(1)}, u32[]{:S(2)}, u32[]{:S(2)}) collective-permute-start(f32[520,128]{1,0:T(8,128)} %get-tuple-element.52), channel_id=1, source_target_pairs={{0,16},{16,0},{1,17},{17,1},{2,18},{18,2},{3,19},{19,3},{4,20},{20... | collective-permute-start | bytes 798728 | tf_op jit(solution)/shard_map/ppermute | solution.py:482
  10.5 6.6 %collective-permute-done.sides_ref = f32[520,128]{1,0:T(8,128)S(1)} collective-permute-done((f32[520,128]{1,0:T(8,128)}, f32[520,128]{1,0:T(8,128)S(1)}, u32[]{:S(2)}, u32[]{:S(2)}) %collective-permute-start) | collective-permute-done | bytes 266272 | tf_op jit(solution)/shard_map/ppermute | solution.py:482
  17.1 0.7 copy-done.4
  17.8 1.8 %shard_map.150 = (f32[80,128]{1,0:T(8,128)}, f32[80,128]{1,0:T(8,128)}, f32[128,128]{1,0:T(8,128)}) custom-call(f32[520,128]{1,0:T(8,128)} %copy-done.4, f32[64,128]{1,0:T(8,128)} %bitcast.27, f32[64,128]{1,0:T(8,128)} %bitcast.28, f32[32,128]{1,0:T(8,128)} %get-tuple-element.55.gate_ref), custom_call_target="tpu_custom_call" | custom-call | bytes 3000000 | tf_op jit(solution)/shard_map/pallas_call | solution.py:405
  19.7 1.4 %collective-permute-start.1 = (f32[80,128]{1,0:T(8,128)}, f32[80,128]{1,0:T(8,128)S(1)}, u32[]{:S(2)}, u32[]{:S(2)}) collective-permute-start(f32[80,128]{1,0:T(8,128)} %get-tuple-element.56), channel_id=1, source_target_pairs={{0,4},{4,8},{8,12},{1,5},{5,9},{9,13},{2,6},{6,10},{10,14},{3,7},{... | collective-permute-start | bytes 122888 | tf_op jit(solution)/shard_map/ppermute | solution.py:497
  21.1 1.4 %collective-permute-start.2 = (f32[80,128]{1,0:T(8,128)}, f32[80,128]{1,0:T(8,128)S(1)}, u32[]{:S(2)}, u32[]{:S(2)}) collective-permute-start(f32[80,128]{1,0:T(8,128)} %get-tuple-element.57), channel_id=1, source_target_pairs={{4,0},{8,4},{12,8},{5,1},{9,5},{13,9},{6,2},{10,6},{14,10},{7,3},{... | collective-permute-start | bytes 122888 | tf_op jit(solution)/shard_map/ppermute | solution.py:498
  22.5 3.2 %collective-permute-done.3 = f32[64,32,128]{2,1,0:T(8,128)S(1)} collective-permute-done((f32[64,32,128]{2,1,0:T(8,128)}, f32[64,32,128]{2,1,0:T(8,128)S(1)}, u32[]{:S(2)}, u32[]{:S(2)}) %collective-permute-start.3) | collective-permute-done | bytes 1048608 | tf_op jit(solution)/shard_map/ppermute | solution.py:445
  26.9 1.9 %shard_map.151 = (f32[568,128]{1,0:T(8,128)}, f32[400,128]{1,0:T(8,128)}, f32[160,128]{1,0:T(8,128)}) custom-call(f32[80,128]{1,0:T(8,128)} %copy-done.15, f32[80,128]{1,0:T(8,128)} %copy-done.16, f32[520,128]{1,0:T(8,128)} %copy-done.4, f32[168,128]{1,0:T(8,128)} %get-tuple-element.58.shares_ref.refs_4_, f32[128,128]{1,0:T(8,128)} %get-tuple-element.60.gates_ref), custom_call_target="tpu_custom_call" | custom-call | bytes 3000000 | tf_op jit(solution)/shard_map/pallas_call | solution.py:405
  28.8 3.9 %collective-permute-start.6 = (f32[568,128]{1,0:T(8,128)}, f32[568,128]{1,0:T(8,128)S(1)}, u32[]{:S(2)}, u32[]{:S(2)}) collective-permute-start(f32[568,128]{1,0:T(8,128)} %get-tuple-element.65.refs_5_), channel_id=1, source_target_pairs={{3,2},{7,6},{11,10},{15,14},{19,18},{23,22},{27,26},{31,30}} | collective-permute-start | bytes 872456 | tf_op jit(solution)/shard_map/ppermute | solution.py:445
  32.7 1.1 %slice.12 = f32[1152,128]{1,0:T(8,128)S(1)} slice(f32[1320,128]{1,0:T(8,128)} %get-tuple-element.62.refs_2_), slice={[0:1152], [0:128]} | slice | bytes 1179648 | tf_op jit(solution)/shard_map/slice | solution.py:527
  33.9 4.3 %shard_map.152 = (bf16[768,512]{1,0:T(8,128)(2,1)}, bf16[768,256]{1,0:T(8,128)(2,1)}, bf16[768,256]{1,0:T(8,128)(2,1)}) custom-call(f32[256,256]{1,0:T(8,128)} %gain_ref, s32[1,256]{1,0:T(1,128)} %bitcast.37, f32[1,256]{1,0:T(1,128)} %bitcast.38, f32[1,256]{1,0:T(1,128)} %bitcast.39, f32[1,256]{1,0:T(1,128)} %bitcast.40, s32[4,4]{1,0:T(4,128)} %pairs_ref.1), custom_call_target="tpu_custom_call" | custom-call | bytes 9000000 | tf_op jit(solution)/shard_map/pallas_call | solution.py:510
  38.7 4.6 %collective-permute-start.7 = (f32[1408,128]{1,0:T(8,128)S(1)}, f32[1408,128]{1,0:T(8,128)S(1)}, u32[]{:S(2)}, u32[]{:S(2)}) collective-permute-start(f32[1408,128]{1,0:T(8,128)S(1)} %pad_maximum_fusion.1), channel_id=1, source_target_pairs={{3,2},{7,6},{11,10},{15,14},{19,18},{23,22},{27,26},{31,30}} | collective-permute-start | bytes 2162696 | tf_op jit(solution)/shard_map/ppermute | solution.py:445
  44.6 0.7 collective-permute-start.11
  46.1 10.4 %shard_map.153 = (f32[17,128,128]{2,1,0:T(8,128)}, f32[15,128,128]{2,1,0:T(8,128)}, f32[18,2,128,128]{3,2,1,0:T(8,128)}, f32[14,2,128,128]{3,2,1,0:T(8,128)}, f3...) custom-call(f32[2048,128]{1,0:T(8,128)} %bitcast.22, ...), custom_call_target="tpu_custom_call" | custom-call | bytes 39000000 | tf_op jit(solution)/shard_map/pallas_call | solution.py:405
  56.5 7.8 %collective-permute-start.13 = (f32[896,128]{1,0:T(8,128)S(1)}, f32[896,128]{1,0:T(8,128)S(1)}, u32[]{:S(2)}, u32[]{:S(2)}) collective-permute-start(f32[896,128]{1,0:T(8,128)S(1)} %copy-done.11), channel_id=1, source_target_pairs={{3,2},{7,6},{11,10},{15,14},{19,18},{23,22},{27,26},{31,30}} | collective-permute-start | bytes 1376264 | tf_op jit(solution)/shard_map/ppermute | solution.py:445
  64.3 0.8 copy-done
  65.2 9.4 %shard_map.154 = (f32[1024,128]{1,0:T(8,128)}, f32[1032,128]{1,0:T(8,128)}, f32[128,128]{1,0:T(8,128)}, f32[2,2,160,128]{3,2,1,0:T(8,128)}, f32[2,160,128]{2,1,0:T(8,128)}) custom-call(f32[1320,128]{1,0:T(8,128)} %copy-done.1, f32[1320,128]{1,0:T(8,128)} %copy-done.2, f32[1320,128]{1,0:T(8,128)} %get-tuple-element.62.refs_2_, f32[1408,128]{1,0:T(8,128)} %copy-done, ...), custom_call_target="tpu_custom_call" | custom-call | bytes 36000000 | tf_op jit(solution)/shard_map/pallas_call | solution.py:405
  74.6 1.3 %collective-permute-start.10 = (f32[1032,128]{1,0:T(8,128)}, f32[1032,128]{1,0:T(8,128)S(1)}, u32[]{:S(2)}, u32[]{:S(2)}) collective-permute-start(f32[1032,128]{1,0:T(8,128)} %get-tuple-element.89), channel_id=1, source_target_pairs={{2,3},{6,7},{10,11},{14,15},{18,19},{22,23},{26,27},{30,31}} | collective-permute-start | bytes 1585160 | tf_op jit(solution)/shard_map/ppermute | solution.py:448
  75.9 0.7 copy-done.12
  77.0 8.2 %shard_map.155 = (f32[1024,128]{1,0:T(8,128)}, f32[1024,128]{1,0:T(8,128)}, f32[8,128]{1,0:T(8,128)}) custom-call(f32[896,128]{1,0:T(8,128)} %copy-done.12, f32[896,128]{1,0:T(8,128)} %copy-done.13, f32[896,128]{1,0:T(8,128)} %get-tuple-element.90.refs_2_, f32[896,128]{1,0:T(8,128)} %copy-done.14, f32[400,128]{1,0:T(8,128)} %copy-done.7, ...), custom_call_target="tpu_custom_call" | custom-call | bytes 30000000 | tf_op jit(solution)/shard_map/pallas_call | solution.py:405
  85.2 1.4 %collective-permute-start.14 = (f32[1024,128]{1,0:T(8,128)}, f32[1024,128]{1,0:T(8,128)S(1)}, u32[]{:S(2)}, u32[]{:S(2)}) collective-permute-start(f32[1024,128]{1,0:T(8,128)} %get-tuple-element.96), channel_id=1, source_target_pairs={{2,3},{6,7},{10,11},{14,15},{18,19},{22,23},{26,27},{30,31}} | collective-permute-start | bytes 1572872 | tf_op jit(solution)/shard_map/ppermute | solution.py:448
  87.3 1.5 %collective-permute-start.15 = (f32[128]{0:T(128)S(1)}, f32[128]{0:T(128)S(1)}, u32[]{:S(2)}, u32[]{:S(2)}) collective-permute-start(f32[128]{0:T(128)S(1)} %slice_bitcast_fusion), channel_id=1, source_target_pairs={{0,16},{16,0},{1,17},{17,1},{2,18},{18,2},{3,19},{19,3},{4,20},{20... | collective-permute-start | bytes 1544 | tf_op jit(solution)/shard_map/ppermute | solution.py:591
  88.8 2.1 %collective-permute-done.15 = f32[128]{0:T(128)S(1)} collective-permute-done((f32[128]{0:T(128)S(1)}, f32[128]{0:T(128)S(1)}, u32[]{:S(2)}, u32[]{:S(2)}) %collective-permute-start.15) | collective-permute-done | bytes 544 | tf_op jit(solution)/shard_map/ppermute | solution.py:591
  91.6 2.7 %collective-permute-start.16 = (f32[128]{0:T(128)S(1)}, f32[128]{0:T(128)S(1)}, u32[]{:S(2)}, u32[]{:S(2)}) collective-permute-start(f32[128]{0:T(128)S(1)} %fusion), channel_id=1, source_target_pairs={{0,3},{1,0},{2,1},{3,2},{4,7},{5,4},{6,5},{7,6},{8,11},{9,8},{10,9... | collective-permute-start | bytes 1544 | tf_op jit(solution)/shard_map/ppermute | solution.py:595
  94.3 2.4 %collective-permute-start.18 = (f32[128]{0:T(128)S(1)}, f32[128]{0:T(128)S(1)}, u32[]{:S(2)}, u32[]{:S(2)}) collective-permute-start(f32[128]{0:T(128)S(1)} %fusion), channel_id=1, source_target_pairs={{0,1},{1,2},{2,3},{3,0},{4,5},{5,6},{6,7},{7,4},{8,9},{9,10},{10,1... | collective-permute-start | bytes 1544 | tf_op jit(solution)/shard_map/ppermute | solution.py:595
  96.9 1.8 %collective-permute-done.17 = f32[128]{0:T(128)S(1)} collective-permute-done((f32[128]{0:T(128)S(1)}, f32[128]{0:T(128)S(1)}, u32[]{:S(2)}, u32[]{:S(2)}) %collective-permute-start.17) | collective-permute-done | bytes 544 | tf_op jit(solution)/shard_map/ppermute | solution.py:595
  98.7 3.6 %collective-permute-done.18 = f32[128]{0:T(128)S(1)} collective-permute-done((f32[128]{0:T(128)S(1)}, f32[128]{0:T(128)S(1)}, u32[]{:S(2)}, u32[]{:S(2)}) %collective-permute-start.18) | collective-permute-done | bytes 544 | tf_op jit(solution)/shard_map/ppermute | solution.py:595
  103.0 1.1 %pad_maximum_fusion = f32[64,32,128]{2,1,0:T(8,128)} fusion(f32[64,16,128]{2,1,0:T(8,128)S(1)} %bitcast.24, f32[64,16,128]{2,1,0:T(8,128)S(1)} %bitcast.23), kind=kLoop, calls=%fused_computation | loop fusion | flops 262144 | bytes 2097152 | tf_op jit(solution)/shard_map/concatenate | solution.py:600
  (58 shorter events, 6.6 us)
Async XLA Ops:
  0.6 25.1 %collective-permute-start.3 = (f32[64,32,128]{2,1,0:T(8,128)}, f32[64,32,128]{2,1,0:T(8,128)S(1)}, u32[]{:S(2)}, u32[]{:S(2)}) collective-permute-start(f32[64,32,128]{2,1,0:T(8,128)} %param.14), channel_id=1, source_target_pairs={{3,2},{7,6},{11,10},{15,14},{19,18},{23,22},{27,26},{31,30}} | collective-permute-start | bytes 3145736 | tf_op jit(solution)/shard_map/ppermute | solution.py:445
  7.6 30.6 %collective-permute-start.4 = (f32[1320,128]{1,0:T(8,128)}, f32[1320,128]{1,0:T(8,128)S(1)}, u32[]{:S(2)}, u32[]{:S(2)}) collective-permute-start(f32[1320,128]{1,0:T(8,128)} %get-tuple-element.62.refs_2_), channel_id=1, source_target_pairs={{0,2},{2,1},{1,0},{4,6},{6,5},{5,4},{8,10},{10,9},{9,8},{12,14},{1... | collective-permute-start | bytes 2027528 | tf_op jit(solution)/shard_map/ppermute | solution.py:439
  8.3 29.9 %collective-permute-start.5 = (f32[1320,128]{1,0:T(8,128)}, f32[1320,128]{1,0:T(8,128)S(1)}, u32[]{:S(2)}, u32[]{:S(2)}) collective-permute-start(f32[1320,128]{1,0:T(8,128)} %get-tuple-element.62.refs_2_), channel_id=1, source_target_pairs={{0,1},{1,2},{4,5},{5,6},{8,9},{9,10},{12,13},{13,14},{16,17},{17,1... | collective-permute-start | bytes 2027528 | tf_op jit(solution)/shard_map/ppermute | solution.py:442
  9.0 8.1 %collective-permute-start = (f32[520,128]{1,0:T(8,128)}, f32[520,128]{1,0:T(8,128)S(1)}, u32[]{:S(2)}, u32[]{:S(2)}) collective-permute-start(f32[520,128]{1,0:T(8,128)} %get-tuple-element.52), channel_id=1, source_target_pairs={{0,16},{16,0},{1,17},{17,1},{2,18},{18,2},{3,19},{19,3},{4,20},{20... | collective-permute-start | bytes 798728 | tf_op jit(solution)/shard_map/ppermute | solution.py:482
  19.7 14.2 %slice-start = ((f32[520,128]{1,0:T(8,128)}), f32[256,128]{1,0:T(8,128)S(1)}, s32[]{:S(2)}) async-start(f32[520,128]{1,0:T(8,128)} %copy-done.4), calls=%async_computation | async-start | bytes 262144 | tf_op jit(solution)/shard_map/slice | solution.py:527
  19.7 6.1 %collective-permute-start.1 = (f32[80,128]{1,0:T(8,128)}, f32[80,128]{1,0:T(8,128)S(1)}, u32[]{:S(2)}, u32[]{:S(2)}) collective-permute-start(f32[80,128]{1,0:T(8,128)} %get-tuple-element.56), channel_id=1, source_target_pairs={{0,4},{4,8},{8,12},{1,5},{5,9},{9,13},{2,6},{6,10},{10,14},{3,7},{... | collective-permute-start | bytes 122888 | tf_op jit(solution)/shard_map/ppermute | solution.py:497
  21.1 23.5 %copy-start.11 = (f32[896,128]{1,0:T(8,128)S(1)}, f32[896,128]{1,0:T(8,128)}, u32[]{:S(2)}) copy-start(f32[896,128]{1,0:T(8,128)} %get-tuple-element.90.refs_2_) | copy-start | bytes 1376260
  21.1 5.2 %collective-permute-start.2 = (f32[80,128]{1,0:T(8,128)}, f32[80,128]{1,0:T(8,128)S(1)}, u32[]{:S(2)}, u32[]{:S(2)}) collective-permute-start(f32[80,128]{1,0:T(8,128)} %get-tuple-element.57), channel_id=1, source_target_pairs={{4,0},{8,4},{12,8},{5,1},{9,5},{13,9},{6,2},{10,6},{14,10},{7,3},{... | collective-permute-start | bytes 122888 | tf_op jit(solution)/shard_map/ppermute | solution.py:498
  25.7 12.9 %copy-start.5 = (f32[64,32,128]{2,1,0:T(8,128)}, f32[64,32,128]{2,1,0:T(8,128)S(1)}, u32[]{:S(2)}) copy-start(f32[64,32,128]{2,1,0:T(8,128)S(1)} %collective-permute-done.3) | copy-start | bytes 3145732
  28.8 14.4 %copy-start.6 = (f32[400,128]{1,0:T(8,128)S(1)}, f32[400,128]{1,0:T(8,128)}, u32[]{:S(2)}) copy-start(f32[400,128]{1,0:T(8,128)} %get-tuple-element.77.refs_6_) | copy-start | bytes 614404
  28.8 9.8 %collective-permute-start.6 = (f32[568,128]{1,0:T(8,128)}, f32[568,128]{1,0:T(8,128)S(1)}, u32[]{:S(2)}, u32[]{:S(2)}) collective-permute-start(f32[568,128]{1,0:T(8,128)} %get-tuple-element.65.refs_5_), channel_id=1, source_target_pairs={{3,2},{7,6},{11,10},{15,14},{19,18},{23,22},{27,26},{31,30}} | collective-permute-start | bytes 872456 | tf_op jit(solution)/shard_map/ppermute | solution.py:445
  38.1 7.9 %copy-start.1 = (f32[1320,128]{1,0:T(8,128)}, f32[1320,128]{1,0:T(8,128)S(1)}, u32[]{:S(2)}) copy-start(f32[1320,128]{1,0:T(8,128)S(1)} %collective-permute-done.4.refs_2_.refs_0_) | copy-start | bytes 2027524
  38.2 7.9 %copy-start.2 = (f32[1320,128]{1,0:T(8,128)}, f32[1320,128]{1,0:T(8,128)S(1)}, u32[]{:S(2)}) copy-start(f32[1320,128]{1,0:T(8,128)S(1)} %collective-permute-done.5.refs_3_.refs_1_) | copy-start | bytes 2027524
  38.7 7.4 %copy-start.3 = (f32[568,128]{1,0:T(8,128)}, f32[568,128]{1,0:T(8,128)S(1)}, u32[]{:S(2)}) copy-start(f32[568,128]{1,0:T(8,128)S(1)} %collective-permute-done.6.refs_6_.refs_7_) | copy-start | bytes 872452
  38.7 25.6 %collective-permute-start.7 = (f32[1408,128]{1,0:T(8,128)S(1)}, f32[1408,128]{1,0:T(8,128)S(1)}, u32[]{:S(2)}, u32[]{:S(2)}) collective-permute-start(f32[1408,128]{1,0:T(8,128)S(1)} %pad_maximum_fusion.1), channel_id=1, source_target_pairs={{3,2},{7,6},{11,10},{15,14},{19,18},{23,22},{27,26},{31,30}} | collective-permute-start | bytes 2162696 | tf_op jit(solution)/shard_map/ppermute | solution.py:445
  43.3 13.2 %collective-permute-start.8 = (f32[400,128]{1,0:T(8,128)S(1)}, f32[400,128]{1,0:T(8,128)S(1)}, u32[]{:S(2)}, u32[]{:S(2)}) collective-permute-start(f32[400,128]{1,0:T(8,128)S(1)} %copy-done.6), channel_id=1, source_target_pairs={{0,2},{2,1},{1,0},{4,6},{6,5},{5,4},{8,10},{10,9},{9,8},{12,14},{1... | collective-permute-start | bytes 614408 | tf_op jit(solution)/shard_map/ppermute | solution.py:439
  43.9 12.5 %collective-permute-start.9 = (f32[400,128]{1,0:T(8,128)S(1)}, f32[400,128]{1,0:T(8,128)S(1)}, u32[]{:S(2)}, u32[]{:S(2)}) collective-permute-start(f32[400,128]{1,0:T(8,128)S(1)} %copy-done.6), channel_id=1, source_target_pairs={{0,1},{1,2},{4,5},{5,6},{8,9},{9,10},{12,13},{13,14},{16,17},{17,1... | collective-permute-start | bytes 614408 | tf_op jit(solution)/shard_map/ppermute | solution.py:442
  44.6 31.2 %collective-permute-start.11 = (f32[896,128]{1,0:T(8,128)S(1)}, f32[896,128]{1,0:T(8,128)S(1)}, u32[]{:S(2)}, u32[]{:S(2)}) collective-permute-start(f32[896,128]{1,0:T(8,128)S(1)} %copy-done.11), channel_id=1, source_target_pairs={{0,2},{2,1},{1,0},{4,6},{6,5},{5,4},{8,10},{10,9},{9,8},{12,14},{1... | collective-permute-start | bytes 1376264 | tf_op jit(solution)/shard_map/ppermute | solution.py:439
  45.3 30.6 %collective-permute-start.12 = (f32[896,128]{1,0:T(8,128)S(1)}, f32[896,128]{1,0:T(8,128)S(1)}, u32[]{:S(2)}, u32[]{:S(2)}) collective-permute-start(f32[896,128]{1,0:T(8,128)S(1)} %copy-done.11), channel_id=1, source_target_pairs={{0,1},{1,2},{4,5},{5,6},{8,9},{9,10},{12,13},{13,14},{16,17},{17,1... | collective-permute-start | bytes 1376264 | tf_op jit(solution)/shard_map/ppermute | solution.py:442
  56.5 7.9 %copy-start.7 = (f32[400,128]{1,0:T(8,128)}, f32[400,128]{1,0:T(8,128)S(1)}, u32[]{:S(2)}) copy-start(f32[400,128]{1,0:T(8,128)S(1)} %collective-permute-done.8.refs_4_) | copy-start | bytes 614404
  56.5 7.8 %copy-start.8 = (f32[400,128]{1,0:T(8,128)}, f32[400,128]{1,0:T(8,128)S(1)}, u32[]{:S(2)}) copy-start(f32[400,128]{1,0:T(8,128)S(1)} %collective-permute-done.9.refs_5_) | copy-start | bytes 614404
  56.5 19.4 %collective-permute-start.13 = (f32[896,128]{1,0:T(8,128)S(1)}, f32[896,128]{1,0:T(8,128)S(1)}, u32[]{:S(2)}, u32[]{:S(2)}) collective-permute-start(f32[896,128]{1,0:T(8,128)S(1)} %copy-done.11), channel_id=1, source_target_pairs={{3,2},{7,6},{11,10},{15,14},{19,18},{23,22},{27,26},{31,30}} | collective-permute-start | bytes 1376264 | tf_op jit(solution)/shard_map/ppermute | solution.py:445
  74.6 28.3 %collective-permute-start.10 = (f32[1032,128]{1,0:T(8,128)}, f32[1032,128]{1,0:T(8,128)S(1)}, u32[]{:S(2)}, u32[]{:S(2)}) collective-permute-start(f32[1032,128]{1,0:T(8,128)} %get-tuple-element.89), channel_id=1, source_target_pairs={{2,3},{6,7},{10,11},{14,15},{18,19},{22,23},{26,27},{30,31}} | collective-permute-start | bytes 1585160 | tf_op jit(solution)/shard_map/ppermute | solution.py:448
  75.9 1.0 copy-start.13
  75.9 1.1 %copy-start.14 = (f32[896,128]{1,0:T(8,128)}, f32[896,128]{1,0:T(8,128)S(1)}, u32[]{:S(2)}) copy-start(f32[896,128]{1,0:T(8,128)S(1)} %collective-permute-done.13.refs_3_) | copy-start | bytes 1376260
  77.0 25.8 %copy-start.9 = (f32[1024,128]{1,0:T(8,128)S(1)}, f32[1024,128]{1,0:T(8,128)}, u32[]{:S(2)}) copy-start(f32[1024,128]{1,0:T(8,128)} %get-tuple-element.98) | copy-start | bytes 1572868
  85.2 17.7 %copy-start.10 = (f32[1024,128]{1,0:T(8,128)S(1)}, f32[1024,128]{1,0:T(8,128)}, u32[]{:S(2)}) copy-start(f32[1024,128]{1,0:T(8,128)} %get-tuple-element.100) | copy-start | bytes 1572868
  85.2 17.6 %collective-permute-start.14 = (f32[1024,128]{1,0:T(8,128)}, f32[1024,128]{1,0:T(8,128)S(1)}, u32[]{:S(2)}, u32[]{:S(2)}) collective-permute-start(f32[1024,128]{1,0:T(8,128)} %get-tuple-element.96), channel_id=1, source_target_pairs={{2,3},{6,7},{10,11},{14,15},{18,19},{22,23},{26,27},{30,31}} | collective-permute-start | bytes 1572872 | tf_op jit(solution)/shard_map/ppermute | solution.py:448
  87.3 3.5 %collective-permute-start.15 = (f32[128]{0:T(128)S(1)}, f32[128]{0:T(128)S(1)}, u32[]{:S(2)}, u32[]{:S(2)}) collective-permute-start(f32[128]{0:T(128)S(1)} %slice_bitcast_fusion), channel_id=1, source_target_pairs={{0,16},{16,0},{1,17},{17,1},{2,18},{18,2},{3,19},{19,3},{4,20},{20... | collective-permute-start | bytes 1544 | tf_op jit(solution)/shard_map/ppermute | solution.py:591
  91.6 5.3 %collective-permute-start.16 = (f32[128]{0:T(128)S(1)}, f32[128]{0:T(128)S(1)}, u32[]{:S(2)}, u32[]{:S(2)}) collective-permute-start(f32[128]{0:T(128)S(1)} %fusion), channel_id=1, source_target_pairs={{0,3},{1,0},{2,1},{3,2},{4,7},{5,4},{6,5},{7,6},{8,11},{9,8},{10,9... | collective-permute-start | bytes 1544 | tf_op jit(solution)/shard_map/ppermute | solution.py:595
  94.3 4.4 %collective-permute-start.17 = (f32[128]{0:T(128)S(1)}, f32[128]{0:T(128)S(1)}, u32[]{:S(2)}, u32[]{:S(2)}) collective-permute-start(f32[128]{0:T(128)S(1)} %fusion), channel_id=1, source_target_pairs={{0,2},{1,3},{2,0},{3,1},{4,6},{5,7},{6,4},{7,5},{8,10},{9,11},{10,... | collective-permute-start | bytes 1544 | tf_op jit(solution)/shard_map/ppermute | solution.py:595
  94.3 8.0 %collective-permute-start.18 = (f32[128]{0:T(128)S(1)}, f32[128]{0:T(128)S(1)}, u32[]{:S(2)}, u32[]{:S(2)}) collective-permute-start(f32[128]{0:T(128)S(1)} %fusion), channel_id=1, source_target_pairs={{0,1},{1,2},{2,3},{3,0},{4,5},{5,6},{6,7},{7,4},{8,9},{9,10},{10,1... | collective-permute-start | bytes 1544 | tf_op jit(solution)/shard_map/ppermute | solution.py:595
  (5 other events, 3.6 us)

commit v9 on v8

--- a/solution.py
+++ b/solution.py
@@ -525,9 +525,6 @@
 
     long_next = ending(long)
     first_next = jnp.concatenate([opening[: own_bins * cuts[1]], other[: 4 * own_bins]], axis=0)
-    short, first_next, late, far_first, near_first, long_next, both = lax.optimization_barrier(
-        (short, first_next, late, far_first, near_first, long_next, both)
-    )
     halo_refs = [far(short), near(short), short, long_next]
     first_next = ending(first_next)
     far_late, near_late = far(late), near(late)

time: 106 us -> 101 us (0.953)
  starting transfers between devices: 36.5 us -> 33.4 us
  waiting for transfers between devices: 18.5 us -> 16.4 us
    ppermute x4, starting transfers between devices: 18.7 us -> 15.8 us  [ending(): return lax.ppermute(x, 'mass', [(3, 2)])]
    unnamed x34 -> x32, local copies, waits for them, and re-layouts: 3.32 us -> 3.35 us
  transfers between devices with their start and end apart: 19 -> 19, of which waited for: 8 -> 6; matrix products, arithmetic and copies ran while one was open for 3% -> 3% of each run, Pallas kernels for 39% -> 41%
where the time goes in v9:
time: 101 us; the launch traced here: 99 us
  Pallas kernels  40.5 us (40%)
  starting transfers between devices  33.4 us (33%)
  waiting for transfers between devices  16.4 us (16%)
  local copies, waits for them, and re-layouts  5.17 us (5%)
  other arithmetic  2.51 us (2%)
    pallas_call x6, Pallas kernels, call(): pl.pallas_call(kernel, out_shape=[jax.ShapeDtypeStruct(o, jnp.float32) fo...  36.2 us
    ppermute x4, starting transfers between devices, ending(): return lax.ppermute(x, 'mass', [(3, 2)])  15.8 us
    ppermute x1, waiting for transfers between devices, per_device(): other = lax.ppermute(sides, 'phi', ring)  5.87 us
    ppermute x3, waiting for transfers between devices, per_device(): lax.ppermute(speed_gradient, 'mass', [(i, (i + k) % size) for i in range(...  5.53 us
    ppermute x3, starting transfers between devices, per_device(): lax.ppermute(speed_gradient, 'mass', [(i, (i + k) % size) for i in range(...  5.06 us
    pallas_call x1, Pallas kernels, per_device(): pl.pallas_call(table_kernel, out_shape=[jax.ShapeDtypeStruct((3 * total_b...  4.26 us
    unnamed x32, local copies, waits for them, and re-layouts  3.35 us
    ppermute x4, waiting for transfers between devices, ending(): return lax.ppermute(x, 'mass', [(3, 2)])  2.95 us
  transfers between devices with their start and end apart: 19, of which 6 were waited for; matrix products, arithmetic and copies ran while one was open for 3% of the time, Pallas kernels for 41%

profile of v9, /device:TPU:24, one launch (start us, length us, event | category | flops | bytes accessed | tf_op | source)
XLA Modules:
  0.0 99.0 jit_solution(5396690974092495905)
XLA Ops:
  0.6 2.4 %collective-permute-start.4 = (f32[64,32,128]{2,1,0:T(8,128)}, f32[64,32,128]{2,1,0:T(8,128)S(1)}, u32[]{:S(2)}, u32[]{:S(2)}) collective-permute-start(f32[64,32,128]{2,1,0:T(8,128)} %param.14), channel_id=1, source_target_pairs={{3,2},{7,6},{11,10},{15,14},{19,18},{23,22},{27,26},{31,30}} | collective-permute-start | bytes 3145736 | tf_op jit(solution)/shard_map/ppermute | solution.py:445
  3.1 4.5 %shard_map.149 = (f32[520,128]{1,0:T(8,128)}, f32[32,128]{1,0:T(8,128)}, f32[128,128]{1,0:T(8,128)}, f32[1320,128]{1,0:T(8,128)}, f32[168,128]{1,0:T(8,128)}, /*...) custom-call(f32[2048,128]{1,0:T(8,128)} %bitcast.25, f32[2048,128]{1,0:T(8,128)} %bitcast.21, ...), custom_call_target="tpu_custom_call" | custom-call | bytes 3000000 | tf_op jit(solution)/shard_map/pallas_call | solution.py:405
  7.6 0.7 collective-permute-start
  8.3 1.6 %collective-permute-start.2 = (f32[520,128]{1,0:T(8,128)}, f32[520,128]{1,0:T(8,128)S(1)}, u32[]{:S(2)}, u32[]{:S(2)}) collective-permute-start(f32[520,128]{1,0:T(8,128)} %get-tuple-element.46), channel_id=1, source_target_pairs={{0,16},{16,0},{1,17},{17,1},{2,18},{18,2},{3,19},{19,3},{4,20},{20... | collective-permute-start | bytes 798728 | tf_op jit(solution)/shard_map/ppermute | solution.py:482
  9.8 0.7 collective-permute-start.1
  10.5 5.9 %collective-permute-done.2.sides_ref = f32[520,128]{1,0:T(8,128)S(1)} collective-permute-done((f32[520,128]{1,0:T(8,128)}, f32[520,128]{1,0:T(8,128)S(1)}, u32[]{:S(2)}, u32[]{:S(2)}) %collective-permute-start.2) | collective-permute-done | bytes 266272 | tf_op jit(solution)/shard_map/ppermute | solution.py:482
  16.4 0.7 copy-done.4
  17.1 1.8 %shard_map.150 = (f32[80,128]{1,0:T(8,128)}, f32[80,128]{1,0:T(8,128)}, f32[128,128]{1,0:T(8,128)}) custom-call(f32[520,128]{1,0:T(8,128)} %copy-done.4, f32[64,128]{1,0:T(8,128)} %bitcast.27, f32[64,128]{1,0:T(8,128)} %bitcast.28, f32[32,128]{1,0:T(8,128)} %get-tuple-element.49.gate_ref), custom_call_target="tpu_custom_call" | custom-call | bytes 3000000 | tf_op jit(solution)/shard_map/pallas_call | solution.py:405
  18.9 1.4 %collective-permute-start.5 = (f32[80,128]{1,0:T(8,128)}, f32[80,128]{1,0:T(8,128)S(1)}, u32[]{:S(2)}, u32[]{:S(2)}) collective-permute-start(f32[80,128]{1,0:T(8,128)} %get-tuple-element.53), channel_id=1, source_target_pairs={{0,4},{4,8},{8,12},{1,5},{5,9},{9,13},{2,6},{6,10},{10,14},{3,7},{... | collective-permute-start | bytes 122888 | tf_op jit(solution)/shard_map/ppermute | solution.py:497
  20.4 1.3 %collective-permute-start.6 = (f32[80,128]{1,0:T(8,128)}, f32[80,128]{1,0:T(8,128)S(1)}, u32[]{:S(2)}, u32[]{:S(2)}) collective-permute-start(f32[80,128]{1,0:T(8,128)} %get-tuple-element.54), channel_id=1, source_target_pairs={{4,0},{8,4},{12,8},{5,1},{9,5},{13,9},{6,2},{10,6},{14,10},{7,3},{... | collective-permute-start | bytes 122888 | tf_op jit(solution)/shard_map/ppermute | solution.py:498
  21.7 1.1 %slice.12 = f32[1152,128]{1,0:T(8,128)S(1)} slice(f32[1320,128]{1,0:T(8,128)} %get-tuple-element.45.refs_2_), slice={[0:1152], [0:128]} | slice | bytes 1179648 | tf_op jit(solution)/shard_map/slice | solution.py:527
  22.8 2.9 %collective-permute-done.4 = f32[64,32,128]{2,1,0:T(8,128)S(1)} collective-permute-done((f32[64,32,128]{2,1,0:T(8,128)}, f32[64,32,128]{2,1,0:T(8,128)S(1)}, u32[]{:S(2)}, u32[]{:S(2)}) %collective-permute-start.4) | collective-permute-done | bytes 1048608 | tf_op jit(solution)/shard_map/ppermute | solution.py:445
  26.4 1.9 %shard_map.151 = (f32[568,128]{1,0:T(8,128)}, f32[400,128]{1,0:T(8,128)}, f32[160,128]{1,0:T(8,128)}) custom-call(f32[80,128]{1,0:T(8,128)} %copy-done.14, f32[80,128]{1,0:T(8,128)} %copy-done.15, f32[520,128]{1,0:T(8,128)} %copy-done.4, f32[168,128]{1,0:T(8,128)} %get-tuple-element.52.shares_ref.refs_4_, f32[128,128]{1,0:T(8,128)} %get-tuple-element.55.gates_ref), custom_call_target="tpu_custom_call" | custom-call | bytes 3000000 | tf_op jit(solution)/shard_map/pallas_call | solution.py:405
  28.3 4.3 %collective-permute-start.7 = (f32[568,128]{1,0:T(8,128)}, f32[568,128]{1,0:T(8,128)S(1)}, u32[]{:S(2)}, u32[]{:S(2)}) collective-permute-start(f32[568,128]{1,0:T(8,128)} %get-tuple-element.57.refs_5_), channel_id=1, source_target_pairs={{3,2},{7,6},{11,10},{15,14},{19,18},{23,22},{27,26},{31,30}} | collective-permute-start | bytes 872456 | tf_op jit(solution)/shard_map/ppermute | solution.py:445
  32.6 1.3 %collective-permute-start.3 = (f32[1408,128]{1,0:T(8,128)S(1)}, f32[1408,128]{1,0:T(8,128)S(1)}, u32[]{:S(2)}, u32[]{:S(2)}) collective-permute-start(f32[1408,128]{1,0:T(8,128)S(1)} %pad_maximum_fusion.1), channel_id=1, source_target_pairs={{3,2},{7,6},{11,10},{15,14},{19,18},{23,22},{27,26},{31,30}} | collective-permute-start | bytes 2162696 | tf_op jit(solution)/shard_map/ppermute | solution.py:445
  35.4 4.3 %shard_map.152 = (bf16[768,512]{1,0:T(8,128)(2,1)}, bf16[768,256]{1,0:T(8,128)(2,1)}, bf16[768,256]{1,0:T(8,128)(2,1)}) custom-call(f32[256,256]{1,0:T(8,128)} %gain_ref, s32[1,256]{1,0:T(1,128)} %bitcast.37, f32[1,256]{1,0:T(1,128)} %bitcast.38, f32[1,256]{1,0:T(1,128)} %bitcast.39, f32[1,256]{1,0:T(1,128)} %bitcast.40, s32[4,4]{1,0:T(4,128)} %pairs_ref.1), custom_call_target="tpu_custom_call" | custom-call | bytes 9000000 | tf_op jit(solution)/shard_map/pallas_call | solution.py:510
  39.6 0.7 collective-permute-start.11
  41.1 10.4 %shard_map.153 = (f32[17,128,128]{2,1,0:T(8,128)}, f32[15,128,128]{2,1,0:T(8,128)}, f32[18,2,128,128]{3,2,1,0:T(8,128)}, f32[14,2,128,128]{3,2,1,0:T(8,128)}, f3...) custom-call(f32[2048,128]{1,0:T(8,128)} %bitcast.22, ...), custom_call_target="tpu_custom_call" | custom-call | bytes 39000000 | tf_op jit(solution)/shard_map/pallas_call | solution.py:405
  51.5 7.8 %collective-permute-start.13 = (f32[896,128]{1,0:T(8,128)S(1)}, f32[896,128]{1,0:T(8,128)S(1)}, u32[]{:S(2)}, u32[]{:S(2)}) collective-permute-start(f32[896,128]{1,0:T(8,128)S(1)} %copy-done.10), channel_id=1, source_target_pairs={{3,2},{7,6},{11,10},{15,14},{19,18},{23,22},{27,26},{31,30}} | collective-permute-start | bytes 1376264 | tf_op jit(solution)/shard_map/ppermute | solution.py:445
  59.3 0.8 copy-done
  60.2 9.4 %shard_map.154 = (f32[1024,128]{1,0:T(8,128)}, f32[1032,128]{1,0:T(8,128)}, f32[128,128]{1,0:T(8,128)}, f32[2,2,160,128]{3,2,1,0:T(8,128)}, f32[2,160,128]{2,1,0:T(8,128)}) custom-call(f32[1320,128]{1,0:T(8,128)} %copy-done.1, f32[1320,128]{1,0:T(8,128)} %copy-done.2, f32[1320,128]{1,0:T(8,128)} %get-tuple-element.45.refs_2_, f32[1408,128]{1,0:T(8,128)} %copy-done, ...), custom_call_target="tpu_custom_call" | custom-call | bytes 36000000 | tf_op jit(solution)/shard_map/pallas_call | solution.py:405
  69.6 1.3 %collective-permute-start.10 = (f32[1032,128]{1,0:T(8,128)}, f32[1032,128]{1,0:T(8,128)S(1)}, u32[]{:S(2)}, u32[]{:S(2)}) collective-permute-start(f32[1032,128]{1,0:T(8,128)} %get-tuple-element.75), channel_id=1, source_target_pairs={{2,3},{6,7},{10,11},{14,15},{18,19},{22,23},{26,27},{30,31}} | collective-permute-start | bytes 1585160 | tf_op jit(solution)/shard_map/ppermute | solution.py:448
  70.9 0.7 copy-done.11
  72.1 8.2 %shard_map.155 = (f32[1024,128]{1,0:T(8,128)}, f32[1024,128]{1,0:T(8,128)}, f32[8,128]{1,0:T(8,128)}) custom-call(f32[896,128]{1,0:T(8,128)} %copy-done.11, f32[896,128]{1,0:T(8,128)} %copy-done.12, f32[896,128]{1,0:T(8,128)} %get-tuple-element.76.refs_2_, f32[896,128]{1,0:T(8,128)} %copy-done.13, f32[400,128]{1,0:T(8,128)} %copy-done.6, ...), custom_call_target="tpu_custom_call" | custom-call | bytes 30000000 | tf_op jit(solution)/shard_map/pallas_call | solution.py:405
  80.2 1.4 %collective-permute-start.14 = (f32[1024,128]{1,0:T(8,128)}, f32[1024,128]{1,0:T(8,128)S(1)}, u32[]{:S(2)}, u32[]{:S(2)}) collective-permute-start(f32[1024,128]{1,0:T(8,128)} %get-tuple-element.82), channel_id=1, source_target_pairs={{2,3},{6,7},{10,11},{14,15},{18,19},{22,23},{26,27},{30,31}} | collective-permute-start | bytes 1572872 | tf_op jit(solution)/shard_map/ppermute | solution.py:448
  82.4 1.5 %collective-permute-start.15 = (f32[128]{0:T(128)S(1)}, f32[128]{0:T(128)S(1)}, u32[]{:S(2)}, u32[]{:S(2)}) collective-permute-start(f32[128]{0:T(128)S(1)} %slice_bitcast_fusion), channel_id=1, source_target_pairs={{0,16},{16,0},{1,17},{17,1},{2,18},{18,2},{3,19},{19,3},{4,20},{20... | collective-permute-start | bytes 1544 | tf_op jit(solution)/shard_map/ppermute | solution.py:588
  83.9 2.1 %collective-permute-done.15 = f32[128]{0:T(128)S(1)} collective-permute-done((f32[128]{0:T(128)S(1)}, f32[128]{0:T(128)S(1)}, u32[]{:S(2)}, u32[]{:S(2)}) %collective-permute-start.15) | collective-permute-done | bytes 544 | tf_op jit(solution)/shard_map/ppermute | solution.py:588
  86.6 2.7 %collective-permute-start.16 = (f32[128]{0:T(128)S(1)}, f32[128]{0:T(128)S(1)}, u32[]{:S(2)}, u32[]{:S(2)}) collective-permute-start(f32[128]{0:T(128)S(1)} %fusion), channel_id=1, source_target_pairs={{0,3},{1,0},{2,1},{3,2},{4,7},{5,4},{6,5},{7,6},{8,11},{9,8},{10,9... | collective-permute-start | bytes 1544 | tf_op jit(solution)/shard_map/ppermute | solution.py:592
  89.3 2.4 %collective-permute-start.18 = (f32[128]{0:T(128)S(1)}, f32[128]{0:T(128)S(1)}, u32[]{:S(2)}, u32[]{:S(2)}) collective-permute-start(f32[128]{0:T(128)S(1)} %fusion), channel_id=1, source_target_pairs={{0,1},{1,2},{2,3},{3,0},{4,5},{5,6},{6,7},{7,4},{8,9},{9,10},{10,1... | collective-permute-start | bytes 1544 | tf_op jit(solution)/shard_map/ppermute | solution.py:592
  91.9 1.8 %collective-permute-done.17 = f32[128]{0:T(128)S(1)} collective-permute-done((f32[128]{0:T(128)S(1)}, f32[128]{0:T(128)S(1)}, u32[]{:S(2)}, u32[]{:S(2)}) %collective-permute-start.17) | collective-permute-done | bytes 544 | tf_op jit(solution)/shard_map/ppermute | solution.py:592
  93.7 3.5 %collective-permute-done.18 = f32[128]{0:T(128)S(1)} collective-permute-done((f32[128]{0:T(128)S(1)}, f32[128]{0:T(128)S(1)}, u32[]{:S(2)}, u32[]{:S(2)}) %collective-permute-start.18) | collective-permute-done | bytes 544 | tf_op jit(solution)/shard_map/ppermute | solution.py:592
  97.9 1.1 %pad_maximum_fusion = f32[64,32,128]{2,1,0:T(8,128)} fusion(f32[64,16,128]{2,1,0:T(8,128)S(1)} %bitcast.24, f32[64,16,128]{2,1,0:T(8,128)S(1)} %bitcast.23), kind=kLoop, calls=%fused_computation | loop fusion | flops 262144 | bytes 2097152 | tf_op jit(solution)/shard_map/concatenate | solution.py:597
  (56 shorter events, 5.5 us)
Async XLA Ops:
  0.6 25.1 %collective-permute-start.4 = (f32[64,32,128]{2,1,0:T(8,128)}, f32[64,32,128]{2,1,0:T(8,128)S(1)}, u32[]{:S(2)}, u32[]{:S(2)}) collective-permute-start(f32[64,32,128]{2,1,0:T(8,128)} %param.14), channel_id=1, source_target_pairs={{3,2},{7,6},{11,10},{15,14},{19,18},{23,22},{27,26},{31,30}} | collective-permute-start | bytes 3145736 | tf_op jit(solution)/shard_map/ppermute | solution.py:445
  7.6 27.1 %collective-permute-start = (f32[1320,128]{1,0:T(8,128)}, f32[1320,128]{1,0:T(8,128)S(1)}, u32[]{:S(2)}, u32[]{:S(2)}) collective-permute-start(f32[1320,128]{1,0:T(8,128)} %get-tuple-element.45.refs_2_), channel_id=1, source_target_pairs={{0,2},{2,1},{1,0},{4,6},{6,5},{5,4},{8,10},{10,9},{9,8},{12,14},{1... | collective-permute-start | bytes 2027528 | tf_op jit(solution)/shard_map/ppermute | solution.py:439
  8.3 8.1 %collective-permute-start.2 = (f32[520,128]{1,0:T(8,128)}, f32[520,128]{1,0:T(8,128)S(1)}, u32[]{:S(2)}, u32[]{:S(2)}) collective-permute-start(f32[520,128]{1,0:T(8,128)} %get-tuple-element.46), channel_id=1, source_target_pairs={{0,16},{16,0},{1,17},{17,1},{2,18},{18,2},{3,19},{19,3},{4,20},{20... | collective-permute-start | bytes 798728 | tf_op jit(solution)/shard_map/ppermute | solution.py:482
  9.8 29.8 %collective-permute-start.1 = (f32[1320,128]{1,0:T(8,128)}, f32[1320,128]{1,0:T(8,128)S(1)}, u32[]{:S(2)}, u32[]{:S(2)}) collective-permute-start(f32[1320,128]{1,0:T(8,128)} %get-tuple-element.45.refs_2_), channel_id=1, source_target_pairs={{0,1},{1,2},{4,5},{5,6},{8,9},{9,10},{12,13},{13,14},{16,17},{17,1... | collective-permute-start | bytes 2027528 | tf_op jit(solution)/shard_map/ppermute | solution.py:442
  18.9 13.6 %slice-start = ((f32[520,128]{1,0:T(8,128)}), f32[256,128]{1,0:T(8,128)S(1)}, s32[]{:S(2)}) async-start(f32[520,128]{1,0:T(8,128)} %copy-done.4), calls=%async_computation | async-start | bytes 262144 | tf_op jit(solution)/shard_map/slice | solution.py:527
  18.9 20.7 %copy-start.10 = (f32[896,128]{1,0:T(8,128)S(1)}, f32[896,128]{1,0:T(8,128)}, u32[]{:S(2)}) copy-start(f32[896,128]{1,0:T(8,128)} %get-tuple-element.76.refs_2_) | copy-start | bytes 1376260
  18.9 6.8 %collective-permute-start.5 = (f32[80,128]{1,0:T(8,128)}, f32[80,128]{1,0:T(8,128)S(1)}, u32[]{:S(2)}, u32[]{:S(2)}) collective-permute-start(f32[80,128]{1,0:T(8,128)} %get-tuple-element.53), channel_id=1, source_target_pairs={{0,4},{4,8},{8,12},{1,5},{5,9},{9,13},{2,6},{6,10},{10,14},{3,7},{... | collective-permute-start | bytes 122888 | tf_op jit(solution)/shard_map/ppermute | solution.py:497
  20.4 5.4 %collective-permute-start.6 = (f32[80,128]{1,0:T(8,128)}, f32[80,128]{1,0:T(8,128)S(1)}, u32[]{:S(2)}, u32[]{:S(2)}) collective-permute-start(f32[80,128]{1,0:T(8,128)} %get-tuple-element.54), channel_id=1, source_target_pairs={{4,0},{8,4},{12,8},{5,1},{9,5},{13,9},{6,2},{10,6},{14,10},{7,3},{... | collective-permute-start | bytes 122888 | tf_op jit(solution)/shard_map/ppermute | solution.py:498
  25.7 15.3 %copy-start.5 = (f32[64,32,128]{2,1,0:T(8,128)}, f32[64,32,128]{2,1,0:T(8,128)S(1)}, u32[]{:S(2)}) copy-start(f32[64,32,128]{2,1,0:T(8,128)S(1)} %collective-permute-done.4) | copy-start | bytes 3145732
  28.3 12.1 %collective-permute-start.7 = (f32[568,128]{1,0:T(8,128)}, f32[568,128]{1,0:T(8,128)S(1)}, u32[]{:S(2)}, u32[]{:S(2)}) collective-permute-start(f32[568,128]{1,0:T(8,128)} %get-tuple-element.57.refs_5_), channel_id=1, source_target_pairs={{3,2},{7,6},{11,10},{15,14},{19,18},{23,22},{27,26},{31,30}} | collective-permute-start | bytes 872456 | tf_op jit(solution)/shard_map/ppermute | solution.py:445
  32.6 26.7 %collective-permute-start.3 = (f32[1408,128]{1,0:T(8,128)S(1)}, f32[1408,128]{1,0:T(8,128)S(1)}, u32[]{:S(2)}, u32[]{:S(2)}) collective-permute-start(f32[1408,128]{1,0:T(8,128)S(1)} %pad_maximum_fusion.1), channel_id=1, source_target_pairs={{3,2},{7,6},{11,10},{15,14},{19,18},{23,22},{27,26},{31,30}} | collective-permute-start | bytes 2162696 | tf_op jit(solution)/shard_map/ppermute | solution.py:445
  34.0 17.5 %collective-permute-start.8 = (f32[400,128]{1,0:T(8,128)}, f32[400,128]{1,0:T(8,128)S(1)}, u32[]{:S(2)}, u32[]{:S(2)}) collective-permute-start(f32[400,128]{1,0:T(8,128)} %get-tuple-element.63.refs_6_), channel_id=1, source_target_pairs={{0,2},{2,1},{1,0},{4,6},{6,5},{5,4},{8,10},{10,9},{9,8},{12,14},{1... | collective-permute-start | bytes 614408 | tf_op jit(solution)/shard_map/ppermute | solution.py:439
  34.7 6.4 %copy-start.1 = (f32[1320,128]{1,0:T(8,128)}, f32[1320,128]{1,0:T(8,128)S(1)}, u32[]{:S(2)}) copy-start(f32[1320,128]{1,0:T(8,128)S(1)} %collective-permute-done.refs_2_.refs_0_) | copy-start | bytes 2027524
  34.7 16.8 %collective-permute-start.9 = (f32[400,128]{1,0:T(8,128)}, f32[400,128]{1,0:T(8,128)S(1)}, u32[]{:S(2)}, u32[]{:S(2)}) collective-permute-start(f32[400,128]{1,0:T(8,128)} %get-tuple-element.63.refs_6_), channel_id=1, source_target_pairs={{0,1},{1,2},{4,5},{5,6},{8,9},{9,10},{12,13},{13,14},{16,17},{17,1... | collective-permute-start | bytes 614408 | tf_op jit(solution)/shard_map/ppermute | solution.py:442
  39.6 1.4 %copy-start.2 = (f32[1320,128]{1,0:T(8,128)}, f32[1320,128]{1,0:T(8,128)S(1)}, u32[]{:S(2)}) copy-start(f32[1320,128]{1,0:T(8,128)S(1)} %collective-permute-done.1.refs_3_.refs_1_) | copy-start | bytes 2027524
  39.6 31.2 %collective-permute-start.11 = (f32[896,128]{1,0:T(8,128)S(1)}, f32[896,128]{1,0:T(8,128)S(1)}, u32[]{:S(2)}, u32[]{:S(2)}) collective-permute-start(f32[896,128]{1,0:T(8,128)S(1)} %copy-done.10), channel_id=1, source_target_pairs={{0,2},{2,1},{1,0},{4,6},{6,5},{5,4},{8,10},{10,9},{9,8},{12,14},{1... | collective-permute-start | bytes 1376264 | tf_op jit(solution)/shard_map/ppermute | solution.py:439
  40.3 30.5 %collective-permute-start.12 = (f32[896,128]{1,0:T(8,128)S(1)}, f32[896,128]{1,0:T(8,128)S(1)}, u32[]{:S(2)}, u32[]{:S(2)}) collective-permute-start(f32[896,128]{1,0:T(8,128)S(1)} %copy-done.10), channel_id=1, source_target_pairs={{0,1},{1,2},{4,5},{5,6},{8,9},{9,10},{12,13},{13,14},{16,17},{17,1... | collective-permute-start | bytes 1376264 | tf_op jit(solution)/shard_map/ppermute | solution.py:442
  51.5 7.8 %copy-start.6 = (f32[400,128]{1,0:T(8,128)}, f32[400,128]{1,0:T(8,128)S(1)}, u32[]{:S(2)}) copy-start(f32[400,128]{1,0:T(8,128)S(1)} %collective-permute-done.8.refs_4_) | copy-start | bytes 614404
  51.5 7.8 %copy-start.7 = (f32[400,128]{1,0:T(8,128)}, f32[400,128]{1,0:T(8,128)S(1)}, u32[]{:S(2)}) copy-start(f32[400,128]{1,0:T(8,128)S(1)} %collective-permute-done.9.refs_5_) | copy-start | bytes 614404
  51.5 19.4 %collective-permute-start.13 = (f32[896,128]{1,0:T(8,128)S(1)}, f32[896,128]{1,0:T(8,128)S(1)}, u32[]{:S(2)}, u32[]{:S(2)}) collective-permute-start(f32[896,128]{1,0:T(8,128)S(1)} %copy-done.10), channel_id=1, source_target_pairs={{3,2},{7,6},{11,10},{15,14},{19,18},{23,22},{27,26},{31,30}} | collective-permute-start | bytes 1376264 | tf_op jit(solution)/shard_map/ppermute | solution.py:445
  59.3 0.9 copy-start
  69.6 28.2 %collective-permute-start.10 = (f32[1032,128]{1,0:T(8,128)}, f32[1032,128]{1,0:T(8,128)S(1)}, u32[]{:S(2)}, u32[]{:S(2)}) collective-permute-start(f32[1032,128]{1,0:T(8,128)} %get-tuple-element.75), channel_id=1, source_target_pairs={{2,3},{6,7},{10,11},{14,15},{18,19},{22,23},{26,27},{30,31}} | collective-permute-start | bytes 1585160 | tf_op jit(solution)/shard_map/ppermute | solution.py:448
  70.9 0.8 copy-start.11
  70.9 1.0 copy-start.12
  70.9 1.1 %copy-start.13 = (f32[896,128]{1,0:T(8,128)}, f32[896,128]{1,0:T(8,128)S(1)}, u32[]{:S(2)}) copy-start(f32[896,128]{1,0:T(8,128)S(1)} %collective-permute-done.13.refs_3_) | copy-start | bytes 1376260
  72.1 25.7 %copy-start.8 = (f32[1024,128]{1,0:T(8,128)S(1)}, f32[1024,128]{1,0:T(8,128)}, u32[]{:S(2)}) copy-start(f32[1024,128]{1,0:T(8,128)} %get-tuple-element.84) | copy-start | bytes 1572868
  80.2 17.6 %copy-start.9 = (f32[1024,128]{1,0:T(8,128)S(1)}, f32[1024,128]{1,0:T(8,128)}, u32[]{:S(2)}) copy-start(f32[1024,128]{1,0:T(8,128)} %get-tuple-element.86) | copy-start | bytes 1572868
  80.2 17.5 %collective-permute-start.14 = (f32[1024,128]{1,0:T(8,128)}, f32[1024,128]{1,0:T(8,128)S(1)}, u32[]{:S(2)}, u32[]{:S(2)}) collective-permute-start(f32[1024,128]{1,0:T(8,128)} %get-tuple-element.82), channel_id=1, source_target_pairs={{2,3},{6,7},{10,11},{14,15},{18,19},{22,23},{26,27},{30,31}} | collective-permute-start | bytes 1572872 | tf_op jit(solution)/shard_map/ppermute | solution.py:448
  82.4 3.5 %collective-permute-start.15 = (f32[128]{0:T(128)S(1)}, f32[128]{0:T(128)S(1)}, u32[]{:S(2)}, u32[]{:S(2)}) collective-permute-start(f32[128]{0:T(128)S(1)} %slice_bitcast_fusion), channel_id=1, source_target_pairs={{0,16},{16,0},{1,17},{17,1},{2,18},{18,2},{3,19},{19,3},{4,20},{20... | collective-permute-start | bytes 1544 | tf_op jit(solution)/shard_map/ppermute | solution.py:588
  86.6 5.3 %collective-permute-start.16 = (f32[128]{0:T(128)S(1)}, f32[128]{0:T(128)S(1)}, u32[]{:S(2)}, u32[]{:S(2)}) collective-permute-start(f32[128]{0:T(128)S(1)} %fusion), channel_id=1, source_target_pairs={{0,3},{1,0},{2,1},{3,2},{4,7},{5,4},{6,5},{7,6},{8,11},{9,8},{10,9... | collective-permute-start | bytes 1544 | tf_op jit(solution)/shard_map/ppermute | solution.py:592
  89.3 4.4 %collective-permute-start.17 = (f32[128]{0:T(128)S(1)}, f32[128]{0:T(128)S(1)}, u32[]{:S(2)}, u32[]{:S(2)}) collective-permute-start(f32[128]{0:T(128)S(1)} %fusion), channel_id=1, source_target_pairs={{0,2},{1,3},{2,0},{3,1},{4,6},{5,7},{6,4},{7,5},{8,10},{9,11},{10,... | collective-permute-start | bytes 1544 | tf_op jit(solution)/shard_map/ppermute | solution.py:592
  89.3 7.9 %collective-permute-start.18 = (f32[128]{0:T(128)S(1)}, f32[128]{0:T(128)S(1)}, u32[]{:S(2)}, u32[]{:S(2)}) collective-permute-start(f32[128]{0:T(128)S(1)} %fusion), channel_id=1, source_target_pairs={{0,1},{1,2},{2,3},{3,0},{4,5},{5,6},{6,7},{7,4},{8,9},{9,10},{10,1... | collective-permute-start | bytes 1544 | tf_op jit(solution)/shard_map/ppermute | solution.py:592
  (4 other events, 2.7 us)

commit v10 on v9

--- a/solution.py
+++ b/solution.py
@@ -12,7 +12,9 @@
 EDGE = 16
 gate_width = 0.5
 BATCH = 8
-MICRO = 3 * 10**6
+EDGE = 16
+gate_width = 0.5
+BATCH = 8
 VMEM_LIMIT = 56 * 2**20
 
 
@@ -192,16 +194,20 @@
     return jnp.concatenate([left[:, lanes], right[:, lanes]], axis=1)
 
 
-def load_shares(shares, length, center_ref, lower_ref, upper_ref, side_ref):
-    for t in range(2):
-        left, right = [ref[pl.ds(start, length + 8), :] for ref, start in shares[2 * t : 2 * t + 2]]
-        inward = pair(left[:length], right[:length], 0)
-        outward = pair(left[:length], right[:length], 1)
-        side = pair(left[length:], right[length:], 0)[:1]
-        lower_ref[t] = inward
-        upper_ref[t] = outward
-        side_ref[t : t + 1] = side
-        center_ref[t] = 1.0 - inward - outward - 2.0 * side
+def moved_spans(cuts):
+    ends = [0, *(cut - 1 for cut in cuts[1:-1]), cuts[-1]]
+    return list(zip(ends, ends[1:]))
+
+
+def load_shares(shares, t, length, center_ref, lower_ref, upper_ref, side_ref):
+    left, right = [ref[pl.ds(start, length + 8), :] for ref, start in shares[2 * t : 2 * t + 2]]
+    inward = pair(left[:length], right[:length], 0)
+    outward = pair(left[:length], right[:length], 1)
+    side = pair(left[length:], right[length:], 0)[:1]
+    lower_ref[t] = inward
+    upper_ref[t] = outward
+    side_ref[t : t + 1] = side
+    center_ref[t] = 1.0 - inward - outward - 2.0 * side
 
 
 def forward_kernel(azimuth, radial, cuts, *refs):
@@ -209,15 +215,28 @@
     refs = refs[10:]
     groups = len(cuts) - 1
     moved_refs, second_refs = refs[:groups], refs[groups : 2 * groups]
-    center_ref, inward_ref, outward_ref, side_ref, slab, mixed = refs[2 * groups :]
+    center_ref, inward_ref, outward_ref, side_ref, slab, mixed, held, moved_all, second_all, sems = refs[2 * groups :]
     inner = pl.ds(EDGE, radial)
     wide = radial + 16
     outer = pl.ds(8, wide)
     length = radial + 2 * EDGE
     strips = 4 * (azimuth + 4)
     first_rows = RANGE * cuts[1]
-    shares = [(far_ref, first_rows), (near_ref, first_rows), (share_ref, 0), (next_halo, strips + 4 * RANGE)]
-    load_shares(shares, length, center_ref, inward_ref, outward_ref, side_ref)
+    loads = [
+        pltpu.make_async_copy(ref.at[pl.ds(first_rows, length + 8)], held.at[k], sems.at[k])
+        for k, ref in enumerate((far_ref, near_ref))
+    ]
+    for load in loads:
+        load.start()
+    stores = []
+
+    def store(source, target):
+        copy = pltpu.make_async_copy(source, target, sems.at[2 + len(stores)])
+        copy.start()
+        stores.append(copy)
+
+    shares = [None, None, (share_ref, 0), (next_halo, strips + 4 * RANGE)]
+    load_shares(shares, 1, length, center_ref, inward_ref, outward_ref, side_ref)
 
     def place(row, source, other, start, stride):
         bins = jnp.concatenate(
@@ -261,27 +280,38 @@
 
     move([1, azimuth + 2])
 
+    for rows in batches(0, azimuth):
+        for a, moved in zip(rows, move([a + 2 for a in rows])):
+            moved_all[a] = widened(slope_ref, slice(None), a) * moved
+    for g, (low, high) in enumerate(moved_spans(cuts)):
+        store(moved_all.at[pl.ds(low, high - low)], moved_refs[g])
+
+    for load in loads:
+        load.wait()
+    shares = [(held.at[0], 0), (held.at[1], 0), (share_ref, 0), (next_halo, strips + 4 * RANGE)]
+    load_shares(shares, 0, length, center_ref, inward_ref, outward_ref, side_ref)
+
     for g, (low, high) in enumerate(zip(cuts, cuts[1:])):
         for rows in batches(low, high):
-            for a, moved in zip(rows, move([a + 2 for a in rows])):
-                h, start = (g, max(low - 1, 0)) if a < high - 1 or high == azimuth else (g + 1, high - 1)
-                moved_refs[h][a - start] = widened(slope_ref, slice(None), a) * moved
-
-    for g, (low, high) in enumerate(zip(cuts, cuts[1:])):
-        for a in range(low, high):
-            slope = widened(slope_ref, slice(None), a)
-            for t in range(2):
-                second = stencil(
-                    mixed,
-                    lambda d: (a + 2 + d, t),
-                    center_ref[t, inner, :],
-                    outward_ref[t, pl.ds(EDGE - 1, radial), :],
-                    inward_ref[t, pl.ds(EDGE + 1, radial), :],
-                    side_ref[t : t + 1, :],
-                    EDGE,
-                    radial,
-                )
-                second_refs[g][a - low, t] = slope * second
+            for a in rows:
+                slope = widened(slope_ref, slice(None), a)
+                for t in range(2):
+                    second = stencil(
+                        mixed,
+                        lambda d: (a + 2 + d, t),
+                        center_ref[t, inner, :],
+                        outward_ref[t, pl.ds(EDGE - 1, radial), :],
+                        inward_ref[t, pl.ds(EDGE + 1, radial), :],
+                        side_ref[t : t + 1, :],
+                        EDGE,
+                        radial,
+                    )
+                    second_all[a, t] = slope * second
+            size = len(rows)
+            store(second_all.at[pl.ds(rows[0], size)], second_refs[g].at[pl.ds(rows[0] - low, size)])
+
+    for copy in stores:
+        copy.wait()
 
 
 def adjoint_kernel(azimuth, radial, low_row, high_row, offsets, *refs):
@@ -295,14 +325,22 @@
 
     slots = take(4)
     halos = take(4)
-    next_sides = take(1) if first or last else None
+    next_sides = slots[3:] if first else take(1)
     center_ref, lower_ref, upper_ref, side_ref = take(4)
     gate_ref, second_ref, moved_ref = take(3)
     table1_ref, table2_ref = take(2)
     carry_second, carry_first, carry_sum = (None, None, None) if first else take(3)
     own_out, next_out, sum_out = take(3)
     keep_second, keep_first = (None, None) if last else take(2)
-    second, initial = refs
+    second, initial, second_held, moved_held, table_held, sems = refs
+    loads = [
+        pltpu.make_async_copy(source, target, sems.at[k])
+        for k, (source, target) in enumerate(
+            ((second_ref, second_held), (moved_ref, moved_held), (table2_ref, table_held))
+        )
+    ]
+    for load in loads:
+        load.start()
 
     inner = pl.ds(EDGE, radial)
     wide = radial + 16
@@ -342,6 +380,8 @@
     total = jnp.zeros((radial, LANES), jnp.float32) if first else carry_sum[...]
     for group in batches(low_row, high_row):
         result = product(jnp.concatenate([bins_of(row) for row in group], axis=1), table1_ref, 0)
+        if group[0] == low_row:
+            loads[0].wait()
         for k, row in enumerate(group):
             part = result[k * radial : (k + 1) * radial]
             gate = widened(gate_ref, inner, row)
@@ -349,8 +389,10 @@
                 frag = part[:, (t + 2) * LANES : (t + 3) * LANES]
                 second[row - base, t, inner, :] = part[:, t * LANES : (t + 1) * LANES] + gate * frag
                 if own_low <= row < own_high:
-                    total += second_ref[row - own_low, t] * frag
-
+                    total += second_held[row - own_low, t] * frag
+
+    loads[1].wait()
+    loads[2].wait()
     for group in batches(first_low, first_high):
         parts = []
         for row in group:
@@ -368,13 +410,13 @@
                 for t in range(2)
             ]
             parts.append(jnp.concatenate(halves, axis=1))
-        result = product(jnp.concatenate(parts, axis=0), table2_ref)
+        result = product(jnp.concatenate(parts, axis=0), table_held)
         for k, row in enumerate(group):
             part = result[k * wide : (k + 1) * wide]
             frag = part[:, LANES:]
             initial[row - first_base, outer, :] = part[:, :LANES] + widened(gate_ref, outer, row) * frag
             if 2 <= row < azimuth + 2:
-                total += moved_ref[row - max(first_low, 2)] * frag[8 : 8 + radial]
+                total += moved_held[row - max(first_low, 2)] * frag[8 : 8 + radial]
     if last:
         sum_out[...] = jnp.broadcast_to(jnp.sum(total.T, axis=0, keepdims=True), sum_out.shape)
     else:
@@ -400,16 +442,21 @@
         keep_first[...] = initial[pl.ds(first_high - 2 - first_base, 2)]
 
 
-def call(kernel, outs, scratch, operands, micros=1):
-    vmem = pl.BlockSpec(memory_space=pltpu.VMEM)
+def call(kernel, outs, scratch, operands, any_in=(), any_out=(), copies=0):
+    def spec(is_any):
+        return pl.BlockSpec(memory_space=pl.ANY if is_any else pltpu.VMEM)
+
+    semaphores = [pltpu.SemaphoreType.DMA((copies,))] if copies else []
     return pl.pallas_call(
         kernel,
         out_shape=[jax.ShapeDtypeStruct(o, jnp.float32) for o in outs],
-        in_specs=[vmem] * len(operands),
-        out_specs=[vmem] * len(outs),
-        scratch_shapes=[pltpu.VMEM(s, jnp.float32) for s in scratch],
+        in_specs=[spec(k in any_in) for k in range(len(operands))],
+        out_specs=[spec(k in any_out) for k in range(len(outs))],
+        scratch_shapes=[
+            pltpu.VMEM(s, jnp.float32) if isinstance(s, tuple) else pltpu.VMEM(s.shape, s.dtype) for s in scratch
+        ]
+        + semaphores,
         compiler_params=pltpu.CompilerParams(vmem_limit_bytes=VMEM_LIMIT),
-        cost_estimate=pl.CostEstimate(flops=0, bytes_accessed=micros * MICRO, transcendentals=0),
     )(*operands)
 
 
@@ -513,7 +560,6 @@
         in_specs=[vmem] * 5 + [pl.BlockSpec(memory_space=pltpu.SMEM)],
         out_specs=[vmem] * 3,
         compiler_params=pltpu.CompilerParams(vmem_limit_bytes=VMEM_LIMIT),
-        cost_estimate=pl.CostEstimate(flops=0, bytes_accessed=3 * MICRO, transcendentals=0),
     )(
         frag_gain,
         dest_bins[None, :],
@@ -524,6 +570,7 @@
     )
 
     long_next = ending(long)
+    long, other = lax.optimization_barrier((long, other))
     first_next = jnp.concatenate([opening[: own_bins * cuts[1]], other[: 4 * own_bins]], axis=0)
     halo_refs = [far(short), near(short), short, long_next]
     first_next = ending(first_next)
@@ -532,10 +579,16 @@
     coefs = [(2, length, LANES)] * 3 + [(2, LANES)]
     products = list(call(
         functools.partial(forward_kernel, azimuth, radial, cuts),
-        [(j - (j < azimuth) - max(i - 1, 0), radial, LANES) for i, j in spans]
+        [(j - i, radial, LANES) for i, j in moved_spans(cuts)]
         + [(j - i, 2, radial, LANES) for i, j in spans]
         + coefs,
-        [(count, length, LANES), (count, 2, length, LANES)],
+        [
+            (count, length, LANES),
+            (count, 2, length, LANES),
+            (2, share_rows, LANES),
+            (azimuth, radial, LANES),
+            (azimuth, 2, radial, LANES),
+        ],
         [
             flat(density),
             flat(density_next),
@@ -548,7 +601,9 @@
             slope,
             own_rows,
         ],
-        13,
+        any_in=(2, 3),
+        any_out=range(2 * len(spans)),
+        copies=2 + len(spans) + sum(len(batches(i, j)) for i, j in spans),
     ))
     groups = len(spans)
     products[0], halo_refs[0], halo_refs[1], late = lax.optimization_barrier(
@@ -566,8 +621,9 @@
         n_out = (azimuth + 2 if last else high_row - 2) - (2 if first else low_row - 2)
         operands = [*gathered[min(g, 1)]]
         offsets = [(cuts[0], cuts[1]) if first else (cuts[1], azimuth - cuts[1])] * 4
-        operands += halo_refs + ([first_next] if first or last else [])
+        operands += halo_refs + ([] if first else [first_next])
         operands += [*coefs, gates, second[g], moved[g]]
+        held = len(operands) - 2
         operands += [both, own_cols, *carry]
         outs = [(RANGE * n_out, radial), (RANGE * n_out + 8 * first, radial), (8, radial) if last else (radial, LANES)]
         if not last:
@@ -575,9 +631,16 @@
         own_out, next_out, total, *kept = call(
             functools.partial(adjoint_kernel, azimuth, radial, low_row, high_row, offsets),
             outs,
-            [(new + 2, 2, length, LANES), (new + 2, length, LANES)],
+            [
+                (new + 2, 2, length, LANES),
+                (new + 2, length, LANES),
+                second[g].shape,
+                moved[g].shape,
+                own_cols,
+            ],
             operands,
-            2 + new // 2,
+            any_in=(held, held + 1, held + 3),
+            copies=3,
         )
         carry = [*kept, total]
         own_outs.append(own_out)

time: 101 us -> 99.9 us (0.989)
  transfers between devices with their start and end apart: 19 -> 19, of which waited for: 6 -> 6; matrix products, arithmetic and copies ran while one was open for 3% -> 3% of each run, Pallas kernels for 41% -> 40%
where the time goes in v10:
time: 99.9 us; the launch traced here: 98.3 us
  Pallas kernels  39.7 us (40%)
  starting transfers between devices  33.5 us (34%)
  waiting for transfers between devices  16.4 us (16%)
  local copies, waits for them, and re-layouts  5.17 us (5%)
  other arithmetic  2.51 us (3%)
  between operations  1.03 us (1%)
    pallas_call x6, Pallas kernels, call(): pl.pallas_call(kernel, out_shape=[jax.ShapeDtypeStruct(o, jnp.float32) fo...  35.4 us
    ppermute x4, starting transfers between devices, ending(): return lax.ppermute(x, 'mass', [(3, 2)])  15.8 us
    ppermute x1, waiting for transfers between devices, per_device(): other = lax.ppermute(sides, 'phi', ring)  5.87 us
    ppermute x3, waiting for transfers between devices, per_device(): lax.ppermute(speed_gradient, 'mass', [(i, (i + k) % size) for i in range(...  5.53 us
    ppermute x3, starting transfers between devices, per_device(): lax.ppermute(speed_gradient, 'mass', [(i, (i + k) % size) for i in range(...  5.06 us
    pallas_call x1, Pallas kernels, per_device(): pl.pallas_call(table_kernel, out_shape=[jax.ShapeDtypeStruct((3 * total_b...  4.26 us
    unnamed x32, local copies, waits for them, and re-layouts  3.35 us
    ppermute x4, waiting for transfers between devices, ending(): return lax.ppermute(x, 'mass', [(3, 2)])  2.95 us
  transfers between devices with their start and end apart: 19, of which 6 were waited for; matrix products, arithmetic and copies ran while one was open for 3% of the time, Pallas kernels for 40%

profile of v10, /device:TPU:24, one launch (start us, length us, event | category | flops | bytes accessed | tf_op | source)
XLA Modules:
  0.0 98.3 jit_solution(9930643722757163715)
XLA Ops:
  0.6 2.4 %collective-permute-start.5 = (f32[64,32,128]{2,1,0:T(8,128)}, f32[64,32,128]{2,1,0:T(8,128)S(1)}, u32[]{:S(2)}, u32[]{:S(2)}) collective-permute-start(f32[64,32,128]{2,1,0:T(8,128)} %param.14), channel_id=1, source_target_pairs={{3,2},{7,6},{11,10},{15,14},{19,18},{23,22},{27,26},{31,30}} | collective-permute-start | bytes 3145736 | tf_op jit(solution)/shard_map/ppermute | solution.py:492
  3.1 4.5 %shard_map.149 = (f32[520,128]{1,0:T(8,128)}, f32[32,128]{1,0:T(8,128)}, f32[128,128]{1,0:T(8,128)}, f32[1320,128]{1,0:T(8,128)}, f32[168,128]{1,0:T(8,128)}, /*...) custom-call(f32[2048,128]{1,0:T(8,128)} %bitcast.25, f32[2048,128]{1,0:T(8,128)} %bitcast.21, ...), custom_call_target="tpu_custom_call" | custom-call | tf_op jit(solution)/shard_map/pallas_call | solution.py:450
  7.6 0.7 collective-permute-start
  8.3 1.6 %collective-permute-start.2 = (f32[520,128]{1,0:T(8,128)}, f32[520,128]{1,0:T(8,128)S(1)}, u32[]{:S(2)}, u32[]{:S(2)}) collective-permute-start(f32[520,128]{1,0:T(8,128)} %get-tuple-element.48), channel_id=1, source_target_pairs={{0,16},{16,0},{1,17},{17,1},{2,18},{18,2},{3,19},{19,3},{4,20},{20... | collective-permute-start | bytes 798728 | tf_op jit(solution)/shard_map/ppermute | solution.py:529
  9.8 0.7 collective-permute-start.1
  10.5 5.9 %collective-permute-done.2.sides_ref = f32[520,128]{1,0:T(8,128)S(1)} collective-permute-done((f32[520,128]{1,0:T(8,128)}, f32[520,128]{1,0:T(8,128)S(1)}, u32[]{:S(2)}, u32[]{:S(2)}) %collective-permute-start.2) | collective-permute-done | bytes 266272 | tf_op jit(solution)/shard_map/ppermute | solution.py:529
  16.4 0.7 copy-done.4
  17.1 1.8 %shard_map.150 = (f32[80,128]{1,0:T(8,128)}, f32[80,128]{1,0:T(8,128)}, f32[128,128]{1,0:T(8,128)}) custom-call(f32[520,128]{1,0:T(8,128)} %copy-done.4, f32[64,128]{1,0:T(8,128)} %bitcast.27, f32[64,128]{1,0:T(8,128)} %bitcast.28, f32[32,128]{1,0:T(8,128)} %get-tuple-element.51.gate_ref), custom_call_target="tpu_custom_call" | custom-call | tf_op jit(solution)/shard_map/pallas_call | solution.py:450
  18.9 1.4 %collective-permute-start.3 = (f32[80,128]{1,0:T(8,128)}, f32[80,128]{1,0:T(8,128)S(1)}, u32[]{:S(2)}, u32[]{:S(2)}) collective-permute-start(f32[80,128]{1,0:T(8,128)} %get-tuple-element.52), channel_id=1, source_target_pairs={{0,4},{4,8},{8,12},{1,5},{5,9},{9,13},{2,6},{6,10},{10,14},{3,7},{... | collective-permute-start | bytes 122888 | tf_op jit(solution)/shard_map/ppermute | solution.py:544
  20.4 1.3 %collective-permute-start.4 = (f32[80,128]{1,0:T(8,128)}, f32[80,128]{1,0:T(8,128)S(1)}, u32[]{:S(2)}, u32[]{:S(2)}) collective-permute-start(f32[80,128]{1,0:T(8,128)} %get-tuple-element.53), channel_id=1, source_target_pairs={{4,0},{8,4},{12,8},{5,1},{9,5},{13,9},{6,2},{10,6},{14,10},{7,3},{... | collective-permute-start | bytes 122888 | tf_op jit(solution)/shard_map/ppermute | solution.py:545
  21.7 1.1 %slice.12 = f32[1152,128]{1,0:T(8,128)S(1)} slice(f32[1320,128]{1,0:T(8,128)} %get-tuple-element.47.refs_2_), slice={[0:1152], [0:128]} | slice | bytes 1179648 | tf_op jit(solution)/shard_map/slice | solution.py:574
  22.8 2.9 %collective-permute-done.5 = f32[64,32,128]{2,1,0:T(8,128)S(1)} collective-permute-done((f32[64,32,128]{2,1,0:T(8,128)}, f32[64,32,128]{2,1,0:T(8,128)S(1)}, u32[]{:S(2)}, u32[]{:S(2)}) %collective-permute-start.5) | collective-permute-done | bytes 1048608 | tf_op jit(solution)/shard_map/ppermute | solution.py:492
  26.4 1.9 %shard_map.151 = (f32[568,128]{1,0:T(8,128)}, f32[400,128]{1,0:T(8,128)}, f32[160,128]{1,0:T(8,128)}) custom-call(f32[80,128]{1,0:T(8,128)} %copy-done.14, f32[80,128]{1,0:T(8,128)} %copy-done.15, f32[520,128]{1,0:T(8,128)} %copy-done.4, f32[168,128]{1,0:T(8,128)} %get-tuple-element.54.shares_ref.refs_4_, f32[128,128]{1,0:T(8,128)} %get-tuple-element.56.gates_ref), custom_call_target="tpu_custom_call" | custom-call | tf_op jit(solution)/shard_map/pallas_call | solution.py:450
  28.3 4.3 %collective-permute-start.7 = (f32[568,128]{1,0:T(8,128)}, f32[568,128]{1,0:T(8,128)S(1)}, u32[]{:S(2)}, u32[]{:S(2)}) collective-permute-start(f32[568,128]{1,0:T(8,128)} %get-tuple-element.61.refs_5_), channel_id=1, source_target_pairs={{3,2},{7,6},{11,10},{15,14},{19,18},{23,22},{27,26},{31,30}} | collective-permute-start | bytes 872456 | tf_op jit(solution)/shard_map/ppermute | solution.py:492
  32.6 1.3 %collective-permute-start.6 = (f32[1408,128]{1,0:T(8,128)S(1)}, f32[1408,128]{1,0:T(8,128)S(1)}, u32[]{:S(2)}, u32[]{:S(2)}) collective-permute-start(f32[1408,128]{1,0:T(8,128)S(1)} %pad_maximum_fusion.1), channel_id=1, source_target_pairs={{3,2},{7,6},{11,10},{15,14},{19,18},{23,22},{27,26},{31,30}} | collective-permute-start | bytes 2162696 | tf_op jit(solution)/shard_map/ppermute | solution.py:492
  35.4 4.3 %shard_map.152 = (bf16[768,512]{1,0:T(8,128)(2,1)}, bf16[768,256]{1,0:T(8,128)(2,1)}, bf16[768,256]{1,0:T(8,128)(2,1)}) custom-call(f32[256,256]{1,0:T(8,128)} %gain_ref, s32[1,256]{1,0:T(1,128)} %bitcast.37, f32[1,256]{1,0:T(1,128)} %bitcast.38, f32[1,256]{1,0:T(1,128)} %bitcast.39, f32[1,256]{1,0:T(1,128)} %bitcast.40, s32[4,4]{1,0:T(4,128)} %pairs_ref.1), custom_call_target="tpu_custom_call" | custom-call | tf_op jit(solution)/shard_map/pallas_call | solution.py:557
  39.6 0.7 collective-permute-start.11
  41.1 9.9 %shard_map.153 = (f32[17,128,128]{2,1,0:T(8,128)}, f32[15,128,128]{2,1,0:T(8,128)}, f32[18,2,128,128]{3,2,1,0:T(8,128)}, f32[14,2,128,128]{3,2,1,0:T(8,128)}, f3...) custom-call(f32[2048,128]{1,0:T(8,128)} %bitcast.22, ...), custom_call_target="tpu_custom_call" | custom-call | tf_op jit(solution)/shard_map/pallas_call | solution.py:450
  51.0 7.8 %collective-permute-start.13 = (f32[896,128]{1,0:T(8,128)S(1)}, f32[896,128]{1,0:T(8,128)S(1)}, u32[]{:S(2)}, u32[]{:S(2)}) collective-permute-start(f32[896,128]{1,0:T(8,128)S(1)} %copy-done.10), channel_id=1, source_target_pairs={{3,2},{7,6},{11,10},{15,14},{19,18},{23,22},{27,26},{31,30}} | collective-permute-start | bytes 1376264 | tf_op jit(solution)/shard_map/ppermute | solution.py:492
  58.8 0.8 copy-done
  59.7 9.1 %shard_map.154 = (f32[1024,128]{1,0:T(8,128)}, f32[1032,128]{1,0:T(8,128)}, f32[128,128]{1,0:T(8,128)}, f32[2,2,160,128]{3,2,1,0:T(8,128)}, f32[2,160,128]{2,1,0:T(8,128)}) custom-call(f32[1320,128]{1,0:T(8,128)} %copy-done.1, f32[1320,128]{1,0:T(8,128)} %copy-done.2, f32[1320,128]{1,0:T(8,128)} %get-tuple-element.47.refs_2_, f32[1408,128]{1,0:T(8,128)} %copy-done, ...), custom_call_target="tpu_custom_call" | custom-call | tf_op jit(solution)/shard_map/pallas_call | solution.py:450
  68.8 1.3 %collective-permute-start.10 = (f32[1032,128]{1,0:T(8,128)}, f32[1032,128]{1,0:T(8,128)S(1)}, u32[]{:S(2)}, u32[]{:S(2)}) collective-permute-start(f32[1032,128]{1,0:T(8,128)} %get-tuple-element.79), channel_id=1, source_target_pairs={{2,3},{6,7},{10,11},{14,15},{18,19},{22,23},{26,27},{30,31}} | collective-permute-start | bytes 1585160 | tf_op jit(solution)/shard_map/ppermute | solution.py:495
  70.2 0.7 copy-done.11
  71.3 8.2 %shard_map.155 = (f32[1024,128]{1,0:T(8,128)}, f32[1024,128]{1,0:T(8,128)}, f32[8,128]{1,0:T(8,128)}) custom-call(f32[896,128]{1,0:T(8,128)} %copy-done.11, f32[896,128]{1,0:T(8,128)} %copy-done.12, f32[896,128]{1,0:T(8,128)} %get-tuple-element.80.refs_2_, f32[896,128]{1,0:T(8,128)} %copy-done.13, f32[400,128]{1,0:T(8,128)} %copy-done.6, ...), custom_call_target="tpu_custom_call" | custom-call | tf_op jit(solution)/shard_map/pallas_call | solution.py:450
  79.5 1.4 %collective-permute-start.14 = (f32[1024,128]{1,0:T(8,128)}, f32[1024,128]{1,0:T(8,128)S(1)}, u32[]{:S(2)}, u32[]{:S(2)}) collective-permute-start(f32[1024,128]{1,0:T(8,128)} %get-tuple-element.86), channel_id=1, source_target_pairs={{2,3},{6,7},{10,11},{14,15},{18,19},{22,23},{26,27},{30,31}} | collective-permute-start | bytes 1572872 | tf_op jit(solution)/shard_map/ppermute | solution.py:495
  81.6 1.5 %collective-permute-start.15 = (f32[128]{0:T(128)S(1)}, f32[128]{0:T(128)S(1)}, u32[]{:S(2)}, u32[]{:S(2)}) collective-permute-start(f32[128]{0:T(128)S(1)} %slice_bitcast_fusion), channel_id=1, source_target_pairs={{0,16},{16,0},{1,17},{17,1},{2,18},{18,2},{3,19},{19,3},{4,20},{20... | collective-permute-start | bytes 1544 | tf_op jit(solution)/shard_map/ppermute | solution.py:651
  83.1 2.1 %collective-permute-done.15 = f32[128]{0:T(128)S(1)} collective-permute-done((f32[128]{0:T(128)S(1)}, f32[128]{0:T(128)S(1)}, u32[]{:S(2)}, u32[]{:S(2)}) %collective-permute-start.15) | collective-permute-done | bytes 544 | tf_op jit(solution)/shard_map/ppermute | solution.py:651
  85.8 2.7 %collective-permute-start.16 = (f32[128]{0:T(128)S(1)}, f32[128]{0:T(128)S(1)}, u32[]{:S(2)}, u32[]{:S(2)}) collective-permute-start(f32[128]{0:T(128)S(1)} %fusion), channel_id=1, source_target_pairs={{0,3},{1,0},{2,1},{3,2},{4,7},{5,4},{6,5},{7,6},{8,11},{9,8},{10,9... | collective-permute-start | bytes 1544 | tf_op jit(solution)/shard_map/ppermute | solution.py:655
  88.5 2.4 %collective-permute-start.18 = (f32[128]{0:T(128)S(1)}, f32[128]{0:T(128)S(1)}, u32[]{:S(2)}, u32[]{:S(2)}) collective-permute-start(f32[128]{0:T(128)S(1)} %fusion), channel_id=1, source_target_pairs={{0,1},{1,2},{2,3},{3,0},{4,5},{5,6},{6,7},{7,4},{8,9},{9,10},{10,1... | collective-permute-start | bytes 1544 | tf_op jit(solution)/shard_map/ppermute | solution.py:655
  91.2 1.8 %collective-permute-done.17 = f32[128]{0:T(128)S(1)} collective-permute-done((f32[128]{0:T(128)S(1)}, f32[128]{0:T(128)S(1)}, u32[]{:S(2)}, u32[]{:S(2)}) %collective-permute-start.17) | collective-permute-done | bytes 544 | tf_op jit(solution)/shard_map/ppermute | solution.py:655
  93.0 3.5 %collective-permute-done.18 = f32[128]{0:T(128)S(1)} collective-permute-done((f32[128]{0:T(128)S(1)}, f32[128]{0:T(128)S(1)}, u32[]{:S(2)}, u32[]{:S(2)}) %collective-permute-start.18) | collective-permute-done | bytes 544 | tf_op jit(solution)/shard_map/ppermute | solution.py:655
  97.1 1.1 %pad_maximum_fusion = f32[64,32,128]{2,1,0:T(8,128)} fusion(f32[64,16,128]{2,1,0:T(8,128)S(1)} %bitcast.24, f32[64,16,128]{2,1,0:T(8,128)S(1)} %bitcast.23), kind=kLoop, calls=%fused_computation | loop fusion | flops 262144 | bytes 2097152 | tf_op jit(solution)/shard_map/concatenate | solution.py:660
  (56 shorter events, 5.5 us)
Async XLA Ops:
  0.6 25.1 %collective-permute-start.5 = (f32[64,32,128]{2,1,0:T(8,128)}, f32[64,32,128]{2,1,0:T(8,128)S(1)}, u32[]{:S(2)}, u32[]{:S(2)}) collective-permute-start(f32[64,32,128]{2,1,0:T(8,128)} %param.14), channel_id=1, source_target_pairs={{3,2},{7,6},{11,10},{15,14},{19,18},{23,22},{27,26},{31,30}} | collective-permute-start | bytes 3145736 | tf_op jit(solution)/shard_map/ppermute | solution.py:492
  7.6 27.1 %collective-permute-start = (f32[1320,128]{1,0:T(8,128)}, f32[1320,128]{1,0:T(8,128)S(1)}, u32[]{:S(2)}, u32[]{:S(2)}) collective-permute-start(f32[1320,128]{1,0:T(8,128)} %get-tuple-element.47.refs_2_), channel_id=1, source_target_pairs={{0,2},{2,1},{1,0},{4,6},{6,5},{5,4},{8,10},{10,9},{9,8},{12,14},{1... | collective-permute-start | bytes 2027528 | tf_op jit(solution)/shard_map/ppermute | solution.py:486
  8.3 8.1 %collective-permute-start.2 = (f32[520,128]{1,0:T(8,128)}, f32[520,128]{1,0:T(8,128)S(1)}, u32[]{:S(2)}, u32[]{:S(2)}) collective-permute-start(f32[520,128]{1,0:T(8,128)} %get-tuple-element.48), channel_id=1, source_target_pairs={{0,16},{16,0},{1,17},{17,1},{2,18},{18,2},{3,19},{19,3},{4,20},{20... | collective-permute-start | bytes 798728 | tf_op jit(solution)/shard_map/ppermute | solution.py:529
  9.8 29.8 %collective-permute-start.1 = (f32[1320,128]{1,0:T(8,128)}, f32[1320,128]{1,0:T(8,128)S(1)}, u32[]{:S(2)}, u32[]{:S(2)}) collective-permute-start(f32[1320,128]{1,0:T(8,128)} %get-tuple-element.47.refs_2_), channel_id=1, source_target_pairs={{0,1},{1,2},{4,5},{5,6},{8,9},{9,10},{12,13},{13,14},{16,17},{17,1... | collective-permute-start | bytes 2027528 | tf_op jit(solution)/shard_map/ppermute | solution.py:489
  18.9 13.6 %slice-start = ((f32[520,128]{1,0:T(8,128)}), f32[256,128]{1,0:T(8,128)S(1)}, s32[]{:S(2)}) async-start(f32[520,128]{1,0:T(8,128)} %copy-done.4), calls=%async_computation | async-start | bytes 262144 | tf_op jit(solution)/shard_map/slice | solution.py:574
  18.9 20.7 %copy-start.10 = (f32[896,128]{1,0:T(8,128)S(1)}, f32[896,128]{1,0:T(8,128)}, u32[]{:S(2)}) copy-start(f32[896,128]{1,0:T(8,128)} %get-tuple-element.80.refs_2_) | copy-start | bytes 1376260
  18.9 6.8 %collective-permute-start.3 = (f32[80,128]{1,0:T(8,128)}, f32[80,128]{1,0:T(8,128)S(1)}, u32[]{:S(2)}, u32[]{:S(2)}) collective-permute-start(f32[80,128]{1,0:T(8,128)} %get-tuple-element.52), channel_id=1, source_target_pairs={{0,4},{4,8},{8,12},{1,5},{5,9},{9,13},{2,6},{6,10},{10,14},{3,7},{... | collective-permute-start | bytes 122888 | tf_op jit(solution)/shard_map/ppermute | solution.py:544
  20.4 5.4 %collective-permute-start.4 = (f32[80,128]{1,0:T(8,128)}, f32[80,128]{1,0:T(8,128)S(1)}, u32[]{:S(2)}, u32[]{:S(2)}) collective-permute-start(f32[80,128]{1,0:T(8,128)} %get-tuple-element.53), channel_id=1, source_target_pairs={{4,0},{8,4},{12,8},{5,1},{9,5},{13,9},{6,2},{10,6},{14,10},{7,3},{... | collective-permute-start | bytes 122888 | tf_op jit(solution)/shard_map/ppermute | solution.py:545
  25.7 15.3 %copy-start.5 = (f32[64,32,128]{2,1,0:T(8,128)}, f32[64,32,128]{2,1,0:T(8,128)S(1)}, u32[]{:S(2)}) copy-start(f32[64,32,128]{2,1,0:T(8,128)S(1)} %collective-permute-done.5) | copy-start | bytes 3145732
  28.3 12.1 %collective-permute-start.7 = (f32[568,128]{1,0:T(8,128)}, f32[568,128]{1,0:T(8,128)S(1)}, u32[]{:S(2)}, u32[]{:S(2)}) collective-permute-start(f32[568,128]{1,0:T(8,128)} %get-tuple-element.61.refs_5_), channel_id=1, source_target_pairs={{3,2},{7,6},{11,10},{15,14},{19,18},{23,22},{27,26},{31,30}} | collective-permute-start | bytes 872456 | tf_op jit(solution)/shard_map/ppermute | solution.py:492
  32.6 26.2 %collective-permute-start.6 = (f32[1408,128]{1,0:T(8,128)S(1)}, f32[1408,128]{1,0:T(8,128)S(1)}, u32[]{:S(2)}, u32[]{:S(2)}) collective-permute-start(f32[1408,128]{1,0:T(8,128)S(1)} %pad_maximum_fusion.1), channel_id=1, source_target_pairs={{3,2},{7,6},{11,10},{15,14},{19,18},{23,22},{27,26},{31,30}} | collective-permute-start | bytes 2162696 | tf_op jit(solution)/shard_map/ppermute | solution.py:492
  34.0 17.0 %collective-permute-start.8 = (f32[400,128]{1,0:T(8,128)}, f32[400,128]{1,0:T(8,128)S(1)}, u32[]{:S(2)}, u32[]{:S(2)}) collective-permute-start(f32[400,128]{1,0:T(8,128)} %get-tuple-element.67.refs_6_), channel_id=1, source_target_pairs={{0,2},{2,1},{1,0},{4,6},{6,5},{5,4},{8,10},{10,9},{9,8},{12,14},{1... | collective-permute-start | bytes 614408 | tf_op jit(solution)/shard_map/ppermute | solution.py:486
  34.7 6.4 %copy-start.1 = (f32[1320,128]{1,0:T(8,128)}, f32[1320,128]{1,0:T(8,128)S(1)}, u32[]{:S(2)}) copy-start(f32[1320,128]{1,0:T(8,128)S(1)} %collective-permute-done.refs_2_.refs_0_) | copy-start | bytes 2027524
  34.7 16.3 %collective-permute-start.9 = (f32[400,128]{1,0:T(8,128)}, f32[400,128]{1,0:T(8,128)S(1)}, u32[]{:S(2)}, u32[]{:S(2)}) collective-permute-start(f32[400,128]{1,0:T(8,128)} %get-tuple-element.67.refs_6_), channel_id=1, source_target_pairs={{0,1},{1,2},{4,5},{5,6},{8,9},{9,10},{12,13},{13,14},{16,17},{17,1... | collective-permute-start | bytes 614408 | tf_op jit(solution)/shard_map/ppermute | solution.py:489
  39.6 1.4 %copy-start.2 = (f32[1320,128]{1,0:T(8,128)}, f32[1320,128]{1,0:T(8,128)S(1)}, u32[]{:S(2)}) copy-start(f32[1320,128]{1,0:T(8,128)S(1)} %collective-permute-done.1.refs_3_.refs_1_) | copy-start | bytes 2027524
  39.6 30.5 %collective-permute-start.11 = (f32[896,128]{1,0:T(8,128)S(1)}, f32[896,128]{1,0:T(8,128)S(1)}, u32[]{:S(2)}, u32[]{:S(2)}) collective-permute-start(f32[896,128]{1,0:T(8,128)S(1)} %copy-done.10), channel_id=1, source_target_pairs={{0,2},{2,1},{1,0},{4,6},{6,5},{5,4},{8,10},{10,9},{9,8},{12,14},{1... | collective-permute-start | bytes 1376264 | tf_op jit(solution)/shard_map/ppermute | solution.py:486
  40.3 29.8 %collective-permute-start.12 = (f32[896,128]{1,0:T(8,128)S(1)}, f32[896,128]{1,0:T(8,128)S(1)}, u32[]{:S(2)}, u32[]{:S(2)}) collective-permute-start(f32[896,128]{1,0:T(8,128)S(1)} %copy-done.10), channel_id=1, source_target_pairs={{0,1},{1,2},{4,5},{5,6},{8,9},{9,10},{12,13},{13,14},{16,17},{17,1... | collective-permute-start | bytes 1376264 | tf_op jit(solution)/shard_map/ppermute | solution.py:489
  51.0 7.8 %copy-start.6 = (f32[400,128]{1,0:T(8,128)}, f32[400,128]{1,0:T(8,128)S(1)}, u32[]{:S(2)}) copy-start(f32[400,128]{1,0:T(8,128)S(1)} %collective-permute-done.8.refs_4_) | copy-start | bytes 614404
  51.0 7.8 %copy-start.7 = (f32[400,128]{1,0:T(8,128)}, f32[400,128]{1,0:T(8,128)S(1)}, u32[]{:S(2)}) copy-start(f32[400,128]{1,0:T(8,128)S(1)} %collective-permute-done.9.refs_5_) | copy-start | bytes 614404
  51.0 19.1 %collective-permute-start.13 = (f32[896,128]{1,0:T(8,128)S(1)}, f32[896,128]{1,0:T(8,128)S(1)}, u32[]{:S(2)}, u32[]{:S(2)}) collective-permute-start(f32[896,128]{1,0:T(8,128)S(1)} %copy-done.10), channel_id=1, source_target_pairs={{3,2},{7,6},{11,10},{15,14},{19,18},{23,22},{27,26},{31,30}} | collective-permute-start | bytes 1376264 | tf_op jit(solution)/shard_map/ppermute | solution.py:492
  58.8 0.9 copy-start
  68.8 28.2 %collective-permute-start.10 = (f32[1032,128]{1,0:T(8,128)}, f32[1032,128]{1,0:T(8,128)S(1)}, u32[]{:S(2)}, u32[]{:S(2)}) collective-permute-start(f32[1032,128]{1,0:T(8,128)} %get-tuple-element.79), channel_id=1, source_target_pairs={{2,3},{6,7},{10,11},{14,15},{18,19},{22,23},{26,27},{30,31}} | collective-permute-start | bytes 1585160 | tf_op jit(solution)/shard_map/ppermute | solution.py:495
  70.1 0.8 copy-start.11
  70.1 1.0 copy-start.12
  70.1 1.1 %copy-start.13 = (f32[896,128]{1,0:T(8,128)}, f32[896,128]{1,0:T(8,128)S(1)}, u32[]{:S(2)}) copy-start(f32[896,128]{1,0:T(8,128)S(1)} %collective-permute-done.13.refs_3_) | copy-start | bytes 1376260
  71.3 25.7 %copy-start.8 = (f32[1024,128]{1,0:T(8,128)S(1)}, f32[1024,128]{1,0:T(8,128)}, u32[]{:S(2)}) copy-start(f32[1024,128]{1,0:T(8,128)} %get-tuple-element.88) | copy-start | bytes 1572868
  79.5 17.6 %copy-start.9 = (f32[1024,128]{1,0:T(8,128)S(1)}, f32[1024,128]{1,0:T(8,128)}, u32[]{:S(2)}) copy-start(f32[1024,128]{1,0:T(8,128)} %get-tuple-element.90) | copy-start | bytes 1572868
  79.5 17.5 %collective-permute-start.14 = (f32[1024,128]{1,0:T(8,128)}, f32[1024,128]{1,0:T(8,128)S(1)}, u32[]{:S(2)}, u32[]{:S(2)}) collective-permute-start(f32[1024,128]{1,0:T(8,128)} %get-tuple-element.86), channel_id=1, source_target_pairs={{2,3},{6,7},{10,11},{14,15},{18,19},{22,23},{26,27},{30,31}} | collective-permute-start | bytes 1572872 | tf_op jit(solution)/shard_map/ppermute | solution.py:495
  81.6 3.5 %collective-permute-start.15 = (f32[128]{0:T(128)S(1)}, f32[128]{0:T(128)S(1)}, u32[]{:S(2)}, u32[]{:S(2)}) collective-permute-start(f32[128]{0:T(128)S(1)} %slice_bitcast_fusion), channel_id=1, source_target_pairs={{0,16},{16,0},{1,17},{17,1},{2,18},{18,2},{3,19},{19,3},{4,20},{20... | collective-permute-start | bytes 1544 | tf_op jit(solution)/shard_map/ppermute | solution.py:651
  85.8 5.3 %collective-permute-start.16 = (f32[128]{0:T(128)S(1)}, f32[128]{0:T(128)S(1)}, u32[]{:S(2)}, u32[]{:S(2)}) collective-permute-start(f32[128]{0:T(128)S(1)} %fusion), channel_id=1, source_target_pairs={{0,3},{1,0},{2,1},{3,2},{4,7},{5,4},{6,5},{7,6},{8,11},{9,8},{10,9... | collective-permute-start | bytes 1544 | tf_op jit(solution)/shard_map/ppermute | solution.py:655
  88.5 4.4 %collective-permute-start.17 = (f32[128]{0:T(128)S(1)}, f32[128]{0:T(128)S(1)}, u32[]{:S(2)}, u32[]{:S(2)}) collective-permute-start(f32[128]{0:T(128)S(1)} %fusion), channel_id=1, source_target_pairs={{0,2},{1,3},{2,0},{3,1},{4,6},{5,7},{6,4},{7,5},{8,10},{9,11},{10,... | collective-permute-start | bytes 1544 | tf_op jit(solution)/shard_map/ppermute | solution.py:655
  88.5 7.9 %collective-permute-start.18 = (f32[128]{0:T(128)S(1)}, f32[128]{0:T(128)S(1)}, u32[]{:S(2)}, u32[]{:S(2)}) collective-permute-start(f32[128]{0:T(128)S(1)} %fusion), channel_id=1, source_target_pairs={{0,1},{1,2},{2,3},{3,0},{4,5},{5,6},{6,7},{7,4},{8,9},{9,10},{10,1... | collective-permute-start | bytes 1544 | tf_op jit(solution)/shard_map/ppermute | solution.py:655
  (4 other events, 2.7 us)

commit v11 on v10

--- a/solution.py
+++ b/solution.py
@@ -625,7 +625,7 @@
         operands += [*coefs, gates, second[g], moved[g]]
         held = len(operands) - 2
         operands += [both, own_cols, *carry]
-        outs = [(RANGE * n_out, radial), (RANGE * n_out + 8 * first, radial), (8, radial) if last else (radial, LANES)]
+        outs = [(RANGE * n_out, radial), (RANGE * n_out + 8 * first, radial), (1, radial) if last else (radial, LANES)]
         if not last:
             outs += [(2, 2, length, LANES), (2, length, LANES)]
         own_out, next_out, total, *kept = call(
@@ -645,17 +645,13 @@
         carry = [*kept, total]
         own_outs.append(own_out)
         next_outs.append(returning(next_out))
-    speed_gradient = total[0]
+    speed_gradient = total
     step = 1
     while step < phis:
         speed_gradient += lax.ppermute(speed_gradient, "phi", [(i, i ^ step) for i in range(phis)])
         step *= 2
-    size = lax.axis_size("mass")
-    shares = [
-        lax.ppermute(speed_gradient, "mass", [(i, (i + k) % size) for i in range(size)]) for k in range(1, size)
-    ]
-    shares = jnp.stack([*reversed(shares), speed_gradient] * 2)
-    speed_gradient = jnp.sum(lax.dynamic_slice_in_dim(shares, size - 1 - place, size, 0), axis=0)
+    shares = [lax.ppermute(speed_gradient, "mass", [(i, i ^ k) for i in range(4)]) for k in range(1, 4)]
+    speed_gradient = ((speed_gradient + shares[0]) + (shares[1] + shares[2]))[0]
     next_outs = lax.optimization_barrier(next_outs)
     result = jnp.concatenate(
         [

time: 99.9 us -> 99.3 us (level)
  transfers between devices with their start and end apart: 19 -> 19, of which waited for: 6 -> 4; matrix products, arithmetic and copies ran while one was open for 3% -> 2% of each run, Pallas kernels for 40% -> 40%
where the time goes in v11:
time: 99.3 us; the launch traced here: 98.2 us
  Pallas kernels  39.7 us (40%)
  starting transfers between devices  33.5 us (34%)
  waiting for transfers between devices  17.1 us (17%)
  local copies, waits for them, and re-layouts  4.47 us (5%)
  other arithmetic  2.46 us (2%)
  between operations  1.03 us (1%)
    pallas_call x6, Pallas kernels, call(): pl.pallas_call(kernel, out_shape=[jax.ShapeDtypeStruct(o, jnp.float32) fo...  35.4 us
    ppermute x4, starting transfers between devices, ending(): return lax.ppermute(x, 'mass', [(3, 2)])  15.8 us
    ppermute x3, waiting for transfers between devices, per_device(): lax.ppermute(speed_gradient, 'mass', [(i, i ^ k) for i in range(4)])  6.03 us
    ppermute x1, waiting for transfers between devices, per_device(): other = lax.ppermute(sides, 'phi', ring)  5.87 us
    ppermute x3, starting transfers between devices, per_device(): lax.ppermute(speed_gradient, 'mass', [(i, i ^ k) for i in range(4)])  5.07 us
    pallas_call x1, Pallas kernels, per_device(): pl.pallas_call(table_kernel, out_shape=[jax.ShapeDtypeStruct((3 * total_b...  4.27 us
    unnamed x32, local copies, waits for them, and re-layouts  3.36 us
    ppermute x4, waiting for transfers between devices, ending(): return lax.ppermute(x, 'mass', [(3, 2)])  2.97 us
  transfers between devices with their start and end apart: 19, of which 4 were waited for; matrix products, arithmetic and copies ran while one was open for 2% of the time, Pallas kernels for 40%

profile of v11, /device:TPU:24, one launch (start us, length us, event | category | flops | bytes accessed | tf_op | source)
XLA Modules:
  0.0 98.2 jit_solution(3122936517698571188)
XLA Ops:
  0.6 2.4 %collective-permute-start.5 = (f32[64,32,128]{2,1,0:T(8,128)}, f32[64,32,128]{2,1,0:T(8,128)S(1)}, u32[]{:S(2)}, u32[]{:S(2)}) collective-permute-start(f32[64,32,128]{2,1,0:T(8,128)} %param.14), channel_id=1, source_target_pairs={{3,2},{7,6},{11,10},{15,14},{19,18},{23,22},{27,26},{31,30}} | collective-permute-start | bytes 3145736 | tf_op jit(solution)/shard_map/ppermute | solution.py:492
  3.1 4.5 %shard_map.149 = (f32[520,128]{1,0:T(8,128)}, f32[32,128]{1,0:T(8,128)}, f32[128,128]{1,0:T(8,128)}, f32[1320,128]{1,0:T(8,128)}, f32[168,128]{1,0:T(8,128)}, /*...) custom-call(f32[2048,128]{1,0:T(8,128)} %bitcast.19, f32[2048,128]{1,0:T(8,128)} %bitcast.15, ...), custom_call_target="tpu_custom_call" | custom-call | tf_op jit(solution)/shard_map/pallas_call | solution.py:450
  7.6 0.7 collective-permute-start
  8.3 1.6 %collective-permute-start.2 = (f32[520,128]{1,0:T(8,128)}, f32[520,128]{1,0:T(8,128)S(1)}, u32[]{:S(2)}, u32[]{:S(2)}) collective-permute-start(f32[520,128]{1,0:T(8,128)} %get-tuple-element.48), channel_id=1, source_target_pairs={{0,16},{16,0},{1,17},{17,1},{2,18},{18,2},{3,19},{19,3},{4,20},{20... | collective-permute-start | bytes 798728 | tf_op jit(solution)/shard_map/ppermute | solution.py:529
  9.8 0.7 collective-permute-start.1
  10.5 5.9 %collective-permute-done.2.sides_ref = f32[520,128]{1,0:T(8,128)S(1)} collective-permute-done((f32[520,128]{1,0:T(8,128)}, f32[520,128]{1,0:T(8,128)S(1)}, u32[]{:S(2)}, u32[]{:S(2)}) %collective-permute-start.2) | collective-permute-done | bytes 266272 | tf_op jit(solution)/shard_map/ppermute | solution.py:529
  16.4 0.7 copy-done.4
  17.1 1.8 %shard_map.150 = (f32[80,128]{1,0:T(8,128)}, f32[80,128]{1,0:T(8,128)}, f32[128,128]{1,0:T(8,128)}) custom-call(f32[520,128]{1,0:T(8,128)} %copy-done.4, f32[64,128]{1,0:T(8,128)} %bitcast.21, f32[64,128]{1,0:T(8,128)} %bitcast.22, f32[32,128]{1,0:T(8,128)} %get-tuple-element.51.gate_ref), custom_call_target="tpu_custom_call" | custom-call | tf_op jit(solution)/shard_map/pallas_call | solution.py:450
  18.9 1.4 %collective-permute-start.3 = (f32[80,128]{1,0:T(8,128)}, f32[80,128]{1,0:T(8,128)S(1)}, u32[]{:S(2)}, u32[]{:S(2)}) collective-permute-start(f32[80,128]{1,0:T(8,128)} %get-tuple-element.52), channel_id=1, source_target_pairs={{0,4},{4,8},{8,12},{1,5},{5,9},{9,13},{2,6},{6,10},{10,14},{3,7},{... | collective-permute-start | bytes 122888 | tf_op jit(solution)/shard_map/ppermute | solution.py:544
  20.3 1.3 %collective-permute-start.4 = (f32[80,128]{1,0:T(8,128)}, f32[80,128]{1,0:T(8,128)S(1)}, u32[]{:S(2)}, u32[]{:S(2)}) collective-permute-start(f32[80,128]{1,0:T(8,128)} %get-tuple-element.53), channel_id=1, source_target_pairs={{4,0},{8,4},{12,8},{5,1},{9,5},{13,9},{6,2},{10,6},{14,10},{7,3},{... | collective-permute-start | bytes 122888 | tf_op jit(solution)/shard_map/ppermute | solution.py:545
  21.6 1.1 %slice.9 = f32[1152,128]{1,0:T(8,128)S(1)} slice(f32[1320,128]{1,0:T(8,128)} %get-tuple-element.47.refs_2_), slice={[0:1152], [0:128]} | slice | bytes 1179648 | tf_op jit(solution)/shard_map/slice | solution.py:574
  22.7 3.0 %collective-permute-done.5 = f32[64,32,128]{2,1,0:T(8,128)S(1)} collective-permute-done((f32[64,32,128]{2,1,0:T(8,128)}, f32[64,32,128]{2,1,0:T(8,128)S(1)}, u32[]{:S(2)}, u32[]{:S(2)}) %collective-permute-start.5) | collective-permute-done | bytes 1048608 | tf_op jit(solution)/shard_map/ppermute | solution.py:492
  26.4 1.9 %shard_map.151 = (f32[568,128]{1,0:T(8,128)}, f32[400,128]{1,0:T(8,128)}, f32[160,128]{1,0:T(8,128)}) custom-call(f32[80,128]{1,0:T(8,128)} %copy-done.14, f32[80,128]{1,0:T(8,128)} %copy-done.15, f32[520,128]{1,0:T(8,128)} %copy-done.4, f32[168,128]{1,0:T(8,128)} %get-tuple-element.54.shares_ref.refs_4_, f32[128,128]{1,0:T(8,128)} %get-tuple-element.56.gates_ref), custom_call_target="tpu_custom_call" | custom-call | tf_op jit(solution)/shard_map/pallas_call | solution.py:450
  28.3 4.3 %collective-permute-start.7 = (f32[568,128]{1,0:T(8,128)}, f32[568,128]{1,0:T(8,128)S(1)}, u32[]{:S(2)}, u32[]{:S(2)}) collective-permute-start(f32[568,128]{1,0:T(8,128)} %get-tuple-element.61.refs_5_), channel_id=1, source_target_pairs={{3,2},{7,6},{11,10},{15,14},{19,18},{23,22},{27,26},{31,30}} | collective-permute-start | bytes 872456 | tf_op jit(solution)/shard_map/ppermute | solution.py:492
  32.6 1.3 %collective-permute-start.6 = (f32[1408,128]{1,0:T(8,128)S(1)}, f32[1408,128]{1,0:T(8,128)S(1)}, u32[]{:S(2)}, u32[]{:S(2)}) collective-permute-start(f32[1408,128]{1,0:T(8,128)S(1)} %pad_maximum_fusion.1), channel_id=1, source_target_pairs={{3,2},{7,6},{11,10},{15,14},{19,18},{23,22},{27,26},{31,30}} | collective-permute-start | bytes 2162696 | tf_op jit(solution)/shard_map/ppermute | solution.py:492
  35.4 4.3 %shard_map.152 = (bf16[768,512]{1,0:T(8,128)(2,1)}, bf16[768,256]{1,0:T(8,128)(2,1)}, bf16[768,256]{1,0:T(8,128)(2,1)}) custom-call(f32[256,256]{1,0:T(8,128)} %gain_ref, s32[1,256]{1,0:T(1,128)} %bitcast.23, f32[1,256]{1,0:T(1,128)} %bitcast.24, f32[1,256]{1,0:T(1,128)} %bitcast.25, f32[1,256]{1,0:T(1,128)} %bitcast.26, s32[4,4]{1,0:T(4,128)} %pairs_ref.1), custom_call_target="tpu_custom_call" | custom-call | tf_op jit(solution)/shard_map/pallas_call | solution.py:557
  39.6 0.7 collective-permute-start.11
  40.3 0.7 collective-permute-start.12
  41.1 9.9 %shard_map.153 = (f32[17,128,128]{2,1,0:T(8,128)}, f32[15,128,128]{2,1,0:T(8,128)}, f32[18,2,128,128]{3,2,1,0:T(8,128)}, f32[14,2,128,128]{3,2,1,0:T(8,128)}, f3...) custom-call(f32[2048,128]{1,0:T(8,128)} %bitcast.16, ...), custom_call_target="tpu_custom_call" | custom-call | tf_op jit(solution)/shard_map/pallas_call | solution.py:450
  51.0 7.8 %collective-permute-start.13 = (f32[896,128]{1,0:T(8,128)S(1)}, f32[896,128]{1,0:T(8,128)S(1)}, u32[]{:S(2)}, u32[]{:S(2)}) collective-permute-start(f32[896,128]{1,0:T(8,128)S(1)} %copy-done.10), channel_id=1, source_target_pairs={{3,2},{7,6},{11,10},{15,14},{19,18},{23,22},{27,26},{31,30}} | collective-permute-start | bytes 1376264 | tf_op jit(solution)/shard_map/ppermute | solution.py:492
  58.8 0.8 copy-done
  59.7 9.1 %shard_map.154 = (f32[1024,128]{1,0:T(8,128)}, f32[1032,128]{1,0:T(8,128)}, f32[128,128]{1,0:T(8,128)}, f32[2,2,160,128]{3,2,1,0:T(8,128)}, f32[2,160,128]{2,1,0:T(8,128)}) custom-call(f32[1320,128]{1,0:T(8,128)} %copy-done.1, f32[1320,128]{1,0:T(8,128)} %copy-done.2, f32[1320,128]{1,0:T(8,128)} %get-tuple-element.47.refs_2_, f32[1408,128]{1,0:T(8,128)} %copy-done, ...), custom_call_target="tpu_custom_call" | custom-call | tf_op jit(solution)/shard_map/pallas_call | solution.py:450
  68.8 1.3 %collective-permute-start.10 = (f32[1032,128]{1,0:T(8,128)}, f32[1032,128]{1,0:T(8,128)S(1)}, u32[]{:S(2)}, u32[]{:S(2)}) collective-permute-start(f32[1032,128]{1,0:T(8,128)} %get-tuple-element.79), channel_id=1, source_target_pairs={{2,3},{6,7},{10,11},{14,15},{18,19},{22,23},{26,27},{30,31}} | collective-permute-start | bytes 1585160 | tf_op jit(solution)/shard_map/ppermute | solution.py:495
  70.2 0.7 copy-done.11
  71.3 8.2 %shard_map.155 = (f32[1024,128]{1,0:T(8,128)}, f32[1024,128]{1,0:T(8,128)}, f32[1,128]{1,0:T(1,128)}) custom-call(f32[896,128]{1,0:T(8,128)} %copy-done.11, f32[896,128]{1,0:T(8,128)} %copy-done.12, f32[896,128]{1,0:T(8,128)} %get-tuple-element.80.refs_2_, f32[896,128]{1,0:T(8,128)} %copy-done.13, f32[400,128]{1,0:T(8,128)} %copy-done.6, ...), custom_call_target="tpu_custom_call" | custom-call | tf_op jit(solution)/shard_map/pallas_call | solution.py:450
  79.5 1.4 %collective-permute-start.14 = (f32[1024,128]{1,0:T(8,128)}, f32[1024,128]{1,0:T(8,128)S(1)}, u32[]{:S(2)}, u32[]{:S(2)}) collective-permute-start(f32[1024,128]{1,0:T(8,128)} %get-tuple-element.86), channel_id=1, source_target_pairs={{2,3},{6,7},{10,11},{14,15},{18,19},{22,23},{26,27},{30,31}} | collective-permute-start | bytes 1572872 | tf_op jit(solution)/shard_map/ppermute | solution.py:495
  80.9 1.6 %collective-permute-start.15 = (f32[1,128]{1,0:T(1,128)}, f32[1,128]{1,0:T(1,128)S(1)}, u32[]{:S(2)}, u32[]{:S(2)}) collective-permute-start(f32[1,128]{1,0:T(1,128)} %get-tuple-element.91), channel_id=1, source_target_pairs={{0,16},{16,0},{1,17},{17,1},{2,18},{18,2},{3,19},{19,3},{4,20},{20... | collective-permute-start | bytes 1544 | tf_op jit(solution)/shard_map/ppermute | solution.py:651
  82.5 2.2 %collective-permute-done.15 = f32[1,128]{1,0:T(1,128)S(1)} collective-permute-done((f32[1,128]{1,0:T(1,128)}, f32[1,128]{1,0:T(1,128)S(1)}, u32[]{:S(2)}, u32[]{:S(2)}) %collective-permute-start.15) | collective-permute-done | bytes 544 | tf_op jit(solution)/shard_map/ppermute | solution.py:651
  85.3 2.7 %collective-permute-start.16 = (f32[1,128]{1,0:T(1,128)S(1)}, f32[1,128]{1,0:T(1,128)S(1)}, u32[]{:S(2)}, u32[]{:S(2)}) collective-permute-start(f32[1,128]{1,0:T(1,128)S(1)} %add.12), channel_id=1, source_target_pairs={{0,1},{1,0},{2,3},{3,2},{4,5},{5,4},{6,7},{7,6},{8,9},{9,8},{10,11... | collective-permute-start | bytes 1544 | tf_op jit(solution)/shard_map/ppermute | solution.py:653
  88.0 2.4 %collective-permute-start.18 = (f32[1,128]{1,0:T(1,128)S(1)}, f32[1,128]{1,0:T(1,128)S(1)}, u32[]{:S(2)}, u32[]{:S(2)}) collective-permute-start(f32[1,128]{1,0:T(1,128)S(1)} %add.12), channel_id=1, source_target_pairs={{0,3},{1,2},{2,1},{3,0},{4,7},{5,6},{6,5},{7,4},{8,11},{9,10},{10,... | collective-permute-start | bytes 1544 | tf_op jit(solution)/shard_map/ppermute | solution.py:653
  90.4 6.0 %collective-permute-done.16 = f32[1,128]{1,0:T(1,128)S(1)} collective-permute-done((f32[1,128]{1,0:T(1,128)S(1)}, f32[1,128]{1,0:T(1,128)S(1)}, u32[]{:S(2)}, u32[]{:S(2)}) %collective-permute-start.16) | collective-permute-done | bytes 544 | tf_op jit(solution)/shard_map/ppermute | solution.py:653
  97.1 1.1 %pad_maximum_fusion = f32[64,32,128]{2,1,0:T(8,128)} fusion(f32[64,16,128]{2,1,0:T(8,128)S(1)} %bitcast.18, f32[64,16,128]{2,1,0:T(8,128)S(1)} %bitcast.17), kind=kLoop, calls=%fused_computation | loop fusion | flops 262144 | bytes 2097152 | tf_op jit(solution)/shard_map/concatenate | solution.py:656
  (54 shorter events, 3.8 us)
Async XLA Ops:
  0.6 25.1 %collective-permute-start.5 = (f32[64,32,128]{2,1,0:T(8,128)}, f32[64,32,128]{2,1,0:T(8,128)S(1)}, u32[]{:S(2)}, u32[]{:S(2)}) collective-permute-start(f32[64,32,128]{2,1,0:T(8,128)} %param.14), channel_id=1, source_target_pairs={{3,2},{7,6},{11,10},{15,14},{19,18},{23,22},{27,26},{31,30}} | collective-permute-start | bytes 3145736 | tf_op jit(solution)/shard_map/ppermute | solution.py:492
  7.6 27.1 %collective-permute-start = (f32[1320,128]{1,0:T(8,128)}, f32[1320,128]{1,0:T(8,128)S(1)}, u32[]{:S(2)}, u32[]{:S(2)}) collective-permute-start(f32[1320,128]{1,0:T(8,128)} %get-tuple-element.47.refs_2_), channel_id=1, source_target_pairs={{0,2},{2,1},{1,0},{4,6},{6,5},{5,4},{8,10},{10,9},{9,8},{12,14},{1... | collective-permute-start | bytes 2027528 | tf_op jit(solution)/shard_map/ppermute | solution.py:486
  8.3 8.1 %collective-permute-start.2 = (f32[520,128]{1,0:T(8,128)}, f32[520,128]{1,0:T(8,128)S(1)}, u32[]{:S(2)}, u32[]{:S(2)}) collective-permute-start(f32[520,128]{1,0:T(8,128)} %get-tuple-element.48), channel_id=1, source_target_pairs={{0,16},{16,0},{1,17},{17,1},{2,18},{18,2},{3,19},{19,3},{4,20},{20... | collective-permute-start | bytes 798728 | tf_op jit(solution)/shard_map/ppermute | solution.py:529
  9.8 29.8 %collective-permute-start.1 = (f32[1320,128]{1,0:T(8,128)}, f32[1320,128]{1,0:T(8,128)S(1)}, u32[]{:S(2)}, u32[]{:S(2)}) collective-permute-start(f32[1320,128]{1,0:T(8,128)} %get-tuple-element.47.refs_2_), channel_id=1, source_target_pairs={{0,1},{1,2},{4,5},{5,6},{8,9},{9,10},{12,13},{13,14},{16,17},{17,1... | collective-permute-start | bytes 2027528 | tf_op jit(solution)/shard_map/ppermute | solution.py:489
  18.9 13.6 %slice-start = ((f32[520,128]{1,0:T(8,128)}), f32[256,128]{1,0:T(8,128)S(1)}, s32[]{:S(2)}) async-start(f32[520,128]{1,0:T(8,128)} %copy-done.4), calls=%async_computation | async-start | bytes 262144 | tf_op jit(solution)/shard_map/slice | solution.py:574
  18.9 20.7 %copy-start.10 = (f32[896,128]{1,0:T(8,128)S(1)}, f32[896,128]{1,0:T(8,128)}, u32[]{:S(2)}) copy-start(f32[896,128]{1,0:T(8,128)} %get-tuple-element.80.refs_2_) | copy-start | bytes 1376260
  18.9 6.8 %collective-permute-start.3 = (f32[80,128]{1,0:T(8,128)}, f32[80,128]{1,0:T(8,128)S(1)}, u32[]{:S(2)}, u32[]{:S(2)}) collective-permute-start(f32[80,128]{1,0:T(8,128)} %get-tuple-element.52), channel_id=1, source_target_pairs={{0,4},{4,8},{8,12},{1,5},{5,9},{9,13},{2,6},{6,10},{10,14},{3,7},{... | collective-permute-start | bytes 122888 | tf_op jit(solution)/shard_map/ppermute | solution.py:544
  20.3 5.4 %collective-permute-start.4 = (f32[80,128]{1,0:T(8,128)}, f32[80,128]{1,0:T(8,128)S(1)}, u32[]{:S(2)}, u32[]{:S(2)}) collective-permute-start(f32[80,128]{1,0:T(8,128)} %get-tuple-element.53), channel_id=1, source_target_pairs={{4,0},{8,4},{12,8},{5,1},{9,5},{13,9},{6,2},{10,6},{14,10},{7,3},{... | collective-permute-start | bytes 122888 | tf_op jit(solution)/shard_map/ppermute | solution.py:545
  25.7 15.3 %copy-start.5 = (f32[64,32,128]{2,1,0:T(8,128)}, f32[64,32,128]{2,1,0:T(8,128)S(1)}, u32[]{:S(2)}) copy-start(f32[64,32,128]{2,1,0:T(8,128)S(1)} %collective-permute-done.5) | copy-start | bytes 3145732
  28.3 12.1 %collective-permute-start.7 = (f32[568,128]{1,0:T(8,128)}, f32[568,128]{1,0:T(8,128)S(1)}, u32[]{:S(2)}, u32[]{:S(2)}) collective-permute-start(f32[568,128]{1,0:T(8,128)} %get-tuple-element.61.refs_5_), channel_id=1, source_target_pairs={{3,2},{7,6},{11,10},{15,14},{19,18},{23,22},{27,26},{31,30}} | collective-permute-start | bytes 872456 | tf_op jit(solution)/shard_map/ppermute | solution.py:492
  32.6 26.2 %collective-permute-start.6 = (f32[1408,128]{1,0:T(8,128)S(1)}, f32[1408,128]{1,0:T(8,128)S(1)}, u32[]{:S(2)}, u32[]{:S(2)}) collective-permute-start(f32[1408,128]{1,0:T(8,128)S(1)} %pad_maximum_fusion.1), channel_id=1, source_target_pairs={{3,2},{7,6},{11,10},{15,14},{19,18},{23,22},{27,26},{31,30}} | collective-permute-start | bytes 2162696 | tf_op jit(solution)/shard_map/ppermute | solution.py:492
  34.0 17.0 %collective-permute-start.8 = (f32[400,128]{1,0:T(8,128)}, f32[400,128]{1,0:T(8,128)S(1)}, u32[]{:S(2)}, u32[]{:S(2)}) collective-permute-start(f32[400,128]{1,0:T(8,128)} %get-tuple-element.67.refs_6_), channel_id=1, source_target_pairs={{0,2},{2,1},{1,0},{4,6},{6,5},{5,4},{8,10},{10,9},{9,8},{12,14},{1... | collective-permute-start | bytes 614408 | tf_op jit(solution)/shard_map/ppermute | solution.py:486
  34.7 6.4 %copy-start.1 = (f32[1320,128]{1,0:T(8,128)}, f32[1320,128]{1,0:T(8,128)S(1)}, u32[]{:S(2)}) copy-start(f32[1320,128]{1,0:T(8,128)S(1)} %collective-permute-done.refs_2_.refs_0_) | copy-start | bytes 2027524
  34.7 16.3 %collective-permute-start.9 = (f32[400,128]{1,0:T(8,128)}, f32[400,128]{1,0:T(8,128)S(1)}, u32[]{:S(2)}, u32[]{:S(2)}) collective-permute-start(f32[400,128]{1,0:T(8,128)} %get-tuple-element.67.refs_6_), channel_id=1, source_target_pairs={{0,1},{1,2},{4,5},{5,6},{8,9},{9,10},{12,13},{13,14},{16,17},{17,1... | collective-permute-start | bytes 614408 | tf_op jit(solution)/shard_map/ppermute | solution.py:489
  39.6 1.4 %copy-start.2 = (f32[1320,128]{1,0:T(8,128)}, f32[1320,128]{1,0:T(8,128)S(1)}, u32[]{:S(2)}) copy-start(f32[1320,128]{1,0:T(8,128)S(1)} %collective-permute-done.1.refs_3_.refs_1_) | copy-start | bytes 2027524
  39.6 30.5 %collective-permute-start.11 = (f32[896,128]{1,0:T(8,128)S(1)}, f32[896,128]{1,0:T(8,128)S(1)}, u32[]{:S(2)}, u32[]{:S(2)}) collective-permute-start(f32[896,128]{1,0:T(8,128)S(1)} %copy-done.10), channel_id=1, source_target_pairs={{0,2},{2,1},{1,0},{4,6},{6,5},{5,4},{8,10},{10,9},{9,8},{12,14},{1... | collective-permute-start | bytes 1376264 | tf_op jit(solution)/shard_map/ppermute | solution.py:486
  40.3 29.8 %collective-permute-start.12 = (f32[896,128]{1,0:T(8,128)S(1)}, f32[896,128]{1,0:T(8,128)S(1)}, u32[]{:S(2)}, u32[]{:S(2)}) collective-permute-start(f32[896,128]{1,0:T(8,128)S(1)} %copy-done.10), channel_id=1, source_target_pairs={{0,1},{1,2},{4,5},{5,6},{8,9},{9,10},{12,13},{13,14},{16,17},{17,1... | collective-permute-start | bytes 1376264 | tf_op jit(solution)/shard_map/ppermute | solution.py:489
  51.0 7.8 %copy-start.6 = (f32[400,128]{1,0:T(8,128)}, f32[400,128]{1,0:T(8,128)S(1)}, u32[]{:S(2)}) copy-start(f32[400,128]{1,0:T(8,128)S(1)} %collective-permute-done.8.refs_4_) | copy-start | bytes 614404
  51.0 7.8 %copy-start.7 = (f32[400,128]{1,0:T(8,128)}, f32[400,128]{1,0:T(8,128)S(1)}, u32[]{:S(2)}) copy-start(f32[400,128]{1,0:T(8,128)S(1)} %collective-permute-done.9.refs_5_) | copy-start | bytes 614404
  51.0 19.1 %collective-permute-start.13 = (f32[896,128]{1,0:T(8,128)S(1)}, f32[896,128]{1,0:T(8,128)S(1)}, u32[]{:S(2)}, u32[]{:S(2)}) collective-permute-start(f32[896,128]{1,0:T(8,128)S(1)} %copy-done.10), channel_id=1, source_target_pairs={{3,2},{7,6},{11,10},{15,14},{19,18},{23,22},{27,26},{31,30}} | collective-permute-start | bytes 1376264 | tf_op jit(solution)/shard_map/ppermute | solution.py:492
  58.8 0.9 copy-start
  68.8 28.1 %collective-permute-start.10 = (f32[1032,128]{1,0:T(8,128)}, f32[1032,128]{1,0:T(8,128)S(1)}, u32[]{:S(2)}, u32[]{:S(2)}) collective-permute-start(f32[1032,128]{1,0:T(8,128)} %get-tuple-element.79), channel_id=1, source_target_pairs={{2,3},{6,7},{10,11},{14,15},{18,19},{22,23},{26,27},{30,31}} | collective-permute-start | bytes 1585160 | tf_op jit(solution)/shard_map/ppermute | solution.py:495
  70.1 0.8 copy-start.11
  70.1 1.0 copy-start.12
  70.2 1.1 %copy-start.13 = (f32[896,128]{1,0:T(8,128)}, f32[896,128]{1,0:T(8,128)S(1)}, u32[]{:S(2)}) copy-start(f32[896,128]{1,0:T(8,128)S(1)} %collective-permute-done.13.refs_3_) | copy-start | bytes 1376260
  71.3 25.6 %copy-start.8 = (f32[1024,128]{1,0:T(8,128)S(1)}, f32[1024,128]{1,0:T(8,128)}, u32[]{:S(2)}) copy-start(f32[1024,128]{1,0:T(8,128)} %get-tuple-element.88) | copy-start | bytes 1572868
  79.5 17.5 %copy-start.9 = (f32[1024,128]{1,0:T(8,128)S(1)}, f32[1024,128]{1,0:T(8,128)}, u32[]{:S(2)}) copy-start(f32[1024,128]{1,0:T(8,128)} %get-tuple-element.90) | copy-start | bytes 1572868
  79.5 17.5 %collective-permute-start.14 = (f32[1024,128]{1,0:T(8,128)}, f32[1024,128]{1,0:T(8,128)S(1)}, u32[]{:S(2)}, u32[]{:S(2)}) collective-permute-start(f32[1024,128]{1,0:T(8,128)} %get-tuple-element.86), channel_id=1, source_target_pairs={{2,3},{6,7},{10,11},{14,15},{18,19},{22,23},{26,27},{30,31}} | collective-permute-start | bytes 1572872 | tf_op jit(solution)/shard_map/ppermute | solution.py:495
  80.9 3.7 %collective-permute-start.15 = (f32[1,128]{1,0:T(1,128)}, f32[1,128]{1,0:T(1,128)S(1)}, u32[]{:S(2)}, u32[]{:S(2)}) collective-permute-start(f32[1,128]{1,0:T(1,128)} %get-tuple-element.91), channel_id=1, source_target_pairs={{0,16},{16,0},{1,17},{17,1},{2,18},{18,2},{3,19},{19,3},{4,20},{20... | collective-permute-start | bytes 1544 | tf_op jit(solution)/shard_map/ppermute | solution.py:651
  85.3 11.1 %collective-permute-start.16 = (f32[1,128]{1,0:T(1,128)S(1)}, f32[1,128]{1,0:T(1,128)S(1)}, u32[]{:S(2)}, u32[]{:S(2)}) collective-permute-start(f32[1,128]{1,0:T(1,128)S(1)} %add.12), channel_id=1, source_target_pairs={{0,1},{1,0},{2,3},{3,2},{4,5},{5,4},{6,7},{7,6},{8,9},{9,8},{10,11... | collective-permute-start | bytes 1544 | tf_op jit(solution)/shard_map/ppermute | solution.py:653
  88.0 8.4 %collective-permute-start.17 = (f32[1,128]{1,0:T(1,128)S(1)}, f32[1,128]{1,0:T(1,128)S(1)}, u32[]{:S(2)}, u32[]{:S(2)}) collective-permute-start(f32[1,128]{1,0:T(1,128)S(1)} %add.12), channel_id=1, source_target_pairs={{0,2},{1,3},{2,0},{3,1},{4,6},{5,7},{6,4},{7,5},{8,10},{9,11},{10,... | collective-permute-start | bytes 1544 | tf_op jit(solution)/shard_map/ppermute | solution.py:653
  88.0 8.4 %collective-permute-start.18 = (f32[1,128]{1,0:T(1,128)S(1)}, f32[1,128]{1,0:T(1,128)S(1)}, u32[]{:S(2)}, u32[]{:S(2)}) collective-permute-start(f32[1,128]{1,0:T(1,128)S(1)} %add.12), channel_id=1, source_target_pairs={{0,3},{1,2},{2,1},{3,0},{4,7},{5,6},{6,5},{7,4},{8,11},{9,10},{10,... | collective-permute-start | bytes 1544 | tf_op jit(solution)/shard_map/ppermute | solution.py:653
  (4 other events, 2.7 us)

commit v12 on v11

--- a/solution.py
+++ b/solution.py
@@ -534,24 +534,7 @@
 
     density_next = ending(density)
     far_first, near_first = far(opening), near(opening)
-    left_cells, right_cells, gates = call(
-        functools.partial(radial_kernel, azimuth, radial),
-        [(2 * count + 8, LANES), (2 * count + 8, LANES), (radial, LANES)],
-        [],
-        [other, flat(first_cells), flat(last_cells), gate],
-    )
-    line = [(i, i + 1) for i in range(rows - 1)]
-    left = lax.ppermute(left_cells, "row", line)
-    right = lax.ppermute(right_cells, "row", [(j, i) for i, j in line])
-    gates, density_next = lax.optimization_barrier((gates, density_next))
-    long, short, gates = call(
-        functools.partial(halo_kernel, azimuth, radial),
-        [(strip_rows + 4 * own_bins + share_rows, LANES), (strip_rows + 4 * own_bins, LANES), (length, LANES)],
-        [],
-        [left, right, other, shares, gates],
-    )
-
-    frag_gain, long = lax.optimization_barrier((frag_gain, long))
+    frag_gain, gate = lax.optimization_barrier((frag_gain, gate))
     vmem = pl.BlockSpec(memory_space=pltpu.VMEM)
     total_bins = frag_gain.shape[0]
     both, own_cols, own_rows = pl.pallas_call(
@@ -567,6 +550,23 @@
         coag_rate[None, :],
         frag_rate[None, :],
         frag_pairs,
+    )
+    gate, both = lax.optimization_barrier((gate, both))
+    left_cells, right_cells, gates = call(
+        functools.partial(radial_kernel, azimuth, radial),
+        [(2 * count + 8, LANES), (2 * count + 8, LANES), (radial, LANES)],
+        [],
+        [other, flat(first_cells), flat(last_cells), gate],
+    )
+    line = [(i, i + 1) for i in range(rows - 1)]
+    left = lax.ppermute(left_cells, "row", line)
+    right = lax.ppermute(right_cells, "row", [(j, i) for i, j in line])
+    gates, density_next = lax.optimization_barrier((gates, density_next))
+    long, short, gates = call(
+        functools.partial(halo_kernel, azimuth, radial),
+        [(strip_rows + 4 * own_bins + share_rows, LANES), (strip_rows + 4 * own_bins, LANES), (length, LANES)],
+        [],
+        [left, right, other, shares, gates],
     )
 
     long_next = ending(long)

time: 99.3 us -> 98.9 us (level)
  the two profiles are of different devices: /device:TPU:24 before, /device:TPU:0 now
where the time goes in v12:
time: 98.9 us; the launch traced here: 98.3 us
  Pallas kernels  39.7 us (40%)
  starting transfers between devices  38.3 us (39%)
  waiting for transfers between devices  12.3 us (12%)
  local copies, waits for them, and re-layouts  4.44 us (4%)
  other arithmetic  2.46 us (2%)
  between operations  1.04 us (1%)
    pallas_call x6, Pallas kernels, call(): pl.pallas_call(kernel, out_shape=[jax.ShapeDtypeStruct(o, jnp.float32) fo...  35.4 us
    ppermute x3, starting transfers between devices, far(): return lax.ppermute(x, 'mass', [(0, 2), (2, 1), (1, 0)])  17 us
    ppermute x3, starting transfers between devices, per_device(): lax.ppermute(speed_gradient, 'mass', [(i, i ^ k) for i in range(4)])  7.09 us
    pallas_call x1, Pallas kernels, per_device(): pl.pallas_call(table_kernel, out_shape=[jax.ShapeDtypeStruct((3 * total_b...  4.27 us
    ppermute x3, starting transfers between devices, near(): return lax.ppermute(x, 'mass', [(0, 1), (1, 2)])  3.94 us
    ppermute x3, waiting for transfers between devices, per_device(): lax.ppermute(speed_gradient, 'mass', [(i, i ^ k) for i in range(4)])  3.87 us
    unnamed x32, local copies, waits for them, and re-layouts  3.33 us
    ppermute x4, starting transfers between devices, ending(): return lax.ppermute(x, 'mass', [(3, 2)])  2.97 us
  transfers between devices with their start and end apart: 19, of which 6 were waited for; matrix products, arithmetic and copies ran while one was open for 2% of the time, Pallas kernels for 40%

profile of v12, /device:TPU:0, one launch (start us, length us, event | category | flops | bytes accessed | tf_op | source)
XLA Modules:
  0.0 98.3 jit_solution(13437109564478412772)
XLA Ops:
  0.6 0.7 collective-permute-start.5
  1.4 4.5 %shard_map.149 = (f32[520,128]{1,0:T(8,128)}, f32[32,128]{1,0:T(8,128)}, f32[128,128]{1,0:T(8,128)}, f32[1320,128]{1,0:T(8,128)}, f32[168,128]{1,0:T(8,128)}, /*...) custom-call(f32[2048,128]{1,0:T(8,128)} %bitcast.19, f32[2048,128]{1,0:T(8,128)} %bitcast.15, ...), custom_call_target="tpu_custom_call" | custom-call | tf_op jit(solution)/shard_map/pallas_call | solution.py:450
  5.9 6.5 %collective-permute-start = (f32[1320,128]{1,0:T(8,128)}, f32[1320,128]{1,0:T(8,128)S(1)}, u32[]{:S(2)}, u32[]{:S(2)}) collective-permute-start(f32[1320,128]{1,0:T(8,128)} %get-tuple-element.49.refs_2_), channel_id=1, source_target_pairs={{0,2},{2,1},{1,0},{4,6},{6,5},{5,4},{8,10},{10,9},{9,8},{12,14},{1... | collective-permute-start | bytes 2027528 | tf_op jit(solution)/shard_map/ppermute | solution.py:486
  12.4 1.6 %collective-permute-start.2 = (f32[520,128]{1,0:T(8,128)}, f32[520,128]{1,0:T(8,128)S(1)}, u32[]{:S(2)}, u32[]{:S(2)}) collective-permute-start(f32[520,128]{1,0:T(8,128)} %get-tuple-element.50), channel_id=1, source_target_pairs={{0,16},{16,0},{1,17},{17,1},{2,18},{18,2},{3,19},{19,3},{4,20},{20... | collective-permute-start | bytes 798728 | tf_op jit(solution)/shard_map/ppermute | solution.py:529
  13.9 1.3 %collective-permute-start.1 = (f32[1320,128]{1,0:T(8,128)}, f32[1320,128]{1,0:T(8,128)S(1)}, u32[]{:S(2)}, u32[]{:S(2)}) collective-permute-start(f32[1320,128]{1,0:T(8,128)} %get-tuple-element.49.refs_2_), channel_id=1, source_target_pairs={{0,1},{1,2},{4,5},{5,6},{8,9},{9,10},{12,13},{13,14},{16,17},{17,1... | collective-permute-start | bytes 2027528 | tf_op jit(solution)/shard_map/ppermute | solution.py:489
  15.3 4.3 %shard_map.150 = (bf16[768,512]{1,0:T(8,128)(2,1)}, bf16[768,256]{1,0:T(8,128)(2,1)}, bf16[768,256]{1,0:T(8,128)(2,1)}) custom-call(f32[256,256]{1,0:T(8,128)} %gain_ref, s32[1,256]{1,0:T(1,128)} %bitcast.23, f32[1,256]{1,0:T(1,128)} %bitcast.24, f32[1,256]{1,0:T(1,128)} %bitcast.25, f32[1,256]{1,0:T(1,128)} %bitcast.26, s32[4,4]{1,0:T(4,128)} %pairs_ref.1), custom_call_target="tpu_custom_call" | custom-call | tf_op jit(solution)/shard_map/pallas_call | solution.py:540
  19.5 1.0 collective-permute-done.2.sides_ref
  21.2 1.9 %shard_map.151 = (f32[80,128]{1,0:T(8,128)}, f32[80,128]{1,0:T(8,128)}, f32[128,128]{1,0:T(8,128)}) custom-call(f32[520,128]{1,0:T(8,128)} %copy-done.4, f32[64,128]{1,0:T(8,128)} %bitcast.21, f32[64,128]{1,0:T(8,128)} %bitcast.22, f32[32,128]{1,0:T(8,128)} %get-tuple-element.57.gate_ref), custom_call_target="tpu_custom_call" | custom-call | tf_op jit(solution)/shard_map/pallas_call | solution.py:450
  23.1 1.4 %collective-permute-start.3 = (f32[80,128]{1,0:T(8,128)}, f32[80,128]{1,0:T(8,128)S(1)}, u32[]{:S(2)}, u32[]{:S(2)}) collective-permute-start(f32[80,128]{1,0:T(8,128)} %get-tuple-element.58), channel_id=1, source_target_pairs={{0,4},{4,8},{8,12},{1,5},{5,9},{9,13},{2,6},{6,10},{10,14},{3,7},{... | collective-permute-start | bytes 122888 | tf_op jit(solution)/shard_map/ppermute | solution.py:562
  24.5 1.3 %collective-permute-start.4 = (f32[80,128]{1,0:T(8,128)}, f32[80,128]{1,0:T(8,128)S(1)}, u32[]{:S(2)}, u32[]{:S(2)}) collective-permute-start(f32[80,128]{1,0:T(8,128)} %get-tuple-element.59), channel_id=1, source_target_pairs={{4,0},{8,4},{12,8},{5,1},{9,5},{13,9},{6,2},{10,6},{14,10},{7,3},{... | collective-permute-start | bytes 122888 | tf_op jit(solution)/shard_map/ppermute | solution.py:563
  25.8 1.1 %slice.9 = f32[1152,128]{1,0:T(8,128)S(1)} slice(f32[1320,128]{1,0:T(8,128)} %get-tuple-element.49.refs_2_), slice={[0:1152], [0:128]} | slice | bytes 1179648 | tf_op jit(solution)/shard_map/slice | solution.py:574
  27.0 2.6 %collective-permute-done.4.right_ref = f32[80,128]{1,0:T(8,128)S(1)} collective-permute-done((f32[80,128]{1,0:T(8,128)}, f32[80,128]{1,0:T(8,128)S(1)}, u32[]{:S(2)}, u32[]{:S(2)}) %collective-permute-start.4) | collective-permute-done | bytes 40992 | tf_op jit(solution)/shard_map/ppermute | solution.py:563
  30.2 1.9 %shard_map.152 = (f32[568,128]{1,0:T(8,128)}, f32[400,128]{1,0:T(8,128)}, f32[160,128]{1,0:T(8,128)}) custom-call(f32[80,128]{1,0:T(8,128)} %copy-done.14, f32[80,128]{1,0:T(8,128)} %copy-done.15, f32[520,128]{1,0:T(8,128)} %copy-done.4, f32[168,128]{1,0:T(8,128)} %get-tuple-element.60.shares_ref.refs_4_, f32[128,128]{1,0:T(8,128)} %get-tuple-element.62.gates_ref), custom_call_target="tpu_custom_call" | custom-call | tf_op jit(solution)/shard_map/pallas_call | solution.py:450
  33.5 5.3 %collective-permute-start.8 = (f32[400,128]{1,0:T(8,128)}, f32[400,128]{1,0:T(8,128)S(1)}, u32[]{:S(2)}, u32[]{:S(2)}) collective-permute-start(f32[400,128]{1,0:T(8,128)} %get-tuple-element.71.refs_6_), channel_id=1, source_target_pairs={{0,2},{2,1},{1,0},{4,6},{6,5},{5,4},{8,10},{10,9},{9,8},{12,14},{1... | collective-permute-start | bytes 614408 | tf_op jit(solution)/shard_map/ppermute | solution.py:486
  38.8 1.3 %collective-permute-start.9 = (f32[400,128]{1,0:T(8,128)}, f32[400,128]{1,0:T(8,128)S(1)}, u32[]{:S(2)}, u32[]{:S(2)}) collective-permute-start(f32[400,128]{1,0:T(8,128)} %get-tuple-element.71.refs_6_), channel_id=1, source_target_pairs={{0,1},{1,2},{4,5},{5,6},{8,9},{9,10},{12,13},{13,14},{16,17},{17,1... | collective-permute-start | bytes 614408 | tf_op jit(solution)/shard_map/ppermute | solution.py:489
  40.1 2.6 %collective-permute-done.1.refs_3_.refs_1_ = f32[1320,128]{1,0:T(8,128)S(1)} collective-permute-done((f32[1320,128]{1,0:T(8,128)}, f32[1320,128]{1,0:T(8,128)S(1)}, u32[]{:S(2)}, u32[]{:S(2)}) %collective-permute-start.1) | collective-permute-done | bytes 675872 | tf_op jit(solution)/shard_map/ppermute | solution.py:489
  42.8 5.2 %collective-permute-start.11 = (f32[896,128]{1,0:T(8,128)S(1)}, f32[896,128]{1,0:T(8,128)S(1)}, u32[]{:S(2)}, u32[]{:S(2)}) collective-permute-start(f32[896,128]{1,0:T(8,128)S(1)} %copy-done.10), channel_id=1, source_target_pairs={{0,2},{2,1},{1,0},{4,6},{6,5},{5,4},{8,10},{10,9},{9,8},{12,14},{1... | collective-permute-start | bytes 1376264 | tf_op jit(solution)/shard_map/ppermute | solution.py:486
  48.0 1.3 %collective-permute-start.12 = (f32[896,128]{1,0:T(8,128)S(1)}, f32[896,128]{1,0:T(8,128)S(1)}, u32[]{:S(2)}, u32[]{:S(2)}) collective-permute-start(f32[896,128]{1,0:T(8,128)S(1)} %copy-done.10), channel_id=1, source_target_pairs={{0,1},{1,2},{4,5},{5,6},{8,9},{9,10},{12,13},{13,14},{16,17},{17,1... | collective-permute-start | bytes 1376264 | tf_op jit(solution)/shard_map/ppermute | solution.py:489
  49.4 9.9 %shard_map.153 = (f32[17,128,128]{2,1,0:T(8,128)}, f32[15,128,128]{2,1,0:T(8,128)}, f32[18,2,128,128]{3,2,1,0:T(8,128)}, f32[14,2,128,128]{3,2,1,0:T(8,128)}, f3...) custom-call(f32[2048,128]{1,0:T(8,128)} %bitcast.16, ...), custom_call_target="tpu_custom_call" | custom-call | tf_op jit(solution)/shard_map/pallas_call | solution.py:450
  59.3 0.9 collective-permute-start.13
  60.3 0.8 copy-done
  61.1 9.1 %shard_map.154 = (f32[1024,128]{1,0:T(8,128)}, f32[1032,128]{1,0:T(8,128)}, f32[128,128]{1,0:T(8,128)}, f32[2,2,160,128]{3,2,1,0:T(8,128)}, f32[2,160,128]{2,1,0:T(8,128)}) custom-call(f32[1320,128]{1,0:T(8,128)} %copy-done.1, f32[1320,128]{1,0:T(8,128)} %copy-done.2, f32[1320,128]{1,0:T(8,128)} %get-tuple-element.49.refs_2_, f32[1408,128]{1,0:T(8,128)} %copy-done, ...), custom_call_target="tpu_custom_call" | custom-call | tf_op jit(solution)/shard_map/pallas_call | solution.py:450
  71.0 0.7 copy-done.11
  72.1 8.2 %shard_map.155 = (f32[1024,128]{1,0:T(8,128)}, f32[1024,128]{1,0:T(8,128)}, f32[1,128]{1,0:T(1,128)}) custom-call(f32[896,128]{1,0:T(8,128)} %copy-done.11, f32[896,128]{1,0:T(8,128)} %copy-done.12, f32[896,128]{1,0:T(8,128)} %get-tuple-element.84.refs_2_, f32[896,128]{1,0:T(8,128)} %copy-done.13, f32[400,128]{1,0:T(8,128)} %copy-done.6, ...), custom_call_target="tpu_custom_call" | custom-call | tf_op jit(solution)/shard_map/pallas_call | solution.py:450
  80.3 0.8 collective-permute-start.14
  81.2 1.6 %collective-permute-start.15 = (f32[1,128]{1,0:T(1,128)}, f32[1,128]{1,0:T(1,128)S(1)}, u32[]{:S(2)}, u32[]{:S(2)}) collective-permute-start(f32[1,128]{1,0:T(1,128)} %get-tuple-element.95), channel_id=1, source_target_pairs={{0,16},{16,0},{1,17},{17,1},{2,18},{18,2},{3,19},{19,3},{4,20},{20... | collective-permute-start | bytes 1544 | tf_op jit(solution)/shard_map/ppermute | solution.py:651
  82.7 2.2 %collective-permute-done.15 = f32[1,128]{1,0:T(1,128)S(1)} collective-permute-done((f32[1,128]{1,0:T(1,128)}, f32[1,128]{1,0:T(1,128)S(1)}, u32[]{:S(2)}, u32[]{:S(2)}) %collective-permute-start.15) | collective-permute-done | bytes 544 | tf_op jit(solution)/shard_map/ppermute | solution.py:651
  85.6 1.7 %collective-permute-start.16 = (f32[1,128]{1,0:T(1,128)S(1)}, f32[1,128]{1,0:T(1,128)S(1)}, u32[]{:S(2)}, u32[]{:S(2)}) collective-permute-start(f32[1,128]{1,0:T(1,128)S(1)} %add.12), channel_id=1, source_target_pairs={{0,1},{1,0},{2,3},{3,2},{4,5},{5,4},{6,7},{7,6},{8,9},{9,8},{10,11... | collective-permute-start | bytes 1544 | tf_op jit(solution)/shard_map/ppermute | solution.py:653
  87.2 4.0 %collective-permute-start.17 = (f32[1,128]{1,0:T(1,128)S(1)}, f32[1,128]{1,0:T(1,128)S(1)}, u32[]{:S(2)}, u32[]{:S(2)}) collective-permute-start(f32[1,128]{1,0:T(1,128)S(1)} %add.12), channel_id=1, source_target_pairs={{0,2},{1,3},{2,0},{3,1},{4,6},{5,7},{6,4},{7,5},{8,10},{9,11},{10,... | collective-permute-start | bytes 1544 | tf_op jit(solution)/shard_map/ppermute | solution.py:653
  91.2 1.5 %collective-permute-start.18 = (f32[1,128]{1,0:T(1,128)S(1)}, f32[1,128]{1,0:T(1,128)S(1)}, u32[]{:S(2)}, u32[]{:S(2)}) collective-permute-start(f32[1,128]{1,0:T(1,128)S(1)} %add.12), channel_id=1, source_target_pairs={{0,3},{1,2},{2,1},{3,0},{4,7},{5,6},{6,5},{7,4},{8,11},{9,10},{10,... | collective-permute-start | bytes 1544 | tf_op jit(solution)/shard_map/ppermute | solution.py:653
  92.7 3.8 %collective-permute-done.18 = f32[1,128]{1,0:T(1,128)S(1)} collective-permute-done((f32[1,128]{1,0:T(1,128)S(1)}, f32[1,128]{1,0:T(1,128)S(1)}, u32[]{:S(2)}, u32[]{:S(2)}) %collective-permute-start.18) | collective-permute-done | bytes 544 | tf_op jit(solution)/shard_map/ppermute | solution.py:653
  97.2 1.1 %pad_maximum_fusion = f32[64,32,128]{2,1,0:T(8,128)} fusion(f32[64,16,128]{2,1,0:T(8,128)S(1)} %bitcast.18, f32[64,16,128]{2,1,0:T(8,128)S(1)} %bitcast.17), kind=kLoop, calls=%fused_computation | loop fusion | flops 262144 | bytes 2097152 | tf_op jit(solution)/shard_map/concatenate | solution.py:656
  (54 shorter events, 5.3 us)
Async XLA Ops:
  0.6 26.3 %collective-permute-start.5 = (f32[64,32,128]{2,1,0:T(8,128)}, f32[64,32,128]{2,1,0:T(8,128)S(1)}, u32[]{:S(2)}, u32[]{:S(2)}) collective-permute-start(f32[64,32,128]{2,1,0:T(8,128)} %param.14), channel_id=1, source_target_pairs={{3,2},{7,6},{11,10},{15,14},{19,18},{23,22},{27,26},{31,30}} | collective-permute-start | bytes 3145736 | tf_op jit(solution)/shard_map/ppermute | solution.py:492
  5.9 32.9 %collective-permute-start = (f32[1320,128]{1,0:T(8,128)}, f32[1320,128]{1,0:T(8,128)S(1)}, u32[]{:S(2)}, u32[]{:S(2)}) collective-permute-start(f32[1320,128]{1,0:T(8,128)} %get-tuple-element.49.refs_2_), channel_id=1, source_target_pairs={{0,2},{2,1},{1,0},{4,6},{6,5},{5,4},{8,10},{10,9},{9,8},{12,14},{1... | collective-permute-start | bytes 2027528 | tf_op jit(solution)/shard_map/ppermute | solution.py:486
  12.4 8.1 %collective-permute-start.2 = (f32[520,128]{1,0:T(8,128)}, f32[520,128]{1,0:T(8,128)S(1)}, u32[]{:S(2)}, u32[]{:S(2)}) collective-permute-start(f32[520,128]{1,0:T(8,128)} %get-tuple-element.50), channel_id=1, source_target_pairs={{0,16},{16,0},{1,17},{17,1},{2,18},{18,2},{3,19},{19,3},{4,20},{20... | collective-permute-start | bytes 798728 | tf_op jit(solution)/shard_map/ppermute | solution.py:529
  13.9 28.8 %collective-permute-start.1 = (f32[1320,128]{1,0:T(8,128)}, f32[1320,128]{1,0:T(8,128)S(1)}, u32[]{:S(2)}, u32[]{:S(2)}) collective-permute-start(f32[1320,128]{1,0:T(8,128)} %get-tuple-element.49.refs_2_), channel_id=1, source_target_pairs={{0,1},{1,2},{4,5},{5,6},{8,9},{9,10},{12,13},{13,14},{16,17},{17,1... | collective-permute-start | bytes 2027528 | tf_op jit(solution)/shard_map/ppermute | solution.py:489
  21.2 21.6 %copy-start.10 = (f32[896,128]{1,0:T(8,128)S(1)}, f32[896,128]{1,0:T(8,128)}, u32[]{:S(2)}) copy-start(f32[896,128]{1,0:T(8,128)} %get-tuple-element.84.refs_2_) | copy-start | bytes 1376260
  23.1 9.7 %slice-start = ((f32[520,128]{1,0:T(8,128)}), f32[256,128]{1,0:T(8,128)S(1)}, s32[]{:S(2)}) async-start(f32[520,128]{1,0:T(8,128)} %copy-done.4), calls=%async_computation | async-start | bytes 262144 | tf_op jit(solution)/shard_map/slice | solution.py:574
  23.1 3.9 %collective-permute-start.3 = (f32[80,128]{1,0:T(8,128)}, f32[80,128]{1,0:T(8,128)S(1)}, u32[]{:S(2)}, u32[]{:S(2)}) collective-permute-start(f32[80,128]{1,0:T(8,128)} %get-tuple-element.58), channel_id=1, source_target_pairs={{0,4},{4,8},{8,12},{1,5},{5,9},{9,13},{2,6},{6,10},{10,14},{3,7},{... | collective-permute-start | bytes 122888 | tf_op jit(solution)/shard_map/ppermute | solution.py:562
  24.5 5.1 %collective-permute-start.4 = (f32[80,128]{1,0:T(8,128)}, f32[80,128]{1,0:T(8,128)S(1)}, u32[]{:S(2)}, u32[]{:S(2)}) collective-permute-start(f32[80,128]{1,0:T(8,128)} %get-tuple-element.59), channel_id=1, source_target_pairs={{4,0},{8,4},{12,8},{5,1},{9,5},{13,9},{6,2},{10,6},{14,10},{7,3},{... | collective-permute-start | bytes 122888 | tf_op jit(solution)/shard_map/ppermute | solution.py:563
  26.9 22.4 %copy-start.5 = (f32[64,32,128]{2,1,0:T(8,128)}, f32[64,32,128]{2,1,0:T(8,128)S(1)}, u32[]{:S(2)}) copy-start(f32[64,32,128]{2,1,0:T(8,128)S(1)} %collective-permute-done.5) | copy-start | bytes 3145732
  26.9 2.6 %copy-start.14 = (f32[80,128]{1,0:T(8,128)}, f32[80,128]{1,0:T(8,128)S(1)}, u32[]{:S(2)}) copy-start(f32[80,128]{1,0:T(8,128)S(1)} %collective-permute-done.3.left_ref) | copy-start | bytes 122884
  32.1 15.9 %collective-permute-start.7 = (f32[568,128]{1,0:T(8,128)}, f32[568,128]{1,0:T(8,128)S(1)}, u32[]{:S(2)}, u32[]{:S(2)}) collective-permute-start(f32[568,128]{1,0:T(8,128)} %get-tuple-element.66.refs_5_), channel_id=1, source_target_pairs={{3,2},{7,6},{11,10},{15,14},{19,18},{23,22},{27,26},{31,30}} | collective-permute-start | bytes 872456 | tf_op jit(solution)/shard_map/ppermute | solution.py:492
  32.8 27.4 %collective-permute-start.6 = (f32[1408,128]{1,0:T(8,128)S(1)}, f32[1408,128]{1,0:T(8,128)S(1)}, u32[]{:S(2)}, u32[]{:S(2)}) collective-permute-start(f32[1408,128]{1,0:T(8,128)S(1)} %pad_maximum_fusion.1), channel_id=1, source_target_pairs={{3,2},{7,6},{11,10},{15,14},{19,18},{23,22},{27,26},{31,30}} | collective-permute-start | bytes 2162696 | tf_op jit(solution)/shard_map/ppermute | solution.py:492
  33.5 25.8 %collective-permute-start.8 = (f32[400,128]{1,0:T(8,128)}, f32[400,128]{1,0:T(8,128)S(1)}, u32[]{:S(2)}, u32[]{:S(2)}) collective-permute-start(f32[400,128]{1,0:T(8,128)} %get-tuple-element.71.refs_6_), channel_id=1, source_target_pairs={{0,2},{2,1},{1,0},{4,6},{6,5},{5,4},{8,10},{10,9},{9,8},{12,14},{1... | collective-permute-start | bytes 614408 | tf_op jit(solution)/shard_map/ppermute | solution.py:486
  38.8 10.6 %copy-start.1 = (f32[1320,128]{1,0:T(8,128)}, f32[1320,128]{1,0:T(8,128)S(1)}, u32[]{:S(2)}) copy-start(f32[1320,128]{1,0:T(8,128)S(1)} %collective-permute-done.refs_2_.refs_0_) | copy-start | bytes 2027524
  38.8 20.5 %collective-permute-start.9 = (f32[400,128]{1,0:T(8,128)}, f32[400,128]{1,0:T(8,128)S(1)}, u32[]{:S(2)}, u32[]{:S(2)}) collective-permute-start(f32[400,128]{1,0:T(8,128)} %get-tuple-element.71.refs_6_), channel_id=1, source_target_pairs={{0,1},{1,2},{4,5},{5,6},{8,9},{9,10},{12,13},{13,14},{16,17},{17,1... | collective-permute-start | bytes 614408 | tf_op jit(solution)/shard_map/ppermute | solution.py:489
  42.8 6.6 %copy-start.2 = (f32[1320,128]{1,0:T(8,128)}, f32[1320,128]{1,0:T(8,128)S(1)}, u32[]{:S(2)}) copy-start(f32[1320,128]{1,0:T(8,128)S(1)} %collective-permute-done.1.refs_3_.refs_1_) | copy-start | bytes 2027524
  42.8 28.2 %collective-permute-start.11 = (f32[896,128]{1,0:T(8,128)S(1)}, f32[896,128]{1,0:T(8,128)S(1)}, u32[]{:S(2)}, u32[]{:S(2)}) collective-permute-start(f32[896,128]{1,0:T(8,128)S(1)} %copy-done.10), channel_id=1, source_target_pairs={{0,2},{2,1},{1,0},{4,6},{6,5},{5,4},{8,10},{10,9},{9,8},{12,14},{1... | collective-permute-start | bytes 1376264 | tf_op jit(solution)/shard_map/ppermute | solution.py:486
  48.0 1.4 %copy-start.3 = (f32[568,128]{1,0:T(8,128)}, f32[568,128]{1,0:T(8,128)S(1)}, u32[]{:S(2)}) copy-start(f32[568,128]{1,0:T(8,128)S(1)} %collective-permute-done.7.refs_6_.refs_7_) | copy-start | bytes 872452
  48.0 22.9 %collective-permute-start.12 = (f32[896,128]{1,0:T(8,128)S(1)}, f32[896,128]{1,0:T(8,128)S(1)}, u32[]{:S(2)}, u32[]{:S(2)}) collective-permute-start(f32[896,128]{1,0:T(8,128)S(1)} %copy-done.10), channel_id=1, source_target_pairs={{0,1},{1,2},{4,5},{5,6},{8,9},{9,10},{12,13},{13,14},{16,17},{17,1... | collective-permute-start | bytes 1376264 | tf_op jit(solution)/shard_map/ppermute | solution.py:489
  59.3 0.9 copy-start.6
  59.3 0.9 copy-start.7
  59.3 11.6 %collective-permute-start.13 = (f32[896,128]{1,0:T(8,128)S(1)}, f32[896,128]{1,0:T(8,128)S(1)}, u32[]{:S(2)}, u32[]{:S(2)}) collective-permute-start(f32[896,128]{1,0:T(8,128)S(1)} %copy-done.10), channel_id=1, source_target_pairs={{3,2},{7,6},{11,10},{15,14},{19,18},{23,22},{27,26},{31,30}} | collective-permute-start | bytes 1376264 | tf_op jit(solution)/shard_map/ppermute | solution.py:492
  70.2 26.8 %collective-permute-start.10 = (f32[1032,128]{1,0:T(8,128)}, f32[1032,128]{1,0:T(8,128)S(1)}, u32[]{:S(2)}, u32[]{:S(2)}) collective-permute-start(f32[1032,128]{1,0:T(8,128)} %get-tuple-element.83), channel_id=1, source_target_pairs={{2,3},{6,7},{10,11},{14,15},{18,19},{22,23},{26,27},{30,31}} | collective-permute-start | bytes 1585160 | tf_op jit(solution)/shard_map/ppermute | solution.py:495
  71.0 1.0 copy-start.12
  71.0 1.1 %copy-start.13 = (f32[896,128]{1,0:T(8,128)}, f32[896,128]{1,0:T(8,128)S(1)}, u32[]{:S(2)}) copy-start(f32[896,128]{1,0:T(8,128)S(1)} %collective-permute-done.13.refs_3_) | copy-start | bytes 1376260
  72.1 24.9 %copy-start.8 = (f32[1024,128]{1,0:T(8,128)S(1)}, f32[1024,128]{1,0:T(8,128)}, u32[]{:S(2)}) copy-start(f32[1024,128]{1,0:T(8,128)} %get-tuple-element.92) | copy-start | bytes 1572868
  80.3 16.8 %copy-start.9 = (f32[1024,128]{1,0:T(8,128)S(1)}, f32[1024,128]{1,0:T(8,128)}, u32[]{:S(2)}) copy-start(f32[1024,128]{1,0:T(8,128)} %get-tuple-element.94) | copy-start | bytes 1572868
  80.3 16.7 %collective-permute-start.14 = (f32[1024,128]{1,0:T(8,128)}, f32[1024,128]{1,0:T(8,128)S(1)}, u32[]{:S(2)}, u32[]{:S(2)}) collective-permute-start(f32[1024,128]{1,0:T(8,128)} %get-tuple-element.90), channel_id=1, source_target_pairs={{2,3},{6,7},{10,11},{14,15},{18,19},{22,23},{26,27},{30,31}} | collective-permute-start | bytes 1572872 | tf_op jit(solution)/shard_map/ppermute | solution.py:495
  81.2 3.7 %collective-permute-start.15 = (f32[1,128]{1,0:T(1,128)}, f32[1,128]{1,0:T(1,128)S(1)}, u32[]{:S(2)}, u32[]{:S(2)}) collective-permute-start(f32[1,128]{1,0:T(1,128)} %get-tuple-element.95), channel_id=1, source_target_pairs={{0,16},{16,0},{1,17},{17,1},{2,18},{18,2},{3,19},{19,3},{4,20},{20... | collective-permute-start | bytes 1544 | tf_op jit(solution)/shard_map/ppermute | solution.py:651
  85.6 7.1 %collective-permute-start.16 = (f32[1,128]{1,0:T(1,128)S(1)}, f32[1,128]{1,0:T(1,128)S(1)}, u32[]{:S(2)}, u32[]{:S(2)}) collective-permute-start(f32[1,128]{1,0:T(1,128)S(1)} %add.12), channel_id=1, source_target_pairs={{0,1},{1,0},{2,3},{3,2},{4,5},{5,4},{6,7},{7,6},{8,9},{9,8},{10,11... | collective-permute-start | bytes 1544 | tf_op jit(solution)/shard_map/ppermute | solution.py:653
  87.2 5.5 %collective-permute-start.17 = (f32[1,128]{1,0:T(1,128)S(1)}, f32[1,128]{1,0:T(1,128)S(1)}, u32[]{:S(2)}, u32[]{:S(2)}) collective-permute-start(f32[1,128]{1,0:T(1,128)S(1)} %add.12), channel_id=1, source_target_pairs={{0,2},{1,3},{2,0},{3,1},{4,6},{5,7},{6,4},{7,5},{8,10},{9,11},{10,... | collective-permute-start | bytes 1544 | tf_op jit(solution)/shard_map/ppermute | solution.py:653
  91.2 5.3 %collective-permute-start.18 = (f32[1,128]{1,0:T(1,128)S(1)}, f32[1,128]{1,0:T(1,128)S(1)}, u32[]{:S(2)}, u32[]{:S(2)}) collective-permute-start(f32[1,128]{1,0:T(1,128)S(1)} %add.12), channel_id=1, source_target_pairs={{0,3},{1,2},{2,1},{3,0},{4,7},{5,6},{6,5},{7,4},{8,11},{9,10},{10,... | collective-permute-start | bytes 1544 | tf_op jit(solution)/shard_map/ppermute | solution.py:653
  (4 other events, 2.9 us)
